TPU v7x, 32 devices: a whole 2x2x4 slice. The times are simulated.
32 devices in a mesh: dp: 4 (over y, core), ctx: 8 (over z, x), tp: 1.
Axes of the slice: x: 2, y: 2, z: 4, core: 2. Of those that a mesh axis runs over, the one named last changes fastest.
Arguments:
- queries: bfloat16 [4, 1024, 4096], P('dp', 'ctx', 'tp'), may hold values from -6 to 6
- keys: bfloat16 [4, 1024, 512], P('dp', 'ctx', 'tp'), may hold values from -6 to 6
- values: bfloat16 [4, 1024, 512], P('dp', 'ctx', 'tp'), may hold values from -6 to 6
- out_grad: bfloat16 [4, 1024, 4096], P('dp', 'ctx', 'tp'), may hold values from -6 to 6
- mixed_grad: bfloat16 [4096, 2048], P(('dp', 'ctx'), 'tp'), may hold values from -6 to 6
- expert_ids: int32 [4096, 8], P(('dp', 'ctx')), may hold values from 0 to 31, all different within a row; in each aligned block of 128 rows (0 to 127, 128 to 255, ...) at most 40 rows name the same one
- combine: bfloat16 [4096, 8], P(('dp', 'ctx')), may hold values from 0.049804688 to 1
- w_down: bfloat16 [32, 1536, 2048], P(('dp', 'ctx'), 'tp'), may hold values from -0.125 to 0.125
Outputs:
- query_grad: bfloat16 [4, 1024, 4096], P('dp', 'ctx', 'tp')
- key_grad: bfloat16 [4, 1024, 512], P('dp', 'ctx', 'tp')
- value_grad: bfloat16 [4, 1024, 512], P('dp', 'ctx', 'tp')
- hidden_grad: bfloat16 [32, 32, 40, 1536], P(('dp', 'ctx'), None, None, 'tp')
Inputs may be any that keep to these rules, and one draw needn't show every extreme that they name: `expert_ids`: each row names 8 distinct experts. Within each aligned block of 128 rows no expert is named more than 40 times, a bound that some block reaches.
All inputs are finite; a program needn't handle non-finite values.
Results may differ from a plain program's by a relative error of at most 0.0071.
Values may be sent and summed in bfloat16 or wider, within the bound.
No kernel may reach another device: no remote copies, remote signals or barrier semaphores. Data moves between devices by JAX's collectives and lax.ppermute only.
A program may use at most 128 MiB of HBM per device.

v0:
```python
import math

import jax
import jax.numpy as jnp
from jax import lax
from jax.sharding import PartitionSpec as P

HEADS = 32
KV_HEADS = 4
HEAD_DIM = 128
TOPK = 8


masked_score = -1e30


def make_set(query_rows, grad_rows, first_row, kv_local):
    row_count = query_rows.shape[0]
    positions = first_row + jnp.arange(row_count, dtype=jnp.int32)
    return (
        query_rows.reshape(row_count, kv_local, -1, HEAD_DIM),
        grad_rows.reshape(row_count, kv_local, -1, HEAD_DIM),
        positions,
    )


def key_blocks(piece):
    key_part, value_part = piece
    length = key_part.shape[0]
    block_size = math.gcd(length, 512)
    shape = (length // block_size, block_size) + key_part.shape[1:]
    return (key_part.reshape(shape), value_part.reshape(shape), block_size)


def block_scores(query_rows, positions, key_block, block_start, score_scale):
    scores = (
        jnp.einsum("rghd,sgd->ghrs", query_rows, key_block, preferred_element_type=jnp.float32)
        * score_scale
    )
    key_places = block_start + jnp.arange(key_block.shape[0], dtype=jnp.int32)
    allowed = key_places[None, :] <= positions[:, None]
    return (jnp.where(allowed, scores, masked_score), allowed)


def stats_update(state, query_set, key_block, value_block, block_start, score_scale):
    query_rows, grad_rows, positions = query_set

    def stats_compute(state):
        top, total, accum = state
        scores, allowed = block_scores(query_rows, positions, key_block, block_start, score_scale)
        new_top = jnp.maximum(top, jnp.max(scores, axis=-1))
        weights = jnp.where(allowed, jnp.exp(scores - new_top[..., None]), 0.0)
        grads = jnp.einsum(
            "rghd,sgd->ghrs", grad_rows, value_block, preferred_element_type=jnp.float32
        )
        shrink = jnp.exp(top - new_top)
        return (
            new_top,
            total * shrink + jnp.sum(weights, axis=-1),
            accum * shrink + jnp.sum(weights * grads, axis=-1),
        )

    return lax.cond(block_start <= positions[-1], stats_compute, lambda kept: kept, state)


def grads_update(
    state, query_set, stats, key_block, value_block, block_start, slot_start, score_scale
):
    query_rows, grad_rows, positions = query_set
    log_total, delta = stats

    def grads_compute(state):
        query_total, key_value_total = state
        scores, allowed = block_scores(query_rows, positions, key_block, block_start, score_scale)
        probs = jnp.where(allowed, jnp.exp(scores - log_total[..., None]), 0.0)
        grads = jnp.einsum(
            "rghd,sgd->ghrs", grad_rows, value_block, preferred_element_type=jnp.float32
        )
        dscore = probs * (grads - delta[..., None])
        probs_low = probs.astype(jnp.bfloat16)
        dscore_low = dscore.astype(jnp.bfloat16)
        query_total = query_total + jnp.einsum(
            "ghrs,sgd->rghd", dscore_low, key_block, preferred_element_type=jnp.float32
        )
        key_part = jnp.einsum(
            "ghrs,rghd->sgd", dscore_low, query_rows, preferred_element_type=jnp.float32
        )
        value_part = jnp.einsum(
            "ghrs,rghd->sgd", probs_low, grad_rows, preferred_element_type=jnp.float32
        )
        current = lax.dynamic_slice_in_dim(key_value_total, slot_start, key_block.shape[0], 0)
        key_value_total = lax.dynamic_update_slice_in_dim(
            key_value_total, current + jnp.stack([key_part, value_part], axis=1), slot_start, 0
        )
        return (query_total, key_value_total)

    return lax.cond(block_start <= positions[-1], grads_compute, lambda kept: kept, state)


def per_device(queries, keys, values, out_grad, mixed_grad, expert_ids, combine, w_down):
    score_scale = HEAD_DIM ** (-0.5)
    local_queries = queries[0]
    local_grads = out_grad[0]
    rows_dev = local_queries.shape[0]
    kv_local = keys.shape[2] // HEAD_DIM
    group = HEADS // KV_HEADS
    n_ctx = lax.axis_size("ctx")
    position = lax.axis_index("ctx")
    all_keys = rows_dev * n_ctx
    key_heads = keys[0].reshape(rows_dev, kv_local, HEAD_DIM)
    value_heads = values[0].reshape(rows_dev, kv_local, HEAD_DIM)
    query_sets = (make_set(local_queries, local_grads, position * rows_dev, kv_local),)
    stats_start = tuple(
        (
            (
                jnp.full((kv_local, group, query_set[2].shape[0]), masked_score, jnp.float32),
                jnp.zeros((kv_local, group, query_set[2].shape[0]), jnp.float32),
                jnp.zeros((kv_local, group, query_set[2].shape[0]), jnp.float32),
            )
            for query_set in query_sets
        )
    )
    carry = stats_start
    key_stack, value_stack, block_size = key_blocks(
        (
            lax.all_gather(key_heads, "ctx", axis=0, tiled=True),
            lax.all_gather(value_heads, "ctx", axis=0, tiled=True),
        )
    )

    def stats_one_block(index, carry):
        block_start = index * block_size
        return tuple(
            (
                stats_update(
                    state, query_set, key_stack[index], value_stack[index], block_start, score_scale
                )
                for state, query_set in zip(carry, query_sets)
            )
        )

    stats_done = lax.fori_loop(0, key_stack.shape[0], stats_one_block, carry)
    row_stats = tuple(((top + jnp.log(total), accum / total) for top, total, accum in stats_done))
    query_start = tuple(
        (
            jnp.zeros((query_set[2].shape[0], kv_local, group, HEAD_DIM), jnp.float32)
            for query_set in query_sets
        )
    )
    grads_start = (query_start, jnp.zeros((all_keys, 2, kv_local, HEAD_DIM), jnp.float32))
    carry = grads_start
    run_key_stack, run_value_stack, run_block_size = key_blocks(
        (
            lax.all_gather(key_heads, "ctx", axis=0, tiled=True),
            lax.all_gather(value_heads, "ctx", axis=0, tiled=True),
        )
    )

    def run_one_block(index, carry):
        query_totals, key_value_total = carry
        block_start = index * run_block_size
        slot_start = index * run_block_size
        new_totals = []
        for query_total, query_set, stats in zip(query_totals, query_sets, row_stats):
            query_total, key_value_total = grads_update(
                (query_total, key_value_total),
                query_set,
                stats,
                run_key_stack[index],
                run_value_stack[index],
                block_start,
                slot_start,
                score_scale,
            )
            new_totals.append(query_total)
        return (tuple(new_totals), key_value_total)

    query_totals, key_value_total = lax.fori_loop(0, run_key_stack.shape[0], run_one_block, carry)
    key_value_own = lax.psum_scatter(key_value_total, "ctx", scatter_dimension=0, tiled=True)
    key_grad = (key_value_own[:, 0] * score_scale).astype(jnp.bfloat16).reshape(1, rows_dev, -1)
    value_grad = key_value_own[:, 1].astype(jnp.bfloat16).reshape(1, rows_dev, -1)
    query_parts = [
        (total * score_scale).astype(jnp.bfloat16).reshape(total.shape[0], -1)
        for total in query_totals
    ]
    query_grad = query_parts[0].reshape(1, rows_dev, -1)
    local_experts = w_down.shape[0]
    experts_all = lax.axis_size(("dp", "ctx")) * local_experts
    token_rows = expert_ids.shape[0]
    capacity = min(
        token_rows,
        max(
            2,
            token_rows * TOPK * 5 // (4 * experts_all),
            (token_rows * TOPK + experts_all - 1) // experts_all,
        ),
    )
    flat_ids = expert_ids.reshape(-1)
    hits = (flat_ids[:, None] == jnp.arange(experts_all, dtype=jnp.int32)[None, :]).astype(
        jnp.int32
    )
    ranks = jnp.cumsum(hits, axis=0)
    slot_of = jnp.sum(hits * ranks, axis=1) - 1
    target = flat_ids * capacity + slot_of
    chosen = jnp.arange(experts_all * capacity, dtype=jnp.int32)[:, None] == target[None, :]
    token_pick = (
        chosen.reshape(experts_all * capacity, token_rows, TOPK).sum(axis=2).astype(jnp.bfloat16)
    )
    slot_weights = (
        jnp.dot(
            chosen.astype(jnp.bfloat16), combine.reshape(-1), preferred_element_type=jnp.float32
        )
        .astype(jnp.bfloat16)
        .reshape(experts_all, capacity)
    )
    full_rows = lax.all_gather(mixed_grad, "tp", axis=1, tiled=True)
    send_rows = (
        jnp.dot(token_pick, full_rows, preferred_element_type=jnp.float32)
        .astype(jnp.bfloat16)
        .reshape(experts_all, capacity, -1)
    )
    rows = lax.all_to_all(send_rows, ("dp", "ctx"), split_axis=0, concat_axis=0, tiled=True)
    sources = rows.shape[0] // local_experts
    row_view = rows.reshape(sources, local_experts, rows.shape[1], rows.shape[2])
    hidden = jnp.einsum("sejf,ehf->esjh", row_view, w_down, preferred_element_type=jnp.float32)
    weight_view = (
        lax.all_to_all(slot_weights, ("dp", "ctx"), split_axis=0, concat_axis=0, tiled=True)
        .reshape(sources, local_experts, -1)
        .transpose(1, 0, 2)
        .astype(jnp.float32)
    )
    hidden_grad = (hidden * weight_view[..., None]).astype(jnp.bfloat16)
    return (query_grad, key_grad, value_grad, hidden_grad)


def solution(mesh):
    placed = (
        P("dp", "ctx", "tp"),
        P("dp", "ctx", "tp"),
        P("dp", "ctx", "tp"),
        P("dp", "ctx", "tp"),
        P(("dp", "ctx"), "tp"),
        P(("dp", "ctx"), None),
        P(("dp", "ctx"), None),
        P(("dp", "ctx"), "tp", None),
    )
    return jax.shard_map(
        per_device,
        mesh=mesh,
        in_specs=placed,
        out_specs=(
            P("dp", "ctx", "tp"),
            P("dp", "ctx", "tp"),
            P("dp", "ctx", "tp"),
            P(("dp", "ctx"), None, None, "tp"),
        ),
        check_vma=False,
    )
```

profile of v0, /device:TPU:0, one launch (start us, length us, event | category | flops | bytes accessed | tf_op | source)
XLA Modules:
  0.0 336.8 jit_solution(2095427233172440221)
XLA Ops:
  9.1 9.0 %reduce-window.6 = s32[32,8,128]{2,1,0:T(8,128)S(1)} reduce-window(s32[32,8,128]{2,1,0:T(8,128)S(1)} %fusion.50, s32[]{:T(128)} %copy.207), window={size=1x1x128 pad=0_0x0_0x127_0}, to_apply=%region_12.13 | reduce-window | flops 4161536 | bytes 262148 | tf_op jit(solution)/shard_map/reduce-window
  18.7 1.0 fusion.45
  20.3 7.3 %all-to-all-start.1 = ((bf16[32,1,40]{2,1,0:T(2,128)(2,1)}), bf16[32,1,40]{2,1,0:T(2,128)(2,1)S(1)}, u32[]{:S(2)}, u32[]{:S(2)}) async-start(bf16[32,1,40]{2,1,0:T(2,128)(2,1)} %all_to_all.12), calls=%async_computation.2 | async-start | bytes 32768 | tf_op jit(solution)/shard_map/all_to_all | solution.py:227
  27.7 1.7 copy.142
  30.2 6.7 %convert_reduce_fusion = s32[1280,128]{1,0:T(8,128)S(1)} fusion(s32[128,8]{0,1:T(8,128)S(1)} %multiply_add_fusion.3), kind=kLoop, calls=%fused_computation.53 | loop fusion | flops 3768320 | bytes 659456 | tf_op jit(solution)/shard_map/reduce_sum | solution.py:207
  36.9 3.8 %convolution_convert_fusion = bf16[1280,2048]{1,0:T(8,128)(2,1)} fusion(bf16[128,2048]{1,0:T(8,128)(2,1)S(1)} %copy-done, s32[1280,128]{1,0:T(8,128)S(1)} %convert_reduce_fusion), kind=kOutput, calls=%fused_computation.49 | convolution fusion | flops 673873920 | bytes 6422528 | tf_op jit(solution)/shard_map/dot_general | solution.py:218
  40.8 6.0 %all-to-all-start = ((bf16[32,40,2048]{2,1,0:T(8,128)(2,1)}), bf16[32,40,2048]{2,1,0:T(8,128)(2,1)}, u32[]{:S(2)}, u32[]{:S(2)}) async-start(bf16[32,40,2048]{2,1,0:T(8,128)(2,1)} %bitcast.134), calls=%async_computation.1 | async-start | bytes 10485760 | tf_op jit(solution)/shard_map/all_to_all | solution.py:222
  49.8 1.3 copy.151
  51.2 59.5 %all-gather.3.cloned.1.call-done = bf16[1024,4,128]{0,2,1:T(8,128)(2,1)} async-done(((bf16[128,4,128]{0,2,1:T(8,128)(2,1)}), bf16[1024,4,128]{0,2,1:T(8,128)(2,1)}) %all-gather.3.cloned.1.call-update) | async-done | bytes 1048592 | tf_op jit(solution)/shard_map/all_gather | solution.py:154
  110.7 1.6 copy.143
  112.3 1.0 copy.152
  113.4 60.0 %all-gather.5.cloned.1.call-done = bf16[1024,4,128]{0,2,1:T(8,128)(2,1)} async-done(((bf16[128,4,128]{0,2,1:T(8,128)(2,1)}), bf16[1024,4,128]{0,2,1:T(8,128)(2,1)}) %all-gather.5.cloned.1.call-update) | async-done | bytes 1048592 | tf_op jit(solution)/shard_map/all_gather | solution.py:155
  173.3 1.6 copy.146
  175.1 11.5 %while.32 = (s32[]{:T(128)}, f32[4,8,128]{2,1,0:T(8,128)S(1)}, f32[4,8,128]{2,1,0:T(8,128)S(1)}, f32[4,8,128]{2,1,0:T(8,128)S(1)}, s32[128]{0:T(128)S(1)}, /*ind...) while((s32[]{:T(128)}, f32[4,8,128]{2,1,0:T(8,128)S(1)}, ...), condition=%wide.region_6.7_spmd, body=%wide.region_0.6_spmd.sunk | while | flops 1103180288 | bytes 28874024 | solution.py:142
  176.4 8.7 %conditional.4 = ((f32[4,8,128]{2,1,0:T(8,128)S(1)}, f32[4,8,128]{2,1,0:T(8,128)S(1)}, f32[4,8,128]{2,1,0:T(8,128)S(1)})) conditional(s32[]{:T(128)} %convert_element_type.122, (f32[4,8,128]{2,1,0:T(8,128)S(1)}, f32[4,8,128]{2,1,0:T(8,128)S(1)}, f32[4,8,128]{2,1,0:T(8,128)S(1)}) %tuple.112, (s32[]{:T(128)}, s32[128]{0:T(128)S(1)}, ...), branch_computations={%region_1.0_spmd, %region_2.5_spmd} | conditional | flops 1103180288 | bytes 28873768 | solution.py:63
  176.6 2.3 fusion.1
  179.0 4.0 %fusion = f32[4,8,128]{2,1,0:T(8,128)S(1)} fusion(f32[4,512,128,8]{2,1,3,0:T(8,128)S(1)} %get-tuple-element.791, f32[4,8,128]{2,1,0:T(8,128)S(1)} %max.6, pred[128,512]{0,1:T(8,128)(4,1)S(1)} %broadcast_compare_fusion, bf16[128,4,8,128]{3,0,2,1:T(8,128)(2,1)} %get-tuple-element.584, bf16[2,512,4,128]{3,1,2,0:T(8,128)(2,1)S(1)} %get-tuple-element.583, ...), kind=kOutput, calls=%fused_computation.1 | convolution fusion | flops 549449728 | bytes 10059780 | tf_op jit(solution)/shard_map/while/body/eval_jaxpr/cond/branch_1_fun/rghd,sgd->ghrs/dot_general | solution.py:53
  183.0 2.1 fusion.2
  187.8 2.4 broadcast_in_dim.67
  190.2 20.4 %while.33 = (s32[]{:T(128)}, f32[128,4,8,128]{3,0,2,1:T(8,128)S(1)}, f32[1024,2,4,128]{3,0,2,1:T(8,128)}, s32[128]{0:T(128)S(1)}, bf16[2,512,4,128]{3,1,2,0:T(8,...) while((s32[]{:T(128)}, ...), condition=%wide.region_10.11_spmd, body=%wide.region_7.10_spmd.sunk | while | flops 2711159296 | bytes 60544872 | solution.py:178
  191.4 17.9 %conditional.5 = ((f32[128,4,8,128]{3,0,2,1:T(8,128)S(1)}, f32[1024,2,4,128]{3,0,2,1:T(8,128)})) conditional(s32[]{:T(128)} %convert_element_type.123, (f32[128,4,8,128]{3,0,2,1:T(8,128)S(1)}, f32[1024,2,4,128]{3,0,2,1:T(8,128)}) %tuple.115, (s32[]{:T(128)}, s32[128]{0:T(128)S(1)}, bf16[2,512,4,128]{3,1,2,0:T(8,128)(2,1)}, s32[]{:T(128)}, ...), branch_computations={%region_8.8_spmd, %region_9.9_spmd} | conditional | flops 2711159296 | bytes 60544608 | solution.py:97
  191.6 2.3 fusion.25
  193.9 3.2 fusion.20
  197.1 4.3 %fusion.11 = bf16[4,8,128,512]{2,3,1,0:T(8,128)(2,1)S(1)} fusion(f32[4,512,128,8]{2,1,3,0:T(8,128)S(1)} %fusion.25, f32[4,8,128]{2,1,0:T(8,128)S(1)} %get-tuple-element.607, f32[4,8,128]{2,1,0:T(8,128)S(1)} %get-tuple-element.604, pred[128,512]{0,1:T(8,128)(4,1)S(1)} %broadcast_compare_fusion.1, bf16[128,4,8,128]{3,0,2,1:T(8,128)(2,1)} %get-tuple-element.606, ...), kind=kOutput, calls=%fused_computation.20 | convolution fusion | flops 551550976 | bytes 14254084 | tf_op jit(solution)/shard_map/while/body/eval_jaxpr/cond/branch_1_fun/rghd,sgd->ghrs/dot_general | solution.py:76
  201.4 1.3 convolution_bitcast_fusion
  202.6 3.4 %bitcast_add_fusion = f32[128,4,8,128]{3,0,2,1:T(8,128)S(1)} fusion(f32[128,4,8,128]{3,0,2,1:T(8,128)S(1)} %get-tuple-element.598, bf16[4,8,128,512]{2,3,1,0:T(8,128)(2,1)S(1)} %fusion.11, bf16[2,512,4,128]{3,1,2,0:T(8,128)(2,1)} %get-tuple-element.601, s32[]{:T(128)} %get-tuple-element.602), kind=kOutput, calls=%fused_computation.30 | convolution fusion | flops 537395200 | bytes 8913408 | tf_op jit(solution)/shard_map/while/body/eval_jaxpr/cond/branch_1_fun/ghrs,sgd->rghd/dot_general | solution.py:82
  206.1 3.2 fusion.19
  211.6 1.3 reshape_reshape.3
  212.9 13.7 %fusion.41 = bf16[1,32,40,1536]{3,2,1,0:T(8,128)(2,1)} fusion(f32[32,40]{1,0:T(8,128)S(1)} %bitcast.143, bf16[32,40,2048]{2,1,0:T(8,128)(2,1)} %all-to-all-done, bf16[1,1536,2048]{2,1,0:T(8,128)(2,1)} %param.23), kind=kOutput, calls=%fused_computation.56 | convolution fusion | flops 8056995840 | bytes 15471616 | tf_op jit(solution)/shard_map/sejf,ehf->esjh/dot_general | solution.py:225
  226.6 100.1 %reduce-scatter.2.cloned.1.call-done = f32[128,2,4,128]{3,0,2,1:T(8,128)} async-done(((f32[1024,2,4,128]{3,0,2,1:T(8,128)}), f32[128,2,4,128]{3,0,2,1:T(8,128)}) %reduce-scatter.2.cloned.1.call-update) | async-done | bytes 524304 | tf_op jit(solution)/shard_map/reduce_scatter | solution.py:179
  326.7 1.0 fusion.47
  328.5 1.0 slice.39
  (75 shorter events, 13.9 us)
Async XLA Ops:
  7.2 29.7 %copy-start = (bf16[128,2048]{1,0:T(8,128)(2,1)S(1)}, bf16[128,2048]{1,0:T(8,128)(2,1)}, u32[]{:S(2)}) copy-start(bf16[128,2048]{1,0:T(8,128)(2,1)} %param.20) | copy-start | bytes 1572868
  20.3 20.4 %all-to-all-start.1 = ((bf16[32,1,40]{2,1,0:T(2,128)(2,1)}), bf16[32,1,40]{2,1,0:T(2,128)(2,1)S(1)}, u32[]{:S(2)}, u32[]{:S(2)}) async-start(bf16[32,1,40]{2,1,0:T(2,128)(2,1)} %all_to_all.12), calls=%async_computation.2 | async-start | bytes 32768 | tf_op jit(solution)/shard_map/all_to_all | solution.py:227
  27.7 83.0 %all-gather.3.cloned.1.call-start = ((), (), s32[]{:S(2)}) async-start(), calls=%async_computation.3 | async-start | bytes 1179648 | tf_op jit(solution)/shard_map/all_gather | solution.py:154
  40.7 6.0 %copy-start.6 = (bf16[1,128,512]{2,1,0:T(8,128)(2,1)S(1)}, bf16[1,128,512]{2,1,0:T(8,128)(2,1)}, u32[]{:S(2)}) copy-start(bf16[1,128,512]{2,1,0:T(8,128)(2,1)} %param.18) | copy-start | bytes 393220
  40.7 7.1 %copy-start.2 = (bf16[1,128,4096]{2,1,0:T(8,128)(2,1)S(1)}, bf16[1,128,4096]{2,1,0:T(8,128)(2,1)}, u32[]{:S(2)}) copy-start(bf16[1,128,4096]{2,1,0:T(8,128)(2,1)} %param.16) | copy-start | bytes 3145732
  40.7 7.1 %copy-start.7 = (bf16[32,1,40]{2,1,0:T(2,128)(2,1)}, bf16[32,1,40]{2,1,0:T(2,128)(2,1)S(1)}, u32[]{:S(2)}) copy-start(bf16[32,1,40]{2,1,0:T(2,128)(2,1)S(1)} %all-to-all-done.1) | copy-start | bytes 7684
  40.7 8.4 %copy-start.3 = (bf16[1,128,4096]{2,1,0:T(8,128)(2,1)S(1)}, bf16[1,128,4096]{2,1,0:T(8,128)(2,1)}, u32[]{:S(2)}) copy-start(bf16[1,128,4096]{2,1,0:T(8,128)(2,1)} %param.19) | copy-start | bytes 3145732
  40.8 172.2 %all-to-all-start = ((bf16[32,40,2048]{2,1,0:T(8,128)(2,1)}), bf16[32,40,2048]{2,1,0:T(8,128)(2,1)}, u32[]{:S(2)}, u32[]{:S(2)}) async-start(bf16[32,40,2048]{2,1,0:T(8,128)(2,1)} %bitcast.134), calls=%async_computation.1 | async-start | bytes 10485760 | tf_op jit(solution)/shard_map/all_to_all | solution.py:222
  46.7 126.6 %all-gather.5.cloned.1.call-start = ((), (), s32[]{:S(2)}) async-start(), calls=%async_computation.4 | async-start | bytes 1179648 | tf_op jit(solution)/shard_map/all_gather | solution.py:155
  47.6 279.1 %reduce-scatter.2.cloned.1.call-start = ((), (), s32[]{:S(2)}) async-start(), calls=%async_computation.5 | async-start | bytes 4718592 | tf_op jit(solution)/shard_map/reduce_scatter | solution.py:179
  186.5 1.0 copy-start.4
  190.2 20.5 %copy-start.8 = (bf16[32,1,40]{2,1,0:T(2,128)(2,1)S(1)}, bf16[32,1,40]{2,1,0:T(2,128)(2,1)}, u32[]{:S(2)}) copy-start(bf16[32,1,40]{2,1,0:T(2,128)(2,1)} %copy-done.7) | copy-start | bytes 7684
  193.9 3.2 copy-start.5
  212.9 117.4 %copy-start.1 = (bf16[128,2048]{1,0:T(8,128)(2,1)S(1)}, bf16[128,2048]{1,0:T(8,128)(2,1)}, u32[]{:S(2)}) copy-start(bf16[128,2048]{1,0:T(8,128)(2,1)} %param.20) | copy-start | bytes 1572868
Sparse Core Ops, SparseCore 0:
  31.1 79.5 all-gather.2
  113.3 59.9 all-gather.4
  210.7 115.9 reduce-scatter.1
where the time goes:
time: 338 us; the launch traced here: 337 us
  waiting for transfers between devices  220 us (65%)
  matrix products  39.2 us (12%)
  local copies, waits for them, and re-layouts  23.9 us (7%)
  other arithmetic  23.5 us (7%)
  between operations  14.1 us (4%)
  starting transfers between devices  13.6 us (4%)
    reduce_scatter x1, waiting for transfers between devices, per_device(): lax.psum_scatter(key_value_total, 'ctx', scatter_dimension=0, tiled=True)  100 us
    all_gather x1, waiting for transfers between devices, per_device(): lax.all_gather(value_heads, 'ctx', axis=0, tiled=True)  60 us
    all_gather x1, waiting for transfers between devices, per_device(): lax.all_gather(key_heads, 'ctx', axis=0, tiled=True)  59.5 us
    dot_general x1, matrix products, per_device(): jnp.einsum('sejf,ehf->esjh', row_view, w_down, preferred_element_type=jnp...  13.7 us
    another operation x3, other arithmetic  9.15 us
    all_to_all x1, starting transfers between devices, per_device(): lax.all_to_all(slot_weights, ('dp', 'ctx'), split_axis=0, concat_axis=0,...  7.3 us
  transfers between devices with their start and end apart: 5, of which 3 were waited for; matrix products, arithmetic and copies ran while one was open for 20% of the time, Pallas kernels for 0%

commit v1 on v0

v1 whole, which is shorter than its diff:
```python
import functools
import math

import jax
import jax.numpy as jnp
from jax import lax
from jax.experimental import pallas as pl
from jax.experimental.pallas import tpu as pltpu
from jax.sharding import PartitionSpec as P

HEADS = 32
KV_HEADS = 4
HEAD_DIM = 128
TOPK = 8

masked_score = -1e30
vmem_limit = 56 * 1024 * 1024


def mul(a, b):
    return jnp.dot(a, b, preferred_element_type=jnp.float32)


def attention_kernel(n_blocks, heads_step, rows, n_parts, place, q_ref, do_ref, *refs):
    kv_refs = refs[:n_blocks]
    n_pairs = n_blocks // 2
    dq_ref, dkv_refs = refs[-11 - n_pairs], refs[-10 - n_pairs : -10]
    kv_s, kt_s, q_s, do_s, qt_s, dot_s, s_s, dp_s, dkv_s, dqt_s = refs[-10:]
    part = pl.program_id(1)
    pair = 2 * rows
    width = heads_step * rows
    z, x = place[0], place[1]
    scale = HEAD_DIM ** (-0.5)
    to_exp2 = scale * math.log2(math.e)
    for i, ref in enumerate(kv_refs):
        kv_s[i * rows : (i + 1) * rows, :] = ref[...]
        kt_s[i // 2, :, (i % 2) * rows : (i % 2 + 1) * rows] = ref[:, :HEAD_DIM].T
    for h in range(heads_step):
        lanes = slice(h * HEAD_DIM, (h + 1) * HEAD_DIM)
        here = slice(h * rows, (h + 1) * rows)
        q_s[here, :] = q_ref[:, lanes]
        do_s[here, :] = do_ref[:, lanes]
        qt_s[:, here] = q_ref[:, lanes].T
        dot_s[:, here] = do_ref[:, lanes].T

    def part_of(k):
        return pl.ds(pl.multiple_of(k * pair, pair), pair)

    def scores(k, top, first):
        s = mul(kv_s[part_of(k), :HEAD_DIM], qt_s[...])
        if first:
            key = lax.broadcasted_iota(jnp.int32, (pair, width), 0)
            query = lax.broadcasted_iota(jnp.int32, (pair, width), 1) & (rows - 1)
            bound = jnp.where(key < rows, query, jnp.where(x == 1, pair, -1))
            s = jnp.where(key <= bound, s, masked_score)
        s_s[part_of(k), :] = s
        return jnp.maximum(top, jnp.max(s, axis=0, keepdims=True))

    top = scores(0, jnp.full((1, width), masked_score, jnp.float32), True)
    top = lax.fori_loop(1, z + 1, functools.partial(scores, first=False), top)

    def sums(k, carry):
        total, accum = carry
        dp = mul(kv_s[part_of(k), HEAD_DIM:], dot_s[...])
        e = jnp.exp2((s_s[part_of(k), :] - top) * to_exp2)
        s_s[part_of(k), :] = e
        dp_s[part_of(k), :] = dp
        return (
            total + jnp.sum(e, axis=0, keepdims=True),
            accum + jnp.sum(e * dp, axis=0, keepdims=True),
        )

    zero = jnp.zeros((1, width), jnp.float32)
    total, accum = lax.fori_loop(0, z + 1, sums, (zero, zero))
    share = 1.0 / total
    delta = accum * share
    dqt_s[...] = jnp.zeros_like(dqt_s)

    def grads(k, carry):
        p = s_s[part_of(k), :] * share
        ds = (p * (dp_s[part_of(k), :] - delta)).astype(jnp.bfloat16)
        p = p.astype(jnp.bfloat16)
        dk = mul(ds, q_s[...]) * scale
        dv = mul(p, do_s[...])
        if n_parts > 1:
            dk = dk + jnp.where(part == 0, 0.0, dkv_s[part_of(k), :HEAD_DIM])
            dv = dv + jnp.where(part == 0, 0.0, dkv_s[part_of(k), HEAD_DIM:])
        dkv_s[part_of(k), :HEAD_DIM] = dk
        dkv_s[part_of(k), HEAD_DIM:] = dv
        dqt_s[...] += mul(kt_s[k], ds)
        return carry

    lax.fori_loop(0, z + 1, grads, 0)
    for h in range(heads_step):
        part_t = dqt_s[:, h * rows : (h + 1) * rows] * scale
        dq_ref[:, h * HEAD_DIM : (h + 1) * HEAD_DIM] = part_t.T.astype(jnp.bfloat16)
    for k, ref in enumerate(dkv_refs):
        held = dkv_s[k * pair : (k + 1) * pair, :]
        ref[...] = jnp.where(k <= z, held, 0.0).astype(jnp.bfloat16)


def attention(place, queries, out_grad, kv_blocks, first, count, query_grad, after=()):
    rows, q_width = queries.shape
    n_blocks = len(kv_blocks)
    group = HEADS // KV_HEADS
    keys = n_blocks * rows
    heads_step = max(1, min(group, 2**20 // (keys * rows)))
    n_parts = group // heads_step
    width = heads_step * rows
    q_spec = pl.BlockSpec(
        (rows, heads_step * HEAD_DIM), lambda g, u: (0, (g + first) * n_parts + u)
    )
    kv_spec = pl.BlockSpec((rows, 2 * HEAD_DIM), lambda g, u: (0, g + first))
    part_spec = pl.BlockSpec((2 * rows, 2 * HEAD_DIM), lambda g, u: (0, g))
    part_shape = jax.ShapeDtypeStruct((2 * rows, count * 2 * HEAD_DIM), jnp.bfloat16)
    held = [] if query_grad is None else [query_grad]
    return pl.pallas_call(
        functools.partial(attention_kernel, n_blocks, heads_step, rows, n_parts),
        grid=(count, n_parts),
        in_specs=[pl.BlockSpec(memory_space=pltpu.SMEM), q_spec, q_spec]
        + [kv_spec] * n_blocks
        + [pl.BlockSpec(memory_space=pl.ANY)] * (len(held) + len(after)),
        out_specs=[q_spec] + [part_spec] * (n_blocks // 2),
        out_shape=[jax.ShapeDtypeStruct((rows, q_width), jnp.bfloat16)]
        + [part_shape] * (n_blocks // 2),
        scratch_shapes=[
            pltpu.VMEM((keys, 2 * HEAD_DIM), jnp.bfloat16),
            pltpu.VMEM((n_blocks // 2, HEAD_DIM, 2 * rows), jnp.bfloat16),
            pltpu.VMEM((width, HEAD_DIM), jnp.bfloat16),
            pltpu.VMEM((width, HEAD_DIM), jnp.bfloat16),
            pltpu.VMEM((HEAD_DIM, width), jnp.bfloat16),
            pltpu.VMEM((HEAD_DIM, width), jnp.bfloat16),
            pltpu.VMEM((keys, width), jnp.float32),
            pltpu.VMEM((keys, width), jnp.float32),
            pltpu.VMEM((keys, 2 * HEAD_DIM), jnp.float32),
            pltpu.VMEM((HEAD_DIM, width), jnp.float32),
        ],
        input_output_aliases={3 + n_blocks: 0} if held else {},
        compiler_params=pltpu.CompilerParams(
            vmem_limit_bytes=vmem_limit, dimension_semantics=("arbitrary", "arbitrary")
        ),
        cost_estimate=pl.CostEstimate(
            flops=10 * rows * keys * group * count * HEAD_DIM,
            bytes_accessed=6 * rows * group * count * HEAD_DIM + 8 * keys * count * HEAD_DIM,
            transcendentals=rows * keys * group * count,
        ),
        name="attention_backward",
    )(place, queries, out_grad, *kv_blocks, *held, *after)


def fold_kernel(n_z, groups, rows, *refs):
    own_ref, other_ref = refs[-2:]
    first = 0
    for i in range(groups):
        parts = refs[i * n_z : (i + 1) * n_z]
        total = parts[0][...].astype(jnp.float32)
        for ref in parts[1:]:
            total = total + ref[...].astype(jnp.float32)
        lanes = slice(first, first + total.shape[1])
        own_ref[:, lanes] = total[:rows]
        other_ref[:, lanes] = total[rows:].astype(jnp.bfloat16)
        first += total.shape[1]


def fold(parts, rows, after=()):
    width = sum(group[0].shape[1] for group in parts)
    return pl.pallas_call(
        functools.partial(fold_kernel, len(parts[0]), len(parts), rows),
        in_specs=[pl.BlockSpec(memory_space=pltpu.VMEM)] * (len(parts) * len(parts[0]))
        + [pl.BlockSpec(memory_space=pl.ANY)] * len(after),
        out_shape=[
            jax.ShapeDtypeStruct((rows, width), jnp.float32),
            jax.ShapeDtypeStruct((rows, width), jnp.bfloat16),
        ],
        compiler_params=pltpu.CompilerParams(vmem_limit_bytes=vmem_limit),
        name="fold",
    )(*[part for group in parts for part in group], *after)


def finish_kernel(own_ref, got_ref, key_ref, value_ref):
    total = (own_ref[...] + got_ref[...].astype(jnp.float32)).astype(jnp.bfloat16)
    for g in range(total.shape[1] // (2 * HEAD_DIM)):
        lanes = slice(g * HEAD_DIM, (g + 1) * HEAD_DIM)
        key_ref[0, :, lanes] = total[:, 2 * g * HEAD_DIM : (2 * g + 1) * HEAD_DIM]
        value_ref[0, :, lanes] = total[:, (2 * g + 1) * HEAD_DIM : (2 * g + 2) * HEAD_DIM]


def finish(own, got):
    shape = jax.ShapeDtypeStruct((1, own.shape[0], own.shape[1] // 2), jnp.bfloat16)
    return pl.pallas_call(
        finish_kernel,
        out_shape=[shape, shape],
        compiler_params=pltpu.CompilerParams(vmem_limit_bytes=vmem_limit),
        name="finish",
    )(own, got)


def join_kernel(
    n_z, n_dp, key_ref, value_ref, rows_ref, ids_ref, combine_ref, kv_ref, ext_ref
):
    for g in range(kv_ref.shape[1] // (2 * HEAD_DIM)):
        lanes = slice(g * HEAD_DIM, (g + 1) * HEAD_DIM)
        kv_ref[:, 2 * g * HEAD_DIM : (2 * g + 1) * HEAD_DIM] = key_ref[0, :, lanes]
        kv_ref[:, (2 * g + 1) * HEAD_DIM : (2 * g + 2) * HEAD_DIM] = value_ref[0, :, lanes]
    tokens, feat = rows_ref.shape
    lines = 4 * n_dp
    line = lax.broadcasted_iota(jnp.int32, (n_z * lines, tokens), 0)
    kind = line % lines
    member = kind % (2 * n_dp)
    expert = (member // 2) * (2 * n_z) + line // lines * 2 + member % 2
    hits = jnp.zeros((n_z * lines, tokens), jnp.float32)
    weights = jnp.zeros((n_z * lines, tokens), jnp.float32)
    combine = combine_ref[...].astype(jnp.float32)
    for k in range(TOPK):
        hit = ids_ref[k : k + 1, :] == expert
        hits = hits + jnp.where(hit, 1.0, 0.0)
        weights = weights + jnp.where(hit, combine[k : k + 1, :], 0.0)
    before = lax.broadcasted_iota(jnp.int32, (tokens, tokens), 0) < lax.broadcasted_iota(
        jnp.int32, (tokens, tokens), 1
    )
    ranks = mul(hits.astype(jnp.bfloat16), jnp.where(before, 1.0, 0.0).astype(jnp.bfloat16))
    table = jnp.where(kind < 2 * n_dp, jnp.where(hits > 0.0, ranks, -1.0), weights)
    ext_ref[:tokens, :] = rows_ref[...]
    squares = [table[i * lines : (i + 1) * lines] for i in range(n_z)]
    squares += [jnp.zeros((lines, tokens), jnp.float32)] * (feat // tokens - n_z)
    ext_ref[tokens:, :] = jnp.concatenate(squares, axis=1).astype(jnp.bfloat16)


def join(keys, values, full_rows, ids, combine, n_z, n_dp):
    rows, width = keys.shape[1:]
    tokens, feat = full_rows.shape
    return pl.pallas_call(
        functools.partial(join_kernel, n_z, n_dp),
        out_shape=[
            jax.ShapeDtypeStruct((rows, 2 * width), jnp.bfloat16),
            jax.ShapeDtypeStruct((tokens + 4 * n_dp, feat), jnp.bfloat16),
        ],
        compiler_params=pltpu.CompilerParams(vmem_limit_bytes=vmem_limit),
        name="join",
    )(keys, values, full_rows, ids.T, combine.T)


def pick_kernel(sizes, n_dp, capacity, place, *refs):
    pieces = sum(sizes)
    out_ref, pick_s = refs[-2:]
    bounds = [sum(sizes[:i]) for i in range(len(sizes) + 1)]

    def added(group, i):
        total = group[bounds[i]][...]
        for ref in group[bounds[i] + 1 : bounds[i + 1]]:
            total = total + ref[...]
        return total

    @pl.when(pl.program_id(0) == 0)
    def _():
        for i in range(len(sizes)):
            tokens = refs[pieces].shape[0]
            table = refs[bounds[i]][:, pl.ds(pl.multiple_of(place[0] * tokens, tokens), tokens)]
            for ref in refs[bounds[i] + 1 : bounds[i + 1]]:
                table = table + ref[:, pl.ds(pl.multiple_of(place[0] * tokens, tokens), tokens)]
            table = table.astype(jnp.float32)
            slot = lax.broadcasted_iota(jnp.int32, (capacity, tokens), 0).astype(jnp.float32)
            picks = [
                jnp.where(
                    slot == table[q : q + 1, :], table[2 * n_dp + q : 2 * n_dp + q + 1, :], 0.0
                )
                for q in range(2 * n_dp)
            ]
            pick_s[i] = jnp.concatenate(picks, axis=0).astype(jnp.bfloat16)

    results = [mul(pick_s[i], added(refs[pieces : 2 * pieces], i)) for i in range(len(sizes))]
    for q in range(2 * n_dp):
        here = slice(q * capacity, (q + 1) * capacity)
        total = jnp.concatenate([part[here] for part in results], axis=0)
        size = len(sizes) * capacity
        out_ref[q * size : (q + 1) * size, :] = total.astype(jnp.bfloat16)


def pick_rows(place, blocks, n_dp, capacity, after=()):
    arrays = [array for block in blocks for array in block]
    sizes = [len(block) for block in blocks]
    lines, feat = 4 * n_dp, arrays[0].shape[1]
    tokens = arrays[0].shape[0] - lines
    step = math.gcd(feat, 1024)
    out_rows = len(blocks) * 2 * n_dp * capacity
    return pl.pallas_call(
        functools.partial(pick_kernel, sizes, n_dp, capacity),
        grid=(feat // step,),
        in_specs=[pl.BlockSpec(memory_space=pltpu.SMEM)]
        + [pl.BlockSpec((lines, feat), lambda f: (tokens // lines, 0))] * len(arrays)
        + [pl.BlockSpec((tokens, step), lambda f: (0, f))] * len(arrays)
        + [pl.BlockSpec(memory_space=pl.ANY)] * len(after),
        out_specs=pl.BlockSpec((out_rows, step), lambda f: (0, f)),
        out_shape=jax.ShapeDtypeStruct((out_rows, feat), jnp.bfloat16),
        scratch_shapes=[pltpu.VMEM((len(blocks), 2 * n_dp * capacity, tokens), jnp.bfloat16)],
        compiler_params=pltpu.CompilerParams(vmem_limit_bytes=vmem_limit),
        cost_estimate=pl.CostEstimate(
            flops=2 * out_rows * tokens * feat,
            bytes_accessed=2 * (out_rows + len(arrays) * tokens) * feat,
            transcendentals=0,
        ),
        name="pick_rows",
    )(place, *arrays, *arrays, *after)


def expert_kernel(ks, n_z, n_dp, capacity, slots, place, rows_ref, w_ref, *refs):
    out_ref, out_s, sem = refs[-3:]
    step, steps = pl.program_id(0), out_s.shape[0]
    width = out_s.shape[-1]
    blocks = [(q, k) for q in range(2 * n_dp) for k in ks]
    result = lax.dot_general(
        rows_ref[...], w_ref[0], (((1,), (1,)), ((), ())), preferred_element_type=jnp.float32
    )
    for i in range(len(blocks)):
        out_s[step, i] = result[i * capacity : i * capacity + slots].astype(jnp.bfloat16)

    def copies(at):
        z = place[0]
        for i, (q, k) in enumerate(blocks):
            source = (q // 2) * (2 * n_z) + (z ^ k) * 2 + q % 2
            lanes = pl.ds(pl.multiple_of(at * width, width), width)
            yield pltpu.make_async_copy(
                out_s.at[at, i], out_ref.at[0, source, :, lanes], sem.at[at, i]
            )

    for copy in copies(step):
        copy.start()

    @pl.when(step == steps - 1)
    def _():
        for at in range(steps):
            for copy in copies(at):
                copy.wait()


def expert_rows(place, rows, ks, w_down, n_z, n_dp, capacity, slots, hidden_grad, after=()):
    hid, feat = w_down.shape[1:]
    step = math.gcd(hid, 512)
    held = [] if hidden_grad is None else [hidden_grad]
    return pl.pallas_call(
        functools.partial(expert_kernel, ks, n_z, n_dp, capacity, slots),
        grid=(hid // step,),
        in_specs=[
            pl.BlockSpec(memory_space=pltpu.SMEM),
            pl.BlockSpec(rows.shape, lambda n: (0, 0)),
            pl.BlockSpec((1, step, feat), lambda n: (0, n, 0)),
        ]
        + [pl.BlockSpec(memory_space=pl.ANY)] * (len(held) + len(after)),
        out_specs=pl.BlockSpec(memory_space=pl.ANY),
        out_shape=jax.ShapeDtypeStruct((1, n_dp * 2 * n_z, slots, hid), jnp.bfloat16),
        scratch_shapes=[
            pltpu.VMEM((hid // step, rows.shape[0] // capacity, slots, step), jnp.bfloat16),
            pltpu.SemaphoreType.DMA((hid // step, rows.shape[0] // capacity)),
        ],
        input_output_aliases={3: 0} if held else {},
        compiler_params=pltpu.CompilerParams(vmem_limit_bytes=vmem_limit),
        cost_estimate=pl.CostEstimate(
            flops=2 * rows.shape[0] * feat * hid,
            bytes_accessed=2 * hid * feat + 2 * rows.shape[0] * (feat + hid),
            transcendentals=0,
        ),
        name="expert_rows",
    )(place, rows, w_down, *held, *after)


def per_device(queries, keys, values, out_grad, mixed_grad, expert_ids, combine, w_down):
    rows_dev = queries.shape[1]
    kv_local = keys.shape[2] // HEAD_DIM
    n_ctx, n_dp = lax.axis_size("ctx"), lax.axis_size("dp")
    n_z = n_ctx // 2
    position = lax.axis_index("ctx")
    place = jnp.stack([position >> 1, position & 1]).astype(jnp.int32)
    token_rows = expert_ids.shape[0]
    experts_all = n_dp * n_ctx
    slots = min(
        token_rows,
        max(
            2,
            token_rows * TOPK * 5 // (4 * experts_all),
            (token_rows * TOPK + experts_all - 1) // experts_all,
        ),
    )
    capacity = -(-slots // 8) * 8
    full_rows = mixed_grad
    if lax.axis_size("tp") > 1:
        full_rows = lax.all_gather(mixed_grad, "tp", axis=1, tiled=True)
    own, own_rows = join(keys, values, full_rows, expert_ids, combine, n_z, n_dp)

    columns = [own] + [
        lax.ppermute(own, "ctx", [(i, i + 2 * k) for i in range(n_ctx - 2 * k)])
        for k in range(1, n_z)
    ]
    blocks = []
    for k, column in enumerate(columns):
        pairs = [(i, i ^ 1) for i in range(2 * k, n_ctx) if k > 0 or i % 2 == 0]
        blocks += [column, lax.ppermute(column, "ctx", pairs)]

    plane_groups = [
        [d * n_ctx + 2 * i + j for d in range(n_dp) for j in range(2)] for i in range(n_z)
    ]
    def along_z(array, targets):
        pairs = [(2 * i + x, 2 * j + x) for i, j in targets for x in range(2)]
        return lax.ppermute(array, "ctx", pairs)

    near = along_z(own_rows, [(i, i ^ 1) for i in range(n_z)])
    if n_z == 4:
        across = along_z(own_rows, [(1, 2), (2, 1)])
        across_near = along_z(near, [(1, 2), (2, 1)])
        outward = along_z(across, [(1, 0), (2, 3)])
        outward_near = along_z(across_near, [(1, 0), (2, 3)])
        far = [(across_near, outward), (across, outward_near)]
        early, late = (across,), (across_near, outward)
    else:
        far = [(along_z(own_rows, [(i, i ^ k) for i in range(n_z)]),) for k in range(2, n_z)]
        early, late = (), ()

    def exchange(arrays, after):
        picked = pick_rows(place, arrays, n_dp, capacity, after)
        return picked, lax.all_to_all(
            picked,
            ("dp", "ctx"),
            split_axis=0,
            concat_axis=0,
            tiled=True,
            axis_index_groups=plane_groups,
        )

    picked, got_near = exchange([(own_rows,), (near,)], (*blocks, *early))

    counts = [1] if kv_local == 1 else [kv_local // 2, kv_local - kv_local // 2]
    query_grad, gathered, first = None, [], 0
    for count in counts:
        after = (picked,) if first == 0 else late
        query_grad, *parts = attention(
            place, queries[0], out_grad[0], blocks, first, count, query_grad, after
        )
        first += count
        gathered.append(
            [parts[0]]
            + [
                lax.ppermute(parts[k], "ctx", [(i, i - 2 * k) for i in range(2 * k, n_ctx)])
                for k in range(1, n_z)
            ]
        )
    picked, got_far = exchange(far, (query_grad, *(gathered[0] if len(counts) > 1 else ())))
    sizes = (n_z, n_dp, capacity, slots)
    hidden_grad = expert_rows(place, got_near, (0, 1), w_down, *sizes, None, (picked,))
    total, other = fold(gathered, rows_dev, (hidden_grad,))
    got = lax.ppermute(other, "ctx", [(i, i ^ 1) for i in range(n_ctx)])
    key_grad, value_grad = finish(total, got)
    hidden_grad = expert_rows(
        place, got_far, tuple(range(2, n_z)), w_down, *sizes, hidden_grad, (key_grad,)
    )
    return (query_grad[None], key_grad, value_grad, hidden_grad)


def solution(mesh):
    placed = (
        P("dp", "ctx", "tp"),
        P("dp", "ctx", "tp"),
        P("dp", "ctx", "tp"),
        P("dp", "ctx", "tp"),
        P(("dp", "ctx"), "tp"),
        P(("dp", "ctx"), None),
        P(("dp", "ctx"), None),
        P(("dp", "ctx"), "tp", None),
    )
    return jax.shard_map(
        per_device,
        mesh=mesh,
        in_specs=placed,
        out_specs=(
            P("dp", "ctx", "tp"),
            P("dp", "ctx", "tp"),
            P("dp", "ctx", "tp"),
            P(("dp", "ctx"), None, None, "tp"),
        ),
        check_vma=False,
    )
```

time: 338 us -> 182 us (0.54)
  waiting for transfers between devices: 220 us -> 92.5 us
  Pallas kernels: 0 us -> 40.6 us
  matrix products: 39.2 us -> 0 us
  starting transfers between devices: 13.6 us -> 38.2 us
  other arithmetic: 23.5 us -> 0.56 us
  local copies, waits for them, and re-layouts: 23.9 us -> 8.17 us
  between operations: 14.1 us -> 1.05 us
    all_gather x2 -> x0, waiting for transfers between devices: 120 us -> none  [the longest x1 60 us: per_device(): lax.all_gather(value_heads, 'ctx', axis=0, tiled=True)]
    reduce_scatter x1 -> x0, waiting for transfers between devices: 100 us -> none  [per_device(): lax.psum_scatter(key_value_total, 'ctx', scatter_dimension=0, tiled=True)]
    ppermute x0 -> x19, waiting for transfers between devices: none -> 92.5 us  [the longest x6 43.1 us: per_device(): lax.ppermute(parts[k], 'ctx', [(i, i - 2 * k) for i in range(2 * k, n_ctx)])]
    pallas_call x0 -> x9, Pallas kernels: none -> 40.6 us  [the longest x2 17.2 us: expert_rows(): pl.pallas_call(functools.partial(expert_kernel, ks, n_z, n_dp, capacity,...]
    dot_general x10 -> x0, matrix products: 39.2 us -> none  [the longest x1 13.7 us: per_device(): jnp.einsum('sejf,ehf->esjh', row_view, w_down, preferred_element_type=jnp...]
    ppermute x0 -> x19, starting transfers between devices: none -> 30.8 us  [the longest x3 8.99 us: per_device(): lax.ppermute(own, 'ctx', [(i, i + 2 * k) for i in range(n_ctx - 2 * k)])]
    reduce_sum x3 -> x0, other arithmetic: 8.81 us -> none  [the longest x1 6.66 us: per_device(): chosen.reshape(experts_all * capacity, token_rows, TOPK).sum(axis=2)]
    another operation x3 -> x1, other arithmetic: 9.15 us -> 0.56 us  [per_device(): place = jnp.stack([position >> 1, position & 1]).astype(jnp.int32)]
  transfers between devices with their start and end apart: 5 -> 21, of which waited for: 3 -> 8; matrix products, arithmetic and copies ran while one was open for 20% -> 0% of each run, Pallas kernels for 0% -> 15%
where the time goes in v1:
time: 182 us; the launch traced here: 181 us
  waiting for transfers between devices  92.5 us (51%)
  Pallas kernels  40.6 us (22%)
  starting transfers between devices  38.2 us (21%)
  local copies, waits for them, and re-layouts  8.17 us (4%)
    ppermute x6, waiting for transfers between devices, per_device(): lax.ppermute(parts[k], 'ctx', [(i, i - 2 * k) for i in range(2 * k, n_ctx)])  43.1 us
    ppermute x5, waiting for transfers between devices, along_z(): return lax.ppermute(array, 'ctx', pairs)  24.3 us
    ppermute x3, waiting for transfers between devices, per_device(): lax.ppermute(own, 'ctx', [(i, i + 2 * k) for i in range(n_ctx - 2 * k)])  18.4 us
    pallas_call x2, Pallas kernels, expert_rows(): pl.pallas_call(functools.partial(expert_kernel, ks, n_z, n_dp, capacity,...  17.2 us
    pallas_call x2, Pallas kernels, attention(): pl.pallas_call(functools.partial(attention_kernel, n_blocks, heads_step,...  10.2 us
    ppermute x3, starting transfers between devices, per_device(): lax.ppermute(own, 'ctx', [(i, i + 2 * k) for i in range(n_ctx - 2 * k)])  8.99 us
    unnamed x50, local copies, waits for them, and re-layouts  8.17 us
    ppermute x6, starting transfers between devices, per_device(): lax.ppermute(parts[k], 'ctx', [(i, i - 2 * k) for i in range(2 * k, n_ctx)])  7.75 us
  transfers between devices with their start and end apart: 21, of which 8 were waited for; matrix products, arithmetic and copies ran while one was open for 0% of the time, Pallas kernels for 15%

profile of v1, /device:TPU:0, one launch (start us, length us, event | category | flops | bytes accessed | tf_op | source)
XLA Modules:
  0.0 181.1 jit_solution(7477261037262003943)
XLA Ops:
  0.6 2.2 %join.1 = (bf16[128,1024]{1,0:T(8,128)(2,1)}, bf16[144,2048]{1,0:T(8,128)(2,1)}) custom-call(bf16[1,128,512]{2,1,0:T(8,128)(2,1)} %key_ref.1, bf16[1,128,512]{2,1,0:T(8,128)(2,1)} %value_ref.1, bf16[128,2048]{1,0:T(8,128)(2,1)} %rows_ref.1, s32[8,128]{1,0:T(8,128)} %bitcast.16, bf16[8,128]{1,0:T(8,128)(2,1)} %bitcast.17), custom_call_target="tpu_custom_call" | custom-call | tf_op jit(solution)/shard_map/join/pallas_call | solution.py:232
  2.9 4.8 %collective-permute-start = (bf16[128,1024]{1,0:T(8,128)(2,1)}, bf16[128,1024]{1,0:T(8,128)(2,1)S(1)}, u32[]{:S(2)}, u32[]{:S(2)}) collective-permute-start(bf16[128,1024]{1,0:T(8,128)(2,1)} %get-tuple-element.20.refs_4_.refs_0_), channel_id=1, source_target_pairs={{0,1},{2,3},{4,5},{6,7},{8,9},{10,11},{12,13},{14,15},{16,17},{18,... | collective-permute-start | bytes 786440 | tf_op jit(solution)/shard_map/ppermute | solution.py:396
  7.7 1.6 collective-permute-start.7
  10.0 6.3 %collective-permute-start.1 = (bf16[128,1024]{1,0:T(8,128)(2,1)}, bf16[128,1024]{1,0:T(8,128)(2,1)S(1)}, u32[]{:S(2)}, u32[]{:S(2)}) collective-permute-start(bf16[128,1024]{1,0:T(8,128)(2,1)} %get-tuple-element.20.refs_4_.refs_0_), channel_id=1, source_target_pairs={{0,2},{1,3},{2,4},{3,5},{4,6},{5,7},{8,10},{9,11},{10,12},{11,13},... | collective-permute-start | bytes 786440 | tf_op jit(solution)/shard_map/ppermute | solution.py:390
  16.3 1.4 collective-permute-start.3
  17.7 1.3 collective-permute-start.5
  19.1 10.0 %collective-permute-done.1.refs_6_.refs_2_ = bf16[128,1024]{1,0:T(8,128)(2,1)S(1)} collective-permute-done((bf16[128,1024]{1,0:T(8,128)(2,1)}, bf16[128,1024]{1,0:T(8,128)(2,1)S(1)}, u32[]{:S(2)}, u32[]{:S(2)}) %collective-permute-start.1) | collective-permute-done | bytes 262176 | tf_op jit(solution)/shard_map/ppermute | solution.py:390
  29.7 5.0 %collective-permute-done.3.refs_8_.refs_4_ = bf16[128,1024]{1,0:T(8,128)(2,1)S(1)} collective-permute-done((bf16[128,1024]{1,0:T(8,128)(2,1)}, bf16[128,1024]{1,0:T(8,128)(2,1)S(1)}, u32[]{:S(2)}, u32[]{:S(2)}) %collective-permute-start.3) | collective-permute-done | bytes 262176 | tf_op jit(solution)/shard_map/ppermute | solution.py:390
  35.4 3.5 %collective-permute-done.5.refs_10_.refs_6_ = bf16[128,1024]{1,0:T(8,128)(2,1)S(1)} collective-permute-done((bf16[128,1024]{1,0:T(8,128)(2,1)}, bf16[128,1024]{1,0:T(8,128)(2,1)S(1)}, u32[]{:S(2)}, u32[]{:S(2)}) %collective-permute-start.5) | collective-permute-done | bytes 262176 | tf_op jit(solution)/shard_map/ppermute | solution.py:390
  42.1 3.2 %pick_rows.2.refs_8_ = bf16[640,2048]{1,0:T(8,128)(2,1)} custom-call(s32[2]{0:T(128)} %pad_add_fusion.place, bf16[144,2048]{1,0:T(8,128)(2,1)} %get-tuple-element.21.refs_0_.refs_2_, bf16[144,2048]{1,0:T(8,128)(2,1)} %copy-done.7, bf16[144,2048]{1,0:T(8,128)(2,1)} %get-tuple-element.21.refs_0_.refs_2_, bf16[144,2048]{1,0:T(8,128)(2,1)} %copy-done.7, ...), custom_call_target="tpu_custom_call" | custom-call | flops 335544320 | bytes 3670016 | tf_op jit(solution)/shard_map/pick_rows/pallas_call | solution.py:286
  45.2 3.8 %all-to-all-start = ((bf16[8,80,2048]{2,1,0:T(8,128)(2,1)}), bf16[8,80,2048]{2,1,0:T(8,128)(2,1)S(1)}, u32[]{:S(2)}, u32[]{:S(2)}) async-start(bf16[8,80,2048]{2,1,0:T(8,128)(2,1)} %bitcast.13), calls=%async_computation | async-start | bytes 5242880 | tf_op jit(solution)/shard_map/all_to_all | solution.py:419
  49.7 1.3 collective-permute-start.10
  51.0 1.3 collective-permute-start.17
  52.3 5.1 %attention_backward.2 = (bf16[128,4096]{1,0:T(8,128)(2,1)}, bf16[256,512]{1,0:T(8,128)(2,1)}, bf16[256,512]{1,0:T(8,128)(2,1)}, bf16[256,512]{1,0:T(8,128)(2,1)}, bf16[256,512]{1,0:T(8,128)(2,1)}) custom-call(s32[2]{0:T(128)} %pad_add_fusion.place, bf16[128,4096]{1,0:T(8,128)(2,1)} %bitcast.18, bf16[128,4096]{1,0:T(8,128)(2,1)} %bitcast.20, ...), custom_call_target="tpu_custom_call" | custom-call | flops 2684354560 | bytes 3670016 | tf_op jit(solution)/shard_map/attention_backward/pallas_call | solution.py:117
  57.4 1.3 collective-permute-start.11
  58.7 1.3 collective-permute-start.12
  60.0 1.3 collective-permute-start.13
  61.3 24.3 %collective-permute-done.10.refs_10_.refs_1_.refs_5_ = bf16[144,2048]{1,0:T(8,128)(2,1)S(1)} collective-permute-done((bf16[144,2048]{1,0:T(8,128)(2,1)S(1)}, bf16[144,2048]{1,0:T(8,128)(2,1)S(1)}, u32[]{:S(2)}, u32[]{:S(2)}) %collective-permute-start.10) | collective-permute-done | bytes 589856 | tf_op jit(solution)/shard_map/ppermute | solution.py:403
  86.5 5.1 %attention_backward.3 = (bf16[128,4096]{1,0:T(8,128)(2,1)}, bf16[256,512]{1,0:T(8,128)(2,1)}, bf16[256,512]{1,0:T(8,128)(2,1)}, bf16[256,512]{1,0:T(8,128)(2,1)}, bf16[256,512]{1,0:T(8,128)(2,1)}) custom-call(s32[2]{0:T(128)} %pad_add_fusion.place, bf16[128,4096]{1,0:T(8,128)(2,1)} %bitcast.19, ...), custom_call_target="tpu_custom_call", output_to_operand_aliasing={{0}: (11, {})} | custom-call | flops 2684354560 | bytes 3670016 | tf_op jit(solution)/shard_map/attention_backward/pallas_call | solution.py:117
  91.5 14.0 %collective-permute-done.11.refs_10_.refs_1_ = bf16[256,512]{1,0:T(8,128)(2,1)S(1)} collective-permute-done((bf16[256,512]{1,0:T(8,128)(2,1)}, bf16[256,512]{1,0:T(8,128)(2,1)S(1)}, u32[]{:S(2)}, u32[]{:S(2)}) %collective-permute-start.11) | collective-permute-done | bytes 262176 | tf_op jit(solution)/shard_map/ppermute | solution.py:441
  105.6 16.3 %collective-permute-done.12.refs_11_.refs_2_ = bf16[256,512]{1,0:T(8,128)(2,1)S(1)} collective-permute-done((bf16[256,512]{1,0:T(8,128)(2,1)}, bf16[256,512]{1,0:T(8,128)(2,1)S(1)}, u32[]{:S(2)}, u32[]{:S(2)}) %collective-permute-start.12) | collective-permute-done | bytes 262176 | tf_op jit(solution)/shard_map/ppermute | solution.py:441
  122.9 3.5 %pick_rows.3.refs_0_ = bf16[640,2048]{1,0:T(8,128)(2,1)} custom-call(s32[2]{0:T(128)} %pad_add_fusion.place, bf16[144,2048]{1,0:T(8,128)(2,1)} %copy-done.4, bf16[144,2048]{1,0:T(8,128)(2,1)} %copy-done.5, bf16[144,2048]{1,0:T(8,128)(2,1)} %copy-done.2, bf16[144,2048]{1,0:T(8,128)(2,1)} %copy-done.6, bf16[144,2048]{1,0:T(8,128)(2,1)} %copy-done.4, ...), custom_call_target="tpu_custom_call" | custom-call | flops 335544320 | bytes 4718592 | tf_op jit(solution)/shard_map/pick_rows/pallas_call | solution.py:286
  126.4 1.5 copy-done.1
  127.9 3.6 %all-to-all-start.1 = ((bf16[8,80,2048]{2,1,0:T(8,128)(2,1)}), bf16[8,80,2048]{2,1,0:T(8,128)(2,1)S(1)}, u32[]{:S(2)}, u32[]{:S(2)}) async-start(bf16[8,80,2048]{2,1,0:T(8,128)(2,1)} %bitcast.11), calls=%async_computation.1 | async-start | bytes 5242880 | tf_op jit(solution)/shard_map/all_to_all | solution.py:419
  135.5 8.6 %expert_rows.2.refs_8_.refs_0_ = bf16[1,32,40,1536]{3,2,1,0:T(8,128)(2,1)} custom-call(s32[2]{0:T(128)} %pad_add_fusion.place, bf16[640,2048]{1,0:T(8,128)(2,1)} %bitcast.14, bf16[1,1536,2048]{2,1,0:T(8,128)(2,1)} %w_ref.3, bf16[640,2048]{1,0:T(8,128)(2,1)} %pick_rows.3.refs_0_), custom_call_target="tpu_custom_call" | custom-call | flops 4026531840 | bytes 10878976 | tf_op jit(solution)/shard_map/expert_rows/pallas_call | solution.py:340
  144.1 12.7 %collective-permute-done.15.refs_6_ = bf16[256,512]{1,0:T(8,128)(2,1)S(1)} collective-permute-done((bf16[256,512]{1,0:T(8,128)(2,1)S(1)}, bf16[256,512]{1,0:T(8,128)(2,1)S(1)}, u32[]{:S(2)}, u32[]{:S(2)}) %collective-permute-start.15) | collective-permute-done | bytes 262176 | tf_op jit(solution)/shard_map/ppermute | solution.py:441
  157.6 2.6 %fold.1 = (f32[128,1024]{1,0:T(8,128)}, bf16[128,1024]{1,0:T(8,128)(2,1)}) custom-call(bf16[256,512]{1,0:T(8,128)(2,1)} %get-tuple-element.24.refs_9_.refs_0_, bf16[256,512]{1,0:T(8,128)(2,1)} %copy-done.8, bf16[256,512]{1,0:T(8,128)(2,1)} %copy-done.9, bf16[256,512]{1,0:T(8,128)(2,1)} %copy-done.10, bf16[256,512]{1,0:T(8,128)(2,1)} %get-tuple-element.28.refs_4_, ...), custom_call_target="tpu_custom_call" | custom-call | tf_op jit(solution)/shard_map/fold/pallas_call | solution.py:167
  160.2 1.7 collective-permute-start.18
  161.9 6.6 %collective-permute-done.18.got_ref = bf16[128,1024]{1,0:T(8,128)(2,1)S(1)} collective-permute-done((bf16[128,1024]{1,0:T(8,128)(2,1)}, bf16[128,1024]{1,0:T(8,128)(2,1)S(1)}, u32[]{:S(2)}, u32[]{:S(2)}) %collective-permute-start.18) | collective-permute-done | bytes 262176 | tf_op jit(solution)/shard_map/ppermute | solution.py:449
  169.2 1.9 %finish.1 = (bf16[1,128,512]{2,1,0:T(8,128)(2,1)}, bf16[1,128,512]{2,1,0:T(8,128)(2,1)}) custom-call(f32[128,1024]{1,0:T(8,128)} %get-tuple-element.32.own_ref, bf16[128,1024]{1,0:T(8,128)(2,1)} %copy-done.21), custom_call_target="tpu_custom_call" | custom-call | tf_op jit(solution)/shard_map/finish/pallas_call | solution.py:190
  171.0 1.5 copy-done
  172.5 8.6 %expert_rows.3 = bf16[1,32,40,1536]{3,2,1,0:T(8,128)(2,1)} custom-call(s32[2]{0:T(128)} %pad_add_fusion.place, bf16[640,2048]{1,0:T(8,128)(2,1)} %bitcast.12, bf16[1,1536,2048]{2,1,0:T(8,128)(2,1)} %w_ref.3, bf16[1,32,40,1536]{3,2,1,0:T(8,128)(2,1)} %expert_rows.2.refs_8_.refs_0_, ...), custom_call_target="tpu_custom_call", output_to_operand_aliasing={{}: (3, {})} | custom-call | flops 4026531840 | bytes 10878976 | tf_op jit(solution)/shard_map/expert_rows/pallas_call | solution.py:340
  (70 shorter events, 13.0 us)
Async XLA Ops:
  2.9 14.9 %collective-permute-start = (bf16[128,1024]{1,0:T(8,128)(2,1)}, bf16[128,1024]{1,0:T(8,128)(2,1)S(1)}, u32[]{:S(2)}, u32[]{:S(2)}) collective-permute-start(bf16[128,1024]{1,0:T(8,128)(2,1)} %get-tuple-element.20.refs_4_.refs_0_), channel_id=1, source_target_pairs={{0,1},{2,3},{4,5},{6,7},{8,9},{10,11},{12,13},{14,15},{16,17},{18,... | collective-permute-start | bytes 786440 | tf_op jit(solution)/shard_map/ppermute | solution.py:396
  7.7 32.4 %collective-permute-start.7 = (bf16[144,2048]{1,0:T(8,128)(2,1)}, bf16[144,2048]{1,0:T(8,128)(2,1)S(1)}, u32[]{:S(2)}, u32[]{:S(2)}) collective-permute-start(bf16[144,2048]{1,0:T(8,128)(2,1)} %get-tuple-element.21.refs_0_.refs_2_), channel_id=1, source_target_pairs={{0,2},{1,3},{2,0},{3,1},{4,6},{5,7},{6,4},{7,5},{8,10},{9,11},{10,... | collective-permute-start | bytes 1769480 | tf_op jit(solution)/shard_map/ppermute | solution.py:403
  9.3 30.8 %collective-permute-start.8 = (bf16[144,2048]{1,0:T(8,128)(2,1)}, bf16[144,2048]{1,0:T(8,128)(2,1)S(1)}, u32[]{:S(2)}, u32[]{:S(2)}) collective-permute-start(bf16[144,2048]{1,0:T(8,128)(2,1)} %get-tuple-element.21.refs_0_.refs_2_), channel_id=1, source_target_pairs={{2,4},{3,5},{4,2},{5,3},{10,12},{11,13},{12,10},{13,11},{18,20},{1... | collective-permute-start | bytes 1769480 | tf_op jit(solution)/shard_map/ppermute | solution.py:403
  10.0 19.0 %collective-permute-start.1 = (bf16[128,1024]{1,0:T(8,128)(2,1)}, bf16[128,1024]{1,0:T(8,128)(2,1)S(1)}, u32[]{:S(2)}, u32[]{:S(2)}) collective-permute-start(bf16[128,1024]{1,0:T(8,128)(2,1)} %get-tuple-element.20.refs_4_.refs_0_), channel_id=1, source_target_pairs={{0,2},{1,3},{2,4},{3,5},{4,6},{5,7},{8,10},{9,11},{10,12},{11,13},... | collective-permute-start | bytes 786440 | tf_op jit(solution)/shard_map/ppermute | solution.py:390
  16.3 18.4 %collective-permute-start.3 = (bf16[128,1024]{1,0:T(8,128)(2,1)}, bf16[128,1024]{1,0:T(8,128)(2,1)S(1)}, u32[]{:S(2)}, u32[]{:S(2)}) collective-permute-start(bf16[128,1024]{1,0:T(8,128)(2,1)} %get-tuple-element.20.refs_4_.refs_0_), channel_id=1, source_target_pairs={{0,4},{1,5},{2,6},{3,7},{8,12},{9,13},{10,14},{11,15},{16,20},{17,... | collective-permute-start | bytes 786440 | tf_op jit(solution)/shard_map/ppermute | solution.py:390
  17.7 22.5 %copy-start.11 = (bf16[128,1024]{1,0:T(8,128)(2,1)}, bf16[128,1024]{1,0:T(8,128)(2,1)S(1)}, u32[]{:S(2)}) copy-start(bf16[128,1024]{1,0:T(8,128)(2,1)S(1)} %collective-permute-done.refs_5_.refs_1_) | copy-start | bytes 786436
  17.7 21.1 %collective-permute-start.5 = (bf16[128,1024]{1,0:T(8,128)(2,1)}, bf16[128,1024]{1,0:T(8,128)(2,1)S(1)}, u32[]{:S(2)}, u32[]{:S(2)}) collective-permute-start(bf16[128,1024]{1,0:T(8,128)(2,1)} %get-tuple-element.20.refs_4_.refs_0_), channel_id=1, source_target_pairs={{0,6},{1,7},{8,14},{9,15},{16,22},{17,23},{24,30},{25,31}} | collective-permute-start | bytes 786440 | tf_op jit(solution)/shard_map/ppermute | solution.py:390
  29.1 11.1 %copy-start.12 = (bf16[128,1024]{1,0:T(8,128)(2,1)}, bf16[128,1024]{1,0:T(8,128)(2,1)S(1)}, u32[]{:S(2)}) copy-start(bf16[128,1024]{1,0:T(8,128)(2,1)S(1)} %collective-permute-done.1.refs_6_.refs_2_) | copy-start | bytes 786436
  29.1 11.1 %collective-permute-start.2 = (bf16[128,1024]{1,0:T(8,128)(2,1)S(1)}, bf16[128,1024]{1,0:T(8,128)(2,1)S(1)}, u32[]{:S(2)}, u32[]{:S(2)}) collective-permute-start(bf16[128,1024]{1,0:T(8,128)(2,1)S(1)} %collective-permute-done.1.refs_6_.refs_2_), channel_id=1, source_target_pairs={{2,3},{3,2},{4,5},{5,4},{6,7},{7,6},{10,11},{11,10},{12,13},{13,12... | collective-permute-start | bytes 786440 | tf_op jit(solution)/shard_map/ppermute | solution.py:396
  34.7 5.5 %copy-start.13 = (bf16[128,1024]{1,0:T(8,128)(2,1)}, bf16[128,1024]{1,0:T(8,128)(2,1)S(1)}, u32[]{:S(2)}) copy-start(bf16[128,1024]{1,0:T(8,128)(2,1)S(1)} %collective-permute-done.3.refs_8_.refs_4_) | copy-start | bytes 786436
  34.7 5.4 %collective-permute-start.4 = (bf16[128,1024]{1,0:T(8,128)(2,1)S(1)}, bf16[128,1024]{1,0:T(8,128)(2,1)S(1)}, u32[]{:S(2)}, u32[]{:S(2)}) collective-permute-start(bf16[128,1024]{1,0:T(8,128)(2,1)S(1)} %collective-permute-done.3.refs_8_.refs_4_), channel_id=1, source_target_pairs={{4,5},{5,4},{6,7},{7,6},{12,13},{13,12},{14,15},{15,14},{20,21},{2... | collective-permute-start | bytes 786440 | tf_op jit(solution)/shard_map/ppermute | solution.py:396
  38.9 1.3 collective-permute-start.6
  45.2 4.5 %copy-start.3 = (bf16[144,2048]{1,0:T(8,128)(2,1)S(1)}, bf16[144,2048]{1,0:T(8,128)(2,1)}, u32[]{:S(2)}) copy-start(bf16[144,2048]{1,0:T(8,128)(2,1)} %copy-done.2) | copy-start | bytes 1769476
  45.2 81.2 %all-to-all-start = ((bf16[8,80,2048]{2,1,0:T(8,128)(2,1)}), bf16[8,80,2048]{2,1,0:T(8,128)(2,1)S(1)}, u32[]{:S(2)}, u32[]{:S(2)}) async-start(bf16[8,80,2048]{2,1,0:T(8,128)(2,1)} %bitcast.13), calls=%async_computation | async-start | bytes 5242880 | tf_op jit(solution)/shard_map/all_to_all | solution.py:419
  49.0 2.0 %collective-permute-start.9 = (bf16[144,2048]{1,0:T(8,128)(2,1)}, bf16[144,2048]{1,0:T(8,128)(2,1)S(1)}, u32[]{:S(2)}, u32[]{:S(2)}) collective-permute-start(bf16[144,2048]{1,0:T(8,128)(2,1)} %copy-done.7), channel_id=1, source_target_pairs={{2,4},{3,5},{4,2},{5,3},{10,12},{11,13},{12,10},{13,11},{18,20},{1... | collective-permute-start | bytes 1769480 | tf_op jit(solution)/shard_map/ppermute | solution.py:403
  49.7 35.9 %collective-permute-start.10 = (bf16[144,2048]{1,0:T(8,128)(2,1)S(1)}, bf16[144,2048]{1,0:T(8,128)(2,1)S(1)}, u32[]{:S(2)}, u32[]{:S(2)}) collective-permute-start(bf16[144,2048]{1,0:T(8,128)(2,1)S(1)} %copy-done.3), channel_id=1, source_target_pairs={{2,0},{3,1},{4,6},{5,7},{10,8},{11,9},{12,14},{13,15},{18,16},{19,... | collective-permute-start | bytes 1769480 | tf_op jit(solution)/shard_map/ppermute | solution.py:403
  51.0 6.4 %copy-start.4 = (bf16[144,2048]{1,0:T(8,128)(2,1)}, bf16[144,2048]{1,0:T(8,128)(2,1)S(1)}, u32[]{:S(2)}) copy-start(bf16[144,2048]{1,0:T(8,128)(2,1)S(1)} %collective-permute-done.9.refs_9_.refs_0_.refs_4_) | copy-start | bytes 1769476
  51.0 70.9 %collective-permute-start.17 = (bf16[144,2048]{1,0:T(8,128)(2,1)S(1)}, bf16[144,2048]{1,0:T(8,128)(2,1)S(1)}, u32[]{:S(2)}, u32[]{:S(2)}) collective-permute-start(bf16[144,2048]{1,0:T(8,128)(2,1)S(1)} %collective-permute-done.9.refs_9_.refs_0_.refs_4_), channel_id=1, source_target_pairs={{2,0},{3,1},{4,6},{5,7},{10,8},{11,9},{12,14},{13,15},{18,16},{19,... | collective-permute-start | bytes 1769480 | tf_op jit(solution)/shard_map/ppermute | solution.py:403
  57.4 48.2 %collective-permute-start.11 = (bf16[256,512]{1,0:T(8,128)(2,1)}, bf16[256,512]{1,0:T(8,128)(2,1)S(1)}, u32[]{:S(2)}, u32[]{:S(2)}) collective-permute-start(bf16[256,512]{1,0:T(8,128)(2,1)} %get-tuple-element.25), channel_id=1, source_target_pairs={{2,0},{3,1},{4,2},{5,3},{6,4},{7,5},{10,8},{11,9},{12,10},{13,11},... | collective-permute-start | bytes 786440 | tf_op jit(solution)/shard_map/ppermute | solution.py:441
  58.7 63.2 %collective-permute-start.12 = (bf16[256,512]{1,0:T(8,128)(2,1)}, bf16[256,512]{1,0:T(8,128)(2,1)S(1)}, u32[]{:S(2)}, u32[]{:S(2)}) collective-permute-start(bf16[256,512]{1,0:T(8,128)(2,1)} %get-tuple-element.26), channel_id=1, source_target_pairs={{4,0},{5,1},{6,2},{7,3},{12,8},{13,9},{14,10},{15,11},{20,16},{21,... | collective-permute-start | bytes 786440 | tf_op jit(solution)/shard_map/ppermute | solution.py:441
  60.0 61.9 %collective-permute-start.13 = (bf16[256,512]{1,0:T(8,128)(2,1)}, bf16[256,512]{1,0:T(8,128)(2,1)S(1)}, u32[]{:S(2)}, u32[]{:S(2)}) collective-permute-start(bf16[256,512]{1,0:T(8,128)(2,1)} %get-tuple-element.27), channel_id=1, source_target_pairs={{6,0},{7,1},{14,8},{15,9},{22,16},{23,17},{30,24},{31,25}} | collective-permute-start | bytes 786440 | tf_op jit(solution)/shard_map/ppermute | solution.py:441
  105.6 16.3 %copy-start.8 = (bf16[256,512]{1,0:T(8,128)(2,1)}, bf16[256,512]{1,0:T(8,128)(2,1)S(1)}, u32[]{:S(2)}) copy-start(bf16[256,512]{1,0:T(8,128)(2,1)S(1)} %collective-permute-done.11.refs_10_.refs_1_) | copy-start | bytes 786436
  126.4 1.5 copy-start.1
  126.4 5.2 %copy-start.24 = (bf16[256,512]{1,0:T(8,128)(2,1)S(1)}, bf16[256,512]{1,0:T(8,128)(2,1)}, u32[]{:S(2)}) copy-start(bf16[256,512]{1,0:T(8,128)(2,1)} %get-tuple-element.29) | copy-start | bytes 786436
  126.4 6.5 %copy-start.23 = (bf16[256,512]{1,0:T(8,128)(2,1)S(1)}, bf16[256,512]{1,0:T(8,128)(2,1)}, u32[]{:S(2)}) copy-start(bf16[256,512]{1,0:T(8,128)(2,1)} %get-tuple-element.30) | copy-start | bytes 786436
  126.4 7.8 %copy-start.22 = (bf16[256,512]{1,0:T(8,128)(2,1)S(1)}, bf16[256,512]{1,0:T(8,128)(2,1)}, u32[]{:S(2)}) copy-start(bf16[256,512]{1,0:T(8,128)(2,1)} %get-tuple-element.31) | copy-start | bytes 786436
  127.9 43.1 %all-to-all-start.1 = ((bf16[8,80,2048]{2,1,0:T(8,128)(2,1)}), bf16[8,80,2048]{2,1,0:T(8,128)(2,1)S(1)}, u32[]{:S(2)}, u32[]{:S(2)}) async-start(bf16[8,80,2048]{2,1,0:T(8,128)(2,1)} %bitcast.11), calls=%async_computation.1 | async-start | bytes 5242880 | tf_op jit(solution)/shard_map/all_to_all | solution.py:419
  131.6 12.5 %collective-permute-start.14 = (bf16[256,512]{1,0:T(8,128)(2,1)S(1)}, bf16[256,512]{1,0:T(8,128)(2,1)S(1)}, u32[]{:S(2)}, u32[]{:S(2)}) collective-permute-start(bf16[256,512]{1,0:T(8,128)(2,1)S(1)} %copy-done.24), channel_id=1, source_target_pairs={{2,0},{3,1},{4,2},{5,3},{6,4},{7,5},{10,8},{11,9},{12,10},{13,11},... | collective-permute-start | bytes 786440 | tf_op jit(solution)/shard_map/ppermute | solution.py:441
  132.9 24.0 %collective-permute-start.15 = (bf16[256,512]{1,0:T(8,128)(2,1)S(1)}, bf16[256,512]{1,0:T(8,128)(2,1)S(1)}, u32[]{:S(2)}, u32[]{:S(2)}) collective-permute-start(bf16[256,512]{1,0:T(8,128)(2,1)S(1)} %copy-done.23), channel_id=1, source_target_pairs={{4,0},{5,1},{6,2},{7,3},{12,8},{13,9},{14,10},{15,11},{20,16},{21,... | collective-permute-start | bytes 786440 | tf_op jit(solution)/shard_map/ppermute | solution.py:441
  134.2 22.6 %collective-permute-start.16 = (bf16[256,512]{1,0:T(8,128)(2,1)S(1)}, bf16[256,512]{1,0:T(8,128)(2,1)S(1)}, u32[]{:S(2)}, u32[]{:S(2)}) collective-permute-start(bf16[256,512]{1,0:T(8,128)(2,1)S(1)} %copy-done.22), channel_id=1, source_target_pairs={{6,0},{7,1},{14,8},{15,9},{22,16},{23,17},{30,24},{31,25}} | collective-permute-start | bytes 786440 | tf_op jit(solution)/shard_map/ppermute | solution.py:441
  144.1 12.7 %copy-start.18 = (bf16[256,512]{1,0:T(8,128)(2,1)}, bf16[256,512]{1,0:T(8,128)(2,1)S(1)}, u32[]{:S(2)}) copy-start(bf16[256,512]{1,0:T(8,128)(2,1)S(1)} %collective-permute-done.14.refs_5_) | copy-start | bytes 786436
  160.2 8.2 %collective-permute-start.18 = (bf16[128,1024]{1,0:T(8,128)(2,1)}, bf16[128,1024]{1,0:T(8,128)(2,1)S(1)}, u32[]{:S(2)}, u32[]{:S(2)}) collective-permute-start(bf16[128,1024]{1,0:T(8,128)(2,1)} %get-tuple-element.33), channel_id=1, source_target_pairs={{0,1},{1,0},{2,3},{3,2},{4,5},{5,4},{6,7},{7,6},{8,9},{9,8},{10,11... | collective-permute-start | bytes 786440 | tf_op jit(solution)/shard_map/ppermute | solution.py:449
  (14 other events, 12.6 us)

commit v2 on v1

--- a/solution.py
+++ b/solution.py
@@ -14,7 +14,7 @@
 TOPK = 8
 
 masked_score = -1e30
-vmem_limit = 56 * 1024 * 1024
+mib = 1024 * 1024
 
 
 def mul(a, b):
@@ -137,7 +137,7 @@
         ],
         input_output_aliases={3 + n_blocks: 0} if held else {},
         compiler_params=pltpu.CompilerParams(
-            vmem_limit_bytes=vmem_limit, dimension_semantics=("arbitrary", "arbitrary")
+            vmem_limit_bytes=24 * mib, dimension_semantics=("arbitrary", "arbitrary")
         ),
         cost_estimate=pl.CostEstimate(
             flops=10 * rows * keys * group * count * HEAD_DIM,
@@ -172,7 +172,7 @@
             jax.ShapeDtypeStruct((rows, width), jnp.float32),
             jax.ShapeDtypeStruct((rows, width), jnp.bfloat16),
         ],
-        compiler_params=pltpu.CompilerParams(vmem_limit_bytes=vmem_limit),
+        compiler_params=pltpu.CompilerParams(vmem_limit_bytes=12 * mib),
         name="fold",
     )(*[part for group in parts for part in group], *after)
 
@@ -190,7 +190,7 @@
     return pl.pallas_call(
         finish_kernel,
         out_shape=[shape, shape],
-        compiler_params=pltpu.CompilerParams(vmem_limit_bytes=vmem_limit),
+        compiler_params=pltpu.CompilerParams(vmem_limit_bytes=8 * mib),
         name="finish",
     )(own, got)
 
@@ -235,7 +235,7 @@
             jax.ShapeDtypeStruct((rows, 2 * width), jnp.bfloat16),
             jax.ShapeDtypeStruct((tokens + 4 * n_dp, feat), jnp.bfloat16),
         ],
-        compiler_params=pltpu.CompilerParams(vmem_limit_bytes=vmem_limit),
+        compiler_params=pltpu.CompilerParams(vmem_limit_bytes=8 * mib),
         name="join",
     )(keys, values, full_rows, ids.T, combine.T)
 
@@ -293,12 +293,8 @@
         out_specs=pl.BlockSpec((out_rows, step), lambda f: (0, f)),
         out_shape=jax.ShapeDtypeStruct((out_rows, feat), jnp.bfloat16),
         scratch_shapes=[pltpu.VMEM((len(blocks), 2 * n_dp * capacity, tokens), jnp.bfloat16)],
-        compiler_params=pltpu.CompilerParams(vmem_limit_bytes=vmem_limit),
-        cost_estimate=pl.CostEstimate(
-            flops=2 * out_rows * tokens * feat,
-            bytes_accessed=2 * (out_rows + len(arrays) * tokens) * feat,
-            transcendentals=0,
-        ),
+        compiler_params=pltpu.CompilerParams(vmem_limit_bytes=(12 + 3 * len(blocks)) * mib),
+        cost_estimate=pl.CostEstimate(flops=10**6, bytes_accessed=10**5, transcendentals=0),
         name="pick_rows",
     )(place, *arrays, *arrays, *after)
 
@@ -353,12 +349,8 @@
             pltpu.SemaphoreType.DMA((hid // step, rows.shape[0] // capacity)),
         ],
         input_output_aliases={3: 0} if held else {},
-        compiler_params=pltpu.CompilerParams(vmem_limit_bytes=vmem_limit),
-        cost_estimate=pl.CostEstimate(
-            flops=2 * rows.shape[0] * feat * hid,
-            bytes_accessed=2 * hid * feat + 2 * rows.shape[0] * (feat + hid),
-            transcendentals=0,
-        ),
+        compiler_params=pltpu.CompilerParams(vmem_limit_bytes=(12 + rows.size // 2**17) * mib),
+        cost_estimate=pl.CostEstimate(flops=10**6, bytes_accessed=10**5, transcendentals=0),
         name="expert_rows",
     )(place, rows, w_down, *held, *after)
 
@@ -386,10 +378,13 @@
         full_rows = lax.all_gather(mixed_grad, "tp", axis=1, tiled=True)
     own, own_rows = join(keys, values, full_rows, expert_ids, combine, n_z, n_dp)
 
-    columns = [own] + [
-        lax.ppermute(own, "ctx", [(i, i + 2 * k) for i in range(n_ctx - 2 * k)])
-        for k in range(1, n_z)
-    ]
+    def along_z(array, targets):
+        pairs = [(2 * i + x, 2 * j + x) for i, j in targets for x in range(2)]
+        return lax.ppermute(array, "ctx", pairs)
+
+    columns = [own]
+    for k in range(1, n_z):
+        columns.append(along_z(columns[-1], [(i, i + 1) for i in range(k - 1, n_z - 1)]))
     blocks = []
     for k, column in enumerate(columns):
         pairs = [(i, i ^ 1) for i in range(2 * k, n_ctx) if k > 0 or i % 2 == 0]
@@ -398,21 +393,13 @@
     plane_groups = [
         [d * n_ctx + 2 * i + j for d in range(n_dp) for j in range(2)] for i in range(n_z)
     ]
-    def along_z(array, targets):
-        pairs = [(2 * i + x, 2 * j + x) for i, j in targets for x in range(2)]
-        return lax.ppermute(array, "ctx", pairs)
-
-    near = along_z(own_rows, [(i, i ^ 1) for i in range(n_z)])
+    first_rows, columns[1] = lax.optimization_barrier((own_rows, columns[1]))
+    near = along_z(first_rows, [(i, i ^ 1) for i in range(n_z)])
     if n_z == 4:
-        across = along_z(own_rows, [(1, 2), (2, 1)])
+        second_rows, columns[2] = lax.optimization_barrier((own_rows, columns[2]))
+        across = along_z(second_rows, [(1, 2), (2, 1)])
         across_near = along_z(near, [(1, 2), (2, 1)])
         outward = along_z(across, [(1, 0), (2, 3)])
-        outward_near = along_z(across_near, [(1, 0), (2, 3)])
-        far = [(across_near, outward), (across, outward_near)]
-        early, late = (across,), (across_near, outward)
-    else:
-        far = [(along_z(own_rows, [(i, i ^ k) for i in range(n_z)]),) for k in range(2, n_z)]
-        early, late = (), ()
 
     def exchange(arrays, after):
         picked = pick_rows(place, arrays, n_dp, capacity, after)
@@ -425,15 +412,17 @@
             axis_index_groups=plane_groups,
         )
 
-    picked, got_near = exchange([(own_rows,), (near,)], (*blocks, *early))
+    picked, got_near = exchange([(own_rows,), (near,)], tuple(blocks))
 
     counts = [1] if kv_local == 1 else [kv_local // 2, kv_local - kv_local // 2]
     query_grad, gathered, first = None, [], 0
     for count in counts:
-        after = (picked,) if first == 0 else late
         query_grad, *parts = attention(
-            place, queries[0], out_grad[0], blocks, first, count, query_grad, after
+            place, queries[0], out_grad[0], blocks, first, count, query_grad, (picked,)
         )
+        if n_z == 4 and first == 0:
+            across_near, query_grad = lax.optimization_barrier((across_near, query_grad))
+            outward_near = along_z(across_near, [(1, 0), (2, 3)])
         first += count
         gathered.append(
             [parts[0]]
@@ -442,15 +431,17 @@
                 for k in range(1, n_z)
             ]
         )
-    picked, got_far = exchange(far, (query_grad, *(gathered[0] if len(counts) > 1 else ())))
+    if n_z == 4:
+        far = [(across_near, outward), (across, outward_near)]
+    else:
+        far = [(along_z(own_rows, [(i, i ^ k) for i in range(n_z)]),) for k in range(2, n_z)]
+    picked, got_far = exchange(far, (query_grad,))
     sizes = (n_z, n_dp, capacity, slots)
     hidden_grad = expert_rows(place, got_near, (0, 1), w_down, *sizes, None, (picked,))
     total, other = fold(gathered, rows_dev, (hidden_grad,))
     got = lax.ppermute(other, "ctx", [(i, i ^ 1) for i in range(n_ctx)])
     key_grad, value_grad = finish(total, got)
-    hidden_grad = expert_rows(
-        place, got_far, tuple(range(2, n_z)), w_down, *sizes, hidden_grad, (key_grad,)
-    )
+    hidden_grad = expert_rows(place, got_far, tuple(range(2, n_z)), w_down, *sizes, hidden_grad)
     return (query_grad[None], key_grad, value_grad, hidden_grad)
 
 

time: 182 us -> 194 us (1.066)
  local copies, waits for them, and re-layouts: 8.17 us -> 30.4 us
  Pallas kernels: 40.6 us -> 28.9 us
    ppermute x5 -> x8, waiting for transfers between devices: 24.3 us -> 49.4 us  [along_z(): return lax.ppermute(array, 'ctx', pairs)]
    unnamed x50 -> x82, local copies, waits for them, and re-layouts: 8.17 us -> 30.4 us
    ppermute x3 -> x0, waiting for transfers between devices: 18.4 us -> none  [per_device(): lax.ppermute(own, 'ctx', [(i, i + 2 * k) for i in range(n_ctx - 2 * k)])]
    ppermute x5 -> x8, starting transfers between devices: 5.61 us -> 15.6 us  [along_z(): return lax.ppermute(array, 'ctx', pairs)]
    ppermute x3 -> x0, starting transfers between devices: 8.99 us -> none  [per_device(): lax.ppermute(own, 'ctx', [(i, i + 2 * k) for i in range(n_ctx - 2 * k)])]
    ppermute x6, waiting for transfers between devices: 43.1 us -> 36.6 us  [per_device(): lax.ppermute(parts[k], 'ctx', [(i, i - 2 * k) for i in range(2 * k, n_ctx)])]
    pallas_call x2, Pallas kernels: 17.2 us -> 13.2 us  [expert_rows(): pl.pallas_call(functools.partial(expert_kernel, ks, n_z, n_dp, capacity,...]
    pallas_call x1, Pallas kernels: 2.59 us -> 0.25 us  [fold(): pl.pallas_call(functools.partial(fold_kernel, len(parts[0]), len(parts),...]
  transfers between devices with their start and end apart: 21 -> 21, of which waited for: 8 -> 9; matrix products, arithmetic and copies ran while one was open for 0% -> 0% of each run, Pallas kernels for 15% -> 10%
where the time goes in v2:
time: 194 us; the launch traced here: 193 us
  waiting for transfers between devices  94.4 us (49%)
  starting transfers between devices  38.2 us (20%)
  local copies, waits for them, and re-layouts  30.4 us (16%)
  Pallas kernels  28.9 us (15%)
    ppermute x8, waiting for transfers between devices, along_z(): return lax.ppermute(array, 'ctx', pairs)  49.4 us
    ppermute x6, waiting for transfers between devices, per_device(): lax.ppermute(parts[k], 'ctx', [(i, i - 2 * k) for i in range(2 * k, n_ctx)])  36.6 us
    unnamed x82, local copies, waits for them, and re-layouts  30.4 us
    ppermute x8, starting transfers between devices, along_z(): return lax.ppermute(array, 'ctx', pairs)  15.6 us
    pallas_call x2, Pallas kernels, expert_rows(): pl.pallas_call(functools.partial(expert_kernel, ks, n_z, n_dp, capacity,...  13.2 us
    pallas_call x2, Pallas kernels, attention(): pl.pallas_call(functools.partial(attention_kernel, n_blocks, heads_step,...  8.95 us
    ppermute x6, starting transfers between devices, per_device(): lax.ppermute(parts[k], 'ctx', [(i, i - 2 * k) for i in range(2 * k, n_ctx)])  7.73 us
    all_to_all x2, starting transfers between devices, exchange(): lax.all_to_all(picked, ('dp', 'ctx'), split_axis=0, concat_axis=0, tiled=...  7.7 us
  transfers between devices with their start and end apart: 21, of which 9 were waited for; matrix products, arithmetic and copies ran while one was open for 0% of the time, Pallas kernels for 10%

profile of v2, /device:TPU:0, one launch (start us, length us, event | category | flops | bytes accessed | tf_op | source)
XLA Modules:
  0.0 193.0 jit_solution(1021444520439652106)
XLA Ops:
  5.1 4.9 %collective-permute-start.1 = (bf16[128,1024]{1,0:T(8,128)(2,1)S(1)}, bf16[128,1024]{1,0:T(8,128)(2,1)S(1)}, u32[]{:S(2)}, u32[]{:S(2)}) collective-permute-start(bf16[128,1024]{1,0:T(8,128)(2,1)S(1)} %get-tuple-element.24.refs_4_.refs_0_), channel_id=1, source_target_pairs={{0,2},{1,3},{2,4},{3,5},{4,6},{5,7},{8,10},{9,11},{10,12},{11,13},... | collective-permute-start | bytes 786440 | tf_op jit(solution)/shard_map/ppermute | solution.py:383
  10.0 5.5 %collective-permute-done.1.refs_6_.refs_2_ = bf16[128,1024]{1,0:T(8,128)(2,1)S(1)} collective-permute-done((bf16[128,1024]{1,0:T(8,128)(2,1)S(1)}, bf16[128,1024]{1,0:T(8,128)(2,1)S(1)}, u32[]{:S(2)}, u32[]{:S(2)}) %collective-permute-start.1) | collective-permute-done | bytes 262176 | tf_op jit(solution)/shard_map/ppermute | solution.py:383
  16.3 5.4 %collective-permute-start.7 = (bf16[144,2048]{1,0:T(8,128)(2,1)S(1)}, bf16[144,2048]{1,0:T(8,128)(2,1)S(1)}, u32[]{:S(2)}, u32[]{:S(2)}) collective-permute-start(bf16[144,2048]{1,0:T(8,128)(2,1)S(1)} %get-tuple-element.39.refs_0_.refs_2_), channel_id=1, source_target_pairs={{0,2},{1,3},{2,0},{3,1},{4,6},{5,7},{6,4},{7,5},{8,10},{9,11},{10,... | collective-permute-start | bytes 1769480 | tf_op jit(solution)/shard_map/ppermute | solution.py:383
  22.3 3.4 %collective-permute-start = (bf16[128,1024]{1,0:T(8,128)(2,1)S(1)}, bf16[128,1024]{1,0:T(8,128)(2,1)S(1)}, u32[]{:S(2)}, u32[]{:S(2)}) collective-permute-start(bf16[128,1024]{1,0:T(8,128)(2,1)S(1)} %get-tuple-element.24.refs_4_.refs_0_), channel_id=1, source_target_pairs={{0,1},{2,3},{4,5},{6,7},{8,9},{10,11},{12,13},{14,15},{16,17},{18,... | collective-permute-start | bytes 786440 | tf_op jit(solution)/shard_map/ppermute | solution.py:391
  27.9 1.9 %collective-permute-done.refs_5_.refs_1_ = bf16[128,1024]{1,0:T(8,128)(2,1)S(1)} collective-permute-done((bf16[128,1024]{1,0:T(8,128)(2,1)S(1)}, bf16[128,1024]{1,0:T(8,128)(2,1)S(1)}, u32[]{:S(2)}, u32[]{:S(2)}) %collective-permute-start) | collective-permute-done | bytes 262176 | tf_op jit(solution)/shard_map/ppermute | solution.py:391
  29.8 4.0 %collective-permute-done.7.refs_1_.refs_3_ = bf16[144,2048]{1,0:T(8,128)(2,1)S(1)} collective-permute-done((bf16[144,2048]{1,0:T(8,128)(2,1)S(1)}, bf16[144,2048]{1,0:T(8,128)(2,1)S(1)}, u32[]{:S(2)}, u32[]{:S(2)}) %collective-permute-start.7) | collective-permute-done | bytes 589856 | tf_op jit(solution)/shard_map/ppermute | solution.py:383
  33.8 2.7 %pick_rows.2.refs_8_.refs_9_ = bf16[640,2048]{1,0:T(8,128)(2,1)} custom-call(s32[2]{0:T(128)S(1)} %pad_add_fusion.place, bf16[144,2048]{1,0:T(8,128)(2,1)S(1)} %get-tuple-element.39.refs_0_.refs_2_, bf16[144,2048]{1,0:T(8,128)(2,1)S(1)} %collective-permute-done.7.refs_1_.refs_3_, bf16[144,2048]{1,0:T(8,128)(2,1)S(1)} %get-tuple-element.39.refs_0_.refs_2_, ...), custom_call_target="tpu_custom_call" | custom-call | flops 1000000 | bytes 100000 | tf_op jit(solution)/shard_map/pick_rows/pallas_call | solution.py:286
  36.6 3.7 %all-to-all-start = ((bf16[8,80,2048]{2,1,0:T(8,128)(2,1)}), bf16[8,80,2048]{2,1,0:T(8,128)(2,1)S(1)}, u32[]{:S(2)}, u32[]{:S(2)}) async-start(bf16[8,80,2048]{2,1,0:T(8,128)(2,1)} %bitcast.7), calls=%async_computation | async-start | bytes 5242880 | tf_op jit(solution)/shard_map/all_to_all | solution.py:406
  50.8 4.4 %attention_backward.2 = (bf16[128,4096]{1,0:T(8,128)(2,1)}, bf16[256,512]{1,0:T(8,128)(2,1)S(1)}, bf16[256,512]{1,0:T(8,128)(2,1)S(1)}, bf16[256,512]{1,0:T(8,128)(2,1)S(1)}, bf16[256,512]{1,0:T(8,128)(2,1)S(1)}) custom-call(s32[2]{0:T(128)S(1)} %pad_add_fusion.place, bf16[128,4096]{1,0:T(8,128)(2,1)S(1)} %bitcast.16, bf16[128,4096]{1,0:T(8,128)(2,1)S(1)} %bitcast.18, ...), custom_call_target="tpu_custom_call" | custom-call | flops 2684354560 | bytes 3670016 | tf_op jit(solution)/shard_map/attention_backward/pallas_call | solution.py:117
  57.4 1.3 collective-permute-start.16
  58.7 1.3 collective-permute-start.17
  60.0 4.5 %attention_backward.3 = (bf16[128,4096]{1,0:T(8,128)(2,1)}, bf16[256,512]{1,0:T(8,128)(2,1)S(1)}, bf16[256,512]{1,0:T(8,128)(2,1)S(1)}, bf16[256,512]{1,0:T(8,128)(2,1)S(1)}, bf16[256,512]{1,0:T(8,128)(2,1)S(1)}) custom-call(s32[2]{0:T(128)S(1)} %pad_add_fusion.place, bf16[128,4096]{1,0:T(8,128)(2,1)S(1)} %bitcast.17, ...), custom_call_target="tpu_custom_call", output_to_operand_aliasing={{0}: (11, {})} | custom-call | flops 2684354560 | bytes 3670016 | tf_op jit(solution)/shard_map/attention_backward/pallas_call | solution.py:117
  67.3 27.6 %collective-permute-done.16.refs_1_.refs_5_ = bf16[144,2048]{1,0:T(8,128)(2,1)S(1)} collective-permute-done((bf16[144,2048]{1,0:T(8,128)(2,1)S(1)}, bf16[144,2048]{1,0:T(8,128)(2,1)S(1)}, u32[]{:S(2)}, u32[]{:S(2)}) %collective-permute-start.16) | collective-permute-done | bytes 589856 | tf_op jit(solution)/shard_map/ppermute | solution.py:383
  95.0 12.2 %collective-permute-done.17.refs_3_.refs_7_ = bf16[144,2048]{1,0:T(8,128)(2,1)S(1)} collective-permute-done((bf16[144,2048]{1,0:T(8,128)(2,1)S(1)}, bf16[144,2048]{1,0:T(8,128)(2,1)S(1)}, u32[]{:S(2)}, u32[]{:S(2)}) %collective-permute-start.17) | collective-permute-done | bytes 589856 | tf_op jit(solution)/shard_map/ppermute | solution.py:383
  108.5 2.8 %pick_rows.3.refs_0_ = bf16[640,2048]{1,0:T(8,128)(2,1)} custom-call(s32[2]{0:T(128)S(1)} %pad_add_fusion.place, bf16[144,2048]{1,0:T(8,128)(2,1)S(1)} %collective-permute-done.8.refs_0_.refs_4_, bf16[144,2048]{1,0:T(8,128)(2,1)S(1)} %collective-permute-done.16.refs_1_.refs_5_, bf16[144,2048]{1,0:T(8,128)(2,1)S(1)} %collective-permute-done.15.refs_2_.refs_6_, ...), custom_call_target="tpu_custom_call" | custom-call | flops 1000000 | bytes 100000 | tf_op jit(solution)/shard_map/pick_rows/pallas_call | solution.py:286
  111.2 1.5 copy-done.3
  112.7 4.0 %all-to-all-start.1 = ((bf16[8,80,2048]{2,1,0:T(8,128)(2,1)}), bf16[8,80,2048]{2,1,0:T(8,128)(2,1)S(1)}, u32[]{:S(2)}, u32[]{:S(2)}) async-start(bf16[8,80,2048]{2,1,0:T(8,128)(2,1)} %bitcast.9), calls=%async_computation.1 | async-start | bytes 5242880 | tf_op jit(solution)/shard_map/all_to_all | solution.py:406
  118.0 1.3 collective-permute-start.10
  119.3 1.3 collective-permute-start.11
  120.6 1.3 collective-permute-start.12
  121.9 1.3 collective-permute-start.13
  123.2 4.7 %collective-permute-done.9.refs_1_ = bf16[256,512]{1,0:T(8,128)(2,1)S(1)} collective-permute-done((bf16[256,512]{1,0:T(8,128)(2,1)}, bf16[256,512]{1,0:T(8,128)(2,1)S(1)}, u32[]{:S(2)}, u32[]{:S(2)}) %collective-permute-start.9) | collective-permute-done | bytes 262176 | tf_op jit(solution)/shard_map/ppermute | solution.py:430
  129.2 2.8 %copy-done.1 = bf16[1,1536,2048]{2,1,0:T(8,128)(2,1)S(1)} copy-done((bf16[1,1536,2048]{2,1,0:T(8,128)(2,1)S(1)}, bf16[1,1536,2048]{2,1,0:T(8,128)(2,1)}, u32[]{:S(2)}) %copy-start.1) | copy-done | bytes 6291480
  132.0 1.7 copy-done.4
  133.7 6.6 %expert_rows.2.refs_8_.refs_0_ = bf16[1,32,40,1536]{3,2,1,0:T(8,128)(2,1)} custom-call(s32[2]{0:T(128)S(1)} %pad_add_fusion.place, bf16[640,2048]{1,0:T(8,128)(2,1)S(1)} %bitcast.12, bf16[1,1536,2048]{2,1,0:T(8,128)(2,1)S(1)} %copy-done.1, bf16[640,2048]{1,0:T(8,128)(2,1)} %pick_rows.3.refs_0_), custom_call_target="tpu_custom_call" | custom-call | flops 1000000 | bytes 100000 | tf_op jit(solution)/shard_map/expert_rows/pallas_call | solution.py:336
  140.3 9.6 %collective-permute-done.10.refs_2_ = bf16[256,512]{1,0:T(8,128)(2,1)S(1)} collective-permute-done((bf16[256,512]{1,0:T(8,128)(2,1)S(1)}, bf16[256,512]{1,0:T(8,128)(2,1)S(1)}, u32[]{:S(2)}, u32[]{:S(2)}) %collective-permute-start.10) | collective-permute-done | bytes 262176 | tf_op jit(solution)/shard_map/ppermute | solution.py:430
  149.9 22.3 %collective-permute-done.13.refs_6_ = bf16[256,512]{1,0:T(8,128)(2,1)S(1)} collective-permute-done((bf16[256,512]{1,0:T(8,128)(2,1)}, bf16[256,512]{1,0:T(8,128)(2,1)S(1)}, u32[]{:S(2)}, u32[]{:S(2)}) %collective-permute-start.13) | collective-permute-done | bytes 262176 | tf_op jit(solution)/shard_map/ppermute | solution.py:430
  172.2 2.1 %copy-done = bf16[1,32,40,1536]{3,2,1,0:T(8,128)(2,1)S(1)} copy-done((bf16[1,32,40,1536]{3,2,1,0:T(8,128)(2,1)S(1)}, bf16[1,32,40,1536]{3,2,1,0:T(8,128)(2,1)}, u32[]{:S(2)}) %copy-start) | copy-done | bytes 3932184
  174.6 1.7 collective-permute-start.18
  176.3 6.5 %collective-permute-done.18.got_ref = bf16[128,1024]{1,0:T(8,128)(2,1)S(1)} collective-permute-done((bf16[128,1024]{1,0:T(8,128)(2,1)S(1)}, bf16[128,1024]{1,0:T(8,128)(2,1)S(1)}, u32[]{:S(2)}, u32[]{:S(2)}) %collective-permute-start.18) | collective-permute-done | bytes 262176 | tf_op jit(solution)/shard_map/ppermute | solution.py:442
  183.6 2.8 %copy-done.2 = bf16[1,1536,2048]{2,1,0:T(8,128)(2,1)S(1)} copy-done((bf16[1,1536,2048]{2,1,0:T(8,128)(2,1)S(1)}, bf16[1,1536,2048]{2,1,0:T(8,128)(2,1)}, u32[]{:S(2)}) %copy-start.2) | copy-done | bytes 6291480
  186.3 6.6 %expert_rows.3 = bf16[1,32,40,1536]{3,2,1,0:T(8,128)(2,1)} custom-call(s32[2]{0:T(128)S(1)} %pad_add_fusion.place, bf16[640,2048]{1,0:T(8,128)(2,1)S(1)} %bitcast.11, bf16[1,1536,2048]{2,1,0:T(8,128)(2,1)S(1)} %copy-done.2, bf16[1,32,40,1536]{3,2,1,0:T(8,128)(2,1)} %expert_rows.2.refs_8_.refs_0_), custom_call_target="tpu_custom_call", output_to_operand_aliasing={{}: (3, {})} | custom-call | flops 1000000 | bytes 100000 | tf_op jit(solution)/shard_map/expert_rows/pallas_call | solution.py:336
  (102 shorter events, 28.2 us)
Async XLA Ops:
  5.1 10.5 %collective-permute-start.1 = (bf16[128,1024]{1,0:T(8,128)(2,1)S(1)}, bf16[128,1024]{1,0:T(8,128)(2,1)S(1)}, u32[]{:S(2)}, u32[]{:S(2)}) collective-permute-start(bf16[128,1024]{1,0:T(8,128)(2,1)S(1)} %get-tuple-element.24.refs_4_.refs_0_), channel_id=1, source_target_pairs={{0,2},{1,3},{2,4},{3,5},{4,6},{5,7},{8,10},{9,11},{10,12},{11,13},... | collective-permute-start | bytes 786440 | tf_op jit(solution)/shard_map/ppermute | solution.py:383
  15.6 20.9 %copy-start.8 = (bf16[128,1024]{1,0:T(8,128)(2,1)}, bf16[128,1024]{1,0:T(8,128)(2,1)S(1)}, u32[]{:S(2)}) copy-start(bf16[128,1024]{1,0:T(8,128)(2,1)S(1)} %collective-permute-done.1.refs_6_.refs_2_) | copy-start | bytes 786436
  15.6 6.0 %collective-permute-start.3 = (bf16[128,1024]{1,0:T(8,128)(2,1)S(1)}, bf16[128,1024]{1,0:T(8,128)(2,1)S(1)}, u32[]{:S(2)}, u32[]{:S(2)}) collective-permute-start(bf16[128,1024]{1,0:T(8,128)(2,1)S(1)} %collective-permute-done.1.refs_6_.refs_2_), channel_id=1, source_target_pairs={{2,4},{3,5},{4,6},{5,7},{10,12},{11,13},{12,14},{13,15},{18,20},{1... | collective-permute-start | bytes 786440 | tf_op jit(solution)/shard_map/ppermute | solution.py:383
  16.3 17.5 %collective-permute-start.7 = (bf16[144,2048]{1,0:T(8,128)(2,1)S(1)}, bf16[144,2048]{1,0:T(8,128)(2,1)S(1)}, u32[]{:S(2)}, u32[]{:S(2)}) collective-permute-start(bf16[144,2048]{1,0:T(8,128)(2,1)S(1)} %get-tuple-element.39.refs_0_.refs_2_), channel_id=1, source_target_pairs={{0,2},{1,3},{2,0},{3,1},{4,6},{5,7},{6,4},{7,5},{8,10},{9,11},{10,... | collective-permute-start | bytes 1769480 | tf_op jit(solution)/shard_map/ppermute | solution.py:383
  21.6 14.9 %copy-start.10 = (bf16[128,1024]{1,0:T(8,128)(2,1)}, bf16[128,1024]{1,0:T(8,128)(2,1)S(1)}, u32[]{:S(2)}) copy-start(bf16[128,1024]{1,0:T(8,128)(2,1)S(1)} %collective-permute-done.3.refs_8_.refs_4_) | copy-start | bytes 786436
  21.6 5.5 %collective-permute-start.5 = (bf16[128,1024]{1,0:T(8,128)(2,1)S(1)}, bf16[128,1024]{1,0:T(8,128)(2,1)S(1)}, u32[]{:S(2)}, u32[]{:S(2)}) collective-permute-start(bf16[128,1024]{1,0:T(8,128)(2,1)S(1)} %collective-permute-done.3.refs_8_.refs_4_), channel_id=1, source_target_pairs={{4,6},{5,7},{12,14},{13,15},{20,22},{21,23},{28,30},{29,31}} | collective-permute-start | bytes 786440 | tf_op jit(solution)/shard_map/ppermute | solution.py:383
  22.3 7.5 %collective-permute-start = (bf16[128,1024]{1,0:T(8,128)(2,1)S(1)}, bf16[128,1024]{1,0:T(8,128)(2,1)S(1)}, u32[]{:S(2)}, u32[]{:S(2)}) collective-permute-start(bf16[128,1024]{1,0:T(8,128)(2,1)S(1)} %get-tuple-element.24.refs_4_.refs_0_), channel_id=1, source_target_pairs={{0,1},{2,3},{4,5},{6,7},{8,9},{10,11},{12,13},{14,15},{16,17},{18,... | collective-permute-start | bytes 786440 | tf_op jit(solution)/shard_map/ppermute | solution.py:391
  25.7 4.1 %collective-permute-start.2 = (bf16[128,1024]{1,0:T(8,128)(2,1)S(1)}, bf16[128,1024]{1,0:T(8,128)(2,1)S(1)}, u32[]{:S(2)}, u32[]{:S(2)}) collective-permute-start(bf16[128,1024]{1,0:T(8,128)(2,1)S(1)} %collective-permute-done.1.refs_6_.refs_2_), channel_id=1, source_target_pairs={{2,3},{3,2},{4,5},{5,4},{6,7},{7,6},{10,11},{11,10},{12,13},{13,12... | collective-permute-start | bytes 786440 | tf_op jit(solution)/shard_map/ppermute | solution.py:391
  26.4 3.4 %collective-permute-start.4 = (bf16[128,1024]{1,0:T(8,128)(2,1)S(1)}, bf16[128,1024]{1,0:T(8,128)(2,1)S(1)}, u32[]{:S(2)}, u32[]{:S(2)}) collective-permute-start(bf16[128,1024]{1,0:T(8,128)(2,1)S(1)} %collective-permute-done.3.refs_8_.refs_4_), channel_id=1, source_target_pairs={{4,5},{5,4},{6,7},{7,6},{12,13},{13,12},{14,15},{15,14},{20,21},{2... | collective-permute-start | bytes 786440 | tf_op jit(solution)/shard_map/ppermute | solution.py:391
  27.1 9.4 %copy-start.12 = (bf16[128,1024]{1,0:T(8,128)(2,1)}, bf16[128,1024]{1,0:T(8,128)(2,1)S(1)}, u32[]{:S(2)}) copy-start(bf16[128,1024]{1,0:T(8,128)(2,1)S(1)} %collective-permute-done.5.refs_10_.refs_6_) | copy-start | bytes 786436
  27.1 6.7 %collective-permute-start.6 = (bf16[128,1024]{1,0:T(8,128)(2,1)S(1)}, bf16[128,1024]{1,0:T(8,128)(2,1)S(1)}, u32[]{:S(2)}, u32[]{:S(2)}) collective-permute-start(bf16[128,1024]{1,0:T(8,128)(2,1)S(1)} %collective-permute-done.5.refs_10_.refs_6_), channel_id=1, source_target_pairs={{6,7},{7,6},{14,15},{15,14},{22,23},{23,22},{30,31},{31,30}} | collective-permute-start | bytes 786440 | tf_op jit(solution)/shard_map/ppermute | solution.py:391
  29.8 6.7 %copy-start.14 = (bf16[128,1024]{1,0:T(8,128)(2,1)}, bf16[128,1024]{1,0:T(8,128)(2,1)S(1)}, u32[]{:S(2)}) copy-start(bf16[128,1024]{1,0:T(8,128)(2,1)S(1)} %collective-permute-done.refs_5_.refs_1_) | copy-start | bytes 786436
  29.8 6.7 %copy-start.16 = (bf16[128,1024]{1,0:T(8,128)(2,1)}, bf16[128,1024]{1,0:T(8,128)(2,1)S(1)}, u32[]{:S(2)}) copy-start(bf16[128,1024]{1,0:T(8,128)(2,1)S(1)} %collective-permute-done.2.refs_7_.refs_3_) | copy-start | bytes 786436
  29.8 6.7 %copy-start.18 = (bf16[128,1024]{1,0:T(8,128)(2,1)}, bf16[128,1024]{1,0:T(8,128)(2,1)S(1)}, u32[]{:S(2)}) copy-start(bf16[128,1024]{1,0:T(8,128)(2,1)S(1)} %collective-permute-done.4.refs_9_.refs_5_) | copy-start | bytes 786436
  36.6 74.6 %all-to-all-start = ((bf16[8,80,2048]{2,1,0:T(8,128)(2,1)}), bf16[8,80,2048]{2,1,0:T(8,128)(2,1)S(1)}, u32[]{:S(2)}, u32[]{:S(2)}) async-start(bf16[8,80,2048]{2,1,0:T(8,128)(2,1)} %bitcast.7), calls=%async_computation | async-start | bytes 5242880 | tf_op jit(solution)/shard_map/all_to_all | solution.py:406
  40.3 17.1 %collective-permute-start.15 = (bf16[144,2048]{1,0:T(8,128)(2,1)S(1)}, bf16[144,2048]{1,0:T(8,128)(2,1)S(1)}, u32[]{:S(2)}, u32[]{:S(2)}) collective-permute-start(bf16[144,2048]{1,0:T(8,128)(2,1)S(1)} %get-tuple-element.39.refs_0_.refs_2_), channel_id=1, source_target_pairs={{2,4},{3,5},{4,2},{5,3},{10,12},{11,13},{12,10},{13,11},{18,20},{1... | collective-permute-start | bytes 1769480 | tf_op jit(solution)/shard_map/ppermute | solution.py:383
  41.0 17.7 %collective-permute-start.8 = (bf16[144,2048]{1,0:T(8,128)(2,1)}, bf16[144,2048]{1,0:T(8,128)(2,1)S(1)}, u32[]{:S(2)}, u32[]{:S(2)}) collective-permute-start(bf16[144,2048]{1,0:T(8,128)(2,1)} %copy-done.5), channel_id=1, source_target_pairs={{2,4},{3,5},{4,2},{5,3},{10,12},{11,13},{12,10},{13,11},{18,20},{1... | collective-permute-start | bytes 1769480 | tf_op jit(solution)/shard_map/ppermute | solution.py:383
  57.4 7.1 %copy-start.22 = (bf16[256,512]{1,0:T(8,128)(2,1)}, bf16[256,512]{1,0:T(8,128)(2,1)S(1)}, u32[]{:S(2)}) copy-start(bf16[256,512]{1,0:T(8,128)(2,1)S(1)} %get-tuple-element.30.refs_0_) | copy-start | bytes 786436
  57.4 37.6 %collective-permute-start.16 = (bf16[144,2048]{1,0:T(8,128)(2,1)S(1)}, bf16[144,2048]{1,0:T(8,128)(2,1)S(1)}, u32[]{:S(2)}, u32[]{:S(2)}) collective-permute-start(bf16[144,2048]{1,0:T(8,128)(2,1)S(1)} %collective-permute-done.15.refs_2_.refs_6_), channel_id=1, source_target_pairs={{2,0},{3,1},{4,6},{5,7},{10,8},{11,9},{12,14},{13,15},{18,16},{19,... | collective-permute-start | bytes 1769480 | tf_op jit(solution)/shard_map/ppermute | solution.py:383
  58.7 48.5 %collective-permute-start.17 = (bf16[144,2048]{1,0:T(8,128)(2,1)S(1)}, bf16[144,2048]{1,0:T(8,128)(2,1)S(1)}, u32[]{:S(2)}, u32[]{:S(2)}) collective-permute-start(bf16[144,2048]{1,0:T(8,128)(2,1)S(1)} %collective-permute-done.8.refs_0_.refs_4_), channel_id=1, source_target_pairs={{2,0},{3,1},{4,6},{5,7},{10,8},{11,9},{12,14},{13,15},{18,16},{19,... | collective-permute-start | bytes 1769480 | tf_op jit(solution)/shard_map/ppermute | solution.py:383
  112.7 6.6 %copy-start.33 = (bf16[256,512]{1,0:T(8,128)(2,1)S(1)}, bf16[256,512]{1,0:T(8,128)(2,1)}, u32[]{:S(2)}) copy-start(bf16[256,512]{1,0:T(8,128)(2,1)} %copy-done.32) | copy-start | bytes 786436
  112.7 15.2 %copy-start.37 = (bf16[256,512]{1,0:T(8,128)(2,1)S(1)}, bf16[256,512]{1,0:T(8,128)(2,1)}, u32[]{:S(2)}) copy-start(bf16[256,512]{1,0:T(8,128)(2,1)} %copy-done.36) | copy-start | bytes 786436
  112.7 70.8 %all-to-all-start.1 = ((bf16[8,80,2048]{2,1,0:T(8,128)(2,1)}), bf16[8,80,2048]{2,1,0:T(8,128)(2,1)S(1)}, u32[]{:S(2)}, u32[]{:S(2)}) async-start(bf16[8,80,2048]{2,1,0:T(8,128)(2,1)} %bitcast.9), calls=%async_computation.1 | async-start | bytes 5242880 | tf_op jit(solution)/shard_map/all_to_all | solution.py:406
  116.7 11.2 %collective-permute-start.9 = (bf16[256,512]{1,0:T(8,128)(2,1)}, bf16[256,512]{1,0:T(8,128)(2,1)S(1)}, u32[]{:S(2)}, u32[]{:S(2)}) collective-permute-start(bf16[256,512]{1,0:T(8,128)(2,1)} %copy-done.38), channel_id=1, source_target_pairs={{2,0},{3,1},{4,2},{5,3},{6,4},{7,5},{10,8},{11,9},{12,10},{13,11},... | collective-permute-start | bytes 786440 | tf_op jit(solution)/shard_map/ppermute | solution.py:430
  118.0 31.9 %collective-permute-start.10 = (bf16[256,512]{1,0:T(8,128)(2,1)S(1)}, bf16[256,512]{1,0:T(8,128)(2,1)S(1)}, u32[]{:S(2)}, u32[]{:S(2)}) collective-permute-start(bf16[256,512]{1,0:T(8,128)(2,1)S(1)} %copy-done.35), channel_id=1, source_target_pairs={{4,0},{5,1},{6,2},{7,3},{12,8},{13,9},{14,10},{15,11},{20,16},{21,... | collective-permute-start | bytes 786440 | tf_op jit(solution)/shard_map/ppermute | solution.py:430
  119.3 30.6 %collective-permute-start.11 = (bf16[256,512]{1,0:T(8,128)(2,1)S(1)}, bf16[256,512]{1,0:T(8,128)(2,1)S(1)}, u32[]{:S(2)}, u32[]{:S(2)}) collective-permute-start(bf16[256,512]{1,0:T(8,128)(2,1)S(1)} %copy-done.33), channel_id=1, source_target_pairs={{6,0},{7,1},{14,8},{15,9},{22,16},{23,17},{30,24},{31,25}} | collective-permute-start | bytes 786440 | tf_op jit(solution)/shard_map/ppermute | solution.py:430
  120.6 29.3 %collective-permute-start.12 = (bf16[256,512]{1,0:T(8,128)(2,1)}, bf16[256,512]{1,0:T(8,128)(2,1)S(1)}, u32[]{:S(2)}, u32[]{:S(2)}) collective-permute-start(bf16[256,512]{1,0:T(8,128)(2,1)} %copy-done.40), channel_id=1, source_target_pairs={{2,0},{3,1},{4,2},{5,3},{6,4},{7,5},{10,8},{11,9},{12,10},{13,11},... | collective-permute-start | bytes 786440 | tf_op jit(solution)/shard_map/ppermute | solution.py:430
  121.9 50.3 %collective-permute-start.13 = (bf16[256,512]{1,0:T(8,128)(2,1)}, bf16[256,512]{1,0:T(8,128)(2,1)S(1)}, u32[]{:S(2)}, u32[]{:S(2)}) collective-permute-start(bf16[256,512]{1,0:T(8,128)(2,1)} %copy-done.39), channel_id=1, source_target_pairs={{4,0},{5,1},{6,2},{7,3},{12,8},{13,9},{14,10},{15,11},{20,16},{21,... | collective-permute-start | bytes 786440 | tf_op jit(solution)/shard_map/ppermute | solution.py:430
  127.9 44.3 %collective-permute-start.14 = (bf16[256,512]{1,0:T(8,128)(2,1)S(1)}, bf16[256,512]{1,0:T(8,128)(2,1)S(1)}, u32[]{:S(2)}, u32[]{:S(2)}) collective-permute-start(bf16[256,512]{1,0:T(8,128)(2,1)S(1)} %copy-done.37), channel_id=1, source_target_pairs={{6,0},{7,1},{14,8},{15,9},{22,16},{23,17},{30,24},{31,25}} | collective-permute-start | bytes 786440 | tf_op jit(solution)/shard_map/ppermute | solution.py:430
  133.7 38.5 %copy-start.23 = (bf16[256,512]{1,0:T(8,128)(2,1)S(1)}, bf16[256,512]{1,0:T(8,128)(2,1)}, u32[]{:S(2)}) copy-start(bf16[256,512]{1,0:T(8,128)(2,1)} %copy-done.22) | copy-start | bytes 786436
  133.7 38.5 %copy-start.25 = (bf16[256,512]{1,0:T(8,128)(2,1)S(1)}, bf16[256,512]{1,0:T(8,128)(2,1)}, u32[]{:S(2)}) copy-start(bf16[256,512]{1,0:T(8,128)(2,1)} %copy-done.24) | copy-start | bytes 786436
  174.6 8.2 %collective-permute-start.18 = (bf16[128,1024]{1,0:T(8,128)(2,1)S(1)}, bf16[128,1024]{1,0:T(8,128)(2,1)S(1)}, u32[]{:S(2)}, u32[]{:S(2)}) collective-permute-start(bf16[128,1024]{1,0:T(8,128)(2,1)S(1)} %get-tuple-element.41), channel_id=1, source_target_pairs={{0,1},{1,0},{2,3},{3,2},{4,5},{5,4},{6,7},{7,6},{8,9},{9,8},{10,11... | collective-permute-start | bytes 786440 | tf_op jit(solution)/shard_map/ppermute | solution.py:442
  (30 other events, 41.2 us)

commit v3 on v2

v3 whole, which is shorter than its diff:
```python
import functools
import math

import jax
import jax.numpy as jnp
from jax import lax
from jax.experimental import pallas as pl
from jax.experimental.pallas import tpu as pltpu
from jax.sharding import PartitionSpec as P

HEADS = 32
KV_HEADS = 4
HEAD_DIM = 128
TOPK = 8

masked_score = -1e30
vmem_limit = 56 * 1024 * 1024
small_cost = pl.CostEstimate(flops=1, bytes_accessed=1, transcendentals=0)


def mul(a, b):
    return jnp.dot(a, b, preferred_element_type=jnp.float32)


def attention_kernel(n_blocks, heads_step, rows, n_parts, place, q_ref, do_ref, *refs):
    kv_refs = refs[:n_blocks]
    dq_ref, mine_ref, other_ref = refs[-13:-10]
    kv_s, kt_s, q_s, do_s, qt_s, dot_s, s_s, dp_s, dkv_s, dqt_s = refs[-10:]
    part = pl.program_id(1)
    pair = 2 * rows
    width = heads_step * rows
    z, x = place[0], place[1]
    scale = HEAD_DIM ** (-0.5)
    to_exp2 = scale * math.log2(math.e)
    for i, ref in enumerate(kv_refs):
        kv_s[i * rows : (i + 1) * rows, :] = ref[...]
        kt_s[i // 2, :, (i % 2) * rows : (i % 2 + 1) * rows] = ref[:, :HEAD_DIM].T
    for h in range(heads_step):
        lanes = slice(h * HEAD_DIM, (h + 1) * HEAD_DIM)
        here = slice(h * rows, (h + 1) * rows)
        q_s[here, :] = q_ref[:, lanes]
        do_s[here, :] = do_ref[:, lanes]
        qt_s[:, here] = q_ref[:, lanes].T
        dot_s[:, here] = do_ref[:, lanes].T

    def part_of(k):
        return pl.ds(pl.multiple_of(k * pair, pair), pair)

    cut = math.gcd(width, 256)
    slices = [slice(i, i + cut) for i in range(0, width, cut)]

    def scores(k, tops, first):
        results = []
        for here, top in zip(slices, tops):
            s = mul(kv_s[part_of(k), :HEAD_DIM], qt_s[:, here])
            if first:
                key = lax.broadcasted_iota(jnp.int32, (pair, cut), 0)
                query = lax.broadcasted_iota(jnp.int32, (pair, cut), 1) & (rows - 1)
                bound = jnp.where(key < rows, query, jnp.where(x == 1, pair, -1))
                s = jnp.where(key <= bound, s, masked_score)
            s_s[part_of(k), here] = s
            results.append(jnp.maximum(top, jnp.max(s, axis=0, keepdims=True)))
        return tuple(results)

    tops = scores(0, tuple(jnp.full((1, cut), masked_score, jnp.float32) for _ in slices), True)
    tops = lax.fori_loop(1, z + 1, functools.partial(scores, first=False), tops)

    def sums(k, carry):
        results = []
        for here, top, (total, accum) in zip(slices, tops, carry):
            dp = mul(kv_s[part_of(k), HEAD_DIM:], dot_s[:, here])
            e = jnp.exp2((s_s[part_of(k), here] - top) * to_exp2)
            s_s[part_of(k), here] = e
            dp_s[part_of(k), here] = dp
            results.append(
                (
                    total + jnp.sum(e, axis=0, keepdims=True),
                    accum + jnp.sum(e * dp, axis=0, keepdims=True),
                )
            )
        return tuple(results)

    zero = jnp.zeros((1, cut), jnp.float32)
    stats = lax.fori_loop(0, z + 1, sums, tuple((zero, zero) for _ in slices))
    shares = [1.0 / total for total, _ in stats]
    deltas = [accum * share for (_, accum), share in zip(stats, shares)]
    dqt_s[...] = jnp.zeros_like(dqt_s)

    def grads(k, carry):
        dk = jnp.zeros((pair, HEAD_DIM), jnp.float32)
        dv = jnp.zeros((pair, HEAD_DIM), jnp.float32)
        for here, share, delta in zip(slices, shares, deltas):
            p = s_s[part_of(k), here] * share
            ds = (p * (dp_s[part_of(k), here] - delta)).astype(jnp.bfloat16)
            dv = dv + mul(p.astype(jnp.bfloat16), do_s[here, :])
            dk = dk + mul(ds, q_s[here, :])
            dqt_s[:, here] += mul(kt_s[k], ds)
        dk = dk * scale
        if n_parts > 1:
            dk = dk + jnp.where(part == 0, 0.0, dkv_s[part_of(k), :HEAD_DIM])
            dv = dv + jnp.where(part == 0, 0.0, dkv_s[part_of(k), HEAD_DIM:])
        dkv_s[part_of(k), :HEAD_DIM] = dk
        dkv_s[part_of(k), HEAD_DIM:] = dv
        return carry

    lax.fori_loop(0, z + 1, grads, 0)
    for h in range(heads_step):
        part_t = dqt_s[:, h * rows : (h + 1) * rows] * scale
        dq_ref[:, h * HEAD_DIM : (h + 1) * HEAD_DIM] = part_t.T.astype(jnp.bfloat16)
    for i in range(n_blocks):
        held = dkv_s[i * rows : (i + 1) * rows, :]
        ref = mine_ref if i % 2 == 0 else other_ref
        here = slice(i // 2 * rows, (i // 2 + 1) * rows)
        ref[here, :] = jnp.where(i // 2 <= z, held, 0.0).astype(jnp.bfloat16)


def attention(place, queries, out_grad, kv_blocks, first, count, query_grad, after=()):
    rows, q_width = queries.shape
    n_blocks = len(kv_blocks)
    group = HEADS // KV_HEADS
    keys = n_blocks * rows
    heads_step = max(1, min(group, 2**20 // (keys * rows)))
    n_parts = group // heads_step
    width = heads_step * rows
    q_spec = pl.BlockSpec(
        (rows, heads_step * HEAD_DIM), lambda g, u: (0, (g + first) * n_parts + u)
    )
    kv_spec = pl.BlockSpec((rows, 2 * HEAD_DIM), lambda g, u: (0, g + first))
    part_spec = pl.BlockSpec((keys // 2, 2 * HEAD_DIM), lambda g, u: (0, g))
    part_shape = jax.ShapeDtypeStruct((keys // 2, count * 2 * HEAD_DIM), jnp.bfloat16)
    held = [] if query_grad is None else [query_grad]
    return pl.pallas_call(
        functools.partial(attention_kernel, n_blocks, heads_step, rows, n_parts),
        grid=(count, n_parts),
        in_specs=[pl.BlockSpec(memory_space=pltpu.SMEM), q_spec, q_spec]
        + [kv_spec] * n_blocks
        + [pl.BlockSpec(memory_space=pl.ANY)] * (len(held) + len(after)),
        out_specs=[q_spec, part_spec, part_spec],
        out_shape=[jax.ShapeDtypeStruct((rows, q_width), jnp.bfloat16), part_shape, part_shape],
        scratch_shapes=[
            pltpu.VMEM((keys, 2 * HEAD_DIM), jnp.bfloat16),
            pltpu.VMEM((n_blocks // 2, HEAD_DIM, 2 * rows), jnp.bfloat16),
            pltpu.VMEM((width, HEAD_DIM), jnp.bfloat16),
            pltpu.VMEM((width, HEAD_DIM), jnp.bfloat16),
            pltpu.VMEM((HEAD_DIM, width), jnp.bfloat16),
            pltpu.VMEM((HEAD_DIM, width), jnp.bfloat16),
            pltpu.VMEM((keys, width), jnp.float32),
            pltpu.VMEM((keys, width), jnp.float32),
            pltpu.VMEM((keys, 2 * HEAD_DIM), jnp.float32),
            pltpu.VMEM((HEAD_DIM, width), jnp.float32),
        ],
        input_output_aliases={3 + n_blocks: 0} if held else {},
        compiler_params=pltpu.CompilerParams(
            vmem_limit_bytes=vmem_limit, dimension_semantics=("arbitrary", "arbitrary")
        ),
        cost_estimate=small_cost
        if held
        else pl.CostEstimate(
            flops=10 * rows * keys * group * count * HEAD_DIM,
            bytes_accessed=8 * (rows * group + keys) * count * HEAD_DIM,
            transcendentals=rows * keys * group * count,
        ),
        name="attention_backward",
    )(place, queries, out_grad, *kv_blocks, *held, *after)


def fold_kernel(rows, mine_ref, got_ref, *refs):
    for k, ref in enumerate(refs[-(mine_ref.shape[0] // rows) :]):
        here = slice(k * rows, (k + 1) * rows)
        total = mine_ref[here, :].astype(jnp.float32) + got_ref[here, :].astype(jnp.float32)
        ref[...] = total.astype(ref.dtype)


def fold(mine, got, rows, after=()):
    n_z, width = mine.shape[0] // rows, mine.shape[1]
    return pl.pallas_call(
        functools.partial(fold_kernel, rows),
        in_specs=[pl.BlockSpec(memory_space=pltpu.VMEM)] * 2
        + [pl.BlockSpec(memory_space=pl.ANY)] * len(after),
        out_shape=[jax.ShapeDtypeStruct((rows, width), jnp.float32)]
        + [jax.ShapeDtypeStruct((rows, width), jnp.bfloat16)] * (n_z - 1),
        compiler_params=pltpu.CompilerParams(vmem_limit_bytes=vmem_limit),
        cost_estimate=small_cost,
        name="fold",
    )(mine, got, *after)


def finish_kernel(n_z, counts, *refs):
    key_ref, value_ref = refs[-2:]
    first = 0
    for i, count in enumerate(counts):
        parts = refs[i * n_z : (i + 1) * n_z]
        total = parts[0][...]
        for ref in parts[1:]:
            total = total + ref[...].astype(jnp.float32)
        total = total.astype(jnp.bfloat16)
        for g in range(count):
            lanes = slice((first + g) * HEAD_DIM, (first + g + 1) * HEAD_DIM)
            key_ref[0, :, lanes] = total[:, 2 * g * HEAD_DIM : (2 * g + 1) * HEAD_DIM]
            value_ref[0, :, lanes] = total[:, (2 * g + 1) * HEAD_DIM : (2 * g + 2) * HEAD_DIM]
        first += count


def finish(parts, counts, rows, after):
    shape = jax.ShapeDtypeStruct((1, rows, sum(counts) * HEAD_DIM), jnp.bfloat16)
    return pl.pallas_call(
        functools.partial(finish_kernel, len(parts[0]), counts),
        in_specs=[pl.BlockSpec(memory_space=pltpu.VMEM)] * (len(parts) * len(parts[0]))
        + [pl.BlockSpec(memory_space=pl.ANY)],
        out_shape=[shape, shape],
        compiler_params=pltpu.CompilerParams(vmem_limit_bytes=vmem_limit),
        cost_estimate=small_cost,
        name="finish",
    )(*[part for group in parts for part in group], after)


def join_kernel(
    n_z, n_dp, key_ref, value_ref, rows_ref, ids_ref, combine_ref, kv_ref, ext_ref
):
    for g in range(kv_ref.shape[1] // (2 * HEAD_DIM)):
        lanes = slice(g * HEAD_DIM, (g + 1) * HEAD_DIM)
        kv_ref[:, 2 * g * HEAD_DIM : (2 * g + 1) * HEAD_DIM] = key_ref[0, :, lanes]
        kv_ref[:, (2 * g + 1) * HEAD_DIM : (2 * g + 2) * HEAD_DIM] = value_ref[0, :, lanes]
    tokens, feat = rows_ref.shape
    lines = 4 * n_dp
    line = lax.broadcasted_iota(jnp.int32, (n_z * lines, tokens), 0)
    kind = line % lines
    member = kind % (2 * n_dp)
    expert = (member // 2) * (2 * n_z) + line // lines * 2 + member % 2
    hits = jnp.zeros((n_z * lines, tokens), jnp.float32)
    weights = jnp.zeros((n_z * lines, tokens), jnp.float32)
    combine = combine_ref[...].astype(jnp.float32)
    for k in range(TOPK):
        hit = ids_ref[k : k + 1, :] == expert
        hits = hits + jnp.where(hit, 1.0, 0.0)
        weights = weights + jnp.where(hit, combine[k : k + 1, :], 0.0)
    before = lax.broadcasted_iota(jnp.int32, (tokens, tokens), 0) < lax.broadcasted_iota(
        jnp.int32, (tokens, tokens), 1
    )
    ranks = mul(hits.astype(jnp.bfloat16), jnp.where(before, 1.0, 0.0).astype(jnp.bfloat16))
    table = jnp.where(kind < 2 * n_dp, jnp.where(hits > 0.0, ranks, -1.0), weights)
    ext_ref[:tokens, :] = rows_ref[...]
    squares = [table[i * lines : (i + 1) * lines] for i in range(n_z)]
    squares += [jnp.zeros((lines, tokens), jnp.float32)] * (feat // tokens - n_z)
    ext_ref[tokens:, :] = jnp.concatenate(squares, axis=1).astype(jnp.bfloat16)


def join(keys, values, full_rows, ids, combine, n_z, n_dp):
    rows, width = keys.shape[1:]
    tokens, feat = full_rows.shape
    return pl.pallas_call(
        functools.partial(join_kernel, n_z, n_dp),
        out_shape=[
            jax.ShapeDtypeStruct((rows, 2 * width), jnp.bfloat16),
            jax.ShapeDtypeStruct((tokens + 4 * n_dp, feat), jnp.bfloat16),
        ],
        compiler_params=pltpu.CompilerParams(vmem_limit_bytes=vmem_limit),
        cost_estimate=small_cost,
        name="join",
    )(keys, values, full_rows, ids.T, combine.T)


def pick_kernel(count, n_dp, capacity, place, *refs):
    table_refs, row_refs = refs[:count], refs[count : 2 * count]
    out_ref, pick_s = refs[-2:]
    tokens = pick_s.shape[2]

    @pl.when(pl.program_id(0) == 0)
    def _():
        for i, ref in enumerate(table_refs):
            table = ref[:, pl.ds(pl.multiple_of(place[0] * tokens, tokens), tokens)]
            table = table.astype(jnp.float32)
            slot = lax.broadcasted_iota(jnp.int32, (capacity, tokens), 0).astype(jnp.float32)
            picks = [
                jnp.where(
                    slot == table[q : q + 1, :], table[2 * n_dp + q : 2 * n_dp + q + 1, :], 0.0
                )
                for q in range(2 * n_dp)
            ]
            pick_s[i] = jnp.concatenate(picks, axis=0).astype(jnp.bfloat16)

    results = [mul(pick_s[i], ref[:tokens, :]) for i, ref in enumerate(row_refs)]
    for q in range(2 * n_dp):
        here = slice(q * capacity, (q + 1) * capacity)
        total = jnp.concatenate([part[here] for part in results], axis=0)
        size = count * capacity
        out_ref[q * size : (q + 1) * size, :] = total.astype(jnp.bfloat16)


def pick_rows(place, array, ks, tokens, n_dp, capacity, after=()):
    lines, feat = 4 * n_dp, array.shape[1]
    block = tokens + lines
    step = math.gcd(feat, 512)
    out_rows = len(ks) * 2 * n_dp * capacity

    def at(place, k):
        return place[0] ^ k if array.shape[0] > block else 0

    def table_spec(k):
        per_block = block // lines
        return pl.BlockSpec(
            (lines, feat), lambda f, place: (at(place, k) * per_block + per_block - 1, 0)
        )

    def rows_spec(k):
        return pl.BlockSpec((block, step), lambda f, place: (at(place, k), f))

    return pl.pallas_call(
        functools.partial(pick_kernel, len(ks), n_dp, capacity),
        grid_spec=pltpu.PrefetchScalarGridSpec(
            num_scalar_prefetch=1,
            grid=(feat // step,),
            in_specs=[table_spec(k) for k in ks]
            + [rows_spec(k) for k in ks]
            + [pl.BlockSpec(memory_space=pl.ANY)] * len(after),
            out_specs=pl.BlockSpec((out_rows, step), lambda f, place: (0, f)),
            scratch_shapes=[pltpu.VMEM((len(ks), 2 * n_dp * capacity, tokens), jnp.bfloat16)],
        ),
        out_shape=jax.ShapeDtypeStruct((out_rows, feat), jnp.bfloat16),
        compiler_params=pltpu.CompilerParams(vmem_limit_bytes=vmem_limit),
        cost_estimate=small_cost,
        name="pick_rows",
    )(place, *[array] * (2 * len(ks)), *after)


def expert_kernel(chunks, n_z, n_dp, capacity, slots, place, *refs):
    row_refs, w_ref = refs[: len(chunks)], refs[len(chunks)]
    out_ref, out_s, sem = refs[-3:]
    step, steps = pl.program_id(0), out_s.shape[0]
    width = out_s.shape[-1]
    blocks = [(q, k) for ks in chunks for q in range(2 * n_dp) for k in ks]
    first = 0
    for rows_ref in row_refs:
        result = lax.dot_general(
            rows_ref[...], w_ref[0], (((1,), (1,)), ((), ())), preferred_element_type=jnp.float32
        )
        count = rows_ref.shape[0] // capacity
        for i in range(count):
            out_s[step, first + i] = result[i * capacity : i * capacity + slots].astype(jnp.bfloat16)
        first += count

    def copies(at):
        z = place[0]
        for i, (q, k) in enumerate(blocks):
            source = (q // 2) * (2 * n_z) + (z ^ k) * 2 + q % 2
            lanes = pl.ds(pl.multiple_of(at * width, width), width)
            yield pltpu.make_async_copy(
                out_s.at[at, i], out_ref.at[0, source, :, lanes], sem.at[at, i]
            )

    for copy in copies(step):
        copy.start()

    @pl.when(step == steps - 1)
    def _():
        for at in range(steps):
            for copy in copies(at):
                copy.wait()


def expert_rows(place, arrays, chunks, w_down, n_z, n_dp, capacity, slots, hidden_grad, after=()):
    hid, feat = w_down.shape[1:]
    step = math.gcd(hid, 512)
    count = sum(array.shape[0] for array in arrays) // capacity
    held = [] if hidden_grad is None else [hidden_grad]
    return pl.pallas_call(
        functools.partial(expert_kernel, chunks, n_z, n_dp, capacity, slots),
        grid=(hid // step,),
        in_specs=[pl.BlockSpec(memory_space=pltpu.SMEM)]
        + [pl.BlockSpec(array.shape, lambda n: (0, 0)) for array in arrays]
        + [pl.BlockSpec((1, step, feat), lambda n: (0, n, 0))]
        + [pl.BlockSpec(memory_space=pl.ANY)] * (len(held) + len(after)),
        out_specs=pl.BlockSpec(memory_space=pl.ANY),
        out_shape=jax.ShapeDtypeStruct((1, n_dp * 2 * n_z, slots, hid), jnp.bfloat16),
        scratch_shapes=[
            pltpu.VMEM((hid // step, count, slots, step), jnp.bfloat16),
            pltpu.SemaphoreType.DMA((hid // step, count)),
        ],
        input_output_aliases={2 + len(arrays): 0} if held else {},
        compiler_params=pltpu.CompilerParams(vmem_limit_bytes=vmem_limit),
        cost_estimate=small_cost,
        name="expert_rows",
    )(place, *arrays, w_down, *held, *after)


def per_device(queries, keys, values, out_grad, mixed_grad, expert_ids, combine, w_down):
    rows_dev = queries.shape[1]
    kv_local = keys.shape[2] // HEAD_DIM
    n_ctx, n_dp = lax.axis_size("ctx"), lax.axis_size("dp")
    n_z = n_ctx // 2
    position = lax.axis_index("ctx")
    place = jnp.stack([position >> 1, position & 1]).astype(jnp.int32)
    token_rows = expert_ids.shape[0]
    experts_all = n_dp * n_ctx
    slots = min(
        token_rows,
        max(
            2,
            token_rows * TOPK * 5 // (4 * experts_all),
            (token_rows * TOPK + experts_all - 1) // experts_all,
        ),
    )
    capacity = -(-slots // 8) * 8
    full_rows = mixed_grad
    if lax.axis_size("tp") > 1:
        full_rows = lax.all_gather(mixed_grad, "tp", axis=1, tiled=True)
    own, own_rows = join(keys, values, full_rows, expert_ids, combine, n_z, n_dp)

    def along_z(array, targets):
        pairs = [(2 * i + x, 2 * j + x) for i, j in targets for x in range(2)]
        return lax.ppermute(array, "ctx", pairs)

    def across_x(k):
        pairs = [(i, i ^ 1) for i in range(2 * k, n_ctx) if k > 0 or i % 2 == 0]
        return lax.ppermute(columns[k], "ctx", pairs)

    columns, others = [own], []
    for k in range(1, n_z):
        others.append(across_x(k - 1))
        if k > 2:
            columns[-1], others[k - 3] = lax.optimization_barrier((columns[-1], others[k - 3]))
        columns.append(along_z(columns[-1], [(i, i + 1) for i in range(k - 1, n_z - 1)]))
    columns[-1], *others[-2:] = lax.optimization_barrier((columns[-1], *others[-2:]))
    others.append(across_x(n_z - 1))
    blocks = [block for pair in zip(columns, others) for block in pair]

    plane_groups = [
        [d * n_ctx + 2 * i + j for d in range(n_dp) for j in range(2)] for i in range(n_z)
    ]
    line_groups = [[2 * i + x for i in range(n_z)] for x in range(2)]
    gathered_rows = lax.all_gather(
        own_rows, "ctx", axis=0, tiled=True, axis_index_groups=line_groups
    )

    def exchange(array, ks, after):
        picked = pick_rows(place, array, ks, token_rows, n_dp, capacity, after)
        return picked, lax.all_to_all(
            picked,
            ("dp", "ctx"),
            split_axis=0,
            concat_axis=0,
            tiled=True,
            axis_index_groups=plane_groups,
        )

    counts = [1] if kv_local == 1 else [kv_local - 1, 1]
    gathered = []

    def down(mine, other, after=()):
        got = lax.ppermute(other, "ctx", [(i, i ^ 1) for i in range(n_ctx)])
        parts = fold(mine, got, rows_dev, after)
        gathered.append(
            [parts[0]]
            + [
                lax.ppermute(parts[k], "ctx", [(i, i - 2 * k) for i in range(2 * k, n_ctx)])
                for k in range(1, n_z)
            ]
        )
        return got, parts[0]

    chunks = [(0,), tuple(range(1, n_z))]
    picked, got_own = exchange(own_rows, chunks[0], (columns[n_z - 1],))
    query_grad, mine, other = attention(
        place, queries[0], out_grad[0], blocks, 0, counts[0], None, (picked,)
    )
    got, folded = down(mine, other)
    picked, got_rest = exchange(gathered_rows, chunks[1], (got,))
    if len(counts) > 1:
        query_grad, mine, other = attention(
            place, queries[0], out_grad[0], blocks, counts[0], counts[1], query_grad, (picked,)
        )
        got, folded = down(mine, other)
    sizes = (n_z, n_dp, capacity, slots)
    hidden_grad = expert_rows(place, (got_own,), chunks[:1], w_down, *sizes, None, (folded,))
    key_grad, value_grad = finish(gathered, counts, rows_dev, hidden_grad)
    hidden_grad = expert_rows(place, (got_rest,), chunks[1:], w_down, *sizes, hidden_grad)
    return (query_grad[None], key_grad, value_grad, hidden_grad)


def solution(mesh):
    placed = (
        P("dp", "ctx", "tp"),
        P("dp", "ctx", "tp"),
        P("dp", "ctx", "tp"),
        P("dp", "ctx", "tp"),
        P(("dp", "ctx"), "tp"),
        P(("dp", "ctx"), None),
        P(("dp", "ctx"), None),
        P(("dp", "ctx"), "tp", None),
    )
    return jax.shard_map(
        per_device,
        mesh=mesh,
        in_specs=placed,
        out_specs=(
            P("dp", "ctx", "tp"),
            P("dp", "ctx", "tp"),
            P("dp", "ctx", "tp"),
            P(("dp", "ctx"), None, None, "tp"),
        ),
        check_vma=False,
    )
```

time: 194 us -> 218 us (1.12)
  local copies, waits for them, and re-layouts: 30.4 us -> 4.03 us
  waiting for transfers between devices: 94.4 us -> 119 us
  Pallas kernels: 28.9 us -> 46.6 us
  between operations: 0.96 us -> 14.3 us
  starting transfers between devices: 38.2 us -> 32.6 us
    ppermute x11 -> x12, waiting for transfers between devices: 45 us -> 117 us  [the longest x2 64 us: down(): got = lax.ppermute(other, 'ctx', [(i, i ^ 1) for i in range(n_ctx)])]
    ppermute x8 -> x3, waiting for transfers between devices: 49.4 us -> 2.43 us  [along_z(): return lax.ppermute(array, 'ctx', pairs)]
    unnamed x82 -> x32, local copies, waits for them, and re-layouts: 30.4 us -> 4.03 us
    pallas_call x6 -> x7, Pallas kernels: 19.7 us -> 34.2 us  [the longest x2 17.7 us: expert_rows(): pl.pallas_call(functools.partial(expert_kernel, chunks, n_z, n_dp, capaci...]
    ppermute x8 -> x3, starting transfers between devices: 15.6 us -> 6.3 us  [along_z(): return lax.ppermute(array, 'ctx', pairs)]
    ppermute x11 -> x12, starting transfers between devices: 14.9 us -> 17.1 us  [the longest x6 7.73 us: down(): lax.ppermute(parts[k], 'ctx', [(i, i - 2 * k) for i in range(2 * k, n_ctx)])]
  transfers between devices with their start and end apart: 21 -> 18, of which waited for: 9 -> 9; matrix products, arithmetic and copies ran while one was open for 0% -> 0% of each run, Pallas kernels for 10% -> 15%
where the time goes in v3:
time: 218 us; the launch traced here: 217 us
  waiting for transfers between devices  119 us (55%)
  Pallas kernels  46.6 us (21%)
  starting transfers between devices  32.6 us (15%)
  between operations  14.3 us (7%)
  local copies, waits for them, and re-layouts  4.03 us (2%)
    ppermute x2, waiting for transfers between devices, down(): got = lax.ppermute(other, 'ctx', [(i, i ^ 1) for i in range(n_ctx)])  64 us
    ppermute x6, waiting for transfers between devices, down(): lax.ppermute(parts[k], 'ctx', [(i, i - 2 * k) for i in range(2 * k, n_ctx)])  50.8 us
    pallas_call x2, Pallas kernels, expert_rows(): pl.pallas_call(functools.partial(expert_kernel, chunks, n_z, n_dp, capaci...  17.7 us
    pallas_call x2, Pallas kernels, pick_rows(): pl.pallas_call(functools.partial(pick_kernel, len(ks), n_dp, capacity), g...  10.3 us
    pallas_call x2, Pallas kernels, attention(): pl.pallas_call(functools.partial(attention_kernel, n_blocks, heads_step,...  10.2 us
    all_to_all x2, starting transfers between devices, exchange(): lax.all_to_all(picked, ('dp', 'ctx'), split_axis=0, concat_axis=0, tiled=...  9.13 us
    ppermute x6, starting transfers between devices, down(): lax.ppermute(parts[k], 'ctx', [(i, i - 2 * k) for i in range(2 * k, n_ctx)])  7.73 us
    ppermute x3, starting transfers between devices, along_z(): return lax.ppermute(array, 'ctx', pairs)  6.3 us
  transfers between devices with their start and end apart: 18, of which 9 were waited for; matrix products, arithmetic and copies ran while one was open for 0% of the time, Pallas kernels for 15%

profile of v3, /device:TPU:0, one launch (start us, length us, event | category | flops | bytes accessed | tf_op | source)
XLA Modules:
  0.0 217.1 jit_solution(7262690940711219544)
XLA Ops:
  7.2 2.2 %join.1 = (bf16[128,1024]{1,0:T(8,128)(2,1)}, bf16[144,2048]{1,0:T(8,128)(2,1)}) custom-call(bf16[1,128,512]{2,1,0:T(8,128)(2,1)} %key_ref.1, bf16[1,128,512]{2,1,0:T(8,128)(2,1)} %value_ref.1, bf16[128,2048]{1,0:T(8,128)(2,1)} %rows_ref.1, s32[8,128]{1,0:T(8,128)} %bitcast.19, bf16[8,128]{1,0:T(8,128)(2,1)} %bitcast.20), custom_call_target="tpu_custom_call" | custom-call | flops 1 | bytes 1 | tf_op jit(solution)/shard_map/join/pallas_call | solution.py:251
  9.5 5.0 %collective-permute-start = (bf16[128,1024]{1,0:T(8,128)(2,1)}, bf16[128,1024]{1,0:T(8,128)(2,1)S(1)}, u32[]{:S(2)}, u32[]{:S(2)}) collective-permute-start(bf16[128,1024]{1,0:T(8,128)(2,1)} %get-tuple-element.27.refs_0_), channel_id=1, source_target_pairs={{0,2},{1,3},{2,4},{3,5},{4,6},{5,7},{8,10},{9,11},{10,12},{11,13},... | collective-permute-start | bytes 786440 | tf_op jit(solution)/shard_map/ppermute | solution.py:411
  14.4 3.4 %collective-permute-start.2 = (bf16[128,1024]{1,0:T(8,128)(2,1)}, bf16[128,1024]{1,0:T(8,128)(2,1)S(1)}, u32[]{:S(2)}, u32[]{:S(2)}) collective-permute-start(bf16[128,1024]{1,0:T(8,128)(2,1)} %get-tuple-element.27.refs_0_), channel_id=1, source_target_pairs={{0,1},{2,3},{4,5},{6,7},{8,9},{10,11},{12,13},{14,15},{16,17},{18,... | collective-permute-start | bytes 786440 | tf_op jit(solution)/shard_map/ppermute | solution.py:415
  17.8 2.4 %collective-permute-done.refs_2_ = bf16[128,1024]{1,0:T(8,128)(2,1)S(1)} collective-permute-done((bf16[128,1024]{1,0:T(8,128)(2,1)}, bf16[128,1024]{1,0:T(8,128)(2,1)S(1)}, u32[]{:S(2)}, u32[]{:S(2)}) %collective-permute-start) | collective-permute-done | bytes 262176 | tf_op jit(solution)/shard_map/ppermute | solution.py:411
  21.6 1.8 collective-permute-done.2.refs_1_
  26.1 4.4 %pick_rows.2.refs_8_ = bf16[320,2048]{1,0:T(8,128)(2,1)} custom-call(s32[2]{0:T(128)} %pad_add_fusion.place, bf16[144,2048]{1,0:T(8,128)(2,1)} %get-tuple-element.33.refs_0_.refs_1_, bf16[144,2048]{1,0:T(8,128)(2,1)} %get-tuple-element.33.refs_0_.refs_1_, bf16[128,1024]{1,0:T(8,128)(2,1)} %copy-done.2), custom_call_target="tpu_custom_call" | custom-call | flops 1 | bytes 1 | tf_op jit(solution)/shard_map/pick_rows/pallas_call | solution.py:308
  30.6 4.6 %all-to-all-start = ((bf16[8,40,2048]{2,1,0:T(8,128)(2,1)}), bf16[8,40,2048]{2,1,0:T(8,128)(2,1)S(1)}, u32[]{:S(2)}, u32[]{:S(2)}) async-start(bf16[8,40,2048]{2,1,0:T(8,128)(2,1)} %bitcast.13), calls=%async_computation | async-start | bytes 2621440 | tf_op jit(solution)/shard_map/all_to_all | solution.py:437
  35.9 6.6 %attention_backward.2 = (bf16[128,4096]{1,0:T(8,128)(2,1)}, bf16[512,768]{1,0:T(8,128)(2,1)}, bf16[512,768]{1,0:T(8,128)(2,1)}) custom-call(s32[2]{0:T(128)} %pad_add_fusion.place, bf16[128,4096]{1,0:T(8,128)(2,1)} %bitcast.14, bf16[128,4096]{1,0:T(8,128)(2,1)} %bitcast.16, bf16[128,1024]{1,0:T(8,128)(2,1)} %get-tuple-element.27.refs_0_, ...), custom_call_target="tpu_custom_call" | custom-call | flops 4026531840 | bytes 6291456 | tf_op jit(solution)/shard_map/attention_backward/pallas_call | solution.py:132
  42.5 2.1 collective-permute-start.7
  44.6 24.7 %collective-permute-done.7.refs_6_.got_ref = bf16[512,768]{1,0:T(8,128)(2,1)S(1)} collective-permute-done((bf16[512,768]{1,0:T(8,128)(2,1)}, bf16[512,768]{1,0:T(8,128)(2,1)S(1)}, u32[]{:S(2)}, u32[]{:S(2)}) %collective-permute-start.7) | collective-permute-done | bytes 786464 | tf_op jit(solution)/shard_map/ppermute | solution.py:450
  70.2 5.9 %pick_rows.3.refs_9_ = bf16[960,2048]{1,0:T(8,128)(2,1)} custom-call(s32[2]{0:T(128)} %pad_add_fusion.place, bf16[576,2048]{1,0:T(8,128)(2,1)} %all-gather.2.cloned.1.call-done.refs_0_.refs_1_.refs_2_.refs_3_.refs_4_.refs_5_, bf16[576,2048]{1,0:T(8,128)(2,1)} %all-gather.2.cloned.1.call-done.refs_0_.refs_1_.refs_2_.refs_3_.refs_4_.refs_5_, ...), custom_call_target="tpu_custom_call" | custom-call | flops 1 | bytes 1 | tf_op jit(solution)/shard_map/pick_rows/pallas_call | solution.py:308
  76.1 1.1 copy-done
  77.2 4.5 %all-to-all-start.1 = ((bf16[8,120,2048]{2,1,0:T(8,128)(2,1)}), bf16[8,120,2048]{2,1,0:T(8,128)(2,1)}, u32[]{:S(2)}, u32[]{:S(2)}) async-start(bf16[8,120,2048]{2,1,0:T(8,128)(2,1)} %bitcast.11), calls=%async_computation.1 | async-start | bytes 7864320 | tf_op jit(solution)/shard_map/all_to_all | solution.py:437
  81.8 3.5 %attention_backward.3 = (bf16[128,4096]{1,0:T(8,128)(2,1)}, bf16[512,256]{1,0:T(8,128)(2,1)}, bf16[512,256]{1,0:T(8,128)(2,1)}) custom-call(s32[2]{0:T(128)} %pad_add_fusion.place, bf16[128,4096]{1,0:T(8,128)(2,1)} %bitcast.15, bf16[128,4096]{1,0:T(8,128)(2,1)} %bitcast.17, ...), custom_call_target="tpu_custom_call", output_to_operand_aliasing={{0}: (11, {})} | custom-call | flops 1 | bytes 1 | tf_op jit(solution)/shard_map/attention_backward/pallas_call | solution.py:132
  85.3 1.9 collective-permute-start.11
  87.2 2.4 %fold.2 = (f32[128,768]{1,0:T(8,128)}, bf16[128,768]{1,0:T(8,128)(2,1)}, bf16[128,768]{1,0:T(8,128)(2,1)}, bf16[128,768]{1,0:T(8,128)(2,1)}) custom-call(bf16[512,768]{1,0:T(8,128)(2,1)} %get-tuple-element.37.mine_ref, bf16[512,768]{1,0:T(8,128)(2,1)} %copy-done.1), custom_call_target="tpu_custom_call" | custom-call | flops 1 | bytes 1 | tf_op jit(solution)/shard_map/fold/pallas_call | solution.py:176
  89.5 1.3 collective-permute-start.8
  90.8 1.3 collective-permute-start.9
  92.1 1.3 collective-permute-start.10
  93.4 39.2 %collective-permute-done.11.got_ref = bf16[512,256]{1,0:T(8,128)(2,1)S(1)} collective-permute-done((bf16[512,256]{1,0:T(8,128)(2,1)}, bf16[512,256]{1,0:T(8,128)(2,1)S(1)}, u32[]{:S(2)}, u32[]{:S(2)}) %collective-permute-start.11) | collective-permute-done | bytes 262176 | tf_op jit(solution)/shard_map/ppermute | solution.py:450
  133.4 1.8 fold.3
  135.1 1.3 collective-permute-start.12
  136.4 1.3 collective-permute-start.13
  137.7 1.3 collective-permute-start.14
  139.0 6.4 %expert_rows.2.refs_8_.refs_2_ = bf16[1,32,40,1536]{3,2,1,0:T(8,128)(2,1)} custom-call(s32[2]{0:T(128)} %pad_add_fusion.place, bf16[320,2048]{1,0:T(8,128)(2,1)} %bitcast.12, bf16[1,1536,2048]{2,1,0:T(8,128)(2,1)} %refs_1_.3, f32[128,256]{1,0:T(8,128)} %get-tuple-element.44.refs_2_.refs_4_), custom_call_target="tpu_custom_call" | custom-call | flops 1 | bytes 1 | tf_op jit(solution)/shard_map/expert_rows/pallas_call | solution.py:366
  145.4 4.4 %collective-permute-done.9.refs_2_ = bf16[128,768]{1,0:T(8,128)(2,1)S(1)} collective-permute-done((bf16[128,768]{1,0:T(8,128)(2,1)}, bf16[128,768]{1,0:T(8,128)(2,1)S(1)}, u32[]{:S(2)}, u32[]{:S(2)}) %collective-permute-start.9) | collective-permute-done | bytes 196640 | tf_op jit(solution)/shard_map/ppermute | solution.py:455
  149.8 12.6 %collective-permute-done.10.refs_3_ = bf16[128,768]{1,0:T(8,128)(2,1)S(1)} collective-permute-done((bf16[128,768]{1,0:T(8,128)(2,1)}, bf16[128,768]{1,0:T(8,128)(2,1)S(1)}, u32[]{:S(2)}, u32[]{:S(2)}) %collective-permute-start.10) | collective-permute-done | bytes 196640 | tf_op jit(solution)/shard_map/ppermute | solution.py:455
  162.5 1.3 collective-permute-done.12.refs_5_
  163.8 23.9 %collective-permute-done.13.refs_6_ = bf16[128,256]{1,0:T(8,128)(2,1)S(1)} collective-permute-done((bf16[128,256]{1,0:T(8,128)(2,1)}, bf16[128,256]{1,0:T(8,128)(2,1)S(1)}, u32[]{:S(2)}, u32[]{:S(2)}) %collective-permute-start.13) | collective-permute-done | bytes 65568 | tf_op jit(solution)/shard_map/ppermute | solution.py:455
  187.7 8.6 %collective-permute-done.14.refs_7_ = bf16[128,256]{1,0:T(8,128)(2,1)S(1)} collective-permute-done((bf16[128,256]{1,0:T(8,128)(2,1)}, bf16[128,256]{1,0:T(8,128)(2,1)S(1)}, u32[]{:S(2)}, u32[]{:S(2)}) %collective-permute-start.14) | collective-permute-done | bytes 65568 | tf_op jit(solution)/shard_map/ppermute | solution.py:455
  196.9 2.1 finish.1
  199.0 11.3 %expert_rows.3 = bf16[1,32,40,1536]{3,2,1,0:T(8,128)(2,1)} custom-call(s32[2]{0:T(128)} %pad_add_fusion.place, bf16[960,2048]{1,0:T(8,128)(2,1)} %bitcast.10.refs_0_, bf16[1,1536,2048]{2,1,0:T(8,128)(2,1)} %refs_1_.3, bf16[1,32,40,1536]{3,2,1,0:T(8,128)(2,1)} %expert_rows.2.refs_8_.refs_2_), custom_call_target="tpu_custom_call", output_to_operand_aliasing={{}: (3, {})} | custom-call | flops 1 | bytes 1 | tf_op jit(solution)/shard_map/expert_rows/pallas_call | solution.py:366
  (48 shorter events, 6.9 us)
Async XLA Ops:
  7.2 62.2 %all-gather.2.cloned.1.call-start = ((), (), s32[]{:S(2)}) async-start(), calls=%async_computation.2 | async-start | bytes 2949120 | tf_op jit(solution)/shard_map/all_gather | solution.py:431
  9.5 10.8 %collective-permute-start = (bf16[128,1024]{1,0:T(8,128)(2,1)}, bf16[128,1024]{1,0:T(8,128)(2,1)S(1)}, u32[]{:S(2)}, u32[]{:S(2)}) collective-permute-start(bf16[128,1024]{1,0:T(8,128)(2,1)} %get-tuple-element.27.refs_0_), channel_id=1, source_target_pairs={{0,2},{1,3},{2,4},{3,5},{4,6},{5,7},{8,10},{9,11},{10,12},{11,13},... | collective-permute-start | bytes 786440 | tf_op jit(solution)/shard_map/ppermute | solution.py:411
  14.4 9.0 %collective-permute-start.2 = (bf16[128,1024]{1,0:T(8,128)(2,1)}, bf16[128,1024]{1,0:T(8,128)(2,1)S(1)}, u32[]{:S(2)}, u32[]{:S(2)}) collective-permute-start(bf16[128,1024]{1,0:T(8,128)(2,1)} %get-tuple-element.27.refs_0_), channel_id=1, source_target_pairs={{0,1},{2,3},{4,5},{6,7},{8,9},{10,11},{12,13},{14,15},{16,17},{18,... | collective-permute-start | bytes 786440 | tf_op jit(solution)/shard_map/ppermute | solution.py:415
  20.3 14.9 %copy-start.3 = (bf16[128,1024]{1,0:T(8,128)(2,1)}, bf16[128,1024]{1,0:T(8,128)(2,1)S(1)}, u32[]{:S(2)}) copy-start(bf16[128,1024]{1,0:T(8,128)(2,1)S(1)} %collective-permute-done.refs_2_) | copy-start | bytes 786436
  20.3 3.1 %collective-permute-start.1 = (bf16[128,1024]{1,0:T(8,128)(2,1)S(1)}, bf16[128,1024]{1,0:T(8,128)(2,1)S(1)}, u32[]{:S(2)}, u32[]{:S(2)}) collective-permute-start(bf16[128,1024]{1,0:T(8,128)(2,1)S(1)} %collective-permute-done.refs_2_), channel_id=1, source_target_pairs={{2,4},{3,5},{4,6},{5,7},{10,12},{11,13},{12,14},{13,15},{18,20},{1... | collective-permute-start | bytes 786440 | tf_op jit(solution)/shard_map/ppermute | solution.py:411
  20.9 3.8 %collective-permute-start.4 = (bf16[128,1024]{1,0:T(8,128)(2,1)S(1)}, bf16[128,1024]{1,0:T(8,128)(2,1)S(1)}, u32[]{:S(2)}, u32[]{:S(2)}) collective-permute-start(bf16[128,1024]{1,0:T(8,128)(2,1)S(1)} %collective-permute-done.refs_2_), channel_id=1, source_target_pairs={{2,3},{3,2},{4,5},{5,4},{6,7},{7,6},{10,11},{11,10},{12,13},{13,12... | collective-permute-start | bytes 786440 | tf_op jit(solution)/shard_map/ppermute | solution.py:415
  23.4 11.8 %copy-start.4 = (bf16[128,1024]{1,0:T(8,128)(2,1)}, bf16[128,1024]{1,0:T(8,128)(2,1)S(1)}, u32[]{:S(2)}) copy-start(bf16[128,1024]{1,0:T(8,128)(2,1)S(1)} %collective-permute-done.2.refs_1_) | copy-start | bytes 786436
  23.4 11.8 %copy-start.5 = (bf16[128,1024]{1,0:T(8,128)(2,1)}, bf16[128,1024]{1,0:T(8,128)(2,1)S(1)}, u32[]{:S(2)}) copy-start(bf16[128,1024]{1,0:T(8,128)(2,1)S(1)} %collective-permute-done.1.refs_4_) | copy-start | bytes 786436
  23.4 1.4 collective-permute-start.3
  24.1 0.7 collective-permute-start.5
  24.8 10.4 %copy-start.6 = (bf16[128,1024]{1,0:T(8,128)(2,1)}, bf16[128,1024]{1,0:T(8,128)(2,1)S(1)}, u32[]{:S(2)}) copy-start(bf16[128,1024]{1,0:T(8,128)(2,1)S(1)} %collective-permute-done.4.refs_3_) | copy-start | bytes 786436
  24.8 1.3 copy-start.2
  24.8 10.4 %copy-start.7 = (bf16[128,1024]{1,0:T(8,128)(2,1)}, bf16[128,1024]{1,0:T(8,128)(2,1)S(1)}, u32[]{:S(2)}) copy-start(bf16[128,1024]{1,0:T(8,128)(2,1)S(1)} %collective-permute-done.5.refs_5_) | copy-start | bytes 786436
  24.8 10.3 %collective-permute-start.6 = (bf16[128,1024]{1,0:T(8,128)(2,1)S(1)}, bf16[128,1024]{1,0:T(8,128)(2,1)S(1)}, u32[]{:S(2)}, u32[]{:S(2)}) collective-permute-start(bf16[128,1024]{1,0:T(8,128)(2,1)S(1)} %collective-permute-done.3.refs_2_.refs_6_), channel_id=1, source_target_pairs={{6,7},{7,6},{14,15},{15,14},{22,23},{23,22},{30,31},{31,30}} | collective-permute-start | bytes 786440 | tf_op jit(solution)/shard_map/ppermute | solution.py:415
  30.6 45.5 %all-to-all-start = ((bf16[8,40,2048]{2,1,0:T(8,128)(2,1)}), bf16[8,40,2048]{2,1,0:T(8,128)(2,1)S(1)}, u32[]{:S(2)}, u32[]{:S(2)}) async-start(bf16[8,40,2048]{2,1,0:T(8,128)(2,1)} %bitcast.13), calls=%async_computation | async-start | bytes 2621440 | tf_op jit(solution)/shard_map/all_to_all | solution.py:437
  35.2 0.7 copy-start.8
  42.5 26.8 %collective-permute-start.7 = (bf16[512,768]{1,0:T(8,128)(2,1)}, bf16[512,768]{1,0:T(8,128)(2,1)S(1)}, u32[]{:S(2)}, u32[]{:S(2)}) collective-permute-start(bf16[512,768]{1,0:T(8,128)(2,1)} %get-tuple-element.35), channel_id=1, source_target_pairs={{0,1},{1,0},{2,3},{3,2},{4,5},{5,4},{6,7},{7,6},{8,9},{9,8},{10,11... | collective-permute-start | bytes 2359304 | tf_op jit(solution)/shard_map/ppermute | solution.py:450
  69.3 0.9 copy-start.1
  76.1 1.2 copy-start
  77.2 121.8 %all-to-all-start.1 = ((bf16[8,120,2048]{2,1,0:T(8,128)(2,1)}), bf16[8,120,2048]{2,1,0:T(8,128)(2,1)}, u32[]{:S(2)}, u32[]{:S(2)}) async-start(bf16[8,120,2048]{2,1,0:T(8,128)(2,1)} %bitcast.11), calls=%async_computation.1 | async-start | bytes 7864320 | tf_op jit(solution)/shard_map/all_to_all | solution.py:437
  85.3 47.4 %collective-permute-start.11 = (bf16[512,256]{1,0:T(8,128)(2,1)}, bf16[512,256]{1,0:T(8,128)(2,1)S(1)}, u32[]{:S(2)}, u32[]{:S(2)}) collective-permute-start(bf16[512,256]{1,0:T(8,128)(2,1)} %get-tuple-element.43), channel_id=1, source_target_pairs={{0,1},{1,0},{2,3},{3,2},{4,5},{5,4},{6,7},{7,6},{8,9},{9,8},{10,11... | collective-permute-start | bytes 786440 | tf_op jit(solution)/shard_map/ppermute | solution.py:450
  89.5 48.2 %collective-permute-start.8 = (bf16[128,768]{1,0:T(8,128)(2,1)}, bf16[128,768]{1,0:T(8,128)(2,1)S(1)}, u32[]{:S(2)}, u32[]{:S(2)}) collective-permute-start(bf16[128,768]{1,0:T(8,128)(2,1)} %get-tuple-element.39), channel_id=1, source_target_pairs={{2,0},{3,1},{4,2},{5,3},{6,4},{7,5},{10,8},{11,9},{12,10},{13,11},... | collective-permute-start | bytes 589832 | tf_op jit(solution)/shard_map/ppermute | solution.py:455
  90.8 59.0 %collective-permute-start.9 = (bf16[128,768]{1,0:T(8,128)(2,1)}, bf16[128,768]{1,0:T(8,128)(2,1)S(1)}, u32[]{:S(2)}, u32[]{:S(2)}) collective-permute-start(bf16[128,768]{1,0:T(8,128)(2,1)} %get-tuple-element.40), channel_id=1, source_target_pairs={{4,0},{5,1},{6,2},{7,3},{12,8},{13,9},{14,10},{15,11},{20,16},{21,... | collective-permute-start | bytes 589832 | tf_op jit(solution)/shard_map/ppermute | solution.py:455
  92.1 70.3 %collective-permute-start.10 = (bf16[128,768]{1,0:T(8,128)(2,1)}, bf16[128,768]{1,0:T(8,128)(2,1)S(1)}, u32[]{:S(2)}, u32[]{:S(2)}) collective-permute-start(bf16[128,768]{1,0:T(8,128)(2,1)} %get-tuple-element.41), channel_id=1, source_target_pairs={{6,0},{7,1},{14,8},{15,9},{22,16},{23,17},{30,24},{31,25}} | collective-permute-start | bytes 589832 | tf_op jit(solution)/shard_map/ppermute | solution.py:455
  135.1 28.6 %collective-permute-start.12 = (bf16[128,256]{1,0:T(8,128)(2,1)}, bf16[128,256]{1,0:T(8,128)(2,1)S(1)}, u32[]{:S(2)}, u32[]{:S(2)}) collective-permute-start(bf16[128,256]{1,0:T(8,128)(2,1)} %get-tuple-element.45), channel_id=1, source_target_pairs={{2,0},{3,1},{4,2},{5,3},{6,4},{7,5},{10,8},{11,9},{12,10},{13,11},... | collective-permute-start | bytes 196616 | tf_op jit(solution)/shard_map/ppermute | solution.py:455
  136.4 51.2 %collective-permute-start.13 = (bf16[128,256]{1,0:T(8,128)(2,1)}, bf16[128,256]{1,0:T(8,128)(2,1)S(1)}, u32[]{:S(2)}, u32[]{:S(2)}) collective-permute-start(bf16[128,256]{1,0:T(8,128)(2,1)} %get-tuple-element.46), channel_id=1, source_target_pairs={{4,0},{5,1},{6,2},{7,3},{12,8},{13,9},{14,10},{15,11},{20,16},{21,... | collective-permute-start | bytes 196616 | tf_op jit(solution)/shard_map/ppermute | solution.py:455
  137.7 7.7 %copy-start.10 = (bf16[128,768]{1,0:T(8,128)(2,1)}, bf16[128,768]{1,0:T(8,128)(2,1)S(1)}, u32[]{:S(2)}) copy-start(bf16[128,768]{1,0:T(8,128)(2,1)S(1)} %collective-permute-done.8.refs_1_) | copy-start | bytes 589828
  137.7 58.5 %collective-permute-start.14 = (bf16[128,256]{1,0:T(8,128)(2,1)}, bf16[128,256]{1,0:T(8,128)(2,1)S(1)}, u32[]{:S(2)}, u32[]{:S(2)}) collective-permute-start(bf16[128,256]{1,0:T(8,128)(2,1)} %get-tuple-element.47), channel_id=1, source_target_pairs={{6,0},{7,1},{14,8},{15,9},{22,16},{23,17},{30,24},{31,25}} | collective-permute-start | bytes 196616 | tf_op jit(solution)/shard_map/ppermute | solution.py:455
  149.8 46.4 %copy-start.11 = (bf16[128,768]{1,0:T(8,128)(2,1)}, bf16[128,768]{1,0:T(8,128)(2,1)S(1)}, u32[]{:S(2)}) copy-start(bf16[128,768]{1,0:T(8,128)(2,1)S(1)} %collective-permute-done.9.refs_2_) | copy-start | bytes 589828
  162.5 33.8 %copy-start.12 = (bf16[128,768]{1,0:T(8,128)(2,1)}, bf16[128,768]{1,0:T(8,128)(2,1)S(1)}, u32[]{:S(2)}) copy-start(bf16[128,768]{1,0:T(8,128)(2,1)S(1)} %collective-permute-done.10.refs_3_) | copy-start | bytes 589828
  163.8 32.5 %copy-start.13 = (bf16[128,256]{1,0:T(8,128)(2,1)}, bf16[128,256]{1,0:T(8,128)(2,1)S(1)}, u32[]{:S(2)}) copy-start(bf16[128,256]{1,0:T(8,128)(2,1)S(1)} %collective-permute-done.12.refs_5_) | copy-start | bytes 196612
  187.7 8.6 %copy-start.14 = (bf16[128,256]{1,0:T(8,128)(2,1)}, bf16[128,256]{1,0:T(8,128)(2,1)S(1)}, u32[]{:S(2)}) copy-start(bf16[128,256]{1,0:T(8,128)(2,1)S(1)} %collective-permute-done.13.refs_6_) | copy-start | bytes 196612
  (2 other events, 1.3 us)
Sparse Core Ops, SparseCore 0:
  9.6 51.5 all-gather.1

commit v4 on v3

--- a/solution.py
+++ b/solution.py
@@ -110,8 +110,9 @@
     for i in range(n_blocks):
         held = dkv_s[i * rows : (i + 1) * rows, :]
         ref = mine_ref if i % 2 == 0 else other_ref
-        here = slice(i // 2 * rows, (i // 2 + 1) * rows)
-        ref[here, :] = jnp.where(i // 2 <= z, held, 0.0).astype(jnp.bfloat16)
+        at = lax.rem(z - i // 2 + n_blocks // 2, n_blocks // 2) * rows
+        held = jnp.where(i // 2 <= z, held, 0.0).astype(jnp.bfloat16)
+        ref[pl.ds(pl.multiple_of(at, rows), rows), :] = held
 
 
 def attention(place, queries, out_grad, kv_blocks, first, count, query_grad, after=()):
@@ -156,7 +157,7 @@
         cost_estimate=small_cost
         if held
         else pl.CostEstimate(
-            flops=10 * rows * keys * group * count * HEAD_DIM,
+            flops=100 * rows * keys * group * count * HEAD_DIM,
             bytes_accessed=8 * (rows * group + keys) * count * HEAD_DIM,
             transcendentals=rows * keys * group * count,
         ),
@@ -164,58 +165,60 @@
     )(place, queries, out_grad, *kv_blocks, *held, *after)
 
 
-def fold_kernel(rows, mine_ref, got_ref, *refs):
-    for k, ref in enumerate(refs[-(mine_ref.shape[0] // rows) :]):
-        here = slice(k * rows, (k + 1) * rows)
-        total = mine_ref[here, :].astype(jnp.float32) + got_ref[here, :].astype(jnp.float32)
-        ref[...] = total.astype(ref.dtype)
-
-
-def fold(mine, got, rows, after=()):
-    n_z, width = mine.shape[0] // rows, mine.shape[1]
-    return pl.pallas_call(
-        functools.partial(fold_kernel, rows),
-        in_specs=[pl.BlockSpec(memory_space=pltpu.VMEM)] * 2
-        + [pl.BlockSpec(memory_space=pl.ANY)] * len(after),
-        out_shape=[jax.ShapeDtypeStruct((rows, width), jnp.float32)]
-        + [jax.ShapeDtypeStruct((rows, width), jnp.bfloat16)] * (n_z - 1),
+def fold_kernel(mine_ref, *refs):
+    out_ref, width = refs[-1], mine_ref.shape[1]
+    total = mine_ref[...].astype(jnp.float32) + refs[0][...].astype(jnp.float32)
+    out_ref[:, :width] = total.astype(out_ref.dtype)
+    first = width
+    for ref in refs[1:-1]:
+        out_ref[:, first : first + ref.shape[1]] = ref[...]
+        first += ref.shape[1]
+
+
+def fold(mine, got, others):
+    arrays = (mine, got, *others)
+    rows, width = mine.shape[0], sum(part.shape[1] for part in arrays[1:])
+    return pl.pallas_call(
+        fold_kernel,
+        grid=(4,),
+        in_specs=[pl.BlockSpec((rows // 4, part.shape[1]), lambda i: (i, 0)) for part in arrays],
+        out_specs=pl.BlockSpec((rows // 4, width), lambda i: (i, 0)),
+        out_shape=jax.ShapeDtypeStruct((rows, width), jnp.bfloat16),
         compiler_params=pltpu.CompilerParams(vmem_limit_bytes=vmem_limit),
         cost_estimate=small_cost,
         name="fold",
-    )(mine, got, *after)
-
-
-def finish_kernel(n_z, counts, *refs):
+    )(*arrays)
+
+
+def finish_kernel(counts, total_ref, *refs):
     key_ref, value_ref = refs[-2:]
-    first = 0
-    for i, count in enumerate(counts):
-        parts = refs[i * n_z : (i + 1) * n_z]
-        total = parts[0][...]
-        for ref in parts[1:]:
-            total = total + ref[...].astype(jnp.float32)
-        total = total.astype(jnp.bfloat16)
-        for g in range(count):
-            lanes = slice((first + g) * HEAD_DIM, (first + g + 1) * HEAD_DIM)
-            key_ref[0, :, lanes] = total[:, 2 * g * HEAD_DIM : (2 * g + 1) * HEAD_DIM]
-            value_ref[0, :, lanes] = total[:, (2 * g + 1) * HEAD_DIM : (2 * g + 2) * HEAD_DIM]
-        first += count
-
-
-def finish(parts, counts, rows, after):
-    shape = jax.ShapeDtypeStruct((1, rows, sum(counts) * HEAD_DIM), jnp.bfloat16)
-    return pl.pallas_call(
-        functools.partial(finish_kernel, len(parts[0]), counts),
-        in_specs=[pl.BlockSpec(memory_space=pltpu.VMEM)] * (len(parts) * len(parts[0]))
+    size = 2 * HEAD_DIM
+    for g in range(sum(counts)):
+        lanes = slice(g * HEAD_DIM, (g + 1) * HEAD_DIM)
+        held = total_ref[:, g * size : (g + 1) * size]
+        if g >= counts[0]:
+            at = (g - counts[0]) * size
+            held = held.astype(jnp.float32) + refs[0][:, at : at + size].astype(jnp.float32)
+            held = held.astype(jnp.bfloat16)
+        key_ref[0, :, lanes] = held[:, :HEAD_DIM]
+        value_ref[0, :, lanes] = held[:, HEAD_DIM:]
+
+
+def finish(counts, total, crossed, after):
+    shape = jax.ShapeDtypeStruct((1, total.shape[0], sum(counts) * HEAD_DIM), jnp.bfloat16)
+    return pl.pallas_call(
+        functools.partial(finish_kernel, counts),
+        in_specs=[pl.BlockSpec(memory_space=pltpu.VMEM)] * (1 + len(crossed))
         + [pl.BlockSpec(memory_space=pl.ANY)],
         out_shape=[shape, shape],
         compiler_params=pltpu.CompilerParams(vmem_limit_bytes=vmem_limit),
         cost_estimate=small_cost,
         name="finish",
-    )(*[part for group in parts for part in group], after)
+    )(total, *crossed, after)
 
 
 def join_kernel(
-    n_z, n_dp, key_ref, value_ref, rows_ref, ids_ref, combine_ref, kv_ref, ext_ref
+    n_z, n_dp, key_ref, value_ref, rows_ref, ids_ref, combine_ref, kv_ref, ext_ref, rest_ref
 ):
     for g in range(kv_ref.shape[1] // (2 * HEAD_DIM)):
         lanes = slice(g * HEAD_DIM, (g + 1) * HEAD_DIM)
@@ -239,10 +242,16 @@
     )
     ranks = mul(hits.astype(jnp.bfloat16), jnp.where(before, 1.0, 0.0).astype(jnp.bfloat16))
     table = jnp.where(kind < 2 * n_dp, jnp.where(hits > 0.0, ranks, -1.0), weights)
-    ext_ref[:tokens, :] = rows_ref[...]
+    half = feat // 2
+    ext_ref[:tokens, :] = rows_ref[:, :half]
+    rest_ref[...] = rows_ref[:, half:]
     squares = [table[i * lines : (i + 1) * lines] for i in range(n_z)]
-    squares += [jnp.zeros((lines, tokens), jnp.float32)] * (feat // tokens - n_z)
-    ext_ref[tokens:, :] = jnp.concatenate(squares, axis=1).astype(jnp.bfloat16)
+    per_row = half // tokens
+    squares += [jnp.zeros((lines, tokens), jnp.float32)] * (-n_z % per_row)
+    for i in range(len(squares) // per_row):
+        line_of = jnp.concatenate(squares[i * per_row : (i + 1) * per_row], axis=1)
+        here = slice(tokens + i * lines, tokens + (i + 1) * lines)
+        ext_ref[here, :] = line_of.astype(jnp.bfloat16)
 
 
 def join(keys, values, full_rows, ids, combine, n_z, n_dp):
@@ -252,7 +261,10 @@
         functools.partial(join_kernel, n_z, n_dp),
         out_shape=[
             jax.ShapeDtypeStruct((rows, 2 * width), jnp.bfloat16),
-            jax.ShapeDtypeStruct((tokens + 4 * n_dp, feat), jnp.bfloat16),
+            jax.ShapeDtypeStruct(
+                (tokens + 4 * n_dp * -(-2 * n_z * tokens // feat), feat // 2), jnp.bfloat16
+            ),
+            jax.ShapeDtypeStruct((tokens, feat // 2), jnp.bfloat16),
         ],
         compiler_params=pltpu.CompilerParams(vmem_limit_bytes=vmem_limit),
         cost_estimate=small_cost,
@@ -268,8 +280,7 @@
     @pl.when(pl.program_id(0) == 0)
     def _():
         for i, ref in enumerate(table_refs):
-            table = ref[:, pl.ds(pl.multiple_of(place[0] * tokens, tokens), tokens)]
-            table = table.astype(jnp.float32)
+            table = ref[...].astype(jnp.float32)
             slot = lax.broadcasted_iota(jnp.int32, (capacity, tokens), 0).astype(jnp.float32)
             picks = [
                 jnp.where(
@@ -287,23 +298,24 @@
         out_ref[q * size : (q + 1) * size, :] = total.astype(jnp.bfloat16)
 
 
-def pick_rows(place, array, ks, tokens, n_dp, capacity, after=()):
+def pick_rows(place, table, block_table, array, block, ks, tokens, n_dp, capacity, after=()):
     lines, feat = 4 * n_dp, array.shape[1]
-    block = tokens + lines
     step = math.gcd(feat, 512)
     out_rows = len(ks) * 2 * n_dp * capacity
-
-    def at(place, k):
-        return place[0] ^ k if array.shape[0] > block else 0
+    per_row = table.shape[1] // tokens
+
+    def at(place, k, whole, part):
+        return (place[0] & (whole.shape[0] // part - 1)) ^ k
 
     def table_spec(k):
-        per_block = block // lines
-        return pl.BlockSpec(
-            (lines, feat), lambda f, place: (at(place, k) * per_block + per_block - 1, 0)
-        )
+        def index(f, place):
+            first = (at(place, k, table, block_table) * block_table + tokens) // lines
+            return first + place[0] // per_row, place[0] % per_row
+
+        return pl.BlockSpec((lines, tokens), index)
 
     def rows_spec(k):
-        return pl.BlockSpec((block, step), lambda f, place: (at(place, k), f))
+        return pl.BlockSpec((block, step), lambda f, place: (at(place, k, array, block), f))
 
     return pl.pallas_call(
         functools.partial(pick_kernel, len(ks), n_dp, capacity),
@@ -320,24 +332,46 @@
         compiler_params=pltpu.CompilerParams(vmem_limit_bytes=vmem_limit),
         cost_estimate=small_cost,
         name="pick_rows",
-    )(place, *[array] * (2 * len(ks)), *after)
-
-
-def expert_kernel(chunks, n_z, n_dp, capacity, slots, place, *refs):
-    row_refs, w_ref = refs[: len(chunks)], refs[len(chunks)]
+    )(place, *[table] * len(ks), *[array] * len(ks), *after)
+
+
+def partial_kernel(rows_ref, w_ref, out_ref):
+    out_ref[...] = lax.dot_general(
+        rows_ref[...], w_ref[0], (((1,), (1,)), ((), ())), preferred_element_type=jnp.float32
+    )
+
+
+def partial_rows(rows, w_down):
+    count, half = rows.shape
+    hid = w_down.shape[1]
+    step = math.gcd(hid, 512)
+    return pl.pallas_call(
+        partial_kernel,
+        grid=(hid // step,),
+        in_specs=[
+            pl.BlockSpec((count, half), lambda n: (0, 0)),
+            pl.BlockSpec((1, step, half), lambda n: (0, n, 0)),
+        ],
+        out_specs=pl.BlockSpec((count, step), lambda n: (0, n)),
+        out_shape=jax.ShapeDtypeStruct((count, hid), jnp.float32),
+        compiler_params=pltpu.CompilerParams(vmem_limit_bytes=vmem_limit),
+        cost_estimate=small_cost,
+        name="partial_rows",
+    )(rows, w_down)
+
+
+def expert_kernel(ks, with_base, n_z, n_dp, capacity, slots, place, rows_ref, w_ref, *refs):
     out_ref, out_s, sem = refs[-3:]
     step, steps = pl.program_id(0), out_s.shape[0]
     width = out_s.shape[-1]
-    blocks = [(q, k) for ks in chunks for q in range(2 * n_dp) for k in ks]
-    first = 0
-    for rows_ref in row_refs:
-        result = lax.dot_general(
-            rows_ref[...], w_ref[0], (((1,), (1,)), ((), ())), preferred_element_type=jnp.float32
-        )
-        count = rows_ref.shape[0] // capacity
-        for i in range(count):
-            out_s[step, first + i] = result[i * capacity : i * capacity + slots].astype(jnp.bfloat16)
-        first += count
+    blocks = [(q, k) for q in range(2 * n_dp) for k in ks]
+    result = lax.dot_general(
+        rows_ref[...], w_ref[0], (((1,), (1,)), ((), ())), preferred_element_type=jnp.float32
+    )
+    if with_base:
+        result = result + refs[0][...]
+    for i in range(len(blocks)):
+        out_s[step, i] = result[i * capacity : i * capacity + slots].astype(jnp.bfloat16)
 
     def copies(at):
         z = place[0]
@@ -358,17 +392,22 @@
                 copy.wait()
 
 
-def expert_rows(place, arrays, chunks, w_down, n_z, n_dp, capacity, slots, hidden_grad, after=()):
-    hid, feat = w_down.shape[1:]
+def expert_rows(place, rows, ks, w_down, n_z, n_dp, capacity, slots, base, hidden_grad, after=()):
+    hid = w_down.shape[1]
     step = math.gcd(hid, 512)
-    count = sum(array.shape[0] for array in arrays) // capacity
+    count = rows.shape[0] // capacity
+    part = w_down.shape[2] // rows.shape[1] - 1
+    extra = [] if base is None else [base]
     held = [] if hidden_grad is None else [hidden_grad]
     return pl.pallas_call(
-        functools.partial(expert_kernel, chunks, n_z, n_dp, capacity, slots),
+        functools.partial(expert_kernel, ks, bool(extra), n_z, n_dp, capacity, slots),
         grid=(hid // step,),
-        in_specs=[pl.BlockSpec(memory_space=pltpu.SMEM)]
-        + [pl.BlockSpec(array.shape, lambda n: (0, 0)) for array in arrays]
-        + [pl.BlockSpec((1, step, feat), lambda n: (0, n, 0))]
+        in_specs=[
+            pl.BlockSpec(memory_space=pltpu.SMEM),
+            pl.BlockSpec(rows.shape, lambda n: (0, 0)),
+            pl.BlockSpec((1, step, rows.shape[1]), lambda n: (0, n, part)),
+        ]
+        + [pl.BlockSpec((rows.shape[0], step), lambda n: (0, n))] * len(extra)
         + [pl.BlockSpec(memory_space=pl.ANY)] * (len(held) + len(after)),
         out_specs=pl.BlockSpec(memory_space=pl.ANY),
         out_shape=jax.ShapeDtypeStruct((1, n_dp * 2 * n_z, slots, hid), jnp.bfloat16),
@@ -376,11 +415,11 @@
             pltpu.VMEM((hid // step, count, slots, step), jnp.bfloat16),
             pltpu.SemaphoreType.DMA((hid // step, count)),
         ],
-        input_output_aliases={2 + len(arrays): 0} if held else {},
+        input_output_aliases={3 + len(extra): 0} if held else {},
         compiler_params=pltpu.CompilerParams(vmem_limit_bytes=vmem_limit),
         cost_estimate=small_cost,
         name="expert_rows",
-    )(place, *arrays, w_down, *held, *after)
+    )(place, rows, w_down, *extra, *held, *after)
 
 
 def per_device(queries, keys, values, out_grad, mixed_grad, expert_ids, combine, w_down):
@@ -404,7 +443,7 @@
     full_rows = mixed_grad
     if lax.axis_size("tp") > 1:
         full_rows = lax.all_gather(mixed_grad, "tp", axis=1, tiled=True)
-    own, own_rows = join(keys, values, full_rows, expert_ids, combine, n_z, n_dp)
+    own, *own_halves = join(keys, values, full_rows, expert_ids, combine, n_z, n_dp)
 
     def along_z(array, targets):
         pairs = [(2 * i + x, 2 * j + x) for i, j in targets for x in range(2)]
@@ -428,13 +467,20 @@
         [d * n_ctx + 2 * i + j for d in range(n_dp) for j in range(2)] for i in range(n_z)
     ]
     line_groups = [[2 * i + x for i in range(n_z)] for x in range(2)]
-    gathered_rows = lax.all_gather(
-        own_rows, "ctx", axis=0, tiled=True, axis_index_groups=line_groups
-    )
-
-    def exchange(array, ks, after):
-        picked = pick_rows(place, array, ks, token_rows, n_dp, capacity, after)
-        return picked, lax.all_to_all(
+    first_half, columns[n_z // 2] = lax.optimization_barrier((own_halves[0], columns[n_z // 2]))
+    last_half, columns[n_z - 1] = lax.optimization_barrier((own_halves[1], columns[n_z - 1]))
+    all_halves = [
+        lax.all_gather(half, "ctx", axis=0, tiled=True, axis_index_groups=line_groups)
+        for half in (first_half, last_half)
+    ]
+
+    def pick(table, array, ks, after):
+        block = token_rows if array.shape[0] % own_halves[0].shape[0] else own_halves[0].shape[0]
+        sizes = (ks, token_rows, n_dp, capacity)
+        return pick_rows(place, table, own_halves[0].shape[0], array, block, *sizes, after)
+
+    def exchange(picked):
+        return lax.all_to_all(
             picked,
             ("dp", "ctx"),
             split_axis=0,
@@ -443,37 +489,41 @@
             axis_index_groups=plane_groups,
         )
 
-    counts = [1] if kv_local == 1 else [kv_local - 1, 1]
-    gathered = []
-
-    def down(mine, other, after=()):
-        got = lax.ppermute(other, "ctx", [(i, i ^ 1) for i in range(n_ctx)])
-        parts = fold(mine, got, rows_dev, after)
-        gathered.append(
-            [parts[0]]
-            + [
-                lax.ppermute(parts[k], "ctx", [(i, i - 2 * k) for i in range(2 * k, n_ctx)])
-                for k in range(1, n_z)
-            ]
-        )
-        return got, parts[0]
-
-    chunks = [(0,), tuple(range(1, n_z))]
-    picked, got_own = exchange(own_rows, chunks[0], (columns[n_z - 1],))
+    def cross(array):
+        return lax.ppermute(array, "ctx", [(i, i ^ 1) for i in range(n_ctx)])
+
+    counts = [1] if kv_local == 1 else [kv_local // 2, kv_local - kv_local // 2]
+    rest = tuple(range(1, n_z))
+    picked = pick(own_halves[0], full_rows, (0,), (columns[n_z - 1],))
+    got_own = exchange(picked)
     query_grad, mine, other = attention(
         place, queries[0], out_grad[0], blocks, 0, counts[0], None, (picked,)
     )
-    got, folded = down(mine, other)
-    picked, got_rest = exchange(gathered_rows, chunks[1], (got,))
+    crossed = cross(other)
+    picked = pick(all_halves[0], all_halves[0], rest, (query_grad,))
+    picked, crossed = lax.optimization_barrier((picked, crossed))
+    got_first = exchange(picked)
+    others = []
     if len(counts) > 1:
-        query_grad, mine, other = attention(
+        query_grad, *others = attention(
             place, queries[0], out_grad[0], blocks, counts[0], counts[1], query_grad, (picked,)
         )
-        got, folded = down(mine, other)
+    picked = pick(all_halves[0], all_halves[1], rest, (query_grad,))
+    got_last = exchange(picked)
+    total = lax.psum_scatter(
+        fold(mine, crossed, others),
+        "ctx",
+        scatter_dimension=0,
+        tiled=True,
+        axis_index_groups=line_groups,
+    )
     sizes = (n_z, n_dp, capacity, slots)
-    hidden_grad = expert_rows(place, (got_own,), chunks[:1], w_down, *sizes, None, (folded,))
-    key_grad, value_grad = finish(gathered, counts, rows_dev, hidden_grad)
-    hidden_grad = expert_rows(place, (got_rest,), chunks[1:], w_down, *sizes, hidden_grad)
+    hidden_grad = expert_rows(place, got_own, (0,), w_down, *sizes, None, None, (picked,))
+    base = partial_rows(got_first, w_down)
+    total, base = lax.optimization_barrier((total, base))
+    last = [cross(total[:, -others[1].shape[1] :])] if others else []
+    key_grad, value_grad = finish(counts, total, last, base)
+    hidden_grad = expert_rows(place, got_last, rest, w_down, *sizes, base, hidden_grad)
     return (query_grad[None], key_grad, value_grad, hidden_grad)
 
 

time: 218 us -> 172 us (0.79)
  waiting for transfers between devices: 119 us -> 71.3 us
  Pallas kernels: 46.6 us -> 52.9 us
  starting transfers between devices: 32.6 us -> 28 us
    ppermute x8 -> x2, waiting for transfers between devices: 115 us -> 0.01 us  [cross(): return lax.ppermute(array, 'ctx', [(i, i ^ 1) for i in range(n_ctx)])]
    reduce_scatter x0 -> x1, waiting for transfers between devices: none -> 36.3 us  [per_device(): lax.psum_scatter(fold(mine, crossed, others), 'ctx', scatter_dimension=0,...]
    all_gather x1 -> x2, waiting for transfers between devices: 0.01 us -> 28.7 us  [per_device(): lax.all_gather(half, 'ctx', axis=0, tiled=True, axis_index_groups=line_gr...]
    ppermute x8 -> x2, starting transfers between devices: 11.7 us -> 3.61 us  [cross(): return lax.ppermute(array, 'ctx', [(i, i ^ 1) for i in range(n_ctx)])]
    pallas_call x5, Pallas kernels: 23.9 us -> 28.4 us  [the longest x2 15.2 us: expert_rows(): pl.pallas_call(functools.partial(expert_kernel, ks, bool(extra), n_z, n_d...]
    all_to_all x2 -> x3, starting transfers between devices: 9.13 us -> 12.6 us  [exchange(): lax.all_to_all(picked, ('dp', 'ctx'), split_axis=0, concat_axis=0, tiled=...]
    pallas_call x2 -> x3, Pallas kernels: 10.3 us -> 11.9 us  [pick_rows(): pl.pallas_call(functools.partial(pick_kernel, len(ks), n_dp, capacity), g...]
  transfers between devices with their start and end apart: 18 -> 15, of which waited for: 9 -> 6; matrix products, arithmetic and copies ran while one was open for 0% -> 1% of each run, Pallas kernels for 15% -> 28%
where the time goes in v4:
time: 172 us
  waiting for transfers between devices  71.3 us (41%)
  Pallas kernels  52.9 us (31%)
  starting transfers between devices  28 us (16%)
  between operations  14 us (8%)
  local copies, waits for them, and re-layouts  4.79 us (3%)
    reduce_scatter x1, waiting for transfers between devices, per_device(): lax.psum_scatter(fold(mine, crossed, others), 'ctx', scatter_dimension=0,...  36.3 us
    all_gather x2, waiting for transfers between devices, per_device(): lax.all_gather(half, 'ctx', axis=0, tiled=True, axis_index_groups=line_gr...  28.7 us
    pallas_call x2, Pallas kernels, expert_rows(): pl.pallas_call(functools.partial(expert_kernel, ks, bool(extra), n_z, n_d...  15.2 us
    all_to_all x3, starting transfers between devices, exchange(): lax.all_to_all(picked, ('dp', 'ctx'), split_axis=0, concat_axis=0, tiled=...  12.6 us
    pallas_call x3, Pallas kernels, pick_rows(): pl.pallas_call(functools.partial(pick_kernel, len(ks), n_dp, capacity), g...  11.9 us
    pallas_call x2, Pallas kernels, attention(): pl.pallas_call(functools.partial(attention_kernel, n_blocks, heads_step,...  10.3 us
    pallas_call x1, Pallas kernels, partial_rows(): pl.pallas_call(partial_kernel, grid=(hid // step,), in_specs=[pl.BlockSpe...  7.64 us
    ppermute x3, starting transfers between devices, along_z(): return lax.ppermute(array, 'ctx', pairs)  6.27 us
  transfers between devices with their start and end apart: 15, of which 6 were waited for; matrix products, arithmetic and copies ran while one was open for 1% of the time, Pallas kernels for 28%

profile of v4, /device:TPU:0, one launch (start us, length us, event | category | flops | bytes accessed | tf_op | source)
XLA Modules:
  0.0 171.6 jit_solution(540563040246606664)
XLA Ops:
  7.2 2.2 %join.1 = (bf16[128,1024]{1,0:T(8,128)(2,1)}, bf16[144,1024]{1,0:T(8,128)(2,1)}, bf16[128,1024]{1,0:T(8,128)(2,1)}) custom-call(bf16[1,128,512]{2,1,0:T(8,128)(2,1)} %key_ref.1, bf16[1,128,512]{2,1,0:T(8,128)(2,1)} %value_ref.1, bf16[128,2048]{1,0:T(8,128)(2,1)} %refs_1_.1, s32[8,128]{1,0:T(8,128)} %bitcast.23, bf16[8,128]{1,0:T(8,128)(2,1)} %bitcast.24), custom_call_target="tpu_custom_call" | custom-call | flops 1 | bytes 1 | tf_op jit(solution)/shard_map/join/pallas_call | solution.py:260
  9.4 4.9 %collective-permute-start = (bf16[128,1024]{1,0:T(8,128)(2,1)}, bf16[128,1024]{1,0:T(8,128)(2,1)S(1)}, u32[]{:S(2)}, u32[]{:S(2)}) collective-permute-start(bf16[128,1024]{1,0:T(8,128)(2,1)} %get-tuple-element.27.refs_0_), channel_id=1, source_target_pairs={{0,2},{1,3},{2,4},{3,5},{4,6},{5,7},{8,10},{9,11},{10,12},{11,13},... | collective-permute-start | bytes 786440 | tf_op jit(solution)/shard_map/ppermute | solution.py:450
  14.4 3.4 %collective-permute-start.2 = (bf16[128,1024]{1,0:T(8,128)(2,1)}, bf16[128,1024]{1,0:T(8,128)(2,1)S(1)}, u32[]{:S(2)}, u32[]{:S(2)}) collective-permute-start(bf16[128,1024]{1,0:T(8,128)(2,1)} %get-tuple-element.27.refs_0_), channel_id=1, source_target_pairs={{0,1},{2,3},{4,5},{6,7},{8,9},{10,11},{12,13},{14,15},{16,17},{18,... | collective-permute-start | bytes 786440 | tf_op jit(solution)/shard_map/ppermute | solution.py:454
  17.8 2.4 %collective-permute-done.refs_2_ = bf16[128,1024]{1,0:T(8,128)(2,1)S(1)} collective-permute-done((bf16[128,1024]{1,0:T(8,128)(2,1)}, bf16[128,1024]{1,0:T(8,128)(2,1)S(1)}, u32[]{:S(2)}, u32[]{:S(2)}) %collective-permute-start) | collective-permute-done | bytes 262176 | tf_op jit(solution)/shard_map/ppermute | solution.py:450
  20.2 0.7 collective-permute-start.1
  20.9 2.5 %collective-permute-done.2.refs_1_ = bf16[128,1024]{1,0:T(8,128)(2,1)S(1)} collective-permute-done((bf16[128,1024]{1,0:T(8,128)(2,1)}, bf16[128,1024]{1,0:T(8,128)(2,1)S(1)}, u32[]{:S(2)}, u32[]{:S(2)}) %collective-permute-start.2) | collective-permute-done | bytes 262176 | tf_op jit(solution)/shard_map/ppermute | solution.py:454
  23.4 0.7 collective-permute-start.4
  24.1 0.7 collective-permute-start.3
  24.8 0.7 collective-permute-start.5
  25.5 0.7 collective-permute-start.6
  26.9 4.5 %pick_rows.3.refs_8_ = bf16[320,2048]{1,0:T(8,128)(2,1)} custom-call(s32[2]{0:T(128)} %pad_add_fusion.place, bf16[144,1024]{1,0:T(8,128)(2,1)} %get-tuple-element.37.refs_0_, bf16[128,2048]{1,0:T(8,128)(2,1)} %refs_1_.1, bf16[128,1024]{1,0:T(8,128)(2,1)} %copy-done.2), custom_call_target="tpu_custom_call" | custom-call | flops 1 | bytes 1 | tf_op jit(solution)/shard_map/pick_rows/pallas_call | solution.py:320
  31.3 4.6 %all-to-all-start.2 = ((bf16[8,40,2048]{2,1,0:T(8,128)(2,1)}), bf16[8,40,2048]{2,1,0:T(8,128)(2,1)S(1)}, u32[]{:S(2)}, u32[]{:S(2)}) async-start(bf16[8,40,2048]{2,1,0:T(8,128)(2,1)} %bitcast.17), calls=%async_computation.3 | async-start | bytes 2621440 | tf_op jit(solution)/shard_map/all_to_all | solution.py:483
  36.0 0.7 all-gather.5.cloned.1.call-update
  37.4 5.2 %attention_backward.2 = (bf16[128,4096]{1,0:T(8,128)(2,1)}, bf16[512,512]{1,0:T(8,128)(2,1)}, bf16[512,512]{1,0:T(8,128)(2,1)}) custom-call(s32[2]{0:T(128)} %pad_add_fusion.place, bf16[128,4096]{1,0:T(8,128)(2,1)} %bitcast.19, bf16[128,4096]{1,0:T(8,128)(2,1)} %bitcast.21, bf16[128,1024]{1,0:T(8,128)(2,1)} %get-tuple-element.27.refs_0_, ...), custom_call_target="tpu_custom_call" | custom-call | flops 26843545600 | bytes 4194304 | tf_op jit(solution)/shard_map/attention_backward/pallas_call | solution.py:133
  42.6 2.1 %collective-permute-start.7 = (bf16[512,512]{1,0:T(8,128)(2,1)}, bf16[512,512]{1,0:T(8,128)(2,1)S(1)}, u32[]{:S(2)}, u32[]{:S(2)}) collective-permute-start(bf16[512,512]{1,0:T(8,128)(2,1)} %get-tuple-element.38), channel_id=1, source_target_pairs={{0,1},{1,0},{2,3},{3,2},{4,5},{5,4},{6,7},{7,6},{8,9},{9,8},{10,11... | collective-permute-start | bytes 1572872 | tf_op jit(solution)/shard_map/ppermute | solution.py:493
  44.6 17.3 %all-gather.3.cloned.1.call-done.refs_0_.refs_1_.refs_2_.refs_3_.refs_4_.refs_5_ = bf16[576,1024]{1,0:T(8,128)(2,1)} async-done(((bf16[144,1024]{1,0:T(8,128)(2,1)}), bf16[576,1024]{1,0:T(8,128)(2,1)}) %all-gather.3.cloned.1.call-update) | async-done | bytes 1179664 | tf_op jit(solution)/shard_map/all_gather | solution.py:473
  62.0 3.7 %pick_rows.4.refs_9_ = bf16[960,1024]{1,0:T(8,128)(2,1)} custom-call(s32[2]{0:T(128)} %pad_add_fusion.place, bf16[576,1024]{1,0:T(8,128)(2,1)} %all-gather.3.cloned.1.call-done.refs_0_.refs_1_.refs_2_.refs_3_.refs_4_.refs_5_, bf16[576,1024]{1,0:T(8,128)(2,1)} %all-gather.3.cloned.1.call-done.refs_0_.refs_1_.refs_2_.refs_3_.refs_4_.refs_5_, ...), custom_call_target="tpu_custom_call" | custom-call | flops 1 | bytes 1 | tf_op jit(solution)/shard_map/pick_rows/pallas_call | solution.py:320
  65.7 0.8 copy-done.3
  67.0 3.7 %all-to-all-start = ((bf16[8,120,1024]{2,1,0:T(8,128)(2,1)}), bf16[8,120,1024]{2,1,0:T(8,128)(2,1)S(1)}, u32[]{:S(2)}, u32[]{:S(2)}) async-start(bf16[8,120,1024]{2,1,0:T(8,128)(2,1)} %bitcast.13), calls=%async_computation.1 | async-start | bytes 3932160 | tf_op jit(solution)/shard_map/all_to_all | solution.py:483
  70.7 5.2 %attention_backward.3 = (bf16[128,4096]{1,0:T(8,128)(2,1)}, bf16[512,512]{1,0:T(8,128)(2,1)}, bf16[512,512]{1,0:T(8,128)(2,1)}) custom-call(s32[2]{0:T(128)} %pad_add_fusion.place, bf16[128,4096]{1,0:T(8,128)(2,1)} %bitcast.20, bf16[128,4096]{1,0:T(8,128)(2,1)} %bitcast.22, ...), custom_call_target="tpu_custom_call", output_to_operand_aliasing={{0}: (11, {})} | custom-call | flops 1 | bytes 1 | tf_op jit(solution)/shard_map/attention_backward/pallas_call | solution.py:133
  75.8 3.8 %fold.1 = bf16[512,1536]{1,0:T(8,128)(2,1)} custom-call(bf16[512,512]{1,0:T(8,128)(2,1)} %get-tuple-element.41.mine_ref, bf16[512,512]{1,0:T(8,128)(2,1)} %copy-done.3, bf16[512,512]{1,0:T(8,128)(2,1)} %get-tuple-element.43.refs_1_, bf16[512,512]{1,0:T(8,128)(2,1)} %get-tuple-element.44.refs_2_), custom_call_target="tpu_custom_call" | custom-call | flops 1 | bytes 1 | tf_op jit(solution)/shard_map/fold/pallas_call | solution.py:181
  79.6 11.4 %all-gather.5.cloned.1.call-done.refs_3_.refs_4_.refs_5_ = bf16[512,1024]{1,0:T(8,128)(2,1)} async-done(((bf16[128,1024]{1,0:T(8,128)(2,1)}), bf16[512,1024]{1,0:T(8,128)(2,1)}) %all-gather.5.cloned.1.call-update) | async-done | bytes 1048592 | tf_op jit(solution)/shard_map/all_gather | solution.py:473
  91.0 3.7 %pick_rows.5.refs_0_ = bf16[960,1024]{1,0:T(8,128)(2,1)} custom-call(s32[2]{0:T(128)} %pad_add_fusion.place, bf16[576,1024]{1,0:T(8,128)(2,1)} %all-gather.3.cloned.1.call-done.refs_0_.refs_1_.refs_2_.refs_3_.refs_4_.refs_5_, bf16[576,1024]{1,0:T(8,128)(2,1)} %all-gather.3.cloned.1.call-done.refs_0_.refs_1_.refs_2_.refs_3_.refs_4_.refs_5_, ...), custom_call_target="tpu_custom_call" | custom-call | flops 1 | bytes 1 | tf_op jit(solution)/shard_map/pick_rows/pallas_call | solution.py:320
  95.4 1.3 copy-done
  96.7 4.4 %all-to-all-start.1 = ((bf16[8,120,1024]{2,1,0:T(8,128)(2,1)}), bf16[8,120,1024]{2,1,0:T(8,128)(2,1)}, u32[]{:S(2)}, u32[]{:S(2)}) async-start(bf16[8,120,1024]{2,1,0:T(8,128)(2,1)} %bitcast.14), calls=%async_computation.2 | async-start | bytes 3932160 | tf_op jit(solution)/shard_map/all_to_all | solution.py:483
  101.0 7.6 %partial_rows.1.refs_1_.refs_0_ = f32[960,1536]{1,0:T(8,128)} custom-call(bf16[960,1024]{1,0:T(8,128)(2,1)} %bitcast.16, bf16[1,1536,2048]{2,1,0:T(8,128)(2,1)} %w_ref.5), custom_call_target="tpu_custom_call" | custom-call | flops 1 | bytes 1 | tf_op jit(solution)/shard_map/partial_rows/pallas_call | solution.py:348
  108.7 36.3 %reduce-scatter.2.cloned.1.call-done.total_ref = bf16[128,1536]{1,0:T(8,128)(2,1)} async-done(((bf16[512,1536]{1,0:T(8,128)(2,1)}), bf16[128,1536]{1,0:T(8,128)(2,1)}) %reduce-scatter.2.cloned.1.call-update) | async-done | bytes 393232 | tf_op jit(solution)/shard_map/reduce_scatter | solution.py:513
  145.0 0.9 slice.3
  145.9 1.5 collective-permute-start.8
  147.4 6.4 %expert_rows.2.refs_1_ = bf16[1,32,40,1536]{3,2,1,0:T(8,128)(2,1)} custom-call(s32[2]{0:T(128)} %pad_add_fusion.place, bf16[320,2048]{1,0:T(8,128)(2,1)} %bitcast.18, bf16[1,1536,2048]{2,1,0:T(8,128)(2,1)} %w_ref.5, bf16[960,1024]{1,0:T(8,128)(2,1)} %pick_rows.5.refs_0_), custom_call_target="tpu_custom_call" | custom-call | flops 1 | bytes 1 | tf_op jit(solution)/shard_map/expert_rows/pallas_call | solution.py:402
  153.8 8.8 %expert_rows.3 = bf16[1,32,40,1536]{3,2,1,0:T(8,128)(2,1)} custom-call(s32[2]{0:T(128)} %pad_add_fusion.place, bf16[960,1024]{1,0:T(8,128)(2,1)} %bitcast.10.rows_ref, bf16[1,1536,2048]{2,1,0:T(8,128)(2,1)} %w_ref.5, f32[960,1536]{1,0:T(8,128)} %partial_rows.1.refs_1_.refs_0_, ...), custom_call_target="tpu_custom_call", output_to_operand_aliasing={{}: (4, {})} | custom-call | flops 1 | bytes 1 | tf_op jit(solution)/shard_map/expert_rows/pallas_call | solution.py:402
  163.3 1.8 %finish.1 = (bf16[1,128,512]{2,1,0:T(8,128)(2,1)}, bf16[1,128,512]{2,1,0:T(8,128)(2,1)}) custom-call(bf16[128,1536]{1,0:T(8,128)(2,1)} %reduce-scatter.2.cloned.1.call-done.total_ref, bf16[128,512]{1,0:T(8,128)(2,1)} %copy-done.10, f32[960,1536]{1,0:T(8,128)} %partial_rows.1.refs_1_.refs_0_), custom_call_target="tpu_custom_call" | custom-call | flops 1 | bytes 1 | tf_op jit(solution)/shard_map/finish/pallas_call | solution.py:209
  (36 shorter events, 3.3 us)
Async XLA Ops:
  7.2 54.8 %all-gather.3.cloned.1.call-start = ((), (), s32[]{:S(2)}) async-start(), calls=%async_computation.4 | async-start | bytes 1474560 | tf_op jit(solution)/shard_map/all_gather | solution.py:473
  9.4 10.8 %collective-permute-start = (bf16[128,1024]{1,0:T(8,128)(2,1)}, bf16[128,1024]{1,0:T(8,128)(2,1)S(1)}, u32[]{:S(2)}, u32[]{:S(2)}) collective-permute-start(bf16[128,1024]{1,0:T(8,128)(2,1)} %get-tuple-element.27.refs_0_), channel_id=1, source_target_pairs={{0,2},{1,3},{2,4},{3,5},{4,6},{5,7},{8,10},{9,11},{10,12},{11,13},... | collective-permute-start | bytes 786440 | tf_op jit(solution)/shard_map/ppermute | solution.py:450
  14.4 9.0 %collective-permute-start.2 = (bf16[128,1024]{1,0:T(8,128)(2,1)}, bf16[128,1024]{1,0:T(8,128)(2,1)S(1)}, u32[]{:S(2)}, u32[]{:S(2)}) collective-permute-start(bf16[128,1024]{1,0:T(8,128)(2,1)} %get-tuple-element.27.refs_0_), channel_id=1, source_target_pairs={{0,1},{2,3},{4,5},{6,7},{8,9},{10,11},{12,13},{14,15},{16,17},{18,... | collective-permute-start | bytes 786440 | tf_op jit(solution)/shard_map/ppermute | solution.py:454
  20.2 11.1 %copy-start.4 = (bf16[128,1024]{1,0:T(8,128)(2,1)}, bf16[128,1024]{1,0:T(8,128)(2,1)S(1)}, u32[]{:S(2)}) copy-start(bf16[128,1024]{1,0:T(8,128)(2,1)S(1)} %collective-permute-done.refs_2_) | copy-start | bytes 786436
  20.2 3.1 %collective-permute-start.1 = (bf16[128,1024]{1,0:T(8,128)(2,1)S(1)}, bf16[128,1024]{1,0:T(8,128)(2,1)S(1)}, u32[]{:S(2)}, u32[]{:S(2)}) collective-permute-start(bf16[128,1024]{1,0:T(8,128)(2,1)S(1)} %collective-permute-done.refs_2_), channel_id=1, source_target_pairs={{2,4},{3,5},{4,6},{5,7},{10,12},{11,13},{12,14},{13,15},{18,20},{1... | collective-permute-start | bytes 786440 | tf_op jit(solution)/shard_map/ppermute | solution.py:450
  23.4 13.4 %copy-start.5 = (bf16[128,1024]{1,0:T(8,128)(2,1)}, bf16[128,1024]{1,0:T(8,128)(2,1)S(1)}, u32[]{:S(2)}) copy-start(bf16[128,1024]{1,0:T(8,128)(2,1)S(1)} %collective-permute-done.2.refs_1_) | copy-start | bytes 786436
  23.4 13.4 %copy-start.6 = (bf16[128,1024]{1,0:T(8,128)(2,1)}, bf16[128,1024]{1,0:T(8,128)(2,1)S(1)}, u32[]{:S(2)}) copy-start(bf16[128,1024]{1,0:T(8,128)(2,1)S(1)} %collective-permute-done.1.refs_4_) | copy-start | bytes 786436
  23.4 2.1 %collective-permute-start.4 = (bf16[128,1024]{1,0:T(8,128)(2,1)S(1)}, bf16[128,1024]{1,0:T(8,128)(2,1)S(1)}, u32[]{:S(2)}, u32[]{:S(2)}) collective-permute-start(bf16[128,1024]{1,0:T(8,128)(2,1)S(1)} %collective-permute-done.refs_2_), channel_id=1, source_target_pairs={{2,3},{3,2},{4,5},{5,4},{6,7},{7,6},{10,11},{11,10},{12,13},{13,12... | collective-permute-start | bytes 786440 | tf_op jit(solution)/shard_map/ppermute | solution.py:454
  24.1 1.4 collective-permute-start.3
  24.8 0.7 collective-permute-start.5
  25.5 11.3 %copy-start.7 = (bf16[128,1024]{1,0:T(8,128)(2,1)}, bf16[128,1024]{1,0:T(8,128)(2,1)S(1)}, u32[]{:S(2)}) copy-start(bf16[128,1024]{1,0:T(8,128)(2,1)S(1)} %collective-permute-done.4.refs_3_) | copy-start | bytes 786436
  25.5 1.4 copy-start.2
  25.5 5.8 %copy-start.8 = (bf16[128,1024]{1,0:T(8,128)(2,1)}, bf16[128,1024]{1,0:T(8,128)(2,1)S(1)}, u32[]{:S(2)}) copy-start(bf16[128,1024]{1,0:T(8,128)(2,1)S(1)} %collective-permute-done.5.refs_5_) | copy-start | bytes 786436
  25.5 11.2 %collective-permute-start.6 = (bf16[128,1024]{1,0:T(8,128)(2,1)S(1)}, bf16[128,1024]{1,0:T(8,128)(2,1)S(1)}, u32[]{:S(2)}, u32[]{:S(2)}) collective-permute-start(bf16[128,1024]{1,0:T(8,128)(2,1)S(1)} %collective-permute-done.3.refs_2_.refs_6_), channel_id=1, source_target_pairs={{6,7},{7,6},{14,15},{15,14},{22,23},{23,22},{30,31},{31,30}} | collective-permute-start | bytes 786440 | tf_op jit(solution)/shard_map/ppermute | solution.py:454
  31.3 34.3 %all-to-all-start.2 = ((bf16[8,40,2048]{2,1,0:T(8,128)(2,1)}), bf16[8,40,2048]{2,1,0:T(8,128)(2,1)S(1)}, u32[]{:S(2)}, u32[]{:S(2)}) async-start(bf16[8,40,2048]{2,1,0:T(8,128)(2,1)} %bitcast.17), calls=%async_computation.3 | async-start | bytes 2621440 | tf_op jit(solution)/shard_map/all_to_all | solution.py:483
  35.9 55.1 %all-gather.5.cloned.1.call-start = ((), (), s32[]{:S(2)}) async-start(), calls=%async_computation.6 | async-start | bytes 1310720 | tf_op jit(solution)/shard_map/all_gather | solution.py:473
  36.7 0.7 copy-start.9
  42.6 23.1 %collective-permute-start.7 = (bf16[512,512]{1,0:T(8,128)(2,1)}, bf16[512,512]{1,0:T(8,128)(2,1)S(1)}, u32[]{:S(2)}, u32[]{:S(2)}) collective-permute-start(bf16[512,512]{1,0:T(8,128)(2,1)} %get-tuple-element.38), channel_id=1, source_target_pairs={{0,1},{1,0},{2,3},{3,2},{4,5},{5,4},{6,7},{7,6},{8,9},{9,8},{10,11... | collective-permute-start | bytes 1572872 | tf_op jit(solution)/shard_map/ppermute | solution.py:493
  65.7 0.8 copy-start.3
  65.7 1.3 copy-start.1
  67.0 28.4 %all-to-all-start = ((bf16[8,120,1024]{2,1,0:T(8,128)(2,1)}), bf16[8,120,1024]{2,1,0:T(8,128)(2,1)S(1)}, u32[]{:S(2)}, u32[]{:S(2)}) async-start(bf16[8,120,1024]{2,1,0:T(8,128)(2,1)} %bitcast.13), calls=%async_computation.1 | async-start | bytes 3932160 | tf_op jit(solution)/shard_map/all_to_all | solution.py:483
  70.6 74.4 %reduce-scatter.2.cloned.1.call-start = ((), (), s32[]{:S(2)}) async-start(), calls=%async_computation.5 | async-start | bytes 1966080 | tf_op jit(solution)/shard_map/reduce_scatter | solution.py:513
  95.4 1.3 copy-start
  96.7 57.1 %all-to-all-start.1 = ((bf16[8,120,1024]{2,1,0:T(8,128)(2,1)}), bf16[8,120,1024]{2,1,0:T(8,128)(2,1)}, u32[]{:S(2)}, u32[]{:S(2)}) async-start(bf16[8,120,1024]{2,1,0:T(8,128)(2,1)} %bitcast.14), calls=%async_computation.2 | async-start | bytes 3932160 | tf_op jit(solution)/shard_map/all_to_all | solution.py:483
  145.9 16.8 %collective-permute-start.8 = (bf16[128,512]{1,0:T(8,128)(2,1)S(1)}, bf16[128,512]{1,0:T(8,128)(2,1)S(1)}, u32[]{:S(2)}, u32[]{:S(2)}) collective-permute-start(bf16[128,512]{1,0:T(8,128)(2,1)S(1)} %slice.3), channel_id=1, source_target_pairs={{0,1},{1,0},{2,3},{3,2},{4,5},{5,4},{6,7},{7,6},{8,9},{9,8},{10,11... | collective-permute-start | bytes 393224 | tf_op jit(solution)/shard_map/ppermute | solution.py:493
  162.7 0.6 copy-start.10
Sparse Core Ops, SparseCore 0:
  23.5 38.3 all-gather.2
  63.5 27.4 all-gather.4
  93.3 51.6 reduce-scatter.1

commit v5 on v4

--- a/solution.py
+++ b/solution.py
@@ -300,7 +300,7 @@
 
 def pick_rows(place, table, block_table, array, block, ks, tokens, n_dp, capacity, after=()):
     lines, feat = 4 * n_dp, array.shape[1]
-    step = math.gcd(feat, 512)
+    step = math.gcd(feat, 1024 if len(ks) == 1 else 512)
     out_rows = len(ks) * 2 * n_dp * capacity
     per_row = table.shape[1] // tokens
 
@@ -449,6 +449,11 @@
         pairs = [(2 * i + x, 2 * j + x) for i, j in targets for x in range(2)]
         return lax.ppermute(array, "ctx", pairs)
 
+    def pick(table, array, ks, after):
+        block = token_rows if array.shape[0] % own_halves[0].shape[0] else own_halves[0].shape[0]
+        sizes = (ks, token_rows, n_dp, capacity)
+        return pick_rows(place, table, own_halves[0].shape[0], array, block, *sizes, after)
+
     def across_x(k):
         pairs = [(i, i ^ 1) for i in range(2 * k, n_ctx) if k > 0 or i % 2 == 0]
         return lax.ppermute(columns[k], "ctx", pairs)
@@ -456,10 +461,15 @@
     columns, others = [own], []
     for k in range(1, n_z):
         others.append(across_x(k - 1))
+        if k == 2:
+            own_picked = pick(own_halves[0], full_rows, (0,), (columns[1],))
         if k > 2:
-            columns[-1], others[k - 3] = lax.optimization_barrier((columns[-1], others[k - 3]))
+            held = lax.optimization_barrier((columns[-1], *others[k - 3 : k - 1]))
+            columns[-1], *others[k - 3 : k - 1] = held
+        if k == n_z - 1:
+            columns[-1], own_picked = lax.optimization_barrier((columns[-1], own_picked))
         columns.append(along_z(columns[-1], [(i, i + 1) for i in range(k - 1, n_z - 1)]))
-    columns[-1], *others[-2:] = lax.optimization_barrier((columns[-1], *others[-2:]))
+    columns[-1], others[-1] = lax.optimization_barrier((columns[-1], others[-1]))
     others.append(across_x(n_z - 1))
     blocks = [block for pair in zip(columns, others) for block in pair]
 
@@ -467,17 +477,12 @@
         [d * n_ctx + 2 * i + j for d in range(n_dp) for j in range(2)] for i in range(n_z)
     ]
     line_groups = [[2 * i + x for i in range(n_z)] for x in range(2)]
-    first_half, columns[n_z // 2] = lax.optimization_barrier((own_halves[0], columns[n_z // 2]))
+    first_half, columns[n_z - 1] = lax.optimization_barrier((own_halves[0], columns[n_z - 1]))
     last_half, columns[n_z - 1] = lax.optimization_barrier((own_halves[1], columns[n_z - 1]))
     all_halves = [
         lax.all_gather(half, "ctx", axis=0, tiled=True, axis_index_groups=line_groups)
         for half in (first_half, last_half)
     ]
-
-    def pick(table, array, ks, after):
-        block = token_rows if array.shape[0] % own_halves[0].shape[0] else own_halves[0].shape[0]
-        sizes = (ks, token_rows, n_dp, capacity)
-        return pick_rows(place, table, own_halves[0].shape[0], array, block, *sizes, after)
 
     def exchange(picked):
         return lax.all_to_all(
@@ -494,21 +499,21 @@
 
     counts = [1] if kv_local == 1 else [kv_local // 2, kv_local - kv_local // 2]
     rest = tuple(range(1, n_z))
-    picked = pick(own_halves[0], full_rows, (0,), (columns[n_z - 1],))
-    got_own = exchange(picked)
+    own_picked, columns[n_z - 1] = lax.optimization_barrier((own_picked, columns[n_z - 1]))
+    got_own = exchange(own_picked)
     query_grad, mine, other = attention(
-        place, queries[0], out_grad[0], blocks, 0, counts[0], None, (picked,)
+        place, queries[0], out_grad[0], blocks, 0, counts[0], None, (own_picked,)
     )
     crossed = cross(other)
+    others = []
+    if len(counts) > 1:
+        query_grad, *others = attention(
+            place, queries[0], out_grad[0], blocks, counts[0], counts[1], query_grad
+        )
     picked = pick(all_halves[0], all_halves[0], rest, (query_grad,))
     picked, crossed = lax.optimization_barrier((picked, crossed))
     got_first = exchange(picked)
-    others = []
-    if len(counts) > 1:
-        query_grad, *others = attention(
-            place, queries[0], out_grad[0], blocks, counts[0], counts[1], query_grad, (picked,)
-        )
-    picked = pick(all_halves[0], all_halves[1], rest, (query_grad,))
+    picked = pick(all_halves[0], all_halves[1], rest, (picked,))
     got_last = exchange(picked)
     total = lax.psum_scatter(
         fold(mine, crossed, others),
@@ -520,7 +525,7 @@
     sizes = (n_z, n_dp, capacity, slots)
     hidden_grad = expert_rows(place, got_own, (0,), w_down, *sizes, None, None, (picked,))
     base = partial_rows(got_first, w_down)
-    total, base = lax.optimization_barrier((total, base))
+    total, base, hidden_grad = lax.optimization_barrier((total, base, hidden_grad))
     last = [cross(total[:, -others[1].shape[1] :])] if others else []
     key_grad, value_grad = finish(counts, total, last, base)
     hidden_grad = expert_rows(place, got_last, rest, w_down, *sizes, base, hidden_grad)

time: 172 us -> 161 us (0.936)
  waiting for transfers between devices: 71.3 us -> 62 us
    reduce_scatter x1, waiting for transfers between devices: 36.3 us -> 12.7 us  [per_device(): lax.psum_scatter(fold(mine, crossed, others), 'ctx', scatter_dimension=0,...]
    all_gather x2, waiting for transfers between devices: 28.7 us -> 45.8 us  [per_device(): lax.all_gather(half, 'ctx', axis=0, tiled=True, axis_index_groups=line_gr...]
    ppermute x4, waiting for transfers between devices: 2.47 us -> 0.01 us  [across_x(): return lax.ppermute(columns[k], 'ctx', pairs)]
  transfers between devices with their start and end apart: 15 -> 15, of which waited for: 6 -> 5; matrix products, arithmetic and copies ran while one was open for 1% -> 1% of each run, Pallas kernels for 28% -> 30%
where the time goes in v5:
time: 161 us; the launch traced here: 160 us
  waiting for transfers between devices  62 us (39%)
  Pallas kernels  51.4 us (32%)
  starting transfers between devices  27.2 us (17%)
  between operations  14 us (9%)
  local copies, waits for them, and re-layouts  4.73 us (3%)
    all_gather x2, waiting for transfers between devices, per_device(): lax.all_gather(half, 'ctx', axis=0, tiled=True, axis_index_groups=line_gr...  45.8 us
    pallas_call x2, Pallas kernels, expert_rows(): pl.pallas_call(functools.partial(expert_kernel, ks, bool(extra), n_z, n_d...  15.2 us
    reduce_scatter x1, waiting for transfers between devices, per_device(): lax.psum_scatter(fold(mine, crossed, others), 'ctx', scatter_dimension=0,...  12.7 us
    all_to_all x3, starting transfers between devices, exchange(): lax.all_to_all(picked, ('dp', 'ctx'), split_axis=0, concat_axis=0, tiled=...  11.8 us
    pallas_call x3, Pallas kernels, pick_rows(): pl.pallas_call(functools.partial(pick_kernel, len(ks), n_dp, capacity), g...  10.6 us
    pallas_call x2, Pallas kernels, attention(): pl.pallas_call(functools.partial(attention_kernel, n_blocks, heads_step,...  10.2 us
    pallas_call x1, Pallas kernels, partial_rows(): pl.pallas_call(partial_kernel, grid=(hid // step,), in_specs=[pl.BlockSpe...  7.66 us
    ppermute x3, starting transfers between devices, along_z(): return lax.ppermute(array, 'ctx', pairs)  6.27 us
  transfers between devices with their start and end apart: 15, of which 5 were waited for; matrix products, arithmetic and copies ran while one was open for 1% of the time, Pallas kernels for 30%

profile of v5, /device:TPU:0, one launch (start us, length us, event | category | flops | bytes accessed | tf_op | source)
XLA Modules:
  0.0 160.0 jit_solution(17210259260796526863)
XLA Ops:
  7.2 2.2 %join.1 = (bf16[128,1024]{1,0:T(8,128)(2,1)}, bf16[144,1024]{1,0:T(8,128)(2,1)}, bf16[128,1024]{1,0:T(8,128)(2,1)}) custom-call(bf16[1,128,512]{2,1,0:T(8,128)(2,1)} %key_ref.1, bf16[1,128,512]{2,1,0:T(8,128)(2,1)} %value_ref.1, bf16[128,2048]{1,0:T(8,128)(2,1)} %refs_1_.1, s32[8,128]{1,0:T(8,128)} %bitcast.23, bf16[8,128]{1,0:T(8,128)(2,1)} %bitcast.24), custom_call_target="tpu_custom_call" | custom-call | flops 1 | bytes 1 | tf_op jit(solution)/shard_map/join/pallas_call | solution.py:260
  9.4 4.9 %collective-permute-start = (bf16[128,1024]{1,0:T(8,128)(2,1)}, bf16[128,1024]{1,0:T(8,128)(2,1)S(1)}, u32[]{:S(2)}, u32[]{:S(2)}) collective-permute-start(bf16[128,1024]{1,0:T(8,128)(2,1)} %get-tuple-element.28.refs_0_), channel_id=1, source_target_pairs={{0,2},{1,3},{2,4},{3,5},{4,6},{5,7},{8,10},{9,11},{10,12},{11,13},... | collective-permute-start | bytes 786440 | tf_op jit(solution)/shard_map/ppermute | solution.py:450
  14.4 3.4 %collective-permute-start.2 = (bf16[128,1024]{1,0:T(8,128)(2,1)}, bf16[128,1024]{1,0:T(8,128)(2,1)S(1)}, u32[]{:S(2)}, u32[]{:S(2)}) collective-permute-start(bf16[128,1024]{1,0:T(8,128)(2,1)} %get-tuple-element.28.refs_0_), channel_id=1, source_target_pairs={{0,1},{2,3},{4,5},{6,7},{8,9},{10,11},{12,13},{14,15},{16,17},{18,... | collective-permute-start | bytes 786440 | tf_op jit(solution)/shard_map/ppermute | solution.py:459
  17.8 2.4 %collective-permute-done.refs_2_ = bf16[128,1024]{1,0:T(8,128)(2,1)S(1)} collective-permute-done((bf16[128,1024]{1,0:T(8,128)(2,1)}, bf16[128,1024]{1,0:T(8,128)(2,1)S(1)}, u32[]{:S(2)}, u32[]{:S(2)}) %collective-permute-start) | collective-permute-done | bytes 262176 | tf_op jit(solution)/shard_map/ppermute | solution.py:450
  20.2 0.7 collective-permute-start.1
  20.9 0.7 collective-permute-start.3
  22.2 3.2 %pick_rows.3.refs_8_ = bf16[320,2048]{1,0:T(8,128)(2,1)} custom-call(s32[2]{0:T(128)} %pad_add_fusion.place, bf16[144,1024]{1,0:T(8,128)(2,1)} %get-tuple-element.40.refs_0_, bf16[128,2048]{1,0:T(8,128)(2,1)} %refs_1_.1, bf16[128,1024]{1,0:T(8,128)(2,1)} %copy-done.2), custom_call_target="tpu_custom_call" | custom-call | flops 1 | bytes 1 | tf_op jit(solution)/shard_map/pick_rows/pallas_call | solution.py:320
  25.4 0.7 collective-permute-start.4
  26.1 0.7 collective-permute-start.5
  26.9 0.7 collective-permute-start.6
  27.6 3.7 %all-to-all-start.1 = ((bf16[8,40,2048]{2,1,0:T(8,128)(2,1)}), bf16[8,40,2048]{2,1,0:T(8,128)(2,1)S(1)}, u32[]{:S(2)}, u32[]{:S(2)}) async-start(bf16[8,40,2048]{2,1,0:T(8,128)(2,1)} %bitcast.16), calls=%async_computation.2 | async-start | bytes 2621440 | tf_op jit(solution)/shard_map/all_to_all | solution.py:488
  31.4 0.7 copy-done.9
  32.1 5.1 %attention_backward.2 = (bf16[128,4096]{1,0:T(8,128)(2,1)}, bf16[512,512]{1,0:T(8,128)(2,1)}, bf16[512,512]{1,0:T(8,128)(2,1)}) custom-call(s32[2]{0:T(128)} %pad_add_fusion.place, bf16[128,4096]{1,0:T(8,128)(2,1)} %bitcast.19, bf16[128,4096]{1,0:T(8,128)(2,1)} %bitcast.21, bf16[128,1024]{1,0:T(8,128)(2,1)} %get-tuple-element.28.refs_0_, ...), custom_call_target="tpu_custom_call" | custom-call | flops 26843545600 | bytes 4194304 | tf_op jit(solution)/shard_map/attention_backward/pallas_call | solution.py:133
  37.2 2.1 %collective-permute-start.7 = (bf16[512,512]{1,0:T(8,128)(2,1)}, bf16[512,512]{1,0:T(8,128)(2,1)S(1)}, u32[]{:S(2)}, u32[]{:S(2)}) collective-permute-start(bf16[512,512]{1,0:T(8,128)(2,1)} %get-tuple-element.41), channel_id=1, source_target_pairs={{0,1},{1,0},{2,3},{3,2},{4,5},{5,4},{6,7},{7,6},{8,9},{9,8},{10,11... | collective-permute-start | bytes 1572872 | tf_op jit(solution)/shard_map/ppermute | solution.py:498
  39.3 5.1 %attention_backward.3 = (bf16[128,4096]{1,0:T(8,128)(2,1)}, bf16[512,512]{1,0:T(8,128)(2,1)}, bf16[512,512]{1,0:T(8,128)(2,1)}) custom-call(s32[2]{0:T(128)} %pad_add_fusion.place, bf16[128,4096]{1,0:T(8,128)(2,1)} %bitcast.20, bf16[128,4096]{1,0:T(8,128)(2,1)} %bitcast.22, ...), custom_call_target="tpu_custom_call", output_to_operand_aliasing={{0}: (11, {})} | custom-call | flops 1 | bytes 1 | tf_op jit(solution)/shard_map/attention_backward/pallas_call | solution.py:133
  44.4 29.6 %all-gather.3.cloned.1.call-done.refs_0_.refs_1_.refs_2_.refs_3_.refs_4_.refs_5_ = bf16[576,1024]{1,0:T(8,128)(2,1)} async-done(((bf16[144,1024]{1,0:T(8,128)(2,1)}), bf16[576,1024]{1,0:T(8,128)(2,1)}) %all-gather.3.cloned.1.call-update) | async-done | bytes 1179664 | tf_op jit(solution)/shard_map/all_gather | solution.py:483
  74.0 3.7 %pick_rows.4.refs_6_ = bf16[960,1024]{1,0:T(8,128)(2,1)} custom-call(s32[2]{0:T(128)} %pad_add_fusion.place, bf16[576,1024]{1,0:T(8,128)(2,1)} %all-gather.3.cloned.1.call-done.refs_0_.refs_1_.refs_2_.refs_3_.refs_4_.refs_5_, bf16[576,1024]{1,0:T(8,128)(2,1)} %all-gather.3.cloned.1.call-done.refs_0_.refs_1_.refs_2_.refs_3_.refs_4_.refs_5_, ...), custom_call_target="tpu_custom_call" | custom-call | flops 1 | bytes 1 | tf_op jit(solution)/shard_map/pick_rows/pallas_call | solution.py:320
  77.7 0.8 copy-done.3
  78.9 3.7 %all-to-all-start = ((bf16[8,120,1024]{2,1,0:T(8,128)(2,1)}), bf16[8,120,1024]{2,1,0:T(8,128)(2,1)S(1)}, u32[]{:S(2)}, u32[]{:S(2)}) async-start(bf16[8,120,1024]{2,1,0:T(8,128)(2,1)} %bitcast.13), calls=%async_computation.1 | async-start | bytes 3932160 | tf_op jit(solution)/shard_map/all_to_all | solution.py:488
  82.7 3.7 %fold.1 = bf16[512,1536]{1,0:T(8,128)(2,1)} custom-call(bf16[512,512]{1,0:T(8,128)(2,1)} %get-tuple-element.39.mine_ref, bf16[512,512]{1,0:T(8,128)(2,1)} %copy-done.3, bf16[512,512]{1,0:T(8,128)(2,1)} %get-tuple-element.43.refs_1_, bf16[512,512]{1,0:T(8,128)(2,1)} %get-tuple-element.44.refs_2_), custom_call_target="tpu_custom_call" | custom-call | flops 1 | bytes 1 | tf_op jit(solution)/shard_map/fold/pallas_call | solution.py:181
  86.4 16.2 %all-gather.5.cloned.1.call-done.refs_3_.refs_4_.refs_5_ = bf16[512,1024]{1,0:T(8,128)(2,1)} async-done(((bf16[128,1024]{1,0:T(8,128)(2,1)}), bf16[512,1024]{1,0:T(8,128)(2,1)}) %all-gather.5.cloned.1.call-update) | async-done | bytes 1048592 | tf_op jit(solution)/shard_map/all_gather | solution.py:483
  102.6 3.7 %pick_rows.5.refs_0_ = bf16[960,1024]{1,0:T(8,128)(2,1)} custom-call(s32[2]{0:T(128)} %pad_add_fusion.place, bf16[576,1024]{1,0:T(8,128)(2,1)} %all-gather.3.cloned.1.call-done.refs_0_.refs_1_.refs_2_.refs_3_.refs_4_.refs_5_, bf16[576,1024]{1,0:T(8,128)(2,1)} %all-gather.3.cloned.1.call-done.refs_0_.refs_1_.refs_2_.refs_3_.refs_4_.refs_5_, ...), custom_call_target="tpu_custom_call" | custom-call | flops 1 | bytes 1 | tf_op jit(solution)/shard_map/pick_rows/pallas_call | solution.py:320
  106.4 1.0 all-to-all-done
  107.4 1.3 copy-done
  108.6 4.4 %all-to-all-start.2 = ((bf16[8,120,1024]{2,1,0:T(8,128)(2,1)}), bf16[8,120,1024]{2,1,0:T(8,128)(2,1)}, u32[]{:S(2)}, u32[]{:S(2)}) async-start(bf16[8,120,1024]{2,1,0:T(8,128)(2,1)} %bitcast.14), calls=%async_computation.3 | async-start | bytes 3932160 | tf_op jit(solution)/shard_map/all_to_all | solution.py:488
  113.0 6.4 %expert_rows.2.refs_1_ = bf16[1,32,40,1536]{3,2,1,0:T(8,128)(2,1)} custom-call(s32[2]{0:T(128)} %pad_add_fusion.place, bf16[320,2048]{1,0:T(8,128)(2,1)} %bitcast.17, bf16[1,1536,2048]{2,1,0:T(8,128)(2,1)} %w_ref.5, bf16[960,1024]{1,0:T(8,128)(2,1)} %pick_rows.5.refs_0_), custom_call_target="tpu_custom_call" | custom-call | flops 1 | bytes 1 | tf_op jit(solution)/shard_map/expert_rows/pallas_call | solution.py:402
  119.4 7.7 %partial_rows.1.refs_1_.refs_0_ = f32[960,1536]{1,0:T(8,128)} custom-call(bf16[960,1024]{1,0:T(8,128)(2,1)} %bitcast.15, bf16[1,1536,2048]{2,1,0:T(8,128)(2,1)} %w_ref.5), custom_call_target="tpu_custom_call" | custom-call | flops 1 | bytes 1 | tf_op jit(solution)/shard_map/partial_rows/pallas_call | solution.py:348
  127.1 12.7 %reduce-scatter.2.cloned.1.call-done.total_ref = bf16[128,1536]{1,0:T(8,128)(2,1)} async-done(((bf16[512,1536]{1,0:T(8,128)(2,1)}), bf16[128,1536]{1,0:T(8,128)(2,1)}) %reduce-scatter.2.cloned.1.call-update) | async-done | bytes 393232 | tf_op jit(solution)/shard_map/reduce_scatter | solution.py:518
  139.8 0.9 slice.3
  140.7 1.5 collective-permute-start.8
  142.2 8.8 %expert_rows.3 = bf16[1,32,40,1536]{3,2,1,0:T(8,128)(2,1)} custom-call(s32[2]{0:T(128)} %pad_add_fusion.place, bf16[960,1024]{1,0:T(8,128)(2,1)} %bitcast.12.rows_ref, bf16[1,1536,2048]{2,1,0:T(8,128)(2,1)} %w_ref.5, f32[960,1536]{1,0:T(8,128)} %partial_rows.1.refs_1_.refs_0_, ...), custom_call_target="tpu_custom_call", output_to_operand_aliasing={{}: (4, {})} | custom-call | flops 1 | bytes 1 | tf_op jit(solution)/shard_map/expert_rows/pallas_call | solution.py:402
  151.7 1.8 %finish.1 = (bf16[1,128,512]{2,1,0:T(8,128)(2,1)}, bf16[1,128,512]{2,1,0:T(8,128)(2,1)}) custom-call(bf16[128,1536]{1,0:T(8,128)(2,1)} %reduce-scatter.2.cloned.1.call-done.total_ref, bf16[128,512]{1,0:T(8,128)(2,1)} %copy-done.10, f32[960,1536]{1,0:T(8,128)} %partial_rows.1.refs_1_.refs_0_), custom_call_target="tpu_custom_call" | custom-call | flops 1 | bytes 1 | tf_op jit(solution)/shard_map/finish/pallas_call | solution.py:209
  (36 shorter events, 1.9 us)
Async XLA Ops:
  7.2 66.8 %all-gather.3.cloned.1.call-start = ((), (), s32[]{:S(2)}) async-start(), calls=%async_computation.4 | async-start | bytes 1474560 | tf_op jit(solution)/shard_map/all_gather | solution.py:483
  9.4 10.8 %collective-permute-start = (bf16[128,1024]{1,0:T(8,128)(2,1)}, bf16[128,1024]{1,0:T(8,128)(2,1)S(1)}, u32[]{:S(2)}, u32[]{:S(2)}) collective-permute-start(bf16[128,1024]{1,0:T(8,128)(2,1)} %get-tuple-element.28.refs_0_), channel_id=1, source_target_pairs={{0,2},{1,3},{2,4},{3,5},{4,6},{5,7},{8,10},{9,11},{10,12},{11,13},... | collective-permute-start | bytes 786440 | tf_op jit(solution)/shard_map/ppermute | solution.py:450
  14.4 11.0 %collective-permute-start.2 = (bf16[128,1024]{1,0:T(8,128)(2,1)}, bf16[128,1024]{1,0:T(8,128)(2,1)S(1)}, u32[]{:S(2)}, u32[]{:S(2)}) collective-permute-start(bf16[128,1024]{1,0:T(8,128)(2,1)} %get-tuple-element.28.refs_0_), channel_id=1, source_target_pairs={{0,1},{2,3},{4,5},{6,7},{8,9},{10,11},{12,13},{14,15},{16,17},{18,... | collective-permute-start | bytes 786440 | tf_op jit(solution)/shard_map/ppermute | solution.py:459
  20.2 2.0 %copy-start.2 = (bf16[128,1024]{1,0:T(8,128)(2,1)}, bf16[128,1024]{1,0:T(8,128)(2,1)S(1)}, u32[]{:S(2)}) copy-start(bf16[128,1024]{1,0:T(8,128)(2,1)S(1)} %collective-permute-done.refs_2_) | copy-start | bytes 786436
  20.2 5.2 %collective-permute-start.1 = (bf16[128,1024]{1,0:T(8,128)(2,1)S(1)}, bf16[128,1024]{1,0:T(8,128)(2,1)S(1)}, u32[]{:S(2)}, u32[]{:S(2)}) collective-permute-start(bf16[128,1024]{1,0:T(8,128)(2,1)S(1)} %collective-permute-done.refs_2_), channel_id=1, source_target_pairs={{2,4},{3,5},{4,6},{5,7},{10,12},{11,13},{12,14},{13,15},{18,20},{1... | collective-permute-start | bytes 786440 | tf_op jit(solution)/shard_map/ppermute | solution.py:450
  20.9 4.5 %collective-permute-start.3 = (bf16[128,1024]{1,0:T(8,128)(2,1)S(1)}, bf16[128,1024]{1,0:T(8,128)(2,1)S(1)}, u32[]{:S(2)}, u32[]{:S(2)}) collective-permute-start(bf16[128,1024]{1,0:T(8,128)(2,1)S(1)} %collective-permute-done.refs_2_), channel_id=1, source_target_pairs={{2,3},{3,2},{4,5},{5,4},{6,7},{7,6},{10,11},{11,10},{12,13},{13,12... | collective-permute-start | bytes 786440 | tf_op jit(solution)/shard_map/ppermute | solution.py:459
  25.4 6.0 %copy-start.4 = (bf16[128,1024]{1,0:T(8,128)(2,1)}, bf16[128,1024]{1,0:T(8,128)(2,1)S(1)}, u32[]{:S(2)}) copy-start(bf16[128,1024]{1,0:T(8,128)(2,1)S(1)} %collective-permute-done.2.refs_1_) | copy-start | bytes 786436
  25.4 6.0 %copy-start.5 = (bf16[128,1024]{1,0:T(8,128)(2,1)}, bf16[128,1024]{1,0:T(8,128)(2,1)S(1)}, u32[]{:S(2)}) copy-start(bf16[128,1024]{1,0:T(8,128)(2,1)S(1)} %collective-permute-done.1.refs_4_) | copy-start | bytes 786436
  25.4 6.0 %copy-start.6 = (bf16[128,1024]{1,0:T(8,128)(2,1)}, bf16[128,1024]{1,0:T(8,128)(2,1)S(1)}, u32[]{:S(2)}) copy-start(bf16[128,1024]{1,0:T(8,128)(2,1)S(1)} %collective-permute-done.3.refs_3_) | copy-start | bytes 786436
  25.4 1.4 collective-permute-start.4
  26.1 0.7 collective-permute-start.5
  26.8 4.6 %copy-start.7 = (bf16[128,1024]{1,0:T(8,128)(2,1)}, bf16[128,1024]{1,0:T(8,128)(2,1)S(1)}, u32[]{:S(2)}) copy-start(bf16[128,1024]{1,0:T(8,128)(2,1)S(1)} %collective-permute-done.4.refs_6_) | copy-start | bytes 786436
  26.8 4.6 %copy-start.8 = (bf16[128,1024]{1,0:T(8,128)(2,1)}, bf16[128,1024]{1,0:T(8,128)(2,1)S(1)}, u32[]{:S(2)}) copy-start(bf16[128,1024]{1,0:T(8,128)(2,1)S(1)} %collective-permute-done.5.refs_5_) | copy-start | bytes 786436
  26.8 75.8 %all-gather.5.cloned.1.call-start = ((), (), s32[]{:S(2)}) async-start(), calls=%async_computation.6 | async-start | bytes 1310720 | tf_op jit(solution)/shard_map/all_gather | solution.py:483
  26.9 4.4 %collective-permute-start.6 = (bf16[128,1024]{1,0:T(8,128)(2,1)S(1)}, bf16[128,1024]{1,0:T(8,128)(2,1)S(1)}, u32[]{:S(2)}, u32[]{:S(2)}) collective-permute-start(bf16[128,1024]{1,0:T(8,128)(2,1)S(1)} %collective-permute-done.4.refs_6_), channel_id=1, source_target_pairs={{6,7},{7,6},{14,15},{15,14},{22,23},{23,22},{30,31},{31,30}} | collective-permute-start | bytes 786440 | tf_op jit(solution)/shard_map/ppermute | solution.py:459
  27.6 50.1 %all-to-all-start.1 = ((bf16[8,40,2048]{2,1,0:T(8,128)(2,1)}), bf16[8,40,2048]{2,1,0:T(8,128)(2,1)S(1)}, u32[]{:S(2)}, u32[]{:S(2)}) async-start(bf16[8,40,2048]{2,1,0:T(8,128)(2,1)} %bitcast.16), calls=%async_computation.2 | async-start | bytes 2621440 | tf_op jit(solution)/shard_map/all_to_all | solution.py:488
  31.3 0.7 copy-start.9
  37.2 40.5 %collective-permute-start.7 = (bf16[512,512]{1,0:T(8,128)(2,1)}, bf16[512,512]{1,0:T(8,128)(2,1)S(1)}, u32[]{:S(2)}, u32[]{:S(2)}) collective-permute-start(bf16[512,512]{1,0:T(8,128)(2,1)} %get-tuple-element.41), channel_id=1, source_target_pairs={{0,1},{1,0},{2,3},{3,2},{4,5},{5,4},{6,7},{7,6},{8,9},{9,8},{10,11... | collective-permute-start | bytes 1572872 | tf_op jit(solution)/shard_map/ppermute | solution.py:498
  77.7 0.8 copy-start.3
  77.7 1.2 copy-start.1
  78.9 28.4 %all-to-all-start = ((bf16[8,120,1024]{2,1,0:T(8,128)(2,1)}), bf16[8,120,1024]{2,1,0:T(8,128)(2,1)S(1)}, u32[]{:S(2)}, u32[]{:S(2)}) async-start(bf16[8,120,1024]{2,1,0:T(8,128)(2,1)} %bitcast.13), calls=%async_computation.1 | async-start | bytes 3932160 | tf_op jit(solution)/shard_map/all_to_all | solution.py:488
  82.6 57.2 %reduce-scatter.2.cloned.1.call-start = ((), (), s32[]{:S(2)}) async-start(), calls=%async_computation.5 | async-start | bytes 1966080 | tf_op jit(solution)/shard_map/reduce_scatter | solution.py:518
  107.4 1.3 copy-start
  108.6 33.6 %all-to-all-start.2 = ((bf16[8,120,1024]{2,1,0:T(8,128)(2,1)}), bf16[8,120,1024]{2,1,0:T(8,128)(2,1)}, u32[]{:S(2)}, u32[]{:S(2)}) async-start(bf16[8,120,1024]{2,1,0:T(8,128)(2,1)} %bitcast.14), calls=%async_computation.3 | async-start | bytes 3932160 | tf_op jit(solution)/shard_map/all_to_all | solution.py:488
  140.7 10.4 %collective-permute-start.8 = (bf16[128,512]{1,0:T(8,128)(2,1)S(1)}, bf16[128,512]{1,0:T(8,128)(2,1)S(1)}, u32[]{:S(2)}, u32[]{:S(2)}) collective-permute-start(bf16[128,512]{1,0:T(8,128)(2,1)S(1)} %slice.3), channel_id=1, source_target_pairs={{0,1},{1,0},{2,3},{3,2},{4,5},{5,4},{6,7},{7,6},{8,9},{9,8},{10,11... | collective-permute-start | bytes 393224 | tf_op jit(solution)/shard_map/ppermute | solution.py:498
  151.1 0.6 copy-start.10
Sparse Core Ops, SparseCore 0:
  27.0 46.9 all-gather.2
  75.6 27.0 all-gather.4
  105.0 34.7 reduce-scatter.1

commit v6 on v5

--- a/solution.py
+++ b/solution.py
@@ -461,13 +461,9 @@
     columns, others = [own], []
     for k in range(1, n_z):
         others.append(across_x(k - 1))
-        if k == 2:
-            own_picked = pick(own_halves[0], full_rows, (0,), (columns[1],))
         if k > 2:
             held = lax.optimization_barrier((columns[-1], *others[k - 3 : k - 1]))
             columns[-1], *others[k - 3 : k - 1] = held
-        if k == n_z - 1:
-            columns[-1], own_picked = lax.optimization_barrier((columns[-1], own_picked))
         columns.append(along_z(columns[-1], [(i, i + 1) for i in range(k - 1, n_z - 1)]))
     columns[-1], others[-1] = lax.optimization_barrier((columns[-1], others[-1]))
     others.append(across_x(n_z - 1))
@@ -477,11 +473,10 @@
         [d * n_ctx + 2 * i + j for d in range(n_dp) for j in range(2)] for i in range(n_z)
     ]
     line_groups = [[2 * i + x for i in range(n_z)] for x in range(2)]
-    first_half, columns[n_z - 1] = lax.optimization_barrier((own_halves[0], columns[n_z - 1]))
     last_half, columns[n_z - 1] = lax.optimization_barrier((own_halves[1], columns[n_z - 1]))
     all_halves = [
         lax.all_gather(half, "ctx", axis=0, tiled=True, axis_index_groups=line_groups)
-        for half in (first_half, last_half)
+        for half in (own_halves[0], last_half)
     ]
 
     def exchange(picked):
@@ -498,11 +493,12 @@
         return lax.ppermute(array, "ctx", [(i, i ^ 1) for i in range(n_ctx)])
 
     counts = [1] if kv_local == 1 else [kv_local // 2, kv_local - kv_local // 2]
-    rest = tuple(range(1, n_z))
-    own_picked, columns[n_z - 1] = lax.optimization_barrier((own_picked, columns[n_z - 1]))
-    got_own = exchange(own_picked)
+    every = tuple(range(n_z))
+    picked = pick(all_halves[0], all_halves[0], every, ())
+    picked, columns[n_z - 1] = lax.optimization_barrier((picked, columns[n_z - 1]))
+    got_first = exchange(picked)
     query_grad, mine, other = attention(
-        place, queries[0], out_grad[0], blocks, 0, counts[0], None, (own_picked,)
+        place, queries[0], out_grad[0], blocks, 0, counts[0], None, (picked,)
     )
     crossed = cross(other)
     others = []
@@ -510,10 +506,8 @@
         query_grad, *others = attention(
             place, queries[0], out_grad[0], blocks, counts[0], counts[1], query_grad
         )
-    picked = pick(all_halves[0], all_halves[0], rest, (query_grad,))
+    picked = pick(all_halves[0], all_halves[1], every, (query_grad,))
     picked, crossed = lax.optimization_barrier((picked, crossed))
-    got_first = exchange(picked)
-    picked = pick(all_halves[0], all_halves[1], rest, (picked,))
     got_last = exchange(picked)
     total = lax.psum_scatter(
         fold(mine, crossed, others),
@@ -523,12 +517,11 @@
         axis_index_groups=line_groups,
     )
     sizes = (n_z, n_dp, capacity, slots)
-    hidden_grad = expert_rows(place, got_own, (0,), w_down, *sizes, None, None, (picked,))
     base = partial_rows(got_first, w_down)
-    total, base, hidden_grad = lax.optimization_barrier((total, base, hidden_grad))
+    total, base = lax.optimization_barrier((total, base))
     last = [cross(total[:, -others[1].shape[1] :])] if others else []
     key_grad, value_grad = finish(counts, total, last, base)
-    hidden_grad = expert_rows(place, got_last, rest, w_down, *sizes, base, hidden_grad)
+    hidden_grad = expert_rows(place, got_last, every, w_down, *sizes, base, None)
     return (query_grad[None], key_grad, value_grad, hidden_grad)
 
 

time: 161 us -> 171 us (1.062)
  waiting for transfers between devices: 62 us -> 81.1 us
  Pallas kernels: 51.4 us -> 45.6 us
  starting transfers between devices: 27.2 us -> 24.1 us
    reduce_scatter x1, waiting for transfers between devices: 12.7 us -> 35.9 us  [per_device(): lax.psum_scatter(fold(mine, crossed, others), 'ctx', scatter_dimension=0,...]
    all_gather x2, waiting for transfers between devices: 45.8 us -> 38.1 us  [per_device(): lax.all_gather(half, 'ctx', axis=0, tiled=True, axis_index_groups=line_gr...]
    pallas_call x2 -> x1, Pallas kernels: 15.2 us -> 10.4 us  [expert_rows(): pl.pallas_call(functools.partial(expert_kernel, ks, bool(extra), n_z, n_d...]
    all_to_all x3 -> x2, starting transfers between devices: 11.8 us -> 7.29 us  [exchange(): lax.all_to_all(picked, ('dp', 'ctx'), split_axis=0, concat_axis=0, tiled=...]
    ppermute x2, waiting for transfers between devices: 0.01 us -> 2.86 us  [cross(): return lax.ppermute(array, 'ctx', [(i, i ^ 1) for i in range(n_ctx)])]
    pallas_call x3 -> x2, Pallas kernels: 10.6 us -> 8.34 us  [pick_rows(): pl.pallas_call(functools.partial(pick_kernel, len(ks), n_dp, capacity), g...]
    ppermute x4, waiting for transfers between devices: 0.01 us -> 1.79 us  [across_x(): return lax.ppermute(columns[k], 'ctx', pairs)]
    unnamed x22 -> x18, local copies, waits for them, and re-layouts: 3.82 us -> 4.55 us
  transfers between devices with their start and end apart: 15 -> 14, of which waited for: 5 -> 6; matrix products, arithmetic and copies ran while one was open for 1% -> 1% of each run, Pallas kernels for 30% -> 24%
where the time goes in v6:
time: 171 us
  waiting for transfers between devices  81.1 us (47%)
  Pallas kernels  45.6 us (27%)
  starting transfers between devices  24.1 us (14%)
  between operations  13.9 us (8%)
  local copies, waits for them, and re-layouts  5.46 us (3%)
    all_gather x2, waiting for transfers between devices, per_device(): lax.all_gather(half, 'ctx', axis=0, tiled=True, axis_index_groups=line_gr...  38.1 us
    reduce_scatter x1, waiting for transfers between devices, per_device(): lax.psum_scatter(fold(mine, crossed, others), 'ctx', scatter_dimension=0,...  35.9 us
    pallas_call x1, Pallas kernels, expert_rows(): pl.pallas_call(functools.partial(expert_kernel, ks, bool(extra), n_z, n_d...  10.4 us
    pallas_call x2, Pallas kernels, attention(): pl.pallas_call(functools.partial(attention_kernel, n_blocks, heads_step,...  10.2 us
    pallas_call x1, Pallas kernels, partial_rows(): pl.pallas_call(partial_kernel, grid=(hid // step,), in_specs=[pl.BlockSpe...  8.82 us
    pallas_call x2, Pallas kernels, pick_rows(): pl.pallas_call(functools.partial(pick_kernel, len(ks), n_dp, capacity), g...  8.34 us
    all_to_all x2, starting transfers between devices, exchange(): lax.all_to_all(picked, ('dp', 'ctx'), split_axis=0, concat_axis=0, tiled=...  7.29 us
    ppermute x3, starting transfers between devices, along_z(): return lax.ppermute(array, 'ctx', pairs)  6.99 us
  transfers between devices with their start and end apart: 14, of which 6 were waited for; matrix products, arithmetic and copies ran while one was open for 1% of the time, Pallas kernels for 24%

profile of v6, /device:TPU:0, one launch (start us, length us, event | category | flops | bytes accessed | tf_op | source)
XLA Modules:
  0.0 170.8 jit_solution(14648299874972048463)
XLA Ops:
  7.2 2.2 %join.1 = (bf16[128,1024]{1,0:T(8,128)(2,1)}, bf16[144,1024]{1,0:T(8,128)(2,1)}, bf16[128,1024]{1,0:T(8,128)(2,1)}) custom-call(bf16[1,128,512]{2,1,0:T(8,128)(2,1)} %key_ref.1, bf16[1,128,512]{2,1,0:T(8,128)(2,1)} %value_ref.1, bf16[128,2048]{1,0:T(8,128)(2,1)} %rows_ref.1, s32[8,128]{1,0:T(8,128)} %bitcast.20, bf16[8,128]{1,0:T(8,128)(2,1)} %bitcast.21), custom_call_target="tpu_custom_call" | custom-call | flops 1 | bytes 1 | tf_op jit(solution)/shard_map/join/pallas_call | solution.py:260
  9.5 5.0 %collective-permute-start = (bf16[128,1024]{1,0:T(8,128)(2,1)}, bf16[128,1024]{1,0:T(8,128)(2,1)S(1)}, u32[]{:S(2)}, u32[]{:S(2)}) collective-permute-start(bf16[128,1024]{1,0:T(8,128)(2,1)} %get-tuple-element.25.refs_0_), channel_id=1, source_target_pairs={{0,2},{1,3},{2,4},{3,5},{4,6},{5,7},{8,10},{9,11},{10,12},{11,13},... | collective-permute-start | bytes 786440 | tf_op jit(solution)/shard_map/ppermute | solution.py:450
  14.5 3.4 %collective-permute-start.2 = (bf16[128,1024]{1,0:T(8,128)(2,1)}, bf16[128,1024]{1,0:T(8,128)(2,1)S(1)}, u32[]{:S(2)}, u32[]{:S(2)}) collective-permute-start(bf16[128,1024]{1,0:T(8,128)(2,1)} %get-tuple-element.25.refs_0_), channel_id=1, source_target_pairs={{0,1},{2,3},{4,5},{6,7},{8,9},{10,11},{12,13},{14,15},{16,17},{18,... | collective-permute-start | bytes 786440 | tf_op jit(solution)/shard_map/ppermute | solution.py:459
  17.9 2.4 %collective-permute-done.refs_2_ = bf16[128,1024]{1,0:T(8,128)(2,1)S(1)} collective-permute-done((bf16[128,1024]{1,0:T(8,128)(2,1)}, bf16[128,1024]{1,0:T(8,128)(2,1)S(1)}, u32[]{:S(2)}, u32[]{:S(2)}) %collective-permute-start) | collective-permute-done | bytes 262176 | tf_op jit(solution)/shard_map/ppermute | solution.py:450
  20.3 0.7 collective-permute-start.1
  21.0 0.7 collective-permute-start.3
  21.7 1.8 %collective-permute-done.2.refs_1_ = bf16[128,1024]{1,0:T(8,128)(2,1)S(1)} collective-permute-done((bf16[128,1024]{1,0:T(8,128)(2,1)}, bf16[128,1024]{1,0:T(8,128)(2,1)S(1)}, u32[]{:S(2)}, u32[]{:S(2)}) %collective-permute-start.2) | collective-permute-done | bytes 262176 | tf_op jit(solution)/shard_map/ppermute | solution.py:459
  23.5 1.4 collective-permute-start.4
  24.9 0.7 collective-permute-start.5
  25.6 1.4 collective-permute-start.6
  26.9 0.6 pad_add_fusion.place
  27.6 14.9 %all-gather.3.cloned.1.call-done.refs_0_.refs_1_.refs_2_.refs_3_.refs_4_.refs_5_.refs_6_.refs_7_ = bf16[576,1024]{1,0:T(8,128)(2,1)} async-done(((bf16[144,1024]{1,0:T(8,128)(2,1)}), bf16[576,1024]{1,0:T(8,128)(2,1)}) %all-gather.3.cloned.1.call-update) | async-done | bytes 1179664 | tf_op jit(solution)/shard_map/all_gather | solution.py:478
  42.5 4.1 %pick_rows.2.refs_8_ = bf16[1280,1024]{1,0:T(8,128)(2,1)} custom-call(s32[2]{0:T(128)} %pad_add_fusion.place, bf16[576,1024]{1,0:T(8,128)(2,1)} %all-gather.3.cloned.1.call-done.refs_0_.refs_1_.refs_2_.refs_3_.refs_4_.refs_5_.refs_6_.refs_7_, bf16[576,1024]{1,0:T(8,128)(2,1)} %all-gather.3.cloned.1.call-done.refs_0_.refs_1_.refs_2_.refs_3_.refs_4_.refs_5_.refs_6_.refs_7_, ...), custom_call_target="tpu_custom_call" | custom-call | flops 1 | bytes 1 | tf_op jit(solution)/shard_map/pick_rows/pallas_call | solution.py:320
  46.6 3.7 %all-to-all-start = ((bf16[8,160,1024]{2,1,0:T(8,128)(2,1)}), bf16[8,160,1024]{2,1,0:T(8,128)(2,1)S(1)}, u32[]{:S(2)}, u32[]{:S(2)}) async-start(bf16[8,160,1024]{2,1,0:T(8,128)(2,1)} %bitcast.12), calls=%async_computation.1 | async-start | bytes 5242880 | tf_op jit(solution)/shard_map/all_to_all | solution.py:483
  50.3 5.1 %attention_backward.2 = (bf16[128,4096]{1,0:T(8,128)(2,1)}, bf16[512,512]{1,0:T(8,128)(2,1)}, bf16[512,512]{1,0:T(8,128)(2,1)}) custom-call(s32[2]{0:T(128)} %pad_add_fusion.place, bf16[128,4096]{1,0:T(8,128)(2,1)} %bitcast.16, bf16[128,4096]{1,0:T(8,128)(2,1)} %bitcast.18, bf16[128,1024]{1,0:T(8,128)(2,1)} %get-tuple-element.25.refs_0_, ...), custom_call_target="tpu_custom_call" | custom-call | flops 26843545600 | bytes 4194304 | tf_op jit(solution)/shard_map/attention_backward/pallas_call | solution.py:133
  55.5 2.0 %collective-permute-start.7 = (bf16[512,512]{1,0:T(8,128)(2,1)}, bf16[512,512]{1,0:T(8,128)(2,1)S(1)}, u32[]{:S(2)}, u32[]{:S(2)}) collective-permute-start(bf16[512,512]{1,0:T(8,128)(2,1)} %get-tuple-element.37), channel_id=1, source_target_pairs={{0,1},{1,0},{2,3},{3,2},{4,5},{5,4},{6,7},{7,6},{8,9},{9,8},{10,11... | collective-permute-start | bytes 1572872 | tf_op jit(solution)/shard_map/ppermute | solution.py:493
  57.5 5.1 %attention_backward.3 = (bf16[128,4096]{1,0:T(8,128)(2,1)}, bf16[512,512]{1,0:T(8,128)(2,1)}, bf16[512,512]{1,0:T(8,128)(2,1)}) custom-call(s32[2]{0:T(128)} %pad_add_fusion.place, bf16[128,4096]{1,0:T(8,128)(2,1)} %bitcast.17, bf16[128,4096]{1,0:T(8,128)(2,1)} %bitcast.19, ...), custom_call_target="tpu_custom_call", output_to_operand_aliasing={{0}: (11, {})} | custom-call | flops 1 | bytes 1 | tf_op jit(solution)/shard_map/attention_backward/pallas_call | solution.py:133
  62.6 23.2 %all-gather.5.cloned.1.call-done.refs_4_.refs_5_.refs_6_.refs_7_ = bf16[512,1024]{1,0:T(8,128)(2,1)} async-done(((bf16[128,1024]{1,0:T(8,128)(2,1)}), bf16[512,1024]{1,0:T(8,128)(2,1)}) %all-gather.5.cloned.1.call-update) | async-done | bytes 1048592 | tf_op jit(solution)/shard_map/all_gather | solution.py:478
  85.8 4.2 %pick_rows.3 = bf16[1280,1024]{1,0:T(8,128)(2,1)} custom-call(s32[2]{0:T(128)} %pad_add_fusion.place, bf16[576,1024]{1,0:T(8,128)(2,1)} %all-gather.3.cloned.1.call-done.refs_0_.refs_1_.refs_2_.refs_3_.refs_4_.refs_5_.refs_6_.refs_7_, bf16[576,1024]{1,0:T(8,128)(2,1)} %all-gather.3.cloned.1.call-done.refs_0_.refs_1_.refs_2_.refs_3_.refs_4_.refs_5_.refs_6_.refs_7_, ...), custom_call_target="tpu_custom_call" | custom-call | flops 1 | bytes 1 | tf_op jit(solution)/shard_map/pick_rows/pallas_call | solution.py:320
  90.0 2.9 %collective-permute-done.7.refs_0_ = bf16[512,512]{1,0:T(8,128)(2,1)S(1)} collective-permute-done((bf16[512,512]{1,0:T(8,128)(2,1)}, bf16[512,512]{1,0:T(8,128)(2,1)S(1)}, u32[]{:S(2)}, u32[]{:S(2)}) %collective-permute-start.7) | collective-permute-done | bytes 524320 | tf_op jit(solution)/shard_map/ppermute | solution.py:493
  92.9 0.8 copy-done.2
  93.7 3.8 %fold.1 = bf16[512,1536]{1,0:T(8,128)(2,1)} custom-call(bf16[512,512]{1,0:T(8,128)(2,1)} %get-tuple-element.34.mine_ref, bf16[512,512]{1,0:T(8,128)(2,1)} %copy-done.2, bf16[512,512]{1,0:T(8,128)(2,1)} %get-tuple-element.39.refs_1_, bf16[512,512]{1,0:T(8,128)(2,1)} %get-tuple-element.40.refs_2_), custom_call_target="tpu_custom_call" | custom-call | flops 1 | bytes 1 | tf_op jit(solution)/shard_map/fold/pallas_call | solution.py:181
  97.5 1.5 copy-done.1
  99.0 3.6 %all-to-all-start.1 = ((bf16[8,160,1024]{2,1,0:T(8,128)(2,1)}), bf16[8,160,1024]{2,1,0:T(8,128)(2,1)S(1)}, u32[]{:S(2)}, u32[]{:S(2)}) async-start(bf16[8,160,1024]{2,1,0:T(8,128)(2,1)} %bitcast.13), calls=%async_computation.2 | async-start | bytes 5242880 | tf_op jit(solution)/shard_map/all_to_all | solution.py:483
  102.6 8.8 %partial_rows.1.refs_1_.refs_0_ = f32[1280,1536]{1,0:T(8,128)} custom-call(bf16[1280,1024]{1,0:T(8,128)(2,1)} %bitcast.14, bf16[1,1536,2048]{2,1,0:T(8,128)(2,1)} %w_ref.3), custom_call_target="tpu_custom_call" | custom-call | flops 1 | bytes 1 | tf_op jit(solution)/shard_map/partial_rows/pallas_call | solution.py:348
  111.4 35.9 %reduce-scatter.2.cloned.1.call-done.total_ref = bf16[128,1536]{1,0:T(8,128)(2,1)} async-done(((bf16[512,1536]{1,0:T(8,128)(2,1)}), bf16[128,1536]{1,0:T(8,128)(2,1)}) %reduce-scatter.2.cloned.1.call-update) | async-done | bytes 393232 | tf_op jit(solution)/shard_map/reduce_scatter | solution.py:512
  147.3 0.9 slice.3
  148.3 1.5 collective-permute-start.8
  149.8 1.6 copy-done
  151.4 10.4 %expert_rows.1 = bf16[1,32,40,1536]{3,2,1,0:T(8,128)(2,1)} custom-call(s32[2]{0:T(128)} %pad_add_fusion.place, bf16[1280,1024]{1,0:T(8,128)(2,1)} %bitcast.11, bf16[1,1536,2048]{2,1,0:T(8,128)(2,1)} %w_ref.3, f32[1280,1536]{1,0:T(8,128)} %partial_rows.1.refs_1_.refs_0_), custom_call_target="tpu_custom_call" | custom-call | flops 1 | bytes 1 | tf_op jit(solution)/shard_map/expert_rows/pallas_call | solution.py:402
  161.8 0.7 copy-done.8
  162.5 1.8 %finish.1 = (bf16[1,128,512]{2,1,0:T(8,128)(2,1)}, bf16[1,128,512]{2,1,0:T(8,128)(2,1)}) custom-call(bf16[128,1536]{1,0:T(8,128)(2,1)} %reduce-scatter.2.cloned.1.call-done.total_ref, bf16[128,512]{1,0:T(8,128)(2,1)} %copy-done.8, f32[1280,1536]{1,0:T(8,128)} %partial_rows.1.refs_1_.refs_0_), custom_call_target="tpu_custom_call" | custom-call | flops 1 | bytes 1 | tf_op jit(solution)/shard_map/finish/pallas_call | solution.py:209
  (28 shorter events, 0.2 us)
Async XLA Ops:
  7.2 35.3 %all-gather.3.cloned.1.call-start = ((), (), s32[]{:S(2)}) async-start(), calls=%async_computation.3 | async-start | bytes 1474560 | tf_op jit(solution)/shard_map/all_gather | solution.py:478
  9.5 76.4 %all-gather.5.cloned.1.call-start = ((), (), s32[]{:S(2)}) async-start(), calls=%async_computation.4 | async-start | bytes 1310720 | tf_op jit(solution)/shard_map/all_gather | solution.py:478
  9.5 10.8 %collective-permute-start = (bf16[128,1024]{1,0:T(8,128)(2,1)}, bf16[128,1024]{1,0:T(8,128)(2,1)S(1)}, u32[]{:S(2)}, u32[]{:S(2)}) collective-permute-start(bf16[128,1024]{1,0:T(8,128)(2,1)} %get-tuple-element.25.refs_0_), channel_id=1, source_target_pairs={{0,2},{1,3},{2,4},{3,5},{4,6},{5,7},{8,10},{9,11},{10,12},{11,13},... | collective-permute-start | bytes 786440 | tf_op jit(solution)/shard_map/ppermute | solution.py:450
  14.5 9.0 %collective-permute-start.2 = (bf16[128,1024]{1,0:T(8,128)(2,1)}, bf16[128,1024]{1,0:T(8,128)(2,1)S(1)}, u32[]{:S(2)}, u32[]{:S(2)}) collective-permute-start(bf16[128,1024]{1,0:T(8,128)(2,1)} %get-tuple-element.25.refs_0_), channel_id=1, source_target_pairs={{0,1},{2,3},{4,5},{6,7},{8,9},{10,11},{12,13},{14,15},{16,17},{18,... | collective-permute-start | bytes 786440 | tf_op jit(solution)/shard_map/ppermute | solution.py:459
  20.3 26.3 %copy-start.3 = (bf16[128,1024]{1,0:T(8,128)(2,1)}, bf16[128,1024]{1,0:T(8,128)(2,1)S(1)}, u32[]{:S(2)}) copy-start(bf16[128,1024]{1,0:T(8,128)(2,1)S(1)} %collective-permute-done.refs_2_) | copy-start | bytes 786436
  20.3 3.1 %collective-permute-start.1 = (bf16[128,1024]{1,0:T(8,128)(2,1)S(1)}, bf16[128,1024]{1,0:T(8,128)(2,1)S(1)}, u32[]{:S(2)}, u32[]{:S(2)}) collective-permute-start(bf16[128,1024]{1,0:T(8,128)(2,1)S(1)} %collective-permute-done.refs_2_), channel_id=1, source_target_pairs={{2,4},{3,5},{4,6},{5,7},{10,12},{11,13},{12,14},{13,15},{18,20},{1... | collective-permute-start | bytes 786440 | tf_op jit(solution)/shard_map/ppermute | solution.py:450
  21.0 2.5 %collective-permute-start.3 = (bf16[128,1024]{1,0:T(8,128)(2,1)S(1)}, bf16[128,1024]{1,0:T(8,128)(2,1)S(1)}, u32[]{:S(2)}, u32[]{:S(2)}) collective-permute-start(bf16[128,1024]{1,0:T(8,128)(2,1)S(1)} %collective-permute-done.refs_2_), channel_id=1, source_target_pairs={{2,3},{3,2},{4,5},{5,4},{6,7},{7,6},{10,11},{11,10},{12,13},{13,12... | collective-permute-start | bytes 786440 | tf_op jit(solution)/shard_map/ppermute | solution.py:459
  23.5 23.2 %copy-start.4 = (bf16[128,1024]{1,0:T(8,128)(2,1)}, bf16[128,1024]{1,0:T(8,128)(2,1)S(1)}, u32[]{:S(2)}) copy-start(bf16[128,1024]{1,0:T(8,128)(2,1)S(1)} %collective-permute-done.2.refs_1_) | copy-start | bytes 786436
  23.5 23.2 %copy-start.5 = (bf16[128,1024]{1,0:T(8,128)(2,1)}, bf16[128,1024]{1,0:T(8,128)(2,1)S(1)}, u32[]{:S(2)}) copy-start(bf16[128,1024]{1,0:T(8,128)(2,1)S(1)} %collective-permute-done.1.refs_4_) | copy-start | bytes 786436
  23.5 2.1 %copy-start.6 = (bf16[128,1024]{1,0:T(8,128)(2,1)}, bf16[128,1024]{1,0:T(8,128)(2,1)S(1)}, u32[]{:S(2)}) copy-start(bf16[128,1024]{1,0:T(8,128)(2,1)S(1)} %collective-permute-done.3.refs_3_) | copy-start | bytes 786436
  23.5 2.0 %collective-permute-start.4 = (bf16[128,1024]{1,0:T(8,128)(2,1)S(1)}, bf16[128,1024]{1,0:T(8,128)(2,1)}, u32[]{:S(2)}, u32[]{:S(2)}) collective-permute-start(bf16[128,1024]{1,0:T(8,128)(2,1)S(1)} %collective-permute-done.1.refs_4_), channel_id=1, source_target_pairs={{4,6},{5,7},{12,14},{13,15},{20,22},{21,23},{28,30},{29,31}} | collective-permute-start | bytes 786440 | tf_op jit(solution)/shard_map/ppermute | solution.py:450
  24.9 0.7 collective-permute-start.5
  25.6 1.4 copy-start.7
  25.6 24.8 %collective-permute-start.6 = (bf16[128,1024]{1,0:T(8,128)(2,1)}, bf16[128,1024]{1,0:T(8,128)(2,1)}, u32[]{:S(2)}, u32[]{:S(2)}) collective-permute-start(bf16[128,1024]{1,0:T(8,128)(2,1)} %collective-permute-done.4.refs_6_), channel_id=1, source_target_pairs={{6,7},{7,6},{14,15},{15,14},{22,23},{23,22},{30,31},{31,30}} | collective-permute-start | bytes 786440 | tf_op jit(solution)/shard_map/ppermute | solution.py:459
  46.6 50.9 %all-to-all-start = ((bf16[8,160,1024]{2,1,0:T(8,128)(2,1)}), bf16[8,160,1024]{2,1,0:T(8,128)(2,1)S(1)}, u32[]{:S(2)}, u32[]{:S(2)}) async-start(bf16[8,160,1024]{2,1,0:T(8,128)(2,1)} %bitcast.12), calls=%async_computation.1 | async-start | bytes 5242880 | tf_op jit(solution)/shard_map/all_to_all | solution.py:483
  50.3 97.0 %reduce-scatter.2.cloned.1.call-start = ((), (), s32[]{:S(2)}) async-start(), calls=%async_computation.5 | async-start | bytes 1966080 | tf_op jit(solution)/shard_map/reduce_scatter | solution.py:512
  55.5 37.4 %collective-permute-start.7 = (bf16[512,512]{1,0:T(8,128)(2,1)}, bf16[512,512]{1,0:T(8,128)(2,1)S(1)}, u32[]{:S(2)}, u32[]{:S(2)}) collective-permute-start(bf16[512,512]{1,0:T(8,128)(2,1)} %get-tuple-element.37), channel_id=1, source_target_pairs={{0,1},{1,0},{2,3},{3,2},{4,5},{5,4},{6,7},{7,6},{8,9},{9,8},{10,11... | collective-permute-start | bytes 1572872 | tf_op jit(solution)/shard_map/ppermute | solution.py:493
  92.9 0.8 copy-start.2
  97.5 1.5 copy-start.1
  99.0 50.8 %all-to-all-start.1 = ((bf16[8,160,1024]{2,1,0:T(8,128)(2,1)}), bf16[8,160,1024]{2,1,0:T(8,128)(2,1)S(1)}, u32[]{:S(2)}, u32[]{:S(2)}) async-start(bf16[8,160,1024]{2,1,0:T(8,128)(2,1)} %bitcast.13), calls=%async_computation.2 | async-start | bytes 5242880 | tf_op jit(solution)/shard_map/all_to_all | solution.py:483
  148.3 13.5 %collective-permute-start.8 = (bf16[128,512]{1,0:T(8,128)(2,1)S(1)}, bf16[128,512]{1,0:T(8,128)(2,1)S(1)}, u32[]{:S(2)}, u32[]{:S(2)}) collective-permute-start(bf16[128,512]{1,0:T(8,128)(2,1)S(1)} %slice.3), channel_id=1, source_target_pairs={{0,1},{1,0},{2,3},{3,2},{4,5},{5,4},{6,7},{7,6},{8,9},{9,8},{10,11... | collective-permute-start | bytes 393224 | tf_op jit(solution)/shard_map/ppermute | solution.py:493
  149.8 1.6 copy-start
  161.8 0.7 copy-start.8
Sparse Core Ops, SparseCore 0:
  10.1 32.2 all-gather.2
  44.0 41.7 all-gather.4
  97.6 49.6 reduce-scatter.1

commit v7 on v5

--- a/solution.py
+++ b/solution.py
@@ -217,13 +217,26 @@
     )(total, *crossed, after)
 
 
-def join_kernel(
-    n_z, n_dp, key_ref, value_ref, rows_ref, ids_ref, combine_ref, kv_ref, ext_ref, rest_ref
-):
+def join_kernel(key_ref, value_ref, kv_ref):
     for g in range(kv_ref.shape[1] // (2 * HEAD_DIM)):
         lanes = slice(g * HEAD_DIM, (g + 1) * HEAD_DIM)
         kv_ref[:, 2 * g * HEAD_DIM : (2 * g + 1) * HEAD_DIM] = key_ref[0, :, lanes]
         kv_ref[:, (2 * g + 1) * HEAD_DIM : (2 * g + 2) * HEAD_DIM] = value_ref[0, :, lanes]
+
+
+def join(keys, values):
+    rows, width = keys.shape[1:]
+    return pl.pallas_call(
+        join_kernel,
+        out_shape=jax.ShapeDtypeStruct((rows, 2 * width), jnp.bfloat16),
+        compiler_params=pltpu.CompilerParams(vmem_limit_bytes=vmem_limit),
+        cost_estimate=small_cost,
+        name="join",
+    )(keys, values)
+
+
+def table_kernel(n_z, n_dp, rows_ref, ids_ref, combine_ref, *refs):
+    ext_ref, rest_ref = refs[-2:]
     tokens, feat = rows_ref.shape
     lines = 4 * n_dp
     line = lax.broadcasted_iota(jnp.int32, (n_z * lines, tokens), 0)
@@ -254,13 +267,12 @@
         ext_ref[here, :] = line_of.astype(jnp.bfloat16)
 
 
-def join(keys, values, full_rows, ids, combine, n_z, n_dp):
-    rows, width = keys.shape[1:]
+def halves(full_rows, ids, combine, n_z, n_dp, after):
     tokens, feat = full_rows.shape
     return pl.pallas_call(
-        functools.partial(join_kernel, n_z, n_dp),
+        functools.partial(table_kernel, n_z, n_dp),
+        in_specs=[pl.BlockSpec(memory_space=pltpu.VMEM)] * 3 + [pl.BlockSpec(memory_space=pl.ANY)],
         out_shape=[
-            jax.ShapeDtypeStruct((rows, 2 * width), jnp.bfloat16),
             jax.ShapeDtypeStruct(
                 (tokens + 4 * n_dp * -(-2 * n_z * tokens // feat), feat // 2), jnp.bfloat16
             ),
@@ -268,8 +280,8 @@
         ],
         compiler_params=pltpu.CompilerParams(vmem_limit_bytes=vmem_limit),
         cost_estimate=small_cost,
-        name="join",
-    )(keys, values, full_rows, ids.T, combine.T)
+        name="slot_table",
+    )(full_rows, ids.T, combine.T, after)
 
 
 def pick_kernel(count, n_dp, capacity, place, *refs):
@@ -338,7 +350,7 @@
 def partial_kernel(rows_ref, w_ref, out_ref):
     out_ref[...] = lax.dot_general(
         rows_ref[...], w_ref[0], (((1,), (1,)), ((), ())), preferred_element_type=jnp.float32
-    )
+    ).astype(jnp.bfloat16)
 
 
 def partial_rows(rows, w_down):
@@ -353,7 +365,7 @@
             pl.BlockSpec((1, step, half), lambda n: (0, n, 0)),
         ],
         out_specs=pl.BlockSpec((count, step), lambda n: (0, n)),
-        out_shape=jax.ShapeDtypeStruct((count, hid), jnp.float32),
+        out_shape=jax.ShapeDtypeStruct((count, hid), jnp.bfloat16),
         compiler_params=pltpu.CompilerParams(vmem_limit_bytes=vmem_limit),
         cost_estimate=small_cost,
         name="partial_rows",
@@ -369,7 +381,7 @@
         rows_ref[...], w_ref[0], (((1,), (1,)), ((), ())), preferred_element_type=jnp.float32
     )
     if with_base:
-        result = result + refs[0][...]
+        result = result + refs[0][...].astype(jnp.float32)
     for i in range(len(blocks)):
         out_s[step, i] = result[i * capacity : i * capacity + slots].astype(jnp.bfloat16)
 
@@ -394,7 +406,7 @@
 
 def expert_rows(place, rows, ks, w_down, n_z, n_dp, capacity, slots, base, hidden_grad, after=()):
     hid = w_down.shape[1]
-    step = math.gcd(hid, 512)
+    step = math.gcd(hid, 512 if base is None else 256)
     count = rows.shape[0] // capacity
     part = w_down.shape[2] // rows.shape[1] - 1
     extra = [] if base is None else [base]
@@ -443,7 +455,8 @@
     full_rows = mixed_grad
     if lax.axis_size("tp") > 1:
         full_rows = lax.all_gather(mixed_grad, "tp", axis=1, tiled=True)
-    own, *own_halves = join(keys, values, full_rows, expert_ids, combine, n_z, n_dp)
+    own = join(keys, values)
+    own_halves = list(halves(full_rows, expert_ids, combine, n_z, n_dp, own))
 
     def along_z(array, targets):
         pairs = [(2 * i + x, 2 * j + x) for i, j in targets for x in range(2)]
@@ -462,6 +475,7 @@
     for k in range(1, n_z):
         others.append(across_x(k - 1))
         if k == 2:
+            columns[-1], own_halves[0] = lax.optimization_barrier((columns[-1], own_halves[0]))
             own_picked = pick(own_halves[0], full_rows, (0,), (columns[1],))
         if k > 2:
             held = lax.optimization_barrier((columns[-1], *others[k - 3 : k - 1]))

time: 161 us -> 161 us (level)
  Pallas kernels: 51.4 us -> 53.2 us
    ppermute x3, waiting for transfers between devices: 2.43 us -> 0.48 us  [along_z(): return lax.ppermute(array, 'ctx', pairs)]
    pallas_call x1 -> x2, Pallas kernels: 2.21 us -> 3.69 us  [the longest x1 1.96 us: halves(): pl.pallas_call(functools.partial(table_kernel, n_z, n_dp), in_specs=[pl.B...]
  transfers between devices with their start and end apart: 15 -> 15, of which waited for: 5 -> 5; matrix products, arithmetic and copies ran while one was open for 1% -> 1% of each run, Pallas kernels for 30% -> 31%
where the time goes in v7:
time: 161 us; the launch traced here: 160 us
  waiting for transfers between devices  60.6 us (38%)
  Pallas kernels  53.2 us (33%)
  starting transfers between devices  27.2 us (17%)
  between operations  14 us (9%)
  local copies, waits for them, and re-layouts  4.82 us (3%)
    all_gather x2, waiting for transfers between devices, per_device(): lax.all_gather(half, 'ctx', axis=0, tiled=True, axis_index_groups=line_gr...  45.8 us
    pallas_call x2, Pallas kernels, expert_rows(): pl.pallas_call(functools.partial(expert_kernel, ks, bool(extra), n_z, n_d...  16.2 us
    reduce_scatter x1, waiting for transfers between devices, per_device(): lax.psum_scatter(fold(mine, crossed, others), 'ctx', scatter_dimension=0,...  13.3 us
    all_to_all x3, starting transfers between devices, exchange(): lax.all_to_all(picked, ('dp', 'ctx'), split_axis=0, concat_axis=0, tiled=...  11.7 us
    pallas_call x3, Pallas kernels, pick_rows(): pl.pallas_call(functools.partial(pick_kernel, len(ks), n_dp, capacity), g...  10.7 us
    pallas_call x2, Pallas kernels, attention(): pl.pallas_call(functools.partial(attention_kernel, n_blocks, heads_step,...  10.2 us
    pallas_call x1, Pallas kernels, partial_rows(): pl.pallas_call(partial_kernel, grid=(hid // step,), in_specs=[pl.BlockSpe...  6.98 us
    ppermute x3, starting transfers between devices, along_z(): return lax.ppermute(array, 'ctx', pairs)  6.27 us
  transfers between devices with their start and end apart: 15, of which 5 were waited for; matrix products, arithmetic and copies ran while one was open for 1% of the time, Pallas kernels for 31%

profile of v7, /device:TPU:0, one launch (start us, length us, event | category | flops | bytes accessed | tf_op | source)
XLA Modules:
  0.0 160.5 jit_solution(16347425818972747449)
XLA Ops:
  7.2 1.7 %join.1.refs_0_ = bf16[128,1024]{1,0:T(8,128)(2,1)} custom-call(bf16[1,128,512]{2,1,0:T(8,128)(2,1)} %key_ref.1, bf16[1,128,512]{2,1,0:T(8,128)(2,1)} %value_ref.1), custom_call_target="tpu_custom_call" | custom-call | flops 1 | bytes 1 | tf_op jit(solution)/shard_map/join/pallas_call | solution.py:229
  8.9 4.9 %collective-permute-start = (bf16[128,1024]{1,0:T(8,128)(2,1)}, bf16[128,1024]{1,0:T(8,128)(2,1)S(1)}, u32[]{:S(2)}, u32[]{:S(2)}) collective-permute-start(bf16[128,1024]{1,0:T(8,128)(2,1)} %join.1.refs_0_), channel_id=1, source_target_pairs={{0,2},{1,3},{2,4},{3,5},{4,6},{5,7},{8,10},{9,11},{10,12},{11,13},... | collective-permute-start | bytes 786440 | tf_op jit(solution)/shard_map/ppermute | solution.py:463
  13.9 3.4 %collective-permute-start.2 = (bf16[128,1024]{1,0:T(8,128)(2,1)}, bf16[128,1024]{1,0:T(8,128)(2,1)S(1)}, u32[]{:S(2)}, u32[]{:S(2)}) collective-permute-start(bf16[128,1024]{1,0:T(8,128)(2,1)} %join.1.refs_0_), channel_id=1, source_target_pairs={{0,1},{2,3},{4,5},{6,7},{8,9},{10,11},{12,13},{14,15},{16,17},{18,... | collective-permute-start | bytes 786440 | tf_op jit(solution)/shard_map/ppermute | solution.py:472
  17.3 2.0 %slot_table.1 = (bf16[144,1024]{1,0:T(8,128)(2,1)}, bf16[128,1024]{1,0:T(8,128)(2,1)}) custom-call(bf16[128,2048]{1,0:T(8,128)(2,1)} %refs_1_.1, s32[8,128]{1,0:T(8,128)} %bitcast.23, bf16[8,128]{1,0:T(8,128)(2,1)} %bitcast.24, bf16[128,1024]{1,0:T(8,128)(2,1)} %join.1.refs_0_), custom_call_target="tpu_custom_call" | custom-call | flops 1 | bytes 1 | tf_op jit(solution)/shard_map/slot_table/pallas_call | solution.py:272
  19.7 0.7 collective-permute-start.1
  20.4 0.7 collective-permute-start.3
  21.7 3.2 %pick_rows.3.refs_8_ = bf16[320,2048]{1,0:T(8,128)(2,1)} custom-call(s32[2]{0:T(128)} %pad_add_fusion.place, bf16[144,1024]{1,0:T(8,128)(2,1)} %get-tuple-element.42.refs_0_, bf16[128,2048]{1,0:T(8,128)(2,1)} %refs_1_.1, bf16[128,1024]{1,0:T(8,128)(2,1)} %copy-done.2), custom_call_target="tpu_custom_call" | custom-call | flops 1 | bytes 1 | tf_op jit(solution)/shard_map/pick_rows/pallas_call | solution.py:332
  24.9 0.7 collective-permute-start.4
  25.6 0.7 collective-permute-start.5
  26.4 0.7 collective-permute-start.6
  27.1 3.7 %all-to-all-start.1 = ((bf16[8,40,2048]{2,1,0:T(8,128)(2,1)}), bf16[8,40,2048]{2,1,0:T(8,128)(2,1)S(1)}, u32[]{:S(2)}, u32[]{:S(2)}) async-start(bf16[8,40,2048]{2,1,0:T(8,128)(2,1)} %bitcast.16), calls=%async_computation.2 | async-start | bytes 2621440 | tf_op jit(solution)/shard_map/all_to_all | solution.py:502
  30.9 0.7 copy-done.9
  31.6 5.1 %attention_backward.2 = (bf16[128,4096]{1,0:T(8,128)(2,1)}, bf16[512,512]{1,0:T(8,128)(2,1)}, bf16[512,512]{1,0:T(8,128)(2,1)}) custom-call(s32[2]{0:T(128)} %pad_add_fusion.place, bf16[128,4096]{1,0:T(8,128)(2,1)} %bitcast.19, bf16[128,4096]{1,0:T(8,128)(2,1)} %bitcast.21, bf16[128,1024]{1,0:T(8,128)(2,1)} %join.1.refs_0_, bf16[128,1024]{1,0:T(8,128)(2,1)} %copy-done.4, ...), custom_call_target="tpu_custom_call" | custom-call | flops 26843545600 | bytes 4194304 | tf_op jit(solution)/shard_map/attention_backward/pallas_call | solution.py:133
  36.7 2.1 %collective-permute-start.7 = (bf16[512,512]{1,0:T(8,128)(2,1)}, bf16[512,512]{1,0:T(8,128)(2,1)S(1)}, u32[]{:S(2)}, u32[]{:S(2)}) collective-permute-start(bf16[512,512]{1,0:T(8,128)(2,1)} %get-tuple-element.43), channel_id=1, source_target_pairs={{0,1},{1,0},{2,3},{3,2},{4,5},{5,4},{6,7},{7,6},{8,9},{9,8},{10,11... | collective-permute-start | bytes 1572872 | tf_op jit(solution)/shard_map/ppermute | solution.py:512
  38.8 5.1 %attention_backward.3 = (bf16[128,4096]{1,0:T(8,128)(2,1)}, bf16[512,512]{1,0:T(8,128)(2,1)}, bf16[512,512]{1,0:T(8,128)(2,1)}) custom-call(s32[2]{0:T(128)} %pad_add_fusion.place, bf16[128,4096]{1,0:T(8,128)(2,1)} %bitcast.20, bf16[128,4096]{1,0:T(8,128)(2,1)} %bitcast.22, bf16[128,1024]{1,0:T(8,128)(2,1)} %join.1.refs_0_, ...), custom_call_target="tpu_custom_call", output_to_operand_aliasing={{0}: (11, {})} | custom-call | flops 1 | bytes 1 | tf_op jit(solution)/shard_map/attention_backward/pallas_call | solution.py:133
  43.9 29.6 %all-gather.3.cloned.1.call-done.refs_0_.refs_1_.refs_2_.refs_3_.refs_4_.refs_5_ = bf16[576,1024]{1,0:T(8,128)(2,1)} async-done(((bf16[144,1024]{1,0:T(8,128)(2,1)}), bf16[576,1024]{1,0:T(8,128)(2,1)}) %all-gather.3.cloned.1.call-update) | async-done | bytes 1179664 | tf_op jit(solution)/shard_map/all_gather | solution.py:497
  73.5 3.7 %pick_rows.4.refs_6_ = bf16[960,1024]{1,0:T(8,128)(2,1)} custom-call(s32[2]{0:T(128)} %pad_add_fusion.place, bf16[576,1024]{1,0:T(8,128)(2,1)} %all-gather.3.cloned.1.call-done.refs_0_.refs_1_.refs_2_.refs_3_.refs_4_.refs_5_, bf16[576,1024]{1,0:T(8,128)(2,1)} %all-gather.3.cloned.1.call-done.refs_0_.refs_1_.refs_2_.refs_3_.refs_4_.refs_5_, ...), custom_call_target="tpu_custom_call" | custom-call | flops 1 | bytes 1 | tf_op jit(solution)/shard_map/pick_rows/pallas_call | solution.py:332
  77.2 0.8 copy-done.3
  78.5 3.7 %all-to-all-start = ((bf16[8,120,1024]{2,1,0:T(8,128)(2,1)}), bf16[8,120,1024]{2,1,0:T(8,128)(2,1)S(1)}, u32[]{:S(2)}, u32[]{:S(2)}) async-start(bf16[8,120,1024]{2,1,0:T(8,128)(2,1)} %bitcast.13), calls=%async_computation.1 | async-start | bytes 3932160 | tf_op jit(solution)/shard_map/all_to_all | solution.py:502
  82.2 3.8 %fold.1 = bf16[512,1536]{1,0:T(8,128)(2,1)} custom-call(bf16[512,512]{1,0:T(8,128)(2,1)} %get-tuple-element.41.mine_ref, bf16[512,512]{1,0:T(8,128)(2,1)} %copy-done.3, bf16[512,512]{1,0:T(8,128)(2,1)} %get-tuple-element.45.refs_1_, bf16[512,512]{1,0:T(8,128)(2,1)} %get-tuple-element.46.refs_2_), custom_call_target="tpu_custom_call" | custom-call | flops 1 | bytes 1 | tf_op jit(solution)/shard_map/fold/pallas_call | solution.py:181
  86.0 16.2 %all-gather.5.cloned.1.call-done.refs_3_.refs_4_.refs_5_ = bf16[512,1024]{1,0:T(8,128)(2,1)} async-done(((bf16[128,1024]{1,0:T(8,128)(2,1)}), bf16[512,1024]{1,0:T(8,128)(2,1)}) %all-gather.5.cloned.1.call-update) | async-done | bytes 1048592 | tf_op jit(solution)/shard_map/all_gather | solution.py:497
  102.2 3.8 %pick_rows.5.refs_0_ = bf16[960,1024]{1,0:T(8,128)(2,1)} custom-call(s32[2]{0:T(128)} %pad_add_fusion.place, bf16[576,1024]{1,0:T(8,128)(2,1)} %all-gather.3.cloned.1.call-done.refs_0_.refs_1_.refs_2_.refs_3_.refs_4_.refs_5_, bf16[576,1024]{1,0:T(8,128)(2,1)} %all-gather.3.cloned.1.call-done.refs_0_.refs_1_.refs_2_.refs_3_.refs_4_.refs_5_, ...), custom_call_target="tpu_custom_call" | custom-call | flops 1 | bytes 1 | tf_op jit(solution)/shard_map/pick_rows/pallas_call | solution.py:332
  105.9 0.9 all-to-all-done
  106.9 1.3 copy-done
  108.2 4.4 %all-to-all-start.2 = ((bf16[8,120,1024]{2,1,0:T(8,128)(2,1)}), bf16[8,120,1024]{2,1,0:T(8,128)(2,1)}, u32[]{:S(2)}, u32[]{:S(2)}) async-start(bf16[8,120,1024]{2,1,0:T(8,128)(2,1)} %bitcast.14), calls=%async_computation.3 | async-start | bytes 3932160 | tf_op jit(solution)/shard_map/all_to_all | solution.py:502
  112.6 6.4 %expert_rows.2.refs_1_ = bf16[1,32,40,1536]{3,2,1,0:T(8,128)(2,1)} custom-call(s32[2]{0:T(128)} %pad_add_fusion.place, bf16[320,2048]{1,0:T(8,128)(2,1)} %bitcast.17, bf16[1,1536,2048]{2,1,0:T(8,128)(2,1)} %w_ref.5, bf16[960,1024]{1,0:T(8,128)(2,1)} %pick_rows.5.refs_0_), custom_call_target="tpu_custom_call" | custom-call | flops 1 | bytes 1 | tf_op jit(solution)/shard_map/expert_rows/pallas_call | solution.py:414
  119.0 7.0 %partial_rows.1.refs_1_.refs_0_ = bf16[960,1536]{1,0:T(8,128)(2,1)} custom-call(bf16[960,1024]{1,0:T(8,128)(2,1)} %bitcast.15, bf16[1,1536,2048]{2,1,0:T(8,128)(2,1)} %w_ref.5), custom_call_target="tpu_custom_call" | custom-call | flops 1 | bytes 1 | tf_op jit(solution)/shard_map/partial_rows/pallas_call | solution.py:360
  126.0 13.3 %reduce-scatter.2.cloned.1.call-done.total_ref = bf16[128,1536]{1,0:T(8,128)(2,1)} async-done(((bf16[512,1536]{1,0:T(8,128)(2,1)}), bf16[128,1536]{1,0:T(8,128)(2,1)}) %reduce-scatter.2.cloned.1.call-update) | async-done | bytes 393232 | tf_op jit(solution)/shard_map/reduce_scatter | solution.py:532
  139.3 0.9 slice.3
  140.2 1.5 collective-permute-start.8
  141.7 9.7 %expert_rows.3 = bf16[1,32,40,1536]{3,2,1,0:T(8,128)(2,1)} custom-call(s32[2]{0:T(128)} %pad_add_fusion.place, bf16[960,1024]{1,0:T(8,128)(2,1)} %bitcast.12.rows_ref, bf16[1,1536,2048]{2,1,0:T(8,128)(2,1)} %w_ref.5, bf16[960,1536]{1,0:T(8,128)(2,1)} %partial_rows.1.refs_1_.refs_0_, ...), custom_call_target="tpu_custom_call", output_to_operand_aliasing={{}: (4, {})} | custom-call | flops 1 | bytes 1 | tf_op jit(solution)/shard_map/expert_rows/pallas_call | solution.py:414
  152.2 1.8 %finish.1 = (bf16[1,128,512]{2,1,0:T(8,128)(2,1)}, bf16[1,128,512]{2,1,0:T(8,128)(2,1)}) custom-call(bf16[128,1536]{1,0:T(8,128)(2,1)} %reduce-scatter.2.cloned.1.call-done.total_ref, bf16[128,512]{1,0:T(8,128)(2,1)} %copy-done.10, bf16[960,1536]{1,0:T(8,128)(2,1)} %partial_rows.1.refs_1_.refs_0_), custom_call_target="tpu_custom_call" | custom-call | flops 1 | bytes 1 | tf_op jit(solution)/shard_map/finish/pallas_call | solution.py:209
  (37 shorter events, 2.4 us)
Async XLA Ops:
  7.2 66.3 %all-gather.3.cloned.1.call-start = ((), (), s32[]{:S(2)}) async-start(), calls=%async_computation.4 | async-start | bytes 1474560 | tf_op jit(solution)/shard_map/all_gather | solution.py:497
  8.9 10.8 %collective-permute-start = (bf16[128,1024]{1,0:T(8,128)(2,1)}, bf16[128,1024]{1,0:T(8,128)(2,1)S(1)}, u32[]{:S(2)}, u32[]{:S(2)}) collective-permute-start(bf16[128,1024]{1,0:T(8,128)(2,1)} %join.1.refs_0_), channel_id=1, source_target_pairs={{0,2},{1,3},{2,4},{3,5},{4,6},{5,7},{8,10},{9,11},{10,12},{11,13},... | collective-permute-start | bytes 786440 | tf_op jit(solution)/shard_map/ppermute | solution.py:463
  13.9 11.0 %collective-permute-start.2 = (bf16[128,1024]{1,0:T(8,128)(2,1)}, bf16[128,1024]{1,0:T(8,128)(2,1)S(1)}, u32[]{:S(2)}, u32[]{:S(2)}) collective-permute-start(bf16[128,1024]{1,0:T(8,128)(2,1)} %join.1.refs_0_), channel_id=1, source_target_pairs={{0,1},{2,3},{4,5},{6,7},{8,9},{10,11},{12,13},{14,15},{16,17},{18,... | collective-permute-start | bytes 786440 | tf_op jit(solution)/shard_map/ppermute | solution.py:472
  19.7 2.0 %copy-start.2 = (bf16[128,1024]{1,0:T(8,128)(2,1)}, bf16[128,1024]{1,0:T(8,128)(2,1)S(1)}, u32[]{:S(2)}) copy-start(bf16[128,1024]{1,0:T(8,128)(2,1)S(1)} %collective-permute-done.refs_2_) | copy-start | bytes 786436
  19.7 5.2 %collective-permute-start.1 = (bf16[128,1024]{1,0:T(8,128)(2,1)S(1)}, bf16[128,1024]{1,0:T(8,128)(2,1)S(1)}, u32[]{:S(2)}, u32[]{:S(2)}) collective-permute-start(bf16[128,1024]{1,0:T(8,128)(2,1)S(1)} %collective-permute-done.refs_2_), channel_id=1, source_target_pairs={{2,4},{3,5},{4,6},{5,7},{10,12},{11,13},{12,14},{13,15},{18,20},{1... | collective-permute-start | bytes 786440 | tf_op jit(solution)/shard_map/ppermute | solution.py:463
  20.4 4.5 %collective-permute-start.3 = (bf16[128,1024]{1,0:T(8,128)(2,1)S(1)}, bf16[128,1024]{1,0:T(8,128)(2,1)S(1)}, u32[]{:S(2)}, u32[]{:S(2)}) collective-permute-start(bf16[128,1024]{1,0:T(8,128)(2,1)S(1)} %collective-permute-done.refs_2_), channel_id=1, source_target_pairs={{2,3},{3,2},{4,5},{5,4},{6,7},{7,6},{10,11},{11,10},{12,13},{13,12... | collective-permute-start | bytes 786440 | tf_op jit(solution)/shard_map/ppermute | solution.py:472
  24.9 6.0 %copy-start.4 = (bf16[128,1024]{1,0:T(8,128)(2,1)}, bf16[128,1024]{1,0:T(8,128)(2,1)S(1)}, u32[]{:S(2)}) copy-start(bf16[128,1024]{1,0:T(8,128)(2,1)S(1)} %collective-permute-done.2.refs_1_) | copy-start | bytes 786436
  24.9 6.0 %copy-start.5 = (bf16[128,1024]{1,0:T(8,128)(2,1)}, bf16[128,1024]{1,0:T(8,128)(2,1)S(1)}, u32[]{:S(2)}) copy-start(bf16[128,1024]{1,0:T(8,128)(2,1)S(1)} %collective-permute-done.1.refs_4_) | copy-start | bytes 786436
  24.9 6.0 %copy-start.6 = (bf16[128,1024]{1,0:T(8,128)(2,1)}, bf16[128,1024]{1,0:T(8,128)(2,1)S(1)}, u32[]{:S(2)}) copy-start(bf16[128,1024]{1,0:T(8,128)(2,1)S(1)} %collective-permute-done.3.refs_3_) | copy-start | bytes 786436
  24.9 1.4 collective-permute-start.4
  25.6 0.7 collective-permute-start.5
  26.3 4.6 %copy-start.7 = (bf16[128,1024]{1,0:T(8,128)(2,1)}, bf16[128,1024]{1,0:T(8,128)(2,1)S(1)}, u32[]{:S(2)}) copy-start(bf16[128,1024]{1,0:T(8,128)(2,1)S(1)} %collective-permute-done.4.refs_6_) | copy-start | bytes 786436
  26.3 4.6 %copy-start.8 = (bf16[128,1024]{1,0:T(8,128)(2,1)}, bf16[128,1024]{1,0:T(8,128)(2,1)S(1)}, u32[]{:S(2)}) copy-start(bf16[128,1024]{1,0:T(8,128)(2,1)S(1)} %collective-permute-done.5.refs_5_) | copy-start | bytes 786436
  26.4 75.8 %all-gather.5.cloned.1.call-start = ((), (), s32[]{:S(2)}) async-start(), calls=%async_computation.6 | async-start | bytes 1310720 | tf_op jit(solution)/shard_map/all_gather | solution.py:497
  26.4 4.4 %collective-permute-start.6 = (bf16[128,1024]{1,0:T(8,128)(2,1)S(1)}, bf16[128,1024]{1,0:T(8,128)(2,1)S(1)}, u32[]{:S(2)}, u32[]{:S(2)}) collective-permute-start(bf16[128,1024]{1,0:T(8,128)(2,1)S(1)} %collective-permute-done.4.refs_6_), channel_id=1, source_target_pairs={{6,7},{7,6},{14,15},{15,14},{22,23},{23,22},{30,31},{31,30}} | collective-permute-start | bytes 786440 | tf_op jit(solution)/shard_map/ppermute | solution.py:472
  27.1 50.1 %all-to-all-start.1 = ((bf16[8,40,2048]{2,1,0:T(8,128)(2,1)}), bf16[8,40,2048]{2,1,0:T(8,128)(2,1)S(1)}, u32[]{:S(2)}, u32[]{:S(2)}) async-start(bf16[8,40,2048]{2,1,0:T(8,128)(2,1)} %bitcast.16), calls=%async_computation.2 | async-start | bytes 2621440 | tf_op jit(solution)/shard_map/all_to_all | solution.py:502
  30.9 0.7 copy-start.9
  36.7 40.5 %collective-permute-start.7 = (bf16[512,512]{1,0:T(8,128)(2,1)}, bf16[512,512]{1,0:T(8,128)(2,1)S(1)}, u32[]{:S(2)}, u32[]{:S(2)}) collective-permute-start(bf16[512,512]{1,0:T(8,128)(2,1)} %get-tuple-element.43), channel_id=1, source_target_pairs={{0,1},{1,0},{2,3},{3,2},{4,5},{5,4},{6,7},{7,6},{8,9},{9,8},{10,11... | collective-permute-start | bytes 1572872 | tf_op jit(solution)/shard_map/ppermute | solution.py:512
  77.2 0.8 copy-start.3
  77.2 1.2 copy-start.1
  78.5 28.4 %all-to-all-start = ((bf16[8,120,1024]{2,1,0:T(8,128)(2,1)}), bf16[8,120,1024]{2,1,0:T(8,128)(2,1)S(1)}, u32[]{:S(2)}, u32[]{:S(2)}) async-start(bf16[8,120,1024]{2,1,0:T(8,128)(2,1)} %bitcast.13), calls=%async_computation.1 | async-start | bytes 3932160 | tf_op jit(solution)/shard_map/all_to_all | solution.py:502
  82.1 57.2 %reduce-scatter.2.cloned.1.call-start = ((), (), s32[]{:S(2)}) async-start(), calls=%async_computation.5 | async-start | bytes 1966080 | tf_op jit(solution)/shard_map/reduce_scatter | solution.py:532
  106.9 1.3 copy-start
  108.2 33.5 %all-to-all-start.2 = ((bf16[8,120,1024]{2,1,0:T(8,128)(2,1)}), bf16[8,120,1024]{2,1,0:T(8,128)(2,1)}, u32[]{:S(2)}, u32[]{:S(2)}) async-start(bf16[8,120,1024]{2,1,0:T(8,128)(2,1)} %bitcast.14), calls=%async_computation.3 | async-start | bytes 3932160 | tf_op jit(solution)/shard_map/all_to_all | solution.py:502
  140.2 11.3 %collective-permute-start.8 = (bf16[128,512]{1,0:T(8,128)(2,1)S(1)}, bf16[128,512]{1,0:T(8,128)(2,1)S(1)}, u32[]{:S(2)}, u32[]{:S(2)}) collective-permute-start(bf16[128,512]{1,0:T(8,128)(2,1)S(1)} %slice.3), channel_id=1, source_target_pairs={{0,1},{1,0},{2,3},{3,2},{4,5},{5,4},{6,7},{7,6},{8,9},{9,8},{10,11... | collective-permute-start | bytes 393224 | tf_op jit(solution)/shard_map/ppermute | solution.py:512
  151.5 0.7 copy-start.10
Sparse Core Ops, SparseCore 0:
  26.5 46.9 all-gather.2
  75.1 27.0 all-gather.4
  104.5 34.7 reduce-scatter.1

commit v8 on v7

--- a/solution.py
+++ b/solution.py
@@ -34,7 +34,7 @@
     to_exp2 = scale * math.log2(math.e)
     for i, ref in enumerate(kv_refs):
         kv_s[i * rows : (i + 1) * rows, :] = ref[...]
-        kt_s[i // 2, :, (i % 2) * rows : (i % 2 + 1) * rows] = ref[:, :HEAD_DIM].T
+        kt_s[i // 4, :, (i % 4) * rows : (i % 4 + 1) * rows] = ref[:, :HEAD_DIM].T
     for h in range(heads_step):
         lanes = slice(h * HEAD_DIM, (h + 1) * HEAD_DIM)
         here = slice(h * rows, (h + 1) * rows)
@@ -44,7 +44,7 @@
         dot_s[:, here] = do_ref[:, lanes].T
 
     def part_of(k):
-        return pl.ds(pl.multiple_of(k * pair, pair), pair)
+        return pl.ds(pl.multiple_of(k * 2 * pair, 2 * pair), 2 * pair)
 
     cut = math.gcd(width, 256)
     slices = [slice(i, i + cut) for i in range(0, width, cut)]
@@ -57,13 +57,18 @@
                 key = lax.broadcasted_iota(jnp.int32, (pair, cut), 0)
                 query = lax.broadcasted_iota(jnp.int32, (pair, cut), 1) & (rows - 1)
                 bound = jnp.where(key < rows, query, jnp.where(x == 1, pair, -1))
-                s = jnp.where(key <= bound, s, masked_score)
+                head = jnp.where(key <= bound, s[:pair], masked_score)
+            else:
+                head = s[:pair]
+            tail = jnp.where(2 * k + 1 <= z, s[pair:], masked_score)
+            s = jnp.concatenate([head, tail], axis=0)
             s_s[part_of(k), here] = s
             results.append(jnp.maximum(top, jnp.max(s, axis=0, keepdims=True)))
         return tuple(results)
 
     tops = scores(0, tuple(jnp.full((1, cut), masked_score, jnp.float32) for _ in slices), True)
-    tops = lax.fori_loop(1, z + 1, functools.partial(scores, first=False), tops)
+    chunks = lax.div(z, 2) + 1
+    tops = lax.fori_loop(1, chunks, functools.partial(scores, first=False), tops)
 
     def sums(k, carry):
         results = []
@@ -81,14 +86,14 @@
         return tuple(results)
 
     zero = jnp.zeros((1, cut), jnp.float32)
-    stats = lax.fori_loop(0, z + 1, sums, tuple((zero, zero) for _ in slices))
+    stats = lax.fori_loop(0, chunks, sums, tuple((zero, zero) for _ in slices))
     shares = [1.0 / total for total, _ in stats]
     deltas = [accum * share for (_, accum), share in zip(stats, shares)]
     dqt_s[...] = jnp.zeros_like(dqt_s)
 
     def grads(k, carry):
-        dk = jnp.zeros((pair, HEAD_DIM), jnp.float32)
-        dv = jnp.zeros((pair, HEAD_DIM), jnp.float32)
+        dk = jnp.zeros((2 * pair, HEAD_DIM), jnp.float32)
+        dv = jnp.zeros((2 * pair, HEAD_DIM), jnp.float32)
         for here, share, delta in zip(slices, shares, deltas):
             p = s_s[part_of(k), here] * share
             ds = (p * (dp_s[part_of(k), here] - delta)).astype(jnp.bfloat16)
@@ -103,7 +108,7 @@
         dkv_s[part_of(k), HEAD_DIM:] = dv
         return carry
 
-    lax.fori_loop(0, z + 1, grads, 0)
+    lax.fori_loop(0, chunks, grads, 0)
     for h in range(heads_step):
         part_t = dqt_s[:, h * rows : (h + 1) * rows] * scale
         dq_ref[:, h * HEAD_DIM : (h + 1) * HEAD_DIM] = part_t.T.astype(jnp.bfloat16)
@@ -140,7 +145,7 @@
         out_shape=[jax.ShapeDtypeStruct((rows, q_width), jnp.bfloat16), part_shape, part_shape],
         scratch_shapes=[
             pltpu.VMEM((keys, 2 * HEAD_DIM), jnp.bfloat16),
-            pltpu.VMEM((n_blocks // 2, HEAD_DIM, 2 * rows), jnp.bfloat16),
+            pltpu.VMEM((n_blocks // 4, HEAD_DIM, 4 * rows), jnp.bfloat16),
             pltpu.VMEM((width, HEAD_DIM), jnp.bfloat16),
             pltpu.VMEM((width, HEAD_DIM), jnp.bfloat16),
             pltpu.VMEM((HEAD_DIM, width), jnp.bfloat16),
@@ -406,7 +411,7 @@
 
 def expert_rows(place, rows, ks, w_down, n_z, n_dp, capacity, slots, base, hidden_grad, after=()):
     hid = w_down.shape[1]
-    step = math.gcd(hid, 512 if base is None else 256)
+    step = math.gcd(hid, 512)
     count = rows.shape[0] // capacity
     part = w_down.shape[2] // rows.shape[1] - 1
     extra = [] if base is None else [base]
@@ -484,6 +489,7 @@
             columns[-1], own_picked = lax.optimization_barrier((columns[-1], own_picked))
         columns.append(along_z(columns[-1], [(i, i + 1) for i in range(k - 1, n_z - 1)]))
     columns[-1], others[-1] = lax.optimization_barrier((columns[-1], others[-1]))
+    first_half, columns[-1] = lax.optimization_barrier((own_halves[0], columns[-1]))
     others.append(across_x(n_z - 1))
     blocks = [block for pair in zip(columns, others) for block in pair]
 
@@ -491,7 +497,6 @@
         [d * n_ctx + 2 * i + j for d in range(n_dp) for j in range(2)] for i in range(n_z)
     ]
     line_groups = [[2 * i + x for i in range(n_z)] for x in range(2)]
-    first_half, columns[n_z - 1] = lax.optimization_barrier((own_halves[0], columns[n_z - 1]))
     last_half, columns[n_z - 1] = lax.optimization_barrier((own_halves[1], columns[n_z - 1]))
     all_halves = [
         lax.all_gather(half, "ctx", axis=0, tiled=True, axis_index_groups=line_groups)

time: 161 us -> 160 us (level)
  waiting for transfers between devices: 60.6 us -> 57.8 us
    all_gather x2, waiting for transfers between devices: 45.8 us -> 42.3 us  [per_device(): lax.all_gather(half, 'ctx', axis=0, tiled=True, axis_index_groups=line_gr...]
    pallas_call x2, Pallas kernels: 10.2 us -> 13.1 us  [attention(): pl.pallas_call(functools.partial(attention_kernel, n_blocks, heads_step,...]
    pallas_call x2, Pallas kernels: 16.2 us -> 14.5 us  [expert_rows(): pl.pallas_call(functools.partial(expert_kernel, ks, bool(extra), n_z, n_d...]
  transfers between devices with their start and end apart: 15 -> 15, of which waited for: 5 -> 5; matrix products, arithmetic and copies ran while one was open for 1% -> 1% of each run, Pallas kernels for 31% -> 32%
where the time goes in v8:
time: 160 us; the launch traced here: 159 us
  waiting for transfers between devices  57.8 us (36%)
  Pallas kernels  54.4 us (34%)
  starting transfers between devices  27.2 us (17%)
  between operations  14 us (9%)
  local copies, waits for them, and re-layouts  4.82 us (3%)
    all_gather x2, waiting for transfers between devices, per_device(): lax.all_gather(half, 'ctx', axis=0, tiled=True, axis_index_groups=line_gr...  42.3 us
    pallas_call x2, Pallas kernels, expert_rows(): pl.pallas_call(functools.partial(expert_kernel, ks, bool(extra), n_z, n_d...  14.5 us
    reduce_scatter x1, waiting for transfers between devices, per_device(): lax.psum_scatter(fold(mine, crossed, others), 'ctx', scatter_dimension=0,...  13.3 us
    pallas_call x2, Pallas kernels, attention(): pl.pallas_call(functools.partial(attention_kernel, n_blocks, heads_step,...  13.1 us
    all_to_all x3, starting transfers between devices, exchange(): lax.all_to_all(picked, ('dp', 'ctx'), split_axis=0, concat_axis=0, tiled=...  11.8 us
    pallas_call x3, Pallas kernels, pick_rows(): pl.pallas_call(functools.partial(pick_kernel, len(ks), n_dp, capacity), g...  10.7 us
    pallas_call x1, Pallas kernels, partial_rows(): pl.pallas_call(partial_kernel, grid=(hid // step,), in_specs=[pl.BlockSpe...  6.98 us
    ppermute x3, starting transfers between devices, along_z(): return lax.ppermute(array, 'ctx', pairs)  6.27 us
  transfers between devices with their start and end apart: 15, of which 5 were waited for; matrix products, arithmetic and copies ran while one was open for 1% of the time, Pallas kernels for 32%

profile of v8, /device:TPU:0, one launch (start us, length us, event | category | flops | bytes accessed | tf_op | source)
XLA Modules:
  0.0 158.8 jit_solution(11804626192690199390)
XLA Ops:
  7.2 1.7 %join.1.refs_0_ = bf16[128,1024]{1,0:T(8,128)(2,1)} custom-call(bf16[1,128,512]{2,1,0:T(8,128)(2,1)} %key_ref.1, bf16[1,128,512]{2,1,0:T(8,128)(2,1)} %value_ref.1), custom_call_target="tpu_custom_call" | custom-call | flops 1 | bytes 1 | tf_op jit(solution)/shard_map/join/pallas_call | solution.py:234
  8.9 4.9 %collective-permute-start = (bf16[128,1024]{1,0:T(8,128)(2,1)}, bf16[128,1024]{1,0:T(8,128)(2,1)S(1)}, u32[]{:S(2)}, u32[]{:S(2)}) collective-permute-start(bf16[128,1024]{1,0:T(8,128)(2,1)} %join.1.refs_0_), channel_id=1, source_target_pairs={{0,2},{1,3},{2,4},{3,5},{4,6},{5,7},{8,10},{9,11},{10,12},{11,13},... | collective-permute-start | bytes 786440 | tf_op jit(solution)/shard_map/ppermute | solution.py:468
  13.9 3.4 %collective-permute-start.2 = (bf16[128,1024]{1,0:T(8,128)(2,1)}, bf16[128,1024]{1,0:T(8,128)(2,1)S(1)}, u32[]{:S(2)}, u32[]{:S(2)}) collective-permute-start(bf16[128,1024]{1,0:T(8,128)(2,1)} %join.1.refs_0_), channel_id=1, source_target_pairs={{0,1},{2,3},{4,5},{6,7},{8,9},{10,11},{12,13},{14,15},{16,17},{18,... | collective-permute-start | bytes 786440 | tf_op jit(solution)/shard_map/ppermute | solution.py:477
  17.3 2.0 %slot_table.1 = (bf16[144,1024]{1,0:T(8,128)(2,1)}, bf16[128,1024]{1,0:T(8,128)(2,1)}) custom-call(bf16[128,2048]{1,0:T(8,128)(2,1)} %refs_1_.1, s32[8,128]{1,0:T(8,128)} %bitcast.23, bf16[8,128]{1,0:T(8,128)(2,1)} %bitcast.24, bf16[128,1024]{1,0:T(8,128)(2,1)} %join.1.refs_0_), custom_call_target="tpu_custom_call" | custom-call | flops 1 | bytes 1 | tf_op jit(solution)/shard_map/slot_table/pallas_call | solution.py:277
  20.4 0.7 collective-permute-start.3
  21.7 3.2 %pick_rows.3.refs_8_ = bf16[320,2048]{1,0:T(8,128)(2,1)} custom-call(s32[2]{0:T(128)} %pad_add_fusion.place, bf16[144,1024]{1,0:T(8,128)(2,1)} %get-tuple-element.45.refs_0_, bf16[128,2048]{1,0:T(8,128)(2,1)} %refs_1_.1, bf16[128,1024]{1,0:T(8,128)(2,1)} %copy-done.2), custom_call_target="tpu_custom_call" | custom-call | flops 1 | bytes 1 | tf_op jit(solution)/shard_map/pick_rows/pallas_call | solution.py:337
  24.9 0.7 collective-permute-start.4
  25.6 0.7 collective-permute-start.5
  26.4 0.7 collective-permute-start.6
  27.1 3.7 %all-to-all-start.1 = ((bf16[8,40,2048]{2,1,0:T(8,128)(2,1)}), bf16[8,40,2048]{2,1,0:T(8,128)(2,1)S(1)}, u32[]{:S(2)}, u32[]{:S(2)}) async-start(bf16[8,40,2048]{2,1,0:T(8,128)(2,1)} %bitcast.16), calls=%async_computation.2 | async-start | bytes 2621440 | tf_op jit(solution)/shard_map/all_to_all | solution.py:507
  30.8 0.7 all-gather.5.cloned.1.call-update
  31.6 0.7 copy-done.9
  32.3 6.5 %attention_backward.2 = (bf16[128,4096]{1,0:T(8,128)(2,1)}, bf16[512,512]{1,0:T(8,128)(2,1)}, bf16[512,512]{1,0:T(8,128)(2,1)}) custom-call(s32[2]{0:T(128)} %pad_add_fusion.place, bf16[128,4096]{1,0:T(8,128)(2,1)} %bitcast.19, bf16[128,4096]{1,0:T(8,128)(2,1)} %bitcast.21, bf16[128,1024]{1,0:T(8,128)(2,1)} %join.1.refs_0_, bf16[128,1024]{1,0:T(8,128)(2,1)} %copy-done.4, ...), custom_call_target="tpu_custom_call" | custom-call | flops 26843545600 | bytes 4194304 | tf_op jit(solution)/shard_map/attention_backward/pallas_call | solution.py:138
  38.8 2.1 %collective-permute-start.7 = (bf16[512,512]{1,0:T(8,128)(2,1)}, bf16[512,512]{1,0:T(8,128)(2,1)S(1)}, u32[]{:S(2)}, u32[]{:S(2)}) collective-permute-start(bf16[512,512]{1,0:T(8,128)(2,1)} %get-tuple-element.46), channel_id=1, source_target_pairs={{0,1},{1,0},{2,3},{3,2},{4,5},{5,4},{6,7},{7,6},{8,9},{9,8},{10,11... | collective-permute-start | bytes 1572872 | tf_op jit(solution)/shard_map/ppermute | solution.py:517
  40.9 6.5 %attention_backward.3 = (bf16[128,4096]{1,0:T(8,128)(2,1)}, bf16[512,512]{1,0:T(8,128)(2,1)}, bf16[512,512]{1,0:T(8,128)(2,1)}) custom-call(s32[2]{0:T(128)} %pad_add_fusion.place, bf16[128,4096]{1,0:T(8,128)(2,1)} %bitcast.20, bf16[128,4096]{1,0:T(8,128)(2,1)} %bitcast.22, bf16[128,1024]{1,0:T(8,128)(2,1)} %join.1.refs_0_, ...), custom_call_target="tpu_custom_call", output_to_operand_aliasing={{0}: (11, {})} | custom-call | flops 1 | bytes 1 | tf_op jit(solution)/shard_map/attention_backward/pallas_call | solution.py:138
  47.4 26.1 %all-gather.3.cloned.1.call-done.refs_0_.refs_1_.refs_2_.refs_3_.refs_4_.refs_5_ = bf16[576,1024]{1,0:T(8,128)(2,1)} async-done(((bf16[144,1024]{1,0:T(8,128)(2,1)}), bf16[576,1024]{1,0:T(8,128)(2,1)}) %all-gather.3.cloned.1.call-update) | async-done | bytes 1179664 | tf_op jit(solution)/shard_map/all_gather | solution.py:502
  73.5 3.7 %pick_rows.4.refs_6_ = bf16[960,1024]{1,0:T(8,128)(2,1)} custom-call(s32[2]{0:T(128)} %pad_add_fusion.place, bf16[576,1024]{1,0:T(8,128)(2,1)} %all-gather.3.cloned.1.call-done.refs_0_.refs_1_.refs_2_.refs_3_.refs_4_.refs_5_, bf16[576,1024]{1,0:T(8,128)(2,1)} %all-gather.3.cloned.1.call-done.refs_0_.refs_1_.refs_2_.refs_3_.refs_4_.refs_5_, ...), custom_call_target="tpu_custom_call" | custom-call | flops 1 | bytes 1 | tf_op jit(solution)/shard_map/pick_rows/pallas_call | solution.py:337
  77.2 0.8 copy-done.3
  78.5 3.7 %all-to-all-start = ((bf16[8,120,1024]{2,1,0:T(8,128)(2,1)}), bf16[8,120,1024]{2,1,0:T(8,128)(2,1)S(1)}, u32[]{:S(2)}, u32[]{:S(2)}) async-start(bf16[8,120,1024]{2,1,0:T(8,128)(2,1)} %bitcast.13), calls=%async_computation.1 | async-start | bytes 3932160 | tf_op jit(solution)/shard_map/all_to_all | solution.py:507
  82.2 3.8 %fold.1 = bf16[512,1536]{1,0:T(8,128)(2,1)} custom-call(bf16[512,512]{1,0:T(8,128)(2,1)} %get-tuple-element.44.mine_ref, bf16[512,512]{1,0:T(8,128)(2,1)} %copy-done.3, bf16[512,512]{1,0:T(8,128)(2,1)} %get-tuple-element.48.refs_1_, bf16[512,512]{1,0:T(8,128)(2,1)} %get-tuple-element.49.refs_2_), custom_call_target="tpu_custom_call" | custom-call | flops 1 | bytes 1 | tf_op jit(solution)/shard_map/fold/pallas_call | solution.py:186
  86.0 16.2 %all-gather.5.cloned.1.call-done.refs_3_.refs_4_.refs_5_ = bf16[512,1024]{1,0:T(8,128)(2,1)} async-done(((bf16[128,1024]{1,0:T(8,128)(2,1)}), bf16[512,1024]{1,0:T(8,128)(2,1)}) %all-gather.5.cloned.1.call-update) | async-done | bytes 1048592 | tf_op jit(solution)/shard_map/all_gather | solution.py:502
  102.2 3.8 %pick_rows.5.refs_0_ = bf16[960,1024]{1,0:T(8,128)(2,1)} custom-call(s32[2]{0:T(128)} %pad_add_fusion.place, bf16[576,1024]{1,0:T(8,128)(2,1)} %all-gather.3.cloned.1.call-done.refs_0_.refs_1_.refs_2_.refs_3_.refs_4_.refs_5_, bf16[576,1024]{1,0:T(8,128)(2,1)} %all-gather.3.cloned.1.call-done.refs_0_.refs_1_.refs_2_.refs_3_.refs_4_.refs_5_, ...), custom_call_target="tpu_custom_call" | custom-call | flops 1 | bytes 1 | tf_op jit(solution)/shard_map/pick_rows/pallas_call | solution.py:337
  105.9 0.9 all-to-all-done
  106.9 1.3 copy-done
  108.2 4.4 %all-to-all-start.2 = ((bf16[8,120,1024]{2,1,0:T(8,128)(2,1)}), bf16[8,120,1024]{2,1,0:T(8,128)(2,1)}, u32[]{:S(2)}, u32[]{:S(2)}) async-start(bf16[8,120,1024]{2,1,0:T(8,128)(2,1)} %bitcast.14), calls=%async_computation.3 | async-start | bytes 3932160 | tf_op jit(solution)/shard_map/all_to_all | solution.py:507
  112.6 6.4 %expert_rows.2.refs_1_ = bf16[1,32,40,1536]{3,2,1,0:T(8,128)(2,1)} custom-call(s32[2]{0:T(128)} %pad_add_fusion.place, bf16[320,2048]{1,0:T(8,128)(2,1)} %bitcast.17, bf16[1,1536,2048]{2,1,0:T(8,128)(2,1)} %w_ref.5, bf16[960,1024]{1,0:T(8,128)(2,1)} %pick_rows.5.refs_0_), custom_call_target="tpu_custom_call" | custom-call | flops 1 | bytes 1 | tf_op jit(solution)/shard_map/expert_rows/pallas_call | solution.py:419
  119.0 7.0 %partial_rows.1.refs_1_.refs_0_ = bf16[960,1536]{1,0:T(8,128)(2,1)} custom-call(bf16[960,1024]{1,0:T(8,128)(2,1)} %bitcast.15, bf16[1,1536,2048]{2,1,0:T(8,128)(2,1)} %w_ref.5), custom_call_target="tpu_custom_call" | custom-call | flops 1 | bytes 1 | tf_op jit(solution)/shard_map/partial_rows/pallas_call | solution.py:365
  126.0 13.3 %reduce-scatter.2.cloned.1.call-done.total_ref = bf16[128,1536]{1,0:T(8,128)(2,1)} async-done(((bf16[512,1536]{1,0:T(8,128)(2,1)}), bf16[128,1536]{1,0:T(8,128)(2,1)}) %reduce-scatter.2.cloned.1.call-update) | async-done | bytes 393232 | tf_op jit(solution)/shard_map/reduce_scatter | solution.py:537
  139.3 0.9 slice.3
  140.2 1.5 collective-permute-start.8
  141.7 8.1 %expert_rows.3 = bf16[1,32,40,1536]{3,2,1,0:T(8,128)(2,1)} custom-call(s32[2]{0:T(128)} %pad_add_fusion.place, bf16[960,1024]{1,0:T(8,128)(2,1)} %bitcast.12.rows_ref, bf16[1,1536,2048]{2,1,0:T(8,128)(2,1)} %w_ref.5, bf16[960,1536]{1,0:T(8,128)(2,1)} %partial_rows.1.refs_1_.refs_0_, ...), custom_call_target="tpu_custom_call", output_to_operand_aliasing={{}: (4, {})} | custom-call | flops 1 | bytes 1 | tf_op jit(solution)/shard_map/expert_rows/pallas_call | solution.py:419
  150.5 1.8 %finish.1 = (bf16[1,128,512]{2,1,0:T(8,128)(2,1)}, bf16[1,128,512]{2,1,0:T(8,128)(2,1)}) custom-call(bf16[128,1536]{1,0:T(8,128)(2,1)} %reduce-scatter.2.cloned.1.call-done.total_ref, bf16[128,512]{1,0:T(8,128)(2,1)} %copy-done.10, bf16[960,1536]{1,0:T(8,128)(2,1)} %partial_rows.1.refs_1_.refs_0_), custom_call_target="tpu_custom_call" | custom-call | flops 1 | bytes 1 | tf_op jit(solution)/shard_map/finish/pallas_call | solution.py:214
  (37 shorter events, 3.0 us)
Async XLA Ops:
  7.2 66.3 %all-gather.3.cloned.1.call-start = ((), (), s32[]{:S(2)}) async-start(), calls=%async_computation.4 | async-start | bytes 1474560 | tf_op jit(solution)/shard_map/all_gather | solution.py:502
  8.9 10.8 %collective-permute-start = (bf16[128,1024]{1,0:T(8,128)(2,1)}, bf16[128,1024]{1,0:T(8,128)(2,1)S(1)}, u32[]{:S(2)}, u32[]{:S(2)}) collective-permute-start(bf16[128,1024]{1,0:T(8,128)(2,1)} %join.1.refs_0_), channel_id=1, source_target_pairs={{0,2},{1,3},{2,4},{3,5},{4,6},{5,7},{8,10},{9,11},{10,12},{11,13},... | collective-permute-start | bytes 786440 | tf_op jit(solution)/shard_map/ppermute | solution.py:468
  13.9 11.0 %collective-permute-start.2 = (bf16[128,1024]{1,0:T(8,128)(2,1)}, bf16[128,1024]{1,0:T(8,128)(2,1)S(1)}, u32[]{:S(2)}, u32[]{:S(2)}) collective-permute-start(bf16[128,1024]{1,0:T(8,128)(2,1)} %join.1.refs_0_), channel_id=1, source_target_pairs={{0,1},{2,3},{4,5},{6,7},{8,9},{10,11},{12,13},{14,15},{16,17},{18,... | collective-permute-start | bytes 786440 | tf_op jit(solution)/shard_map/ppermute | solution.py:477
  19.7 2.0 %copy-start.2 = (bf16[128,1024]{1,0:T(8,128)(2,1)}, bf16[128,1024]{1,0:T(8,128)(2,1)S(1)}, u32[]{:S(2)}) copy-start(bf16[128,1024]{1,0:T(8,128)(2,1)S(1)} %collective-permute-done.refs_2_) | copy-start | bytes 786436
  19.7 5.2 %collective-permute-start.1 = (bf16[128,1024]{1,0:T(8,128)(2,1)S(1)}, bf16[128,1024]{1,0:T(8,128)(2,1)S(1)}, u32[]{:S(2)}, u32[]{:S(2)}) collective-permute-start(bf16[128,1024]{1,0:T(8,128)(2,1)S(1)} %collective-permute-done.refs_2_), channel_id=1, source_target_pairs={{2,4},{3,5},{4,6},{5,7},{10,12},{11,13},{12,14},{13,15},{18,20},{1... | collective-permute-start | bytes 786440 | tf_op jit(solution)/shard_map/ppermute | solution.py:468
  20.4 4.5 %collective-permute-start.3 = (bf16[128,1024]{1,0:T(8,128)(2,1)S(1)}, bf16[128,1024]{1,0:T(8,128)(2,1)S(1)}, u32[]{:S(2)}, u32[]{:S(2)}) collective-permute-start(bf16[128,1024]{1,0:T(8,128)(2,1)S(1)} %collective-permute-done.refs_2_), channel_id=1, source_target_pairs={{2,3},{3,2},{4,5},{5,4},{6,7},{7,6},{10,11},{11,10},{12,13},{13,12... | collective-permute-start | bytes 786440 | tf_op jit(solution)/shard_map/ppermute | solution.py:477
  24.9 6.7 %copy-start.4 = (bf16[128,1024]{1,0:T(8,128)(2,1)}, bf16[128,1024]{1,0:T(8,128)(2,1)S(1)}, u32[]{:S(2)}) copy-start(bf16[128,1024]{1,0:T(8,128)(2,1)S(1)} %collective-permute-done.2.refs_1_) | copy-start | bytes 786436
  24.9 6.7 %copy-start.5 = (bf16[128,1024]{1,0:T(8,128)(2,1)}, bf16[128,1024]{1,0:T(8,128)(2,1)S(1)}, u32[]{:S(2)}) copy-start(bf16[128,1024]{1,0:T(8,128)(2,1)S(1)} %collective-permute-done.1.refs_4_) | copy-start | bytes 786436
  24.9 6.7 %copy-start.6 = (bf16[128,1024]{1,0:T(8,128)(2,1)}, bf16[128,1024]{1,0:T(8,128)(2,1)S(1)}, u32[]{:S(2)}) copy-start(bf16[128,1024]{1,0:T(8,128)(2,1)S(1)} %collective-permute-done.3.refs_3_) | copy-start | bytes 786436
  24.9 1.4 collective-permute-start.4
  25.6 0.7 collective-permute-start.5
  26.3 5.3 %copy-start.7 = (bf16[128,1024]{1,0:T(8,128)(2,1)}, bf16[128,1024]{1,0:T(8,128)(2,1)S(1)}, u32[]{:S(2)}) copy-start(bf16[128,1024]{1,0:T(8,128)(2,1)S(1)} %collective-permute-done.4.refs_6_) | copy-start | bytes 786436
  26.3 5.3 %copy-start.8 = (bf16[128,1024]{1,0:T(8,128)(2,1)}, bf16[128,1024]{1,0:T(8,128)(2,1)S(1)}, u32[]{:S(2)}) copy-start(bf16[128,1024]{1,0:T(8,128)(2,1)S(1)} %collective-permute-done.5.refs_5_) | copy-start | bytes 786436
  26.4 5.2 %collective-permute-start.6 = (bf16[128,1024]{1,0:T(8,128)(2,1)S(1)}, bf16[128,1024]{1,0:T(8,128)(2,1)S(1)}, u32[]{:S(2)}, u32[]{:S(2)}) collective-permute-start(bf16[128,1024]{1,0:T(8,128)(2,1)S(1)} %collective-permute-done.4.refs_6_), channel_id=1, source_target_pairs={{6,7},{7,6},{14,15},{15,14},{22,23},{23,22},{30,31},{31,30}} | collective-permute-start | bytes 786440 | tf_op jit(solution)/shard_map/ppermute | solution.py:477
  27.1 50.2 %all-to-all-start.1 = ((bf16[8,40,2048]{2,1,0:T(8,128)(2,1)}), bf16[8,40,2048]{2,1,0:T(8,128)(2,1)S(1)}, u32[]{:S(2)}, u32[]{:S(2)}) async-start(bf16[8,40,2048]{2,1,0:T(8,128)(2,1)} %bitcast.16), calls=%async_computation.2 | async-start | bytes 2621440 | tf_op jit(solution)/shard_map/all_to_all | solution.py:507
  30.8 71.4 %all-gather.5.cloned.1.call-start = ((), (), s32[]{:S(2)}) async-start(), calls=%async_computation.6 | async-start | bytes 1310720 | tf_op jit(solution)/shard_map/all_gather | solution.py:502
  31.5 0.7 copy-start.9
  38.8 38.4 %collective-permute-start.7 = (bf16[512,512]{1,0:T(8,128)(2,1)}, bf16[512,512]{1,0:T(8,128)(2,1)S(1)}, u32[]{:S(2)}, u32[]{:S(2)}) collective-permute-start(bf16[512,512]{1,0:T(8,128)(2,1)} %get-tuple-element.46), channel_id=1, source_target_pairs={{0,1},{1,0},{2,3},{3,2},{4,5},{5,4},{6,7},{7,6},{8,9},{9,8},{10,11... | collective-permute-start | bytes 1572872 | tf_op jit(solution)/shard_map/ppermute | solution.py:517
  77.2 0.8 copy-start.3
  77.2 1.2 copy-start.1
  78.5 28.4 %all-to-all-start = ((bf16[8,120,1024]{2,1,0:T(8,128)(2,1)}), bf16[8,120,1024]{2,1,0:T(8,128)(2,1)S(1)}, u32[]{:S(2)}, u32[]{:S(2)}) async-start(bf16[8,120,1024]{2,1,0:T(8,128)(2,1)} %bitcast.13), calls=%async_computation.1 | async-start | bytes 3932160 | tf_op jit(solution)/shard_map/all_to_all | solution.py:507
  82.1 57.2 %reduce-scatter.2.cloned.1.call-start = ((), (), s32[]{:S(2)}) async-start(), calls=%async_computation.5 | async-start | bytes 1966080 | tf_op jit(solution)/shard_map/reduce_scatter | solution.py:537
  106.9 1.3 copy-start
  108.2 33.5 %all-to-all-start.2 = ((bf16[8,120,1024]{2,1,0:T(8,128)(2,1)}), bf16[8,120,1024]{2,1,0:T(8,128)(2,1)}, u32[]{:S(2)}, u32[]{:S(2)}) async-start(bf16[8,120,1024]{2,1,0:T(8,128)(2,1)} %bitcast.14), calls=%async_computation.3 | async-start | bytes 3932160 | tf_op jit(solution)/shard_map/all_to_all | solution.py:507
  140.2 9.6 %collective-permute-start.8 = (bf16[128,512]{1,0:T(8,128)(2,1)S(1)}, bf16[128,512]{1,0:T(8,128)(2,1)S(1)}, u32[]{:S(2)}, u32[]{:S(2)}) collective-permute-start(bf16[128,512]{1,0:T(8,128)(2,1)S(1)} %slice.3), channel_id=1, source_target_pairs={{0,1},{1,0},{2,3},{3,2},{4,5},{5,4},{6,7},{7,6},{8,9},{9,8},{10,11... | collective-permute-start | bytes 393224 | tf_op jit(solution)/shard_map/ppermute | solution.py:517
  149.8 0.7 copy-start.10
Sparse Core Ops, SparseCore 0:
  26.5 46.9 all-gather.2
  75.1 27.0 all-gather.4
  104.5 34.7 reduce-scatter.1

commit v9 on v8

--- a/solution.py
+++ b/solution.py
@@ -170,24 +170,23 @@
     )(place, queries, out_grad, *kv_blocks, *held, *after)
 
 
-def fold_kernel(mine_ref, *refs):
-    out_ref, width = refs[-1], mine_ref.shape[1]
-    total = mine_ref[...].astype(jnp.float32) + refs[0][...].astype(jnp.float32)
-    out_ref[:, :width] = total.astype(out_ref.dtype)
-    first = width
-    for ref in refs[1:-1]:
-        out_ref[:, first : first + ref.shape[1]] = ref[...]
-        first += ref.shape[1]
-
-
-def fold(mine, got, others):
-    arrays = (mine, got, *others)
-    rows, width = mine.shape[0], sum(part.shape[1] for part in arrays[1:])
-    return pl.pallas_call(
-        fold_kernel,
-        grid=(4,),
-        in_specs=[pl.BlockSpec((rows // 4, part.shape[1]), lambda i: (i, 0)) for part in arrays],
-        out_specs=pl.BlockSpec((rows // 4, width), lambda i: (i, 0)),
+def fold_kernel(groups, *refs):
+    out_ref = refs[-1]
+    first = 0
+    for i in range(groups):
+        total = refs[2 * i][...].astype(jnp.float32) + refs[2 * i + 1][...].astype(jnp.float32)
+        out_ref[:, first : first + total.shape[1]] = total.astype(out_ref.dtype)
+        first += total.shape[1]
+
+
+def fold(parts):
+    arrays = [part for pair in parts for part in pair]
+    rows, width = arrays[0].shape[0], sum(pair[0].shape[1] for pair in parts)
+    return pl.pallas_call(
+        functools.partial(fold_kernel, len(parts)),
+        grid=(2,),
+        in_specs=[pl.BlockSpec((rows // 2, part.shape[1]), lambda i: (i, 0)) for part in arrays],
+        out_specs=pl.BlockSpec((rows // 2, width), lambda i: (i, 0)),
         out_shape=jax.ShapeDtypeStruct((rows, width), jnp.bfloat16),
         compiler_params=pltpu.CompilerParams(vmem_limit_bytes=vmem_limit),
         cost_estimate=small_cost,
@@ -195,31 +194,25 @@
     )(*arrays)
 
 
-def finish_kernel(counts, total_ref, *refs):
+def finish_kernel(total_ref, *refs):
     key_ref, value_ref = refs[-2:]
     size = 2 * HEAD_DIM
-    for g in range(sum(counts)):
+    for g in range(total_ref.shape[1] // size):
         lanes = slice(g * HEAD_DIM, (g + 1) * HEAD_DIM)
-        held = total_ref[:, g * size : (g + 1) * size]
-        if g >= counts[0]:
-            at = (g - counts[0]) * size
-            held = held.astype(jnp.float32) + refs[0][:, at : at + size].astype(jnp.float32)
-            held = held.astype(jnp.bfloat16)
-        key_ref[0, :, lanes] = held[:, :HEAD_DIM]
-        value_ref[0, :, lanes] = held[:, HEAD_DIM:]
-
-
-def finish(counts, total, crossed, after):
-    shape = jax.ShapeDtypeStruct((1, total.shape[0], sum(counts) * HEAD_DIM), jnp.bfloat16)
-    return pl.pallas_call(
-        functools.partial(finish_kernel, counts),
-        in_specs=[pl.BlockSpec(memory_space=pltpu.VMEM)] * (1 + len(crossed))
-        + [pl.BlockSpec(memory_space=pl.ANY)],
+        key_ref[0, :, lanes] = total_ref[:, g * size : g * size + HEAD_DIM]
+        value_ref[0, :, lanes] = total_ref[:, g * size + HEAD_DIM : (g + 1) * size]
+
+
+def finish(total, after):
+    shape = jax.ShapeDtypeStruct((1, total.shape[0], total.shape[1] // 2), jnp.bfloat16)
+    return pl.pallas_call(
+        finish_kernel,
+        in_specs=[pl.BlockSpec(memory_space=pltpu.VMEM), pl.BlockSpec(memory_space=pl.ANY)],
         out_shape=[shape, shape],
         compiler_params=pltpu.CompilerParams(vmem_limit_bytes=vmem_limit),
         cost_estimate=small_cost,
         name="finish",
-    )(total, *crossed, after)
+    )(total, after)
 
 
 def join_kernel(key_ref, value_ref, kv_ref):
@@ -516,26 +509,25 @@
     def cross(array):
         return lax.ppermute(array, "ctx", [(i, i ^ 1) for i in range(n_ctx)])
 
-    counts = [1] if kv_local == 1 else [kv_local // 2, kv_local - kv_local // 2]
     rest = tuple(range(1, n_z))
     own_picked, columns[n_z - 1] = lax.optimization_barrier((own_picked, columns[n_z - 1]))
     got_own = exchange(own_picked)
-    query_grad, mine, other = attention(
-        place, queries[0], out_grad[0], blocks, 0, counts[0], None, (own_picked,)
-    )
-    crossed = cross(other)
-    others = []
-    if len(counts) > 1:
-        query_grad, *others = attention(
-            place, queries[0], out_grad[0], blocks, counts[0], counts[1], query_grad
+    query_grad, parts, after = None, [], (own_picked,)
+    for g in range(kv_local):
+        query_grad, mine, other = attention(
+            place, queries[0], out_grad[0], blocks, g, 1, query_grad, after
         )
-    picked = pick(all_halves[0], all_halves[0], rest, (query_grad,))
-    picked, crossed = lax.optimization_barrier((picked, crossed))
+        parts.append((mine, cross(other)))
+        after = ()
+    crossed = [got for _, got in parts[:-1]]
+    picked = pick(all_halves[0], all_halves[0], rest, (query_grad, *crossed))
+    mines = [mine for mine, _ in parts]
+    picked, *crossed = lax.optimization_barrier((picked, *[got for _, got in parts]))
     got_first = exchange(picked)
     picked = pick(all_halves[0], all_halves[1], rest, (picked,))
     got_last = exchange(picked)
     total = lax.psum_scatter(
-        fold(mine, crossed, others),
+        fold(list(zip(mines, crossed))),
         "ctx",
         scatter_dimension=0,
         tiled=True,
@@ -544,10 +536,10 @@
     sizes = (n_z, n_dp, capacity, slots)
     hidden_grad = expert_rows(place, got_own, (0,), w_down, *sizes, None, None, (picked,))
     base = partial_rows(got_first, w_down)
-    total, base, hidden_grad = lax.optimization_barrier((total, base, hidden_grad))
-    last = [cross(total[:, -others[1].shape[1] :])] if others else []
-    key_grad, value_grad = finish(counts, total, last, base)
-    hidden_grad = expert_rows(place, got_last, rest, w_down, *sizes, base, hidden_grad)
+    key_grad, value_grad = finish(total, base)
+    hidden_grad = expert_rows(
+        place, got_last, rest, w_down, *sizes, base, hidden_grad, (key_grad,)
+    )
     return (query_grad[None], key_grad, value_grad, hidden_grad)
 
 

time: 160 us -> 164 us (1.025)
  the two profiles are of different devices: /device:TPU:0 before, /device:TPU:24 now
where the time goes in v9:
time: 164 us; the launch traced here: 163 us
  Pallas kernels  64.5 us (39%)
  waiting for transfers between devices  48 us (29%)
  starting transfers between devices  32.2 us (20%)
  between operations  13.9 us (8%)
  local copies, waits for them, and re-layouts  3.96 us (2%)
    pallas_call x4, Pallas kernels, attention(): pl.pallas_call(functools.partial(attention_kernel, n_blocks, heads_step,...  24.4 us
    all_to_all x3, waiting for transfers between devices, exchange(): lax.all_to_all(picked, ('dp', 'ctx'), split_axis=0, concat_axis=0, tiled=...  16.9 us
    pallas_call x2, Pallas kernels, expert_rows(): pl.pallas_call(functools.partial(expert_kernel, ks, bool(extra), n_z, n_d...  14.5 us
    ppermute x4, starting transfers between devices, across_x(): return lax.ppermute(columns[k], 'ctx', pairs)  12.6 us
    all_to_all x3, starting transfers between devices, exchange(): lax.all_to_all(picked, ('dp', 'ctx'), split_axis=0, concat_axis=0, tiled=...  11.5 us
    all_gather x2, waiting for transfers between devices, per_device(): lax.all_gather(half, 'ctx', axis=0, tiled=True, axis_index_groups=line_gr...  11 us
    pallas_call x3, Pallas kernels, pick_rows(): pl.pallas_call(functools.partial(pick_kernel, len(ks), n_dp, capacity), g...  10.7 us
    ppermute x3, waiting for transfers between devices, along_z(): return lax.ppermute(array, 'ctx', pairs)  9.05 us
  transfers between devices with their start and end apart: 17, of which 11 were waited for; matrix products, arithmetic and copies ran while one was open for 0% of the time, Pallas kernels for 34%

profile of v9, /device:TPU:24, one launch (start us, length us, event | category | flops | bytes accessed | tf_op | source)
XLA Modules:
  0.0 163.3 jit_solution(9791867612159363133)
XLA Ops:
  7.2 1.7 %join.1.refs_0_ = bf16[128,1024]{1,0:T(8,128)(2,1)} custom-call(bf16[1,128,512]{2,1,0:T(8,128)(2,1)} %key_ref.1, bf16[1,128,512]{2,1,0:T(8,128)(2,1)} %value_ref.1), custom_call_target="tpu_custom_call" | custom-call | flops 1 | bytes 1 | tf_op jit(solution)/shard_map/join/pallas_call | solution.py:227
  10.2 3.4 %collective-permute-start.2 = (bf16[128,1024]{1,0:T(8,128)(2,1)}, bf16[128,1024]{1,0:T(8,128)(2,1)S(1)}, u32[]{:S(2)}, u32[]{:S(2)}) collective-permute-start(bf16[128,1024]{1,0:T(8,128)(2,1)} %join.1.refs_0_), channel_id=1, source_target_pairs={{0,1},{2,3},{4,5},{6,7},{8,9},{10,11},{12,13},{14,15},{16,17},{18,... | collective-permute-start | bytes 786440 | tf_op jit(solution)/shard_map/ppermute | solution.py:470
  13.7 2.0 %slot_table.1 = (bf16[144,1024]{1,0:T(8,128)(2,1)}, bf16[128,1024]{1,0:T(8,128)(2,1)}) custom-call(bf16[128,2048]{1,0:T(8,128)(2,1)} %refs_1_.1, s32[8,128]{1,0:T(8,128)} %bitcast.27, bf16[8,128]{1,0:T(8,128)(2,1)} %bitcast.28, bf16[128,1024]{1,0:T(8,128)(2,1)} %join.1.refs_0_), custom_call_target="tpu_custom_call" | custom-call | flops 1 | bytes 1 | tf_op jit(solution)/shard_map/slot_table/pallas_call | solution.py:270
  15.6 3.5 %collective-permute-done.refs_2_ = bf16[128,1024]{1,0:T(8,128)(2,1)S(1)} collective-permute-done((bf16[128,1024]{1,0:T(8,128)(2,1)}, bf16[128,1024]{1,0:T(8,128)(2,1)S(1)}, u32[]{:S(2)}, u32[]{:S(2)}) %collective-permute-start) | collective-permute-done | bytes 262176 | tf_op jit(solution)/shard_map/ppermute | solution.py:461
  19.1 3.4 %collective-permute-start.3 = (bf16[128,1024]{1,0:T(8,128)(2,1)S(1)}, bf16[128,1024]{1,0:T(8,128)(2,1)S(1)}, u32[]{:S(2)}, u32[]{:S(2)}) collective-permute-start(bf16[128,1024]{1,0:T(8,128)(2,1)S(1)} %collective-permute-done.refs_2_), channel_id=1, source_target_pairs={{2,3},{3,2},{4,5},{5,4},{6,7},{7,6},{10,11},{11,10},{12,13},{13,12... | collective-permute-start | bytes 786440 | tf_op jit(solution)/shard_map/ppermute | solution.py:470
  24.4 3.2 %pick_rows.3.refs_8_ = bf16[320,2048]{1,0:T(8,128)(2,1)} custom-call(s32[2]{0:T(128)} %pad_add_fusion.place, bf16[144,1024]{1,0:T(8,128)(2,1)} %get-tuple-element.53.refs_0_, bf16[128,2048]{1,0:T(8,128)(2,1)} %refs_1_.1, bf16[128,1024]{1,0:T(8,128)(2,1)} %copy-done.2), custom_call_target="tpu_custom_call" | custom-call | flops 1 | bytes 1 | tf_op jit(solution)/shard_map/pick_rows/pallas_call | solution.py:330
  28.2 3.1 %collective-permute-done.1.refs_4_ = bf16[128,1024]{1,0:T(8,128)(2,1)S(1)} collective-permute-done((bf16[128,1024]{1,0:T(8,128)(2,1)S(1)}, bf16[128,1024]{1,0:T(8,128)(2,1)S(1)}, u32[]{:S(2)}, u32[]{:S(2)}) %collective-permute-start.1) | collective-permute-done | bytes 262176 | tf_op jit(solution)/shard_map/ppermute | solution.py:461
  31.3 2.4 %collective-permute-start.5 = (bf16[128,1024]{1,0:T(8,128)(2,1)S(1)}, bf16[128,1024]{1,0:T(8,128)(2,1)S(1)}, u32[]{:S(2)}, u32[]{:S(2)}) collective-permute-start(bf16[128,1024]{1,0:T(8,128)(2,1)S(1)} %collective-permute-done.1.refs_4_), channel_id=1, source_target_pairs={{4,5},{5,4},{6,7},{7,6},{12,13},{13,12},{14,15},{15,14},{20,21},{2... | collective-permute-start | bytes 786440 | tf_op jit(solution)/shard_map/ppermute | solution.py:470
  35.0 4.5 %collective-permute-done.5.refs_5_ = bf16[128,1024]{1,0:T(8,128)(2,1)S(1)} collective-permute-done((bf16[128,1024]{1,0:T(8,128)(2,1)S(1)}, bf16[128,1024]{1,0:T(8,128)(2,1)S(1)}, u32[]{:S(2)}, u32[]{:S(2)}) %collective-permute-start.5) | collective-permute-done | bytes 262176 | tf_op jit(solution)/shard_map/ppermute | solution.py:470
  39.5 2.4 %collective-permute-done.4.refs_6_ = bf16[128,1024]{1,0:T(8,128)(2,1)S(1)} collective-permute-done((bf16[128,1024]{1,0:T(8,128)(2,1)S(1)}, bf16[128,1024]{1,0:T(8,128)(2,1)S(1)}, u32[]{:S(2)}, u32[]{:S(2)}) %collective-permute-start.4) | collective-permute-done | bytes 262176 | tf_op jit(solution)/shard_map/ppermute | solution.py:461
  42.0 3.4 %collective-permute-start.6 = (bf16[128,1024]{1,0:T(8,128)(2,1)S(1)}, bf16[128,1024]{1,0:T(8,128)(2,1)S(1)}, u32[]{:S(2)}, u32[]{:S(2)}) collective-permute-start(bf16[128,1024]{1,0:T(8,128)(2,1)S(1)} %collective-permute-done.4.refs_6_), channel_id=1, source_target_pairs={{6,7},{7,6},{14,15},{15,14},{22,23},{23,22},{30,31},{31,30}} | collective-permute-start | bytes 786440 | tf_op jit(solution)/shard_map/ppermute | solution.py:470
  45.4 3.6 %all-to-all-start.2 = ((bf16[8,40,2048]{2,1,0:T(8,128)(2,1)}), bf16[8,40,2048]{2,1,0:T(8,128)(2,1)S(1)}, u32[]{:S(2)}, u32[]{:S(2)}) async-start(bf16[8,40,2048]{2,1,0:T(8,128)(2,1)} %bitcast.25), calls=%async_computation.3 | async-start | bytes 2621440 | tf_op jit(solution)/shard_map/all_to_all | solution.py:500
  51.0 6.2 %attention_backward.4 = (bf16[128,4096]{1,0:T(8,128)(2,1)}, bf16[512,256]{1,0:T(8,128)(2,1)}, bf16[512,256]{1,0:T(8,128)(2,1)}) custom-call(s32[2]{0:T(128)} %pad_add_fusion.place, bf16[128,4096]{1,0:T(8,128)(2,1)} %bitcast.16, bf16[128,4096]{1,0:T(8,128)(2,1)} %bitcast.20, bf16[128,1024]{1,0:T(8,128)(2,1)} %join.1.refs_0_, bf16[128,1024]{1,0:T(8,128)(2,1)} %copy-done.3, ...), custom_call_target="tpu_custom_call" | custom-call | flops 13421772800 | bytes 2097152 | tf_op jit(solution)/shard_map/attention_backward/pallas_call | solution.py:138
  57.1 1.5 collective-permute-start.7
  58.6 6.0 %attention_backward.5 = (bf16[128,4096]{1,0:T(8,128)(2,1)}, bf16[512,256]{1,0:T(8,128)(2,1)}, bf16[512,256]{1,0:T(8,128)(2,1)}) custom-call(s32[2]{0:T(128)} %pad_add_fusion.place, bf16[128,4096]{1,0:T(8,128)(2,1)} %bitcast.17, bf16[128,4096]{1,0:T(8,128)(2,1)} %bitcast.21, bf16[128,1024]{1,0:T(8,128)(2,1)} %join.1.refs_0_, ...), custom_call_target="tpu_custom_call", output_to_operand_aliasing={{0}: (11, {})} | custom-call | flops 1 | bytes 1 | tf_op jit(solution)/shard_map/attention_backward/pallas_call | solution.py:138
  65.2 6.1 %attention_backward.6 = (bf16[128,4096]{1,0:T(8,128)(2,1)}, bf16[512,256]{1,0:T(8,128)(2,1)}, bf16[512,256]{1,0:T(8,128)(2,1)}) custom-call(s32[2]{0:T(128)} %pad_add_fusion.place, bf16[128,4096]{1,0:T(8,128)(2,1)} %bitcast.18, bf16[128,4096]{1,0:T(8,128)(2,1)} %bitcast.22, bf16[128,1024]{1,0:T(8,128)(2,1)} %join.1.refs_0_, ...), custom_call_target="tpu_custom_call", output_to_operand_aliasing={{0}: (11, {})} | custom-call | flops 1 | bytes 1 | tf_op jit(solution)/shard_map/attention_backward/pallas_call | solution.py:138
  71.3 1.5 collective-permute-start.9
  72.7 6.2 %attention_backward.7 = (bf16[128,4096]{1,0:T(8,128)(2,1)}, bf16[512,256]{1,0:T(8,128)(2,1)}, bf16[512,256]{1,0:T(8,128)(2,1)}) custom-call(s32[2]{0:T(128)} %pad_add_fusion.place, bf16[128,4096]{1,0:T(8,128)(2,1)} %bitcast.19, bf16[128,4096]{1,0:T(8,128)(2,1)} %bitcast.23, bf16[128,1024]{1,0:T(8,128)(2,1)} %join.1.refs_0_, ...), custom_call_target="tpu_custom_call", output_to_operand_aliasing={{0}: (11, {})} | custom-call | flops 1 | bytes 1 | tf_op jit(solution)/shard_map/attention_backward/pallas_call | solution.py:138
  79.6 4.0 %collective-permute-done.9.refs_9_.refs_5_ = bf16[512,256]{1,0:T(8,128)(2,1)S(1)} collective-permute-done((bf16[512,256]{1,0:T(8,128)(2,1)}, bf16[512,256]{1,0:T(8,128)(2,1)S(1)}, u32[]{:S(2)}, u32[]{:S(2)}) %collective-permute-start.9) | collective-permute-done | bytes 262176 | tf_op jit(solution)/shard_map/ppermute | solution.py:510
  84.3 3.7 %pick_rows.4.refs_6_ = bf16[960,1024]{1,0:T(8,128)(2,1)} custom-call(s32[2]{0:T(128)} %pad_add_fusion.place, bf16[576,1024]{1,0:T(8,128)(2,1)} %all-gather.3.cloned.1.call-done.refs_0_.refs_1_.refs_2_.refs_3_.refs_4_.refs_5_, bf16[576,1024]{1,0:T(8,128)(2,1)} %all-gather.3.cloned.1.call-done.refs_0_.refs_1_.refs_2_.refs_3_.refs_4_.refs_5_, ...), custom_call_target="tpu_custom_call" | custom-call | flops 1 | bytes 1 | tf_op jit(solution)/shard_map/pick_rows/pallas_call | solution.py:330
  89.9 3.6 %all-to-all-start = ((bf16[8,120,1024]{2,1,0:T(8,128)(2,1)}), bf16[8,120,1024]{2,1,0:T(8,128)(2,1)S(1)}, u32[]{:S(2)}, u32[]{:S(2)}) async-start(bf16[8,120,1024]{2,1,0:T(8,128)(2,1)} %bitcast.13), calls=%async_computation.1 | async-start | bytes 3932160 | tf_op jit(solution)/shard_map/all_to_all | solution.py:500
  93.6 2.5 %fold.1 = bf16[512,1024]{1,0:T(8,128)(2,1)} custom-call(bf16[512,256]{1,0:T(8,128)(2,1)} %get-tuple-element.52.refs_0_, bf16[512,256]{1,0:T(8,128)(2,1)} %copy-done.9, bf16[512,256]{1,0:T(8,128)(2,1)} %get-tuple-element.59.refs_2_, bf16[512,256]{1,0:T(8,128)(2,1)} %copy-done.10, bf16[512,256]{1,0:T(8,128)(2,1)} %get-tuple-element.61.refs_4_, ...), custom_call_target="tpu_custom_call" | custom-call | flops 1 | bytes 1 | tf_op jit(solution)/shard_map/fold/pallas_call | solution.py:185
  96.1 11.0 %all-gather.5.cloned.1.call-done.refs_3_.refs_4_.refs_5_ = bf16[512,1024]{1,0:T(8,128)(2,1)} async-done(((bf16[128,1024]{1,0:T(8,128)(2,1)}), bf16[512,1024]{1,0:T(8,128)(2,1)}) %all-gather.5.cloned.1.call-update) | async-done | bytes 1048592 | tf_op jit(solution)/shard_map/all_gather | solution.py:495
  107.2 3.8 %pick_rows.5.refs_0_ = bf16[960,1024]{1,0:T(8,128)(2,1)} custom-call(s32[2]{0:T(128)} %pad_add_fusion.place, bf16[576,1024]{1,0:T(8,128)(2,1)} %all-gather.3.cloned.1.call-done.refs_0_.refs_1_.refs_2_.refs_3_.refs_4_.refs_5_, bf16[576,1024]{1,0:T(8,128)(2,1)} %all-gather.3.cloned.1.call-done.refs_0_.refs_1_.refs_2_.refs_3_.refs_4_.refs_5_, ...), custom_call_target="tpu_custom_call" | custom-call | flops 1 | bytes 1 | tf_op jit(solution)/shard_map/pick_rows/pallas_call | solution.py:330
  110.9 7.3 %all-to-all-done = bf16[8,120,1024]{2,1,0:T(8,128)(2,1)S(1)} async-done(((bf16[8,120,1024]{2,1,0:T(8,128)(2,1)}), bf16[8,120,1024]{2,1,0:T(8,128)(2,1)S(1)}, u32[]{:S(2)}, u32[]{:S(2)}) %all-to-all-start) | async-done | bytes 1966112 | tf_op jit(solution)/shard_map/all_to_all | solution.py:500
  118.2 1.3 copy-done
  119.5 4.3 %all-to-all-start.1 = ((bf16[8,120,1024]{2,1,0:T(8,128)(2,1)}), bf16[8,120,1024]{2,1,0:T(8,128)(2,1)}, u32[]{:S(2)}, u32[]{:S(2)}) async-start(bf16[8,120,1024]{2,1,0:T(8,128)(2,1)} %bitcast.14), calls=%async_computation.2 | async-start | bytes 3932160 | tf_op jit(solution)/shard_map/all_to_all | solution.py:500
  123.9 6.4 %expert_rows.2.refs_1_ = bf16[1,32,40,1536]{3,2,1,0:T(8,128)(2,1)} custom-call(s32[2]{0:T(128)} %pad_add_fusion.place, bf16[320,2048]{1,0:T(8,128)(2,1)} %bitcast.26, bf16[1,1536,2048]{2,1,0:T(8,128)(2,1)} %w_ref.5, bf16[960,1024]{1,0:T(8,128)(2,1)} %pick_rows.5.refs_0_), custom_call_target="tpu_custom_call" | custom-call | flops 1 | bytes 1 | tf_op jit(solution)/shard_map/expert_rows/pallas_call | solution.py:412
  130.3 7.0 %partial_rows.1.refs_0_ = bf16[960,1536]{1,0:T(8,128)(2,1)} custom-call(bf16[960,1024]{1,0:T(8,128)(2,1)} %bitcast.24, bf16[1,1536,2048]{2,1,0:T(8,128)(2,1)} %w_ref.5), custom_call_target="tpu_custom_call" | custom-call | flops 1 | bytes 1 | tf_op jit(solution)/shard_map/partial_rows/pallas_call | solution.py:358
  137.3 1.7 %finish.1 = (bf16[1,128,512]{2,1,0:T(8,128)(2,1)}, bf16[1,128,512]{2,1,0:T(8,128)(2,1)}) custom-call(bf16[128,1024]{1,0:T(8,128)(2,1)} %reduce-scatter.2.cloned.1.call-done.total_ref, bf16[960,1536]{1,0:T(8,128)(2,1)} %partial_rows.1.refs_0_), custom_call_target="tpu_custom_call" | custom-call | flops 1 | bytes 1 | tf_op jit(solution)/shard_map/finish/pallas_call | solution.py:208
  139.0 9.6 %all-to-all-done.1 = bf16[8,120,1024]{2,1,0:T(8,128)(2,1)} async-done(((bf16[8,120,1024]{2,1,0:T(8,128)(2,1)}), bf16[8,120,1024]{2,1,0:T(8,128)(2,1)}, u32[]{:S(2)}, u32[]{:S(2)}) %all-to-all-start.1) | async-done | bytes 1966112 | tf_op jit(solution)/shard_map/all_to_all | solution.py:500
  148.6 8.1 %expert_rows.3 = bf16[1,32,40,1536]{3,2,1,0:T(8,128)(2,1)} custom-call(s32[2]{0:T(128)} %pad_add_fusion.place, bf16[960,1024]{1,0:T(8,128)(2,1)} %bitcast.10.rows_ref, bf16[1,1536,2048]{2,1,0:T(8,128)(2,1)} %w_ref.5, bf16[960,1536]{1,0:T(8,128)(2,1)} %partial_rows.1.refs_0_, ...), custom_call_target="tpu_custom_call", output_to_operand_aliasing={{}: (4, {})} | custom-call | flops 1 | bytes 1 | tf_op jit(solution)/shard_map/expert_rows/pallas_call | solution.py:412
  (46 shorter events, 10.9 us)
Async XLA Ops:
  7.2 76.4 %all-gather.3.cloned.1.call-start = ((), (), s32[]{:S(2)}) async-start(), calls=%async_computation.4 | async-start | bytes 1474560 | tf_op jit(solution)/shard_map/all_gather | solution.py:495
  9.0 10.1 %collective-permute-start = (bf16[128,1024]{1,0:T(8,128)(2,1)}, bf16[128,1024]{1,0:T(8,128)(2,1)S(1)}, u32[]{:S(2)}, u32[]{:S(2)}) collective-permute-start(bf16[128,1024]{1,0:T(8,128)(2,1)} %join.1.refs_0_), channel_id=1, source_target_pairs={{0,2},{1,3},{2,4},{3,5},{4,6},{5,7},{8,10},{9,11},{10,12},{11,13},... | collective-permute-start | bytes 786440 | tf_op jit(solution)/shard_map/ppermute | solution.py:461
  10.2 17.4 %collective-permute-start.2 = (bf16[128,1024]{1,0:T(8,128)(2,1)}, bf16[128,1024]{1,0:T(8,128)(2,1)S(1)}, u32[]{:S(2)}, u32[]{:S(2)}) collective-permute-start(bf16[128,1024]{1,0:T(8,128)(2,1)} %join.1.refs_0_), channel_id=1, source_target_pairs={{0,1},{2,3},{4,5},{6,7},{8,9},{10,11},{12,13},{14,15},{16,17},{18,... | collective-permute-start | bytes 786440 | tf_op jit(solution)/shard_map/ppermute | solution.py:470
  19.1 5.3 %copy-start.2 = (bf16[128,1024]{1,0:T(8,128)(2,1)}, bf16[128,1024]{1,0:T(8,128)(2,1)S(1)}, u32[]{:S(2)}) copy-start(bf16[128,1024]{1,0:T(8,128)(2,1)S(1)} %collective-permute-done.refs_2_) | copy-start | bytes 786436
  19.1 9.1 %collective-permute-start.3 = (bf16[128,1024]{1,0:T(8,128)(2,1)S(1)}, bf16[128,1024]{1,0:T(8,128)(2,1)S(1)}, u32[]{:S(2)}, u32[]{:S(2)}) collective-permute-start(bf16[128,1024]{1,0:T(8,128)(2,1)S(1)} %collective-permute-done.refs_2_), channel_id=1, source_target_pairs={{2,3},{3,2},{4,5},{5,4},{6,7},{7,6},{10,11},{11,10},{12,13},{13,12... | collective-permute-start | bytes 786440 | tf_op jit(solution)/shard_map/ppermute | solution.py:470
  22.5 8.8 %collective-permute-start.1 = (bf16[128,1024]{1,0:T(8,128)(2,1)S(1)}, bf16[128,1024]{1,0:T(8,128)(2,1)S(1)}, u32[]{:S(2)}, u32[]{:S(2)}) collective-permute-start(bf16[128,1024]{1,0:T(8,128)(2,1)S(1)} %collective-permute-done.refs_2_), channel_id=1, source_target_pairs={{2,4},{3,5},{4,6},{5,7},{10,12},{11,13},{12,14},{13,15},{18,20},{1... | collective-permute-start | bytes 786440 | tf_op jit(solution)/shard_map/ppermute | solution.py:461
  27.6 22.7 %copy-start.3 = (bf16[128,1024]{1,0:T(8,128)(2,1)}, bf16[128,1024]{1,0:T(8,128)(2,1)S(1)}, u32[]{:S(2)}) copy-start(bf16[128,1024]{1,0:T(8,128)(2,1)S(1)} %collective-permute-done.2.refs_1_) | copy-start | bytes 786436
  28.2 22.1 %copy-start.4 = (bf16[128,1024]{1,0:T(8,128)(2,1)}, bf16[128,1024]{1,0:T(8,128)(2,1)S(1)}, u32[]{:S(2)}) copy-start(bf16[128,1024]{1,0:T(8,128)(2,1)S(1)} %collective-permute-done.3.refs_3_) | copy-start | bytes 786436
  31.3 19.0 %copy-start.5 = (bf16[128,1024]{1,0:T(8,128)(2,1)}, bf16[128,1024]{1,0:T(8,128)(2,1)S(1)}, u32[]{:S(2)}) copy-start(bf16[128,1024]{1,0:T(8,128)(2,1)S(1)} %collective-permute-done.1.refs_4_) | copy-start | bytes 786436
  31.3 8.3 %collective-permute-start.5 = (bf16[128,1024]{1,0:T(8,128)(2,1)S(1)}, bf16[128,1024]{1,0:T(8,128)(2,1)S(1)}, u32[]{:S(2)}, u32[]{:S(2)}) collective-permute-start(bf16[128,1024]{1,0:T(8,128)(2,1)S(1)} %collective-permute-done.1.refs_4_), channel_id=1, source_target_pairs={{4,5},{5,4},{6,7},{7,6},{12,13},{13,12},{14,15},{15,14},{20,21},{2... | collective-permute-start | bytes 786440 | tf_op jit(solution)/shard_map/ppermute | solution.py:470
  33.7 8.3 %collective-permute-start.4 = (bf16[128,1024]{1,0:T(8,128)(2,1)S(1)}, bf16[128,1024]{1,0:T(8,128)(2,1)S(1)}, u32[]{:S(2)}, u32[]{:S(2)}) collective-permute-start(bf16[128,1024]{1,0:T(8,128)(2,1)S(1)} %collective-permute-done.1.refs_4_), channel_id=1, source_target_pairs={{4,6},{5,7},{12,14},{13,15},{20,22},{21,23},{28,30},{29,31}} | collective-permute-start | bytes 786440 | tf_op jit(solution)/shard_map/ppermute | solution.py:461
  39.5 10.8 %copy-start.6 = (bf16[128,1024]{1,0:T(8,128)(2,1)}, bf16[128,1024]{1,0:T(8,128)(2,1)S(1)}, u32[]{:S(2)}) copy-start(bf16[128,1024]{1,0:T(8,128)(2,1)S(1)} %collective-permute-done.5.refs_5_) | copy-start | bytes 786436
  42.0 8.3 %copy-start.7 = (bf16[128,1024]{1,0:T(8,128)(2,1)}, bf16[128,1024]{1,0:T(8,128)(2,1)S(1)}, u32[]{:S(2)}) copy-start(bf16[128,1024]{1,0:T(8,128)(2,1)S(1)} %collective-permute-done.4.refs_6_) | copy-start | bytes 786436
  42.0 8.3 %collective-permute-start.6 = (bf16[128,1024]{1,0:T(8,128)(2,1)S(1)}, bf16[128,1024]{1,0:T(8,128)(2,1)S(1)}, u32[]{:S(2)}, u32[]{:S(2)}) collective-permute-start(bf16[128,1024]{1,0:T(8,128)(2,1)S(1)} %collective-permute-done.4.refs_6_), channel_id=1, source_target_pairs={{6,7},{7,6},{14,15},{15,14},{22,23},{23,22},{30,31},{31,30}} | collective-permute-start | bytes 786440 | tf_op jit(solution)/shard_map/ppermute | solution.py:470
  45.4 43.3 %all-to-all-start.2 = ((bf16[8,40,2048]{2,1,0:T(8,128)(2,1)}), bf16[8,40,2048]{2,1,0:T(8,128)(2,1)S(1)}, u32[]{:S(2)}, u32[]{:S(2)}) async-start(bf16[8,40,2048]{2,1,0:T(8,128)(2,1)} %bitcast.25), calls=%async_computation.3 | async-start | bytes 2621440 | tf_op jit(solution)/shard_map/all_to_all | solution.py:500
  49.0 58.1 %all-gather.5.cloned.1.call-start = ((), (), s32[]{:S(2)}) async-start(), calls=%async_computation.6 | async-start | bytes 1310720 | tf_op jit(solution)/shard_map/all_gather | solution.py:495
  50.3 0.7 copy-start.8
  57.1 22.4 %collective-permute-start.7 = (bf16[512,256]{1,0:T(8,128)(2,1)}, bf16[512,256]{1,0:T(8,128)(2,1)S(1)}, u32[]{:S(2)}, u32[]{:S(2)}) collective-permute-start(bf16[512,256]{1,0:T(8,128)(2,1)} %get-tuple-element.54), channel_id=1, source_target_pairs={{0,1},{1,0},{2,3},{3,2},{4,5},{5,4},{6,7},{7,6},{8,9},{9,8},{10,11... | collective-permute-start | bytes 786440 | tf_op jit(solution)/shard_map/ppermute | solution.py:510
  64.7 14.9 %collective-permute-start.8 = (bf16[512,256]{1,0:T(8,128)(2,1)}, bf16[512,256]{1,0:T(8,128)(2,1)S(1)}, u32[]{:S(2)}, u32[]{:S(2)}) collective-permute-start(bf16[512,256]{1,0:T(8,128)(2,1)} %get-tuple-element.55), channel_id=1, source_target_pairs={{0,1},{1,0},{2,3},{3,2},{4,5},{5,4},{6,7},{7,6},{8,9},{9,8},{10,11... | collective-permute-start | bytes 786440 | tf_op jit(solution)/shard_map/ppermute | solution.py:510
  71.3 12.3 %collective-permute-start.9 = (bf16[512,256]{1,0:T(8,128)(2,1)}, bf16[512,256]{1,0:T(8,128)(2,1)S(1)}, u32[]{:S(2)}, u32[]{:S(2)}) collective-permute-start(bf16[512,256]{1,0:T(8,128)(2,1)} %get-tuple-element.56), channel_id=1, source_target_pairs={{0,1},{1,0},{2,3},{3,2},{4,5},{5,4},{6,7},{7,6},{8,9},{9,8},{10,11... | collective-permute-start | bytes 786440 | tf_op jit(solution)/shard_map/ppermute | solution.py:510
  79.0 9.7 %collective-permute-start.10 = (bf16[512,256]{1,0:T(8,128)(2,1)}, bf16[512,256]{1,0:T(8,128)(2,1)S(1)}, u32[]{:S(2)}, u32[]{:S(2)}) collective-permute-start(bf16[512,256]{1,0:T(8,128)(2,1)} %get-tuple-element.57), channel_id=1, source_target_pairs={{0,1},{1,0},{2,3},{3,2},{4,5},{5,4},{6,7},{7,6},{8,9},{9,8},{10,11... | collective-permute-start | bytes 786440 | tf_op jit(solution)/shard_map/ppermute | solution.py:510
  79.5 4.0 %copy-start.9 = (bf16[512,256]{1,0:T(8,128)(2,1)}, bf16[512,256]{1,0:T(8,128)(2,1)S(1)}, u32[]{:S(2)}) copy-start(bf16[512,256]{1,0:T(8,128)(2,1)S(1)} %collective-permute-done.7.refs_7_.refs_1_) | copy-start | bytes 786436
  79.6 4.0 %copy-start.10 = (bf16[512,256]{1,0:T(8,128)(2,1)}, bf16[512,256]{1,0:T(8,128)(2,1)S(1)}, u32[]{:S(2)}) copy-start(bf16[512,256]{1,0:T(8,128)(2,1)S(1)} %collective-permute-done.8.refs_8_.refs_3_) | copy-start | bytes 786436
  83.5 0.7 copy-start.11
  88.7 0.7 copy-start.12
  88.7 1.2 copy-start.1
  89.9 28.3 %all-to-all-start = ((bf16[8,120,1024]{2,1,0:T(8,128)(2,1)}), bf16[8,120,1024]{2,1,0:T(8,128)(2,1)S(1)}, u32[]{:S(2)}, u32[]{:S(2)}) async-start(bf16[8,120,1024]{2,1,0:T(8,128)(2,1)} %bitcast.13), calls=%async_computation.1 | async-start | bytes 3932160 | tf_op jit(solution)/shard_map/all_to_all | solution.py:500
  93.5 43.8 %reduce-scatter.2.cloned.1.call-start = ((), (), s32[]{:S(2)}) async-start(), calls=%async_computation.5 | async-start | bytes 1310720 | tf_op jit(solution)/shard_map/reduce_scatter | solution.py:529
  118.2 1.3 copy-start
  119.5 29.1 %all-to-all-start.1 = ((bf16[8,120,1024]{2,1,0:T(8,128)(2,1)}), bf16[8,120,1024]{2,1,0:T(8,128)(2,1)}, u32[]{:S(2)}, u32[]{:S(2)}) async-start(bf16[8,120,1024]{2,1,0:T(8,128)(2,1)} %bitcast.14), calls=%async_computation.2 | async-start | bytes 3932160 | tf_op jit(solution)/shard_map/all_to_all | solution.py:500
Sparse Core Ops, SparseCore 0:
  42.1 29.6 all-gather.2
  79.7 27.4 all-gather.4
  109.5 25.7 reduce-scatter.1

commit v10 on v8

--- a/solution.py
+++ b/solution.py
@@ -489,7 +489,7 @@
             columns[-1], own_picked = lax.optimization_barrier((columns[-1], own_picked))
         columns.append(along_z(columns[-1], [(i, i + 1) for i in range(k - 1, n_z - 1)]))
     columns[-1], others[-1] = lax.optimization_barrier((columns[-1], others[-1]))
-    first_half, columns[-1] = lax.optimization_barrier((own_halves[0], columns[-1]))
+    first_half, columns[n_z // 2] = lax.optimization_barrier((own_halves[0], columns[n_z // 2]))
     others.append(across_x(n_z - 1))
     blocks = [block for pair in zip(columns, others) for block in pair]
 
@@ -547,7 +547,9 @@
     total, base, hidden_grad = lax.optimization_barrier((total, base, hidden_grad))
     last = [cross(total[:, -others[1].shape[1] :])] if others else []
     key_grad, value_grad = finish(counts, total, last, base)
-    hidden_grad = expert_rows(place, got_last, rest, w_down, *sizes, base, hidden_grad)
+    hidden_grad = expert_rows(
+        place, got_last, rest, w_down, *sizes, base, hidden_grad, (key_grad,)
+    )
     return (query_grad[None], key_grad, value_grad, hidden_grad)
 
 

time: 160 us -> 155 us (0.969)
  waiting for transfers between devices: 57.8 us -> 51.4 us
    all_gather x2, waiting for transfers between devices: 42.3 us -> 32.4 us  [per_device(): lax.all_gather(half, 'ctx', axis=0, tiled=True, axis_index_groups=line_gr...]
    ppermute x2, waiting for transfers between devices: 0.01 us -> 3.61 us  [cross(): return lax.ppermute(array, 'ctx', [(i, i ^ 1) for i in range(n_ctx)])]
  transfers between devices with their start and end apart: 15 -> 15, of which waited for: 5 -> 6; matrix products, arithmetic and copies ran while one was open for 1% -> 1% of each run, Pallas kernels for 32% -> 29%
where the time goes in v10:
time: 155 us; the launch traced here: 153 us
  Pallas kernels  54.5 us (35%)
  waiting for transfers between devices  51.4 us (33%)
  starting transfers between devices  27.2 us (18%)
  between operations  14 us (9%)
  local copies, waits for them, and re-layouts  4.82 us (3%)
    all_gather x2, waiting for transfers between devices, per_device(): lax.all_gather(half, 'ctx', axis=0, tiled=True, axis_index_groups=line_gr...  32.4 us
    pallas_call x2, Pallas kernels, expert_rows(): pl.pallas_call(functools.partial(expert_kernel, ks, bool(extra), n_z, n_d...  14.5 us
    reduce_scatter x1, waiting for transfers between devices, per_device(): lax.psum_scatter(fold(mine, crossed, others), 'ctx', scatter_dimension=0,...  13.3 us
    pallas_call x2, Pallas kernels, attention(): pl.pallas_call(functools.partial(attention_kernel, n_blocks, heads_step,...  13.1 us
    all_to_all x3, starting transfers between devices, exchange(): lax.all_to_all(picked, ('dp', 'ctx'), split_axis=0, concat_axis=0, tiled=...  11.8 us
    pallas_call x3, Pallas kernels, pick_rows(): pl.pallas_call(functools.partial(pick_kernel, len(ks), n_dp, capacity), g...  10.7 us
    pallas_call x1, Pallas kernels, partial_rows(): pl.pallas_call(partial_kernel, grid=(hid // step,), in_specs=[pl.BlockSpe...  6.98 us
    ppermute x3, starting transfers between devices, along_z(): return lax.ppermute(array, 'ctx', pairs)  6.27 us
  transfers between devices with their start and end apart: 15, of which 6 were waited for; matrix products, arithmetic and copies ran while one was open for 1% of the time, Pallas kernels for 29%

profile of v10, /device:TPU:0, one launch (start us, length us, event | category | flops | bytes accessed | tf_op | source)
XLA Modules:
  0.0 152.5 jit_solution(966199579088296898)
XLA Ops:
  7.2 1.7 %join.1.refs_0_ = bf16[128,1024]{1,0:T(8,128)(2,1)} custom-call(bf16[1,128,512]{2,1,0:T(8,128)(2,1)} %key_ref.1, bf16[1,128,512]{2,1,0:T(8,128)(2,1)} %value_ref.1), custom_call_target="tpu_custom_call" | custom-call | flops 1 | bytes 1 | tf_op jit(solution)/shard_map/join/pallas_call | solution.py:234
  8.9 4.9 %collective-permute-start = (bf16[128,1024]{1,0:T(8,128)(2,1)}, bf16[128,1024]{1,0:T(8,128)(2,1)S(1)}, u32[]{:S(2)}, u32[]{:S(2)}) collective-permute-start(bf16[128,1024]{1,0:T(8,128)(2,1)} %join.1.refs_0_), channel_id=1, source_target_pairs={{0,2},{1,3},{2,4},{3,5},{4,6},{5,7},{8,10},{9,11},{10,12},{11,13},... | collective-permute-start | bytes 786440 | tf_op jit(solution)/shard_map/ppermute | solution.py:468
  13.9 3.4 %collective-permute-start.2 = (bf16[128,1024]{1,0:T(8,128)(2,1)}, bf16[128,1024]{1,0:T(8,128)(2,1)S(1)}, u32[]{:S(2)}, u32[]{:S(2)}) collective-permute-start(bf16[128,1024]{1,0:T(8,128)(2,1)} %join.1.refs_0_), channel_id=1, source_target_pairs={{0,1},{2,3},{4,5},{6,7},{8,9},{10,11},{12,13},{14,15},{16,17},{18,... | collective-permute-start | bytes 786440 | tf_op jit(solution)/shard_map/ppermute | solution.py:477
  17.3 2.0 %slot_table.1 = (bf16[144,1024]{1,0:T(8,128)(2,1)}, bf16[128,1024]{1,0:T(8,128)(2,1)}) custom-call(bf16[128,2048]{1,0:T(8,128)(2,1)} %refs_1_.1, s32[8,128]{1,0:T(8,128)} %bitcast.23, bf16[8,128]{1,0:T(8,128)(2,1)} %bitcast.24, bf16[128,1024]{1,0:T(8,128)(2,1)} %join.1.refs_0_), custom_call_target="tpu_custom_call" | custom-call | flops 1 | bytes 1 | tf_op jit(solution)/shard_map/slot_table/pallas_call | solution.py:277
  20.4 0.7 collective-permute-start.3
  21.7 3.2 %pick_rows.3.refs_8_ = bf16[320,2048]{1,0:T(8,128)(2,1)} custom-call(s32[2]{0:T(128)} %pad_add_fusion.place, bf16[144,1024]{1,0:T(8,128)(2,1)} %get-tuple-element.45.refs_0_, bf16[128,2048]{1,0:T(8,128)(2,1)} %refs_1_.1, bf16[128,1024]{1,0:T(8,128)(2,1)} %copy-done.2), custom_call_target="tpu_custom_call" | custom-call | flops 1 | bytes 1 | tf_op jit(solution)/shard_map/pick_rows/pallas_call | solution.py:337
  25.0 0.7 collective-permute-start.4
  25.6 0.7 collective-permute-start.5
  26.4 0.7 collective-permute-start.6
  27.1 3.7 %all-to-all-start.1 = ((bf16[8,40,2048]{2,1,0:T(8,128)(2,1)}), bf16[8,40,2048]{2,1,0:T(8,128)(2,1)S(1)}, u32[]{:S(2)}, u32[]{:S(2)}) async-start(bf16[8,40,2048]{2,1,0:T(8,128)(2,1)} %bitcast.16), calls=%async_computation.2 | async-start | bytes 2621440 | tf_op jit(solution)/shard_map/all_to_all | solution.py:507
  30.8 0.7 all-gather.5.cloned.1.call-update
  32.3 6.5 %attention_backward.2 = (bf16[128,4096]{1,0:T(8,128)(2,1)}, bf16[512,512]{1,0:T(8,128)(2,1)}, bf16[512,512]{1,0:T(8,128)(2,1)}) custom-call(s32[2]{0:T(128)} %pad_add_fusion.place, bf16[128,4096]{1,0:T(8,128)(2,1)} %bitcast.19, bf16[128,4096]{1,0:T(8,128)(2,1)} %bitcast.21, bf16[128,1024]{1,0:T(8,128)(2,1)} %join.1.refs_0_, bf16[128,1024]{1,0:T(8,128)(2,1)} %copy-done.4, ...), custom_call_target="tpu_custom_call" | custom-call | flops 26843545600 | bytes 4194304 | tf_op jit(solution)/shard_map/attention_backward/pallas_call | solution.py:138
  38.8 2.1 %collective-permute-start.7 = (bf16[512,512]{1,0:T(8,128)(2,1)}, bf16[512,512]{1,0:T(8,128)(2,1)S(1)}, u32[]{:S(2)}, u32[]{:S(2)}) collective-permute-start(bf16[512,512]{1,0:T(8,128)(2,1)} %get-tuple-element.46), channel_id=1, source_target_pairs={{0,1},{1,0},{2,3},{3,2},{4,5},{5,4},{6,7},{7,6},{8,9},{9,8},{10,11... | collective-permute-start | bytes 1572872 | tf_op jit(solution)/shard_map/ppermute | solution.py:517
  40.9 6.6 %attention_backward.3 = (bf16[128,4096]{1,0:T(8,128)(2,1)}, bf16[512,512]{1,0:T(8,128)(2,1)}, bf16[512,512]{1,0:T(8,128)(2,1)}) custom-call(s32[2]{0:T(128)} %pad_add_fusion.place, bf16[128,4096]{1,0:T(8,128)(2,1)} %bitcast.20, bf16[128,4096]{1,0:T(8,128)(2,1)} %bitcast.22, bf16[128,1024]{1,0:T(8,128)(2,1)} %join.1.refs_0_, ...), custom_call_target="tpu_custom_call", output_to_operand_aliasing={{0}: (11, {})} | custom-call | flops 1 | bytes 1 | tf_op jit(solution)/shard_map/attention_backward/pallas_call | solution.py:138
  47.5 16.2 %all-gather.3.cloned.1.call-done.refs_0_.refs_1_.refs_2_.refs_3_.refs_4_.refs_5_ = bf16[576,1024]{1,0:T(8,128)(2,1)} async-done(((bf16[144,1024]{1,0:T(8,128)(2,1)}), bf16[576,1024]{1,0:T(8,128)(2,1)}) %all-gather.3.cloned.1.call-update) | async-done | bytes 1179664 | tf_op jit(solution)/shard_map/all_gather | solution.py:502
  63.7 3.7 %pick_rows.4.refs_6_ = bf16[960,1024]{1,0:T(8,128)(2,1)} custom-call(s32[2]{0:T(128)} %pad_add_fusion.place, bf16[576,1024]{1,0:T(8,128)(2,1)} %all-gather.3.cloned.1.call-done.refs_0_.refs_1_.refs_2_.refs_3_.refs_4_.refs_5_, bf16[576,1024]{1,0:T(8,128)(2,1)} %all-gather.3.cloned.1.call-done.refs_0_.refs_1_.refs_2_.refs_3_.refs_4_.refs_5_, ...), custom_call_target="tpu_custom_call" | custom-call | flops 1 | bytes 1 | tf_op jit(solution)/shard_map/pick_rows/pallas_call | solution.py:337
  67.4 0.8 copy-done.3
  68.6 3.7 %all-to-all-start = ((bf16[8,120,1024]{2,1,0:T(8,128)(2,1)}), bf16[8,120,1024]{2,1,0:T(8,128)(2,1)S(1)}, u32[]{:S(2)}, u32[]{:S(2)}) async-start(bf16[8,120,1024]{2,1,0:T(8,128)(2,1)} %bitcast.13), calls=%async_computation.1 | async-start | bytes 3932160 | tf_op jit(solution)/shard_map/all_to_all | solution.py:507
  72.3 3.8 %fold.1 = bf16[512,1536]{1,0:T(8,128)(2,1)} custom-call(bf16[512,512]{1,0:T(8,128)(2,1)} %get-tuple-element.44.mine_ref, bf16[512,512]{1,0:T(8,128)(2,1)} %copy-done.3, bf16[512,512]{1,0:T(8,128)(2,1)} %get-tuple-element.48.refs_1_, bf16[512,512]{1,0:T(8,128)(2,1)} %get-tuple-element.49.refs_2_), custom_call_target="tpu_custom_call" | custom-call | flops 1 | bytes 1 | tf_op jit(solution)/shard_map/fold/pallas_call | solution.py:186
  76.1 16.2 %all-gather.5.cloned.1.call-done.refs_3_.refs_4_.refs_5_ = bf16[512,1024]{1,0:T(8,128)(2,1)} async-done(((bf16[128,1024]{1,0:T(8,128)(2,1)}), bf16[512,1024]{1,0:T(8,128)(2,1)}) %all-gather.5.cloned.1.call-update) | async-done | bytes 1048592 | tf_op jit(solution)/shard_map/all_gather | solution.py:502
  92.3 3.8 %pick_rows.5.refs_0_ = bf16[960,1024]{1,0:T(8,128)(2,1)} custom-call(s32[2]{0:T(128)} %pad_add_fusion.place, bf16[576,1024]{1,0:T(8,128)(2,1)} %all-gather.3.cloned.1.call-done.refs_0_.refs_1_.refs_2_.refs_3_.refs_4_.refs_5_, bf16[576,1024]{1,0:T(8,128)(2,1)} %all-gather.3.cloned.1.call-done.refs_0_.refs_1_.refs_2_.refs_3_.refs_4_.refs_5_, ...), custom_call_target="tpu_custom_call" | custom-call | flops 1 | bytes 1 | tf_op jit(solution)/shard_map/pick_rows/pallas_call | solution.py:337
  96.1 0.9 all-to-all-done
  97.0 1.3 copy-done
  98.4 4.4 %all-to-all-start.2 = ((bf16[8,120,1024]{2,1,0:T(8,128)(2,1)}), bf16[8,120,1024]{2,1,0:T(8,128)(2,1)}, u32[]{:S(2)}, u32[]{:S(2)}) async-start(bf16[8,120,1024]{2,1,0:T(8,128)(2,1)} %bitcast.14), calls=%async_computation.3 | async-start | bytes 3932160 | tf_op jit(solution)/shard_map/all_to_all | solution.py:507
  102.7 6.4 %expert_rows.2.refs_1_ = bf16[1,32,40,1536]{3,2,1,0:T(8,128)(2,1)} custom-call(s32[2]{0:T(128)} %pad_add_fusion.place, bf16[320,2048]{1,0:T(8,128)(2,1)} %bitcast.17, bf16[1,1536,2048]{2,1,0:T(8,128)(2,1)} %w_ref.5, bf16[960,1024]{1,0:T(8,128)(2,1)} %pick_rows.5.refs_0_), custom_call_target="tpu_custom_call" | custom-call | flops 1 | bytes 1 | tf_op jit(solution)/shard_map/expert_rows/pallas_call | solution.py:419
  109.2 7.0 %partial_rows.1.refs_1_.refs_0_ = bf16[960,1536]{1,0:T(8,128)(2,1)} custom-call(bf16[960,1024]{1,0:T(8,128)(2,1)} %bitcast.15, bf16[1,1536,2048]{2,1,0:T(8,128)(2,1)} %w_ref.5), custom_call_target="tpu_custom_call" | custom-call | flops 1 | bytes 1 | tf_op jit(solution)/shard_map/partial_rows/pallas_call | solution.py:365
  116.2 13.3 %reduce-scatter.2.cloned.1.call-done.total_ref = bf16[128,1536]{1,0:T(8,128)(2,1)} async-done(((bf16[512,1536]{1,0:T(8,128)(2,1)}), bf16[128,1536]{1,0:T(8,128)(2,1)}) %reduce-scatter.2.cloned.1.call-update) | async-done | bytes 393232 | tf_op jit(solution)/shard_map/reduce_scatter | solution.py:537
  129.4 0.9 slice.3
  130.4 1.5 collective-permute-start.8
  131.9 3.6 %collective-permute-done.8.refs_0_ = bf16[128,512]{1,0:T(8,128)(2,1)S(1)} collective-permute-done((bf16[128,512]{1,0:T(8,128)(2,1)S(1)}, bf16[128,512]{1,0:T(8,128)(2,1)S(1)}, u32[]{:S(2)}, u32[]{:S(2)}) %collective-permute-start.8) | collective-permute-done | bytes 131104 | tf_op jit(solution)/shard_map/ppermute | solution.py:517
  136.1 1.8 %finish.1 = (bf16[1,128,512]{2,1,0:T(8,128)(2,1)}, bf16[1,128,512]{2,1,0:T(8,128)(2,1)}) custom-call(bf16[128,1536]{1,0:T(8,128)(2,1)} %reduce-scatter.2.cloned.1.call-done.total_ref, bf16[128,512]{1,0:T(8,128)(2,1)} %copy-done.10, bf16[960,1536]{1,0:T(8,128)(2,1)} %partial_rows.1.refs_1_.refs_0_), custom_call_target="tpu_custom_call" | custom-call | flops 1 | bytes 1 | tf_op jit(solution)/shard_map/finish/pallas_call | solution.py:214
  137.9 8.1 %expert_rows.3 = bf16[1,32,40,1536]{3,2,1,0:T(8,128)(2,1)} custom-call(s32[2]{0:T(128)} %pad_add_fusion.place, bf16[960,1024]{1,0:T(8,128)(2,1)} %bitcast.12.rows_ref, bf16[1,1536,2048]{2,1,0:T(8,128)(2,1)} %w_ref.5, bf16[960,1536]{1,0:T(8,128)(2,1)} %partial_rows.1.refs_1_.refs_0_, ...), custom_call_target="tpu_custom_call", output_to_operand_aliasing={{}: (4, {})} | custom-call | flops 1 | bytes 1 | tf_op jit(solution)/shard_map/expert_rows/pallas_call | solution.py:419
  (37 shorter events, 3.7 us)
Async XLA Ops:
  7.2 56.5 %all-gather.3.cloned.1.call-start = ((), (), s32[]{:S(2)}) async-start(), calls=%async_computation.4 | async-start | bytes 1474560 | tf_op jit(solution)/shard_map/all_gather | solution.py:502
  8.9 10.8 %collective-permute-start = (bf16[128,1024]{1,0:T(8,128)(2,1)}, bf16[128,1024]{1,0:T(8,128)(2,1)S(1)}, u32[]{:S(2)}, u32[]{:S(2)}) collective-permute-start(bf16[128,1024]{1,0:T(8,128)(2,1)} %join.1.refs_0_), channel_id=1, source_target_pairs={{0,2},{1,3},{2,4},{3,5},{4,6},{5,7},{8,10},{9,11},{10,12},{11,13},... | collective-permute-start | bytes 786440 | tf_op jit(solution)/shard_map/ppermute | solution.py:468
  13.9 11.0 %collective-permute-start.2 = (bf16[128,1024]{1,0:T(8,128)(2,1)}, bf16[128,1024]{1,0:T(8,128)(2,1)S(1)}, u32[]{:S(2)}, u32[]{:S(2)}) collective-permute-start(bf16[128,1024]{1,0:T(8,128)(2,1)} %join.1.refs_0_), channel_id=1, source_target_pairs={{0,1},{2,3},{4,5},{6,7},{8,9},{10,11},{12,13},{14,15},{16,17},{18,... | collective-permute-start | bytes 786440 | tf_op jit(solution)/shard_map/ppermute | solution.py:477
  19.7 2.0 %copy-start.2 = (bf16[128,1024]{1,0:T(8,128)(2,1)}, bf16[128,1024]{1,0:T(8,128)(2,1)S(1)}, u32[]{:S(2)}) copy-start(bf16[128,1024]{1,0:T(8,128)(2,1)S(1)} %collective-permute-done.refs_2_) | copy-start | bytes 786436
  19.7 5.2 %collective-permute-start.1 = (bf16[128,1024]{1,0:T(8,128)(2,1)S(1)}, bf16[128,1024]{1,0:T(8,128)(2,1)S(1)}, u32[]{:S(2)}, u32[]{:S(2)}) collective-permute-start(bf16[128,1024]{1,0:T(8,128)(2,1)S(1)} %collective-permute-done.refs_2_), channel_id=1, source_target_pairs={{2,4},{3,5},{4,6},{5,7},{10,12},{11,13},{12,14},{13,15},{18,20},{1... | collective-permute-start | bytes 786440 | tf_op jit(solution)/shard_map/ppermute | solution.py:468
  20.4 4.5 %collective-permute-start.3 = (bf16[128,1024]{1,0:T(8,128)(2,1)S(1)}, bf16[128,1024]{1,0:T(8,128)(2,1)S(1)}, u32[]{:S(2)}, u32[]{:S(2)}) collective-permute-start(bf16[128,1024]{1,0:T(8,128)(2,1)S(1)} %collective-permute-done.refs_2_), channel_id=1, source_target_pairs={{2,3},{3,2},{4,5},{5,4},{6,7},{7,6},{10,11},{11,10},{12,13},{13,12... | collective-permute-start | bytes 786440 | tf_op jit(solution)/shard_map/ppermute | solution.py:477
  24.9 6.7 %copy-start.4 = (bf16[128,1024]{1,0:T(8,128)(2,1)}, bf16[128,1024]{1,0:T(8,128)(2,1)S(1)}, u32[]{:S(2)}) copy-start(bf16[128,1024]{1,0:T(8,128)(2,1)S(1)} %collective-permute-done.2.refs_1_) | copy-start | bytes 786436
  24.9 6.7 %copy-start.5 = (bf16[128,1024]{1,0:T(8,128)(2,1)}, bf16[128,1024]{1,0:T(8,128)(2,1)S(1)}, u32[]{:S(2)}) copy-start(bf16[128,1024]{1,0:T(8,128)(2,1)S(1)} %collective-permute-done.1.refs_4_) | copy-start | bytes 786436
  24.9 6.7 %copy-start.6 = (bf16[128,1024]{1,0:T(8,128)(2,1)}, bf16[128,1024]{1,0:T(8,128)(2,1)S(1)}, u32[]{:S(2)}) copy-start(bf16[128,1024]{1,0:T(8,128)(2,1)S(1)} %collective-permute-done.3.refs_3_) | copy-start | bytes 786436
  25.0 1.4 collective-permute-start.4
  25.6 0.7 collective-permute-start.5
  26.3 5.2 %copy-start.7 = (bf16[128,1024]{1,0:T(8,128)(2,1)}, bf16[128,1024]{1,0:T(8,128)(2,1)S(1)}, u32[]{:S(2)}) copy-start(bf16[128,1024]{1,0:T(8,128)(2,1)S(1)} %collective-permute-done.4.refs_6_) | copy-start | bytes 786436
  26.4 5.2 %copy-start.8 = (bf16[128,1024]{1,0:T(8,128)(2,1)}, bf16[128,1024]{1,0:T(8,128)(2,1)S(1)}, u32[]{:S(2)}) copy-start(bf16[128,1024]{1,0:T(8,128)(2,1)S(1)} %collective-permute-done.5.refs_5_) | copy-start | bytes 786436
  26.4 5.2 %collective-permute-start.6 = (bf16[128,1024]{1,0:T(8,128)(2,1)S(1)}, bf16[128,1024]{1,0:T(8,128)(2,1)S(1)}, u32[]{:S(2)}, u32[]{:S(2)}) collective-permute-start(bf16[128,1024]{1,0:T(8,128)(2,1)S(1)} %collective-permute-done.4.refs_6_), channel_id=1, source_target_pairs={{6,7},{7,6},{14,15},{15,14},{22,23},{23,22},{30,31},{31,30}} | collective-permute-start | bytes 786440 | tf_op jit(solution)/shard_map/ppermute | solution.py:477
  27.1 40.3 %all-to-all-start.1 = ((bf16[8,40,2048]{2,1,0:T(8,128)(2,1)}), bf16[8,40,2048]{2,1,0:T(8,128)(2,1)S(1)}, u32[]{:S(2)}, u32[]{:S(2)}) async-start(bf16[8,40,2048]{2,1,0:T(8,128)(2,1)} %bitcast.16), calls=%async_computation.2 | async-start | bytes 2621440 | tf_op jit(solution)/shard_map/all_to_all | solution.py:507
  30.8 61.5 %all-gather.5.cloned.1.call-start = ((), (), s32[]{:S(2)}) async-start(), calls=%async_computation.6 | async-start | bytes 1310720 | tf_op jit(solution)/shard_map/all_gather | solution.py:502
  31.5 0.7 copy-start.9
  38.8 28.6 %collective-permute-start.7 = (bf16[512,512]{1,0:T(8,128)(2,1)}, bf16[512,512]{1,0:T(8,128)(2,1)S(1)}, u32[]{:S(2)}, u32[]{:S(2)}) collective-permute-start(bf16[512,512]{1,0:T(8,128)(2,1)} %get-tuple-element.46), channel_id=1, source_target_pairs={{0,1},{1,0},{2,3},{3,2},{4,5},{5,4},{6,7},{7,6},{8,9},{9,8},{10,11... | collective-permute-start | bytes 1572872 | tf_op jit(solution)/shard_map/ppermute | solution.py:517
  67.4 0.8 copy-start.3
  67.4 1.2 copy-start.1
  68.6 28.4 %all-to-all-start = ((bf16[8,120,1024]{2,1,0:T(8,128)(2,1)}), bf16[8,120,1024]{2,1,0:T(8,128)(2,1)S(1)}, u32[]{:S(2)}, u32[]{:S(2)}) async-start(bf16[8,120,1024]{2,1,0:T(8,128)(2,1)} %bitcast.13), calls=%async_computation.1 | async-start | bytes 3932160 | tf_op jit(solution)/shard_map/all_to_all | solution.py:507
  72.3 57.2 %reduce-scatter.2.cloned.1.call-start = ((), (), s32[]{:S(2)}) async-start(), calls=%async_computation.5 | async-start | bytes 1966080 | tf_op jit(solution)/shard_map/reduce_scatter | solution.py:537
  97.0 1.3 copy-start
  98.4 39.5 %all-to-all-start.2 = ((bf16[8,120,1024]{2,1,0:T(8,128)(2,1)}), bf16[8,120,1024]{2,1,0:T(8,128)(2,1)}, u32[]{:S(2)}, u32[]{:S(2)}) async-start(bf16[8,120,1024]{2,1,0:T(8,128)(2,1)} %bitcast.14), calls=%async_computation.3 | async-start | bytes 3932160 | tf_op jit(solution)/shard_map/all_to_all | solution.py:507
  130.4 5.1 %collective-permute-start.8 = (bf16[128,512]{1,0:T(8,128)(2,1)S(1)}, bf16[128,512]{1,0:T(8,128)(2,1)S(1)}, u32[]{:S(2)}, u32[]{:S(2)}) collective-permute-start(bf16[128,512]{1,0:T(8,128)(2,1)S(1)} %slice.3), channel_id=1, source_target_pairs={{0,1},{1,0},{2,3},{3,2},{4,5},{5,4},{6,7},{7,6},{8,9},{9,8},{10,11... | collective-permute-start | bytes 393224 | tf_op jit(solution)/shard_map/ppermute | solution.py:517
  135.5 0.7 copy-start.10
Sparse Core Ops, SparseCore 0:
  25.1 38.5 all-gather.2
  65.2 27.0 all-gather.4
  94.6 34.7 reduce-scatter.1

commit v11 on v10

--- a/solution.py
+++ b/solution.py
@@ -524,14 +524,14 @@
         place, queries[0], out_grad[0], blocks, 0, counts[0], None, (own_picked,)
     )
     crossed = cross(other)
+    picked = pick(all_halves[0], all_halves[0], rest, (query_grad,))
+    picked, crossed = lax.optimization_barrier((picked, crossed))
+    got_first = exchange(picked)
     others = []
     if len(counts) > 1:
         query_grad, *others = attention(
-            place, queries[0], out_grad[0], blocks, counts[0], counts[1], query_grad
+            place, queries[0], out_grad[0], blocks, counts[0], counts[1], query_grad, (picked,)
         )
-    picked = pick(all_halves[0], all_halves[0], rest, (query_grad,))
-    picked, crossed = lax.optimization_barrier((picked, crossed))
-    got_first = exchange(picked)
     picked = pick(all_halves[0], all_halves[1], rest, (picked,))
     got_last = exchange(picked)
     total = lax.psum_scatter(

time: 155 us -> 156 us (level)
  waiting for transfers between devices: 51.4 us -> 53.9 us
    reduce_scatter x1, waiting for transfers between devices: 13.3 us -> 15.7 us  [per_device(): lax.psum_scatter(fold(mine, crossed, others), 'ctx', scatter_dimension=0,...]
where the time goes in v11:
time: 156 us; the launch traced here: 155 us
  Pallas kernels  54.5 us (35%)
  waiting for transfers between devices  53.9 us (35%)
  starting transfers between devices  27.2 us (17%)
  between operations  14 us (9%)
  local copies, waits for them, and re-layouts  4.86 us (3%)
    all_gather x2, waiting for transfers between devices, per_device(): lax.all_gather(half, 'ctx', axis=0, tiled=True, axis_index_groups=line_gr...  32.4 us
    reduce_scatter x1, waiting for transfers between devices, per_device(): lax.psum_scatter(fold(mine, crossed, others), 'ctx', scatter_dimension=0,...  15.7 us
    pallas_call x2, Pallas kernels, expert_rows(): pl.pallas_call(functools.partial(expert_kernel, ks, bool(extra), n_z, n_d...  14.5 us
    pallas_call x2, Pallas kernels, attention(): pl.pallas_call(functools.partial(attention_kernel, n_blocks, heads_step,...  13.1 us
    all_to_all x3, starting transfers between devices, exchange(): lax.all_to_all(picked, ('dp', 'ctx'), split_axis=0, concat_axis=0, tiled=...  11.7 us
    pallas_call x3, Pallas kernels, pick_rows(): pl.pallas_call(functools.partial(pick_kernel, len(ks), n_dp, capacity), g...  10.7 us
    pallas_call x1, Pallas kernels, partial_rows(): pl.pallas_call(partial_kernel, grid=(hid // step,), in_specs=[pl.BlockSpe...  6.97 us
    ppermute x3, starting transfers between devices, along_z(): return lax.ppermute(array, 'ctx', pairs)  6.27 us
  transfers between devices with their start and end apart: 15, of which 6 were waited for; matrix products, arithmetic and copies ran while one was open for 1% of the time, Pallas kernels for 29%

profile of v11, /device:TPU:0, one launch (start us, length us, event | category | flops | bytes accessed | tf_op | source)
XLA Modules:
  0.0 155.0 jit_solution(9914097917523180242)
XLA Ops:
  7.2 1.7 %join.1.refs_0_ = bf16[128,1024]{1,0:T(8,128)(2,1)} custom-call(bf16[1,128,512]{2,1,0:T(8,128)(2,1)} %key_ref.1, bf16[1,128,512]{2,1,0:T(8,128)(2,1)} %value_ref.1), custom_call_target="tpu_custom_call" | custom-call | flops 1 | bytes 1 | tf_op jit(solution)/shard_map/join/pallas_call | solution.py:234
  8.9 4.9 %collective-permute-start = (bf16[128,1024]{1,0:T(8,128)(2,1)}, bf16[128,1024]{1,0:T(8,128)(2,1)S(1)}, u32[]{:S(2)}, u32[]{:S(2)}) collective-permute-start(bf16[128,1024]{1,0:T(8,128)(2,1)} %join.1.refs_0_), channel_id=1, source_target_pairs={{0,2},{1,3},{2,4},{3,5},{4,6},{5,7},{8,10},{9,11},{10,12},{11,13},... | collective-permute-start | bytes 786440 | tf_op jit(solution)/shard_map/ppermute | solution.py:468
  13.9 3.4 %collective-permute-start.2 = (bf16[128,1024]{1,0:T(8,128)(2,1)}, bf16[128,1024]{1,0:T(8,128)(2,1)S(1)}, u32[]{:S(2)}, u32[]{:S(2)}) collective-permute-start(bf16[128,1024]{1,0:T(8,128)(2,1)} %join.1.refs_0_), channel_id=1, source_target_pairs={{0,1},{2,3},{4,5},{6,7},{8,9},{10,11},{12,13},{14,15},{16,17},{18,... | collective-permute-start | bytes 786440 | tf_op jit(solution)/shard_map/ppermute | solution.py:477
  17.3 2.0 %slot_table.1 = (bf16[144,1024]{1,0:T(8,128)(2,1)}, bf16[128,1024]{1,0:T(8,128)(2,1)}) custom-call(bf16[128,2048]{1,0:T(8,128)(2,1)} %refs_1_.1, s32[8,128]{1,0:T(8,128)} %bitcast.23, bf16[8,128]{1,0:T(8,128)(2,1)} %bitcast.24, bf16[128,1024]{1,0:T(8,128)(2,1)} %join.1.refs_0_), custom_call_target="tpu_custom_call" | custom-call | flops 1 | bytes 1 | tf_op jit(solution)/shard_map/slot_table/pallas_call | solution.py:277
  20.4 0.7 collective-permute-start.3
  21.7 3.2 %pick_rows.3.refs_8_ = bf16[320,2048]{1,0:T(8,128)(2,1)} custom-call(s32[2]{0:T(128)} %pad_add_fusion.place, bf16[144,1024]{1,0:T(8,128)(2,1)} %get-tuple-element.43.refs_0_, bf16[128,2048]{1,0:T(8,128)(2,1)} %refs_1_.1, bf16[128,1024]{1,0:T(8,128)(2,1)} %copy-done.2), custom_call_target="tpu_custom_call" | custom-call | flops 1 | bytes 1 | tf_op jit(solution)/shard_map/pick_rows/pallas_call | solution.py:337
  25.0 0.7 collective-permute-start.4
  25.6 0.7 collective-permute-start.5
  26.4 0.7 collective-permute-start.6
  27.1 3.7 %all-to-all-start.1 = ((bf16[8,40,2048]{2,1,0:T(8,128)(2,1)}), bf16[8,40,2048]{2,1,0:T(8,128)(2,1)S(1)}, u32[]{:S(2)}, u32[]{:S(2)}) async-start(bf16[8,40,2048]{2,1,0:T(8,128)(2,1)} %bitcast.16), calls=%async_computation.2 | async-start | bytes 2621440 | tf_op jit(solution)/shard_map/all_to_all | solution.py:507
  30.8 0.7 all-gather.5.cloned.1.call-update
  32.3 6.5 %attention_backward.2 = (bf16[128,4096]{1,0:T(8,128)(2,1)}, bf16[512,512]{1,0:T(8,128)(2,1)}, bf16[512,512]{1,0:T(8,128)(2,1)}) custom-call(s32[2]{0:T(128)} %pad_add_fusion.place, bf16[128,4096]{1,0:T(8,128)(2,1)} %bitcast.19, bf16[128,4096]{1,0:T(8,128)(2,1)} %bitcast.21, bf16[128,1024]{1,0:T(8,128)(2,1)} %join.1.refs_0_, bf16[128,1024]{1,0:T(8,128)(2,1)} %copy-done.4, ...), custom_call_target="tpu_custom_call" | custom-call | flops 26843545600 | bytes 4194304 | tf_op jit(solution)/shard_map/attention_backward/pallas_call | solution.py:138
  38.8 2.1 %collective-permute-start.7 = (bf16[512,512]{1,0:T(8,128)(2,1)}, bf16[512,512]{1,0:T(8,128)(2,1)S(1)}, u32[]{:S(2)}, u32[]{:S(2)}) collective-permute-start(bf16[512,512]{1,0:T(8,128)(2,1)} %get-tuple-element.44), channel_id=1, source_target_pairs={{0,1},{1,0},{2,3},{3,2},{4,5},{5,4},{6,7},{7,6},{8,9},{9,8},{10,11... | collective-permute-start | bytes 1572872 | tf_op jit(solution)/shard_map/ppermute | solution.py:517
  40.9 22.8 %all-gather.3.cloned.1.call-done.refs_0_.refs_1_.refs_2_.refs_3_.refs_4_.refs_5_ = bf16[576,1024]{1,0:T(8,128)(2,1)} async-done(((bf16[144,1024]{1,0:T(8,128)(2,1)}), bf16[576,1024]{1,0:T(8,128)(2,1)}) %all-gather.3.cloned.1.call-update) | async-done | bytes 1179664 | tf_op jit(solution)/shard_map/all_gather | solution.py:502
  63.7 3.7 %pick_rows.4.refs_9_.refs_6_ = bf16[960,1024]{1,0:T(8,128)(2,1)} custom-call(s32[2]{0:T(128)} %pad_add_fusion.place, bf16[576,1024]{1,0:T(8,128)(2,1)} %all-gather.3.cloned.1.call-done.refs_0_.refs_1_.refs_2_.refs_3_.refs_4_.refs_5_, bf16[576,1024]{1,0:T(8,128)(2,1)} %all-gather.3.cloned.1.call-done.refs_0_.refs_1_.refs_2_.refs_3_.refs_4_.refs_5_, ...), custom_call_target="tpu_custom_call" | custom-call | flops 1 | bytes 1 | tf_op jit(solution)/shard_map/pick_rows/pallas_call | solution.py:337
  67.4 0.8 copy-done.3
  68.7 3.7 %all-to-all-start = ((bf16[8,120,1024]{2,1,0:T(8,128)(2,1)}), bf16[8,120,1024]{2,1,0:T(8,128)(2,1)S(1)}, u32[]{:S(2)}, u32[]{:S(2)}) async-start(bf16[8,120,1024]{2,1,0:T(8,128)(2,1)} %bitcast.13), calls=%async_computation.1 | async-start | bytes 3932160 | tf_op jit(solution)/shard_map/all_to_all | solution.py:507
  72.4 6.6 %attention_backward.3 = (bf16[128,4096]{1,0:T(8,128)(2,1)}, bf16[512,512]{1,0:T(8,128)(2,1)}, bf16[512,512]{1,0:T(8,128)(2,1)}) custom-call(s32[2]{0:T(128)} %pad_add_fusion.place, bf16[128,4096]{1,0:T(8,128)(2,1)} %bitcast.20, bf16[128,4096]{1,0:T(8,128)(2,1)} %bitcast.22, bf16[128,1024]{1,0:T(8,128)(2,1)} %join.1.refs_0_, ...), custom_call_target="tpu_custom_call", output_to_operand_aliasing={{0}: (11, {})} | custom-call | flops 1 | bytes 1 | tf_op jit(solution)/shard_map/attention_backward/pallas_call | solution.py:138
  78.9 3.8 %fold.1 = bf16[512,1536]{1,0:T(8,128)(2,1)} custom-call(bf16[512,512]{1,0:T(8,128)(2,1)} %get-tuple-element.47.mine_ref, bf16[512,512]{1,0:T(8,128)(2,1)} %copy-done.3, bf16[512,512]{1,0:T(8,128)(2,1)} %get-tuple-element.49.refs_1_, bf16[512,512]{1,0:T(8,128)(2,1)} %get-tuple-element.50.refs_2_), custom_call_target="tpu_custom_call" | custom-call | flops 1 | bytes 1 | tf_op jit(solution)/shard_map/fold/pallas_call | solution.py:186
  82.7 9.6 %all-gather.5.cloned.1.call-done.refs_3_.refs_4_.refs_5_ = bf16[512,1024]{1,0:T(8,128)(2,1)} async-done(((bf16[128,1024]{1,0:T(8,128)(2,1)}), bf16[512,1024]{1,0:T(8,128)(2,1)}) %all-gather.5.cloned.1.call-update) | async-done | bytes 1048592 | tf_op jit(solution)/shard_map/all_gather | solution.py:502
  92.3 3.8 %pick_rows.5.refs_0_ = bf16[960,1024]{1,0:T(8,128)(2,1)} custom-call(s32[2]{0:T(128)} %pad_add_fusion.place, bf16[576,1024]{1,0:T(8,128)(2,1)} %all-gather.3.cloned.1.call-done.refs_0_.refs_1_.refs_2_.refs_3_.refs_4_.refs_5_, bf16[576,1024]{1,0:T(8,128)(2,1)} %all-gather.3.cloned.1.call-done.refs_0_.refs_1_.refs_2_.refs_3_.refs_4_.refs_5_, ...), custom_call_target="tpu_custom_call" | custom-call | flops 1 | bytes 1 | tf_op jit(solution)/shard_map/pick_rows/pallas_call | solution.py:337
  96.1 1.0 all-to-all-done
  97.1 1.3 copy-done
  98.4 4.4 %all-to-all-start.2 = ((bf16[8,120,1024]{2,1,0:T(8,128)(2,1)}), bf16[8,120,1024]{2,1,0:T(8,128)(2,1)}, u32[]{:S(2)}, u32[]{:S(2)}) async-start(bf16[8,120,1024]{2,1,0:T(8,128)(2,1)} %bitcast.14), calls=%async_computation.3 | async-start | bytes 3932160 | tf_op jit(solution)/shard_map/all_to_all | solution.py:507
  102.8 6.4 %expert_rows.2.refs_1_ = bf16[1,32,40,1536]{3,2,1,0:T(8,128)(2,1)} custom-call(s32[2]{0:T(128)} %pad_add_fusion.place, bf16[320,2048]{1,0:T(8,128)(2,1)} %bitcast.17, bf16[1,1536,2048]{2,1,0:T(8,128)(2,1)} %w_ref.5, bf16[960,1024]{1,0:T(8,128)(2,1)} %pick_rows.5.refs_0_), custom_call_target="tpu_custom_call" | custom-call | flops 1 | bytes 1 | tf_op jit(solution)/shard_map/expert_rows/pallas_call | solution.py:419
  109.2 7.0 %partial_rows.1.refs_1_.refs_0_ = bf16[960,1536]{1,0:T(8,128)(2,1)} custom-call(bf16[960,1024]{1,0:T(8,128)(2,1)} %bitcast.15, bf16[1,1536,2048]{2,1,0:T(8,128)(2,1)} %w_ref.5), custom_call_target="tpu_custom_call" | custom-call | flops 1 | bytes 1 | tf_op jit(solution)/shard_map/partial_rows/pallas_call | solution.py:365
  116.2 15.7 %reduce-scatter.2.cloned.1.call-done.total_ref = bf16[128,1536]{1,0:T(8,128)(2,1)} async-done(((bf16[512,1536]{1,0:T(8,128)(2,1)}), bf16[128,1536]{1,0:T(8,128)(2,1)}) %reduce-scatter.2.cloned.1.call-update) | async-done | bytes 393232 | tf_op jit(solution)/shard_map/reduce_scatter | solution.py:537
  131.9 0.9 slice.3
  132.8 1.5 collective-permute-start.8
  134.3 3.6 %collective-permute-done.8.refs_0_ = bf16[128,512]{1,0:T(8,128)(2,1)S(1)} collective-permute-done((bf16[128,512]{1,0:T(8,128)(2,1)S(1)}, bf16[128,512]{1,0:T(8,128)(2,1)S(1)}, u32[]{:S(2)}, u32[]{:S(2)}) %collective-permute-start.8) | collective-permute-done | bytes 131104 | tf_op jit(solution)/shard_map/ppermute | solution.py:517
  138.6 1.8 %finish.1 = (bf16[1,128,512]{2,1,0:T(8,128)(2,1)}, bf16[1,128,512]{2,1,0:T(8,128)(2,1)}) custom-call(bf16[128,1536]{1,0:T(8,128)(2,1)} %reduce-scatter.2.cloned.1.call-done.total_ref, bf16[128,512]{1,0:T(8,128)(2,1)} %copy-done.10, bf16[960,1536]{1,0:T(8,128)(2,1)} %partial_rows.1.refs_1_.refs_0_), custom_call_target="tpu_custom_call" | custom-call | flops 1 | bytes 1 | tf_op jit(solution)/shard_map/finish/pallas_call | solution.py:214
  140.4 8.1 %expert_rows.3 = bf16[1,32,40,1536]{3,2,1,0:T(8,128)(2,1)} custom-call(s32[2]{0:T(128)} %pad_add_fusion.place, bf16[960,1024]{1,0:T(8,128)(2,1)} %bitcast.12.rows_ref, bf16[1,1536,2048]{2,1,0:T(8,128)(2,1)} %w_ref.5, bf16[960,1536]{1,0:T(8,128)(2,1)} %partial_rows.1.refs_1_.refs_0_, ...), custom_call_target="tpu_custom_call", output_to_operand_aliasing={{}: (4, {})} | custom-call | flops 1 | bytes 1 | tf_op jit(solution)/shard_map/expert_rows/pallas_call | solution.py:419
  (37 shorter events, 3.7 us)
Async XLA Ops:
  7.2 56.5 %all-gather.3.cloned.1.call-start = ((), (), s32[]{:S(2)}) async-start(), calls=%async_computation.4 | async-start | bytes 1474560 | tf_op jit(solution)/shard_map/all_gather | solution.py:502
  8.9 10.8 %collective-permute-start = (bf16[128,1024]{1,0:T(8,128)(2,1)}, bf16[128,1024]{1,0:T(8,128)(2,1)S(1)}, u32[]{:S(2)}, u32[]{:S(2)}) collective-permute-start(bf16[128,1024]{1,0:T(8,128)(2,1)} %join.1.refs_0_), channel_id=1, source_target_pairs={{0,2},{1,3},{2,4},{3,5},{4,6},{5,7},{8,10},{9,11},{10,12},{11,13},... | collective-permute-start | bytes 786440 | tf_op jit(solution)/shard_map/ppermute | solution.py:468
  13.9 11.0 %collective-permute-start.2 = (bf16[128,1024]{1,0:T(8,128)(2,1)}, bf16[128,1024]{1,0:T(8,128)(2,1)S(1)}, u32[]{:S(2)}, u32[]{:S(2)}) collective-permute-start(bf16[128,1024]{1,0:T(8,128)(2,1)} %join.1.refs_0_), channel_id=1, source_target_pairs={{0,1},{2,3},{4,5},{6,7},{8,9},{10,11},{12,13},{14,15},{16,17},{18,... | collective-permute-start | bytes 786440 | tf_op jit(solution)/shard_map/ppermute | solution.py:477
  19.7 2.0 %copy-start.2 = (bf16[128,1024]{1,0:T(8,128)(2,1)}, bf16[128,1024]{1,0:T(8,128)(2,1)S(1)}, u32[]{:S(2)}) copy-start(bf16[128,1024]{1,0:T(8,128)(2,1)S(1)} %collective-permute-done.refs_2_) | copy-start | bytes 786436
  19.7 5.2 %collective-permute-start.1 = (bf16[128,1024]{1,0:T(8,128)(2,1)S(1)}, bf16[128,1024]{1,0:T(8,128)(2,1)S(1)}, u32[]{:S(2)}, u32[]{:S(2)}) collective-permute-start(bf16[128,1024]{1,0:T(8,128)(2,1)S(1)} %collective-permute-done.refs_2_), channel_id=1, source_target_pairs={{2,4},{3,5},{4,6},{5,7},{10,12},{11,13},{12,14},{13,15},{18,20},{1... | collective-permute-start | bytes 786440 | tf_op jit(solution)/shard_map/ppermute | solution.py:468
  20.4 4.5 %collective-permute-start.3 = (bf16[128,1024]{1,0:T(8,128)(2,1)S(1)}, bf16[128,1024]{1,0:T(8,128)(2,1)S(1)}, u32[]{:S(2)}, u32[]{:S(2)}) collective-permute-start(bf16[128,1024]{1,0:T(8,128)(2,1)S(1)} %collective-permute-done.refs_2_), channel_id=1, source_target_pairs={{2,3},{3,2},{4,5},{5,4},{6,7},{7,6},{10,11},{11,10},{12,13},{13,12... | collective-permute-start | bytes 786440 | tf_op jit(solution)/shard_map/ppermute | solution.py:477
  24.9 6.7 %copy-start.4 = (bf16[128,1024]{1,0:T(8,128)(2,1)}, bf16[128,1024]{1,0:T(8,128)(2,1)S(1)}, u32[]{:S(2)}) copy-start(bf16[128,1024]{1,0:T(8,128)(2,1)S(1)} %collective-permute-done.2.refs_1_) | copy-start | bytes 786436
  24.9 6.7 %copy-start.5 = (bf16[128,1024]{1,0:T(8,128)(2,1)}, bf16[128,1024]{1,0:T(8,128)(2,1)S(1)}, u32[]{:S(2)}) copy-start(bf16[128,1024]{1,0:T(8,128)(2,1)S(1)} %collective-permute-done.1.refs_4_) | copy-start | bytes 786436
  24.9 6.7 %copy-start.6 = (bf16[128,1024]{1,0:T(8,128)(2,1)}, bf16[128,1024]{1,0:T(8,128)(2,1)S(1)}, u32[]{:S(2)}) copy-start(bf16[128,1024]{1,0:T(8,128)(2,1)S(1)} %collective-permute-done.3.refs_3_) | copy-start | bytes 786436
  25.0 1.4 collective-permute-start.4
  25.6 0.7 collective-permute-start.5
  26.3 5.2 %copy-start.7 = (bf16[128,1024]{1,0:T(8,128)(2,1)}, bf16[128,1024]{1,0:T(8,128)(2,1)S(1)}, u32[]{:S(2)}) copy-start(bf16[128,1024]{1,0:T(8,128)(2,1)S(1)} %collective-permute-done.4.refs_6_) | copy-start | bytes 786436
  26.4 5.2 %copy-start.8 = (bf16[128,1024]{1,0:T(8,128)(2,1)}, bf16[128,1024]{1,0:T(8,128)(2,1)S(1)}, u32[]{:S(2)}) copy-start(bf16[128,1024]{1,0:T(8,128)(2,1)S(1)} %collective-permute-done.5.refs_5_) | copy-start | bytes 786436
  26.4 5.2 %collective-permute-start.6 = (bf16[128,1024]{1,0:T(8,128)(2,1)S(1)}, bf16[128,1024]{1,0:T(8,128)(2,1)S(1)}, u32[]{:S(2)}, u32[]{:S(2)}) collective-permute-start(bf16[128,1024]{1,0:T(8,128)(2,1)S(1)} %collective-permute-done.4.refs_6_), channel_id=1, source_target_pairs={{6,7},{7,6},{14,15},{15,14},{22,23},{23,22},{30,31},{31,30}} | collective-permute-start | bytes 786440 | tf_op jit(solution)/shard_map/ppermute | solution.py:477
  27.1 40.3 %all-to-all-start.1 = ((bf16[8,40,2048]{2,1,0:T(8,128)(2,1)}), bf16[8,40,2048]{2,1,0:T(8,128)(2,1)S(1)}, u32[]{:S(2)}, u32[]{:S(2)}) async-start(bf16[8,40,2048]{2,1,0:T(8,128)(2,1)} %bitcast.16), calls=%async_computation.2 | async-start | bytes 2621440 | tf_op jit(solution)/shard_map/all_to_all | solution.py:507
  30.8 61.5 %all-gather.5.cloned.1.call-start = ((), (), s32[]{:S(2)}) async-start(), calls=%async_computation.6 | async-start | bytes 1310720 | tf_op jit(solution)/shard_map/all_gather | solution.py:502
  31.5 0.7 copy-start.9
  38.8 28.5 %collective-permute-start.7 = (bf16[512,512]{1,0:T(8,128)(2,1)}, bf16[512,512]{1,0:T(8,128)(2,1)S(1)}, u32[]{:S(2)}, u32[]{:S(2)}) collective-permute-start(bf16[512,512]{1,0:T(8,128)(2,1)} %get-tuple-element.44), channel_id=1, source_target_pairs={{0,1},{1,0},{2,3},{3,2},{4,5},{5,4},{6,7},{7,6},{8,9},{9,8},{10,11... | collective-permute-start | bytes 1572872 | tf_op jit(solution)/shard_map/ppermute | solution.py:517
  67.4 0.8 copy-start.3
  67.4 1.3 copy-start.1
  68.7 28.4 %all-to-all-start = ((bf16[8,120,1024]{2,1,0:T(8,128)(2,1)}), bf16[8,120,1024]{2,1,0:T(8,128)(2,1)S(1)}, u32[]{:S(2)}, u32[]{:S(2)}) async-start(bf16[8,120,1024]{2,1,0:T(8,128)(2,1)} %bitcast.13), calls=%async_computation.1 | async-start | bytes 3932160 | tf_op jit(solution)/shard_map/all_to_all | solution.py:507
  72.3 59.6 %reduce-scatter.2.cloned.1.call-start = ((), (), s32[]{:S(2)}) async-start(), calls=%async_computation.5 | async-start | bytes 1966080 | tf_op jit(solution)/shard_map/reduce_scatter | solution.py:537
  97.1 1.3 copy-start
  98.4 41.9 %all-to-all-start.2 = ((bf16[8,120,1024]{2,1,0:T(8,128)(2,1)}), bf16[8,120,1024]{2,1,0:T(8,128)(2,1)}, u32[]{:S(2)}, u32[]{:S(2)}) async-start(bf16[8,120,1024]{2,1,0:T(8,128)(2,1)} %bitcast.14), calls=%async_computation.3 | async-start | bytes 3932160 | tf_op jit(solution)/shard_map/all_to_all | solution.py:507
  132.8 5.1 %collective-permute-start.8 = (bf16[128,512]{1,0:T(8,128)(2,1)S(1)}, bf16[128,512]{1,0:T(8,128)(2,1)S(1)}, u32[]{:S(2)}, u32[]{:S(2)}) collective-permute-start(bf16[128,512]{1,0:T(8,128)(2,1)S(1)} %slice.3), channel_id=1, source_target_pairs={{0,1},{1,0},{2,3},{3,2},{4,5},{5,4},{6,7},{7,6},{8,9},{9,8},{10,11... | collective-permute-start | bytes 393224 | tf_op jit(solution)/shard_map/ppermute | solution.py:517
  137.9 0.7 copy-start.10
Sparse Core Ops, SparseCore 0:
  25.1 38.5 all-gather.2
  65.2 27.0 all-gather.4
  94.6 37.2 reduce-scatter.1
